TPU v7x, 1024 devices: a whole 4x4x32 slice. The times are simulated.
1024 devices in a mesh: dp: 256 (over y, x, z_lo, core), fsdp: 4 (over z_hi).
Axes of the slice: x: 4, y: 4, z: 32 (z_hi: 4, z_lo: 8; z = z_hi * 8 + z_lo), core: 2. Of those that a mesh axis runs over, the one named last changes fastest.
Arguments:
- img_raw: bfloat16 [131072, 1536], P(('dp', 'fsdp')), may hold values from -0.15625 to 0.15625
- txt_raw: bfloat16 [131072, 1536], P(('dp', 'fsdp')), may hold values from -0.15625 to 0.15625
- logit_scale: float32 [], replicated, may hold values from 2 to 8
- logit_bias: float32 [], replicated, may hold values from -4 to -1
Outputs:
- img_grad: bfloat16 [131072, 1536], P(('dp', 'fsdp'))
- txt_grad: bfloat16 [131072, 1536], P(('dp', 'fsdp'))
All inputs are finite; a program needn't handle non-finite values.
Results may differ from a plain program's by a relative error of at most 0.015.
Values may be sent and summed in bfloat16 or wider, within the bound.
No kernel may reach another device: no remote copies, remote signals or barrier semaphores. Data moves between devices by JAX's collectives and lax.ppermute only.
A program may use at most 32 MiB of HBM per device.

v0:
```python
import jax
import jax.numpy as jnp
from jax import lax
from jax.sharding import PartitionSpec as P

HALF = 1


def shifted(block, axis, distance):
    devices = range(lax.axis_size(axis))
    route = [((i - distance) % len(devices), i) for i in devices]
    return lax.ppermute(block, axis, route)


def normalize(raw):
    values = raw.astype(jnp.float32)
    inverse = lax.rsqrt(jnp.sum(values * values, axis=-1, keepdims=True) + 1e-06)
    return (values * inverse, inverse)


def pair_terms(img_block, txt_low, logit_scale, logit_bias, labels):
    scores = lax.dot_general(
        img_block, txt_low, (((1,), (1,)), ((), ())), preferred_element_type=jnp.float32
    )
    logits = logit_scale * scores + logit_bias
    coef = (-labels * jax.nn.sigmoid(-labels * logits) * logit_scale).astype(jnp.bfloat16)
    img_term = jnp.dot(coef, txt_low, preferred_element_type=jnp.float32)
    txt_term = lax.dot_general(
        coef, img_block, (((0,), (0,)), ((), ())), preferred_element_type=jnp.float32
    )
    return (img_term, txt_term)


def local(img_raw, txt_raw, logit_scale, logit_bias):
    img_norm, img_inv = normalize(img_raw)
    txt_norm, txt_inv = normalize(txt_raw)
    img_low = img_norm.astype(jnp.bfloat16)
    txt_low = txt_norm.astype(jnp.bfloat16)
    img_block = lax.all_gather(img_low, "fsdp", axis=0, tiled=True)
    img_count = img_block.shape[0]
    txt_count = txt_raw.shape[0]
    first_row = lax.axis_index("fsdp") * txt_count
    positive = lax.broadcasted_iota(
        jnp.int32, (img_count, txt_count), 0
    ) == first_row + lax.broadcasted_iota(jnp.int32, (img_count, txt_count), 1)
    own_labels = jnp.where(positive, 1.0, -1.0).astype(jnp.float32)
    img_dir, own_term = pair_terms(img_block, txt_low, logit_scale, logit_bias, own_labels)
    negative = jnp.float32(-1.0)
    moving = shifted(txt_low, "dp", -HALF)
    term_list = []
    for offset in range(-HALF, HALF + 1):
        if offset > -HALF:
            moving = shifted(moving, "dp", 1)
        if offset == 0:
            term_list.append(own_term)
        else:
            img_term, txt_term = pair_terms(img_block, moving, logit_scale, logit_bias, negative)
            img_dir = img_dir + img_term
            term_list.append(txt_term)
    carried = jnp.zeros_like(own_term)
    for offset in range(HALF, -HALF - 1, -1):
        carried = carried + term_list[offset + HALF]
        if offset > -HALF:
            carried = shifted(carried.astype(jnp.bfloat16), "dp", -1).astype(carried.dtype)
    txt_dir = shifted(carried.astype(jnp.bfloat16), "dp", HALF).astype(carried.dtype)
    txt_inner = jnp.sum(txt_norm * txt_dir, axis=-1, keepdims=True)
    txt_grad = ((txt_dir - txt_norm * txt_inner) * txt_inv).astype(jnp.bfloat16)
    own_dir = lax.psum_scatter(
        img_dir.astype(jnp.bfloat16), "fsdp", scatter_dimension=0, tiled=True
    ).astype(jnp.float32)
    img_inner = jnp.sum(img_norm * own_dir, axis=-1, keepdims=True)
    img_grad = ((own_dir - img_norm * img_inner) * img_inv).astype(jnp.bfloat16)
    return (img_grad, txt_grad)


def solution(mesh):
    in_specs = (P(("dp", "fsdp"), None), P(("dp", "fsdp"), None), P(), P())
    out_specs = (P(("dp", "fsdp"), None), P(("dp", "fsdp"), None))
    return jax.shard_map(local, mesh=mesh, in_specs=in_specs, out_specs=out_specs, check_vma=False)
```

profile of v0, /device:TPU:52, one launch (start us, length us, event | category | flops | bytes accessed | tf_op | source)
XLA Modules:
  0.0 328.4 jit_solution(5851429460594015295)
XLA Ops:
  7.2 0.0 copy-start.1
  7.2 0.0 all-gather.2.cloned.1.call-start
  7.2 1.2 fusion.28
  8.4 1.9 fusion.27
  10.3 0.0 all-gather.2.cloned.1.call-update
  10.3 0.0 reduce-scatter.2.cloned.1.call-start
  10.4 0.0 copy-done.1
  10.4 0.2 fusion.29
  10.6 0.1 fusion.25
  10.7 1.9 collective-permute-start
  12.6 5.3 %collective-permute-done = bf16[128,1536]{1,0:T(8,128)(2,1)S(1)} collective-permute-done((bf16[128,1536]{1,0:T(8,128)(2,1)S(1)}, bf16[128,1536]{1,0:T(8,128)(2,1)S(1)}, u32[]{:S(2)}, u32[]{:S(2)}) %collective-permute-start) | collective-permute-done | bytes 393248 | tf_op jit(solution)/shard_map/ppermute | solution.py:12
  17.9 4.1 %collective-permute-start.1 = (bf16[128,1536]{1,0:T(8,128)(2,1)S(1)}, bf16[128,1536]{1,0:T(8,128)(2,1)}, u32[]{:S(2)}, u32[]{:S(2)}) collective-permute-start(bf16[128,1536]{1,0:T(8,128)(2,1)S(1)} %collective-permute-done), channel_id=1, source_target_pairs={{1020,0},{0,4},{4,8},{8,12},{12,16},{16,20},{20,24},{24,28},{28,32... | collective-permute-start | bytes 1179656 | tf_op jit(solution)/shard_map/ppermute | solution.py:12
  23.3 6.1 %collective-permute-done.1 = bf16[128,1536]{1,0:T(8,128)(2,1)} collective-permute-done((bf16[128,1536]{1,0:T(8,128)(2,1)S(1)}, bf16[128,1536]{1,0:T(8,128)(2,1)}, u32[]{:S(2)}, u32[]{:S(2)}) %collective-permute-start.1) | collective-permute-done | bytes 393248 | tf_op jit(solution)/shard_map/ppermute | solution.py:12
  29.5 3.4 %collective-permute-start.2 = (bf16[128,1536]{1,0:T(8,128)(2,1)}, bf16[128,1536]{1,0:T(8,128)(2,1)S(1)}, u32[]{:S(2)}, u32[]{:S(2)}) collective-permute-start(bf16[128,1536]{1,0:T(8,128)(2,1)} %collective-permute-done.1), channel_id=1, source_target_pairs={{1020,0},{0,4},{4,8},{8,12},{12,16},{16,20},{20,24},{24,28},{28,32... | collective-permute-start | bytes 1179656 | tf_op jit(solution)/shard_map/ppermute | solution.py:12
  32.8 130.6 %all-gather.2.cloned.1.call-done = bf16[512,1536]{1,0:T(8,128)(2,1)} async-done(((bf16[128,1536]{1,0:T(8,128)(2,1)}), bf16[512,1536]{1,0:T(8,128)(2,1)}) %all-gather.2.cloned.1.call-update) | async-done | bytes 1572880 | tf_op jit(solution)/shard_map/all_gather | solution.py:39
  163.4 0.0 copy-start
  163.4 2.1 fusion.21
  165.5 0.0 copy-done
  165.5 0.6 fusion.22
  166.1 0.6 fusion.36
  166.7 0.0 collective-permute-done.2
  166.7 0.6 fusion.23
  167.3 0.6 convolution_add_fusion.1
  167.8 1.7 fusion
  169.6 0.0 reduce-scatter.2.cloned.1.call-update
  169.6 0.4 convolution_convert_fusion
  170.0 1.9 collective-permute-start.3
  171.9 5.3 %collective-permute-done.3 = bf16[128,1536]{1,0:T(8,128)(2,1)S(1)} collective-permute-done((bf16[128,1536]{1,0:T(8,128)(2,1)S(1)}, bf16[128,1536]{1,0:T(8,128)(2,1)S(1)}, u32[]{:S(2)}, u32[]{:S(2)}) %collective-permute-start.3) | collective-permute-done | bytes 393248 | tf_op jit(solution)/shard_map/ppermute | solution.py:12
  177.2 0.4 add_convert_fusion.1
  177.6 3.8 %collective-permute-start.4 = (bf16[128,1536]{1,0:T(8,128)(2,1)S(1)}, bf16[128,1536]{1,0:T(8,128)(2,1)S(1)}, u32[]{:S(2)}, u32[]{:S(2)}) collective-permute-start(bf16[128,1536]{1,0:T(8,128)(2,1)S(1)} %add_convert_fusion.1), channel_id=1, source_target_pairs={{4,0},{8,4},{12,8},{16,12},{20,16},{24,20},{28,24},{32,28},{36,32}... | collective-permute-start | bytes 1179656 | tf_op jit(solution)/shard_map/ppermute | solution.py:12
  181.4 0.4 fusion.37
  181.8 0.0 copy-start.2
  181.8 4.9 %collective-permute-done.4 = bf16[128,1536]{1,0:T(8,128)(2,1)S(1)} collective-permute-done((bf16[128,1536]{1,0:T(8,128)(2,1)S(1)}, bf16[128,1536]{1,0:T(8,128)(2,1)S(1)}, u32[]{:S(2)}, u32[]{:S(2)}) %collective-permute-start.4) | collective-permute-done | bytes 393248 | tf_op jit(solution)/shard_map/ppermute | solution.py:12
  186.7 0.1 add_convert_fusion
  186.8 3.8 %collective-permute-start.5 = (bf16[128,1536]{1,0:T(8,128)(2,1)S(1)}, bf16[128,1536]{1,0:T(8,128)(2,1)S(1)}, u32[]{:S(2)}, u32[]{:S(2)}) collective-permute-start(bf16[128,1536]{1,0:T(8,128)(2,1)S(1)} %add_convert_fusion), channel_id=1, source_target_pairs={{1020,0},{0,4},{4,8},{8,12},{12,16},{16,20},{20,24},{24,28},{28,32... | collective-permute-start | bytes 1179656 | tf_op jit(solution)/shard_map/ppermute | solution.py:12
  190.6 16.8 %collective-permute-done.5 = bf16[128,1536]{1,0:T(8,128)(2,1)S(1)} collective-permute-done((bf16[128,1536]{1,0:T(8,128)(2,1)S(1)}, bf16[128,1536]{1,0:T(8,128)(2,1)S(1)}, u32[]{:S(2)}, u32[]{:S(2)}) %collective-permute-start.5) | collective-permute-done | bytes 393248 | tf_op jit(solution)/shard_map/ppermute | solution.py:12
  207.4 0.3 fusion.33
  207.7 1.1 fusion.35
  208.8 109.4 %reduce-scatter.2.cloned.1.call-done = bf16[128,1536]{1,0:T(8,128)(2,1)} async-done(((bf16[512,1536]{1,0:T(8,128)(2,1)}), bf16[128,1536]{1,0:T(8,128)(2,1)}) %reduce-scatter.2.cloned.1.call-update) | async-done | bytes 393232 | tf_op jit(solution)/shard_map/reduce_scatter | solution.py:68
  318.2 0.0 copy-done.2
  318.2 1.3 fusion.30
  319.5 2.1 fusion.32
  (3 shorter events, 0.0 us)
Async XLA Ops:
  7.2 3.2 copy-start.1
  7.2 156.2 %all-gather.2.cloned.1.call-start = ((), (), s32[]{:S(2)}) async-start(), calls=%async_computation.1 | async-start | bytes 1966080 | tf_op jit(solution)/shard_map/all_gather | solution.py:39
  10.3 307.8 %reduce-scatter.2.cloned.1.call-start = ((), (), s32[]{:S(2)}) async-start(), calls=%async_computation.2 | async-start | bytes 1966080 | tf_op jit(solution)/shard_map/reduce_scatter | solution.py:68
  10.7 7.2 %collective-permute-start = (bf16[128,1536]{1,0:T(8,128)(2,1)S(1)}, bf16[128,1536]{1,0:T(8,128)(2,1)S(1)}, u32[]{:S(2)}, u32[]{:S(2)}) collective-permute-start(bf16[128,1536]{1,0:T(8,128)(2,1)S(1)} %fusion.25), channel_id=1, source_target_pairs={{4,0},{8,4},{12,8},{16,12},{20,16},{24,20},{28,24},{32,28},{36,32}... | collective-permute-start | bytes 1179656 | tf_op jit(solution)/shard_map/ppermute | solution.py:12
  17.9 11.6 %collective-permute-start.1 = (bf16[128,1536]{1,0:T(8,128)(2,1)S(1)}, bf16[128,1536]{1,0:T(8,128)(2,1)}, u32[]{:S(2)}, u32[]{:S(2)}) collective-permute-start(bf16[128,1536]{1,0:T(8,128)(2,1)S(1)} %collective-permute-done), channel_id=1, source_target_pairs={{1020,0},{0,4},{4,8},{8,12},{12,16},{16,20},{20,24},{24,28},{28,32... | collective-permute-start | bytes 1179656 | tf_op jit(solution)/shard_map/ppermute | solution.py:12
  29.5 137.2 %collective-permute-start.2 = (bf16[128,1536]{1,0:T(8,128)(2,1)}, bf16[128,1536]{1,0:T(8,128)(2,1)S(1)}, u32[]{:S(2)}, u32[]{:S(2)}) collective-permute-start(bf16[128,1536]{1,0:T(8,128)(2,1)} %collective-permute-done.1), channel_id=1, source_target_pairs={{1020,0},{0,4},{4,8},{8,12},{12,16},{16,20},{20,24},{24,28},{28,32... | collective-permute-start | bytes 1179656 | tf_op jit(solution)/shard_map/ppermute | solution.py:12
  163.4 2.1 copy-start
  170.0 7.2 %collective-permute-start.3 = (bf16[128,1536]{1,0:T(8,128)(2,1)S(1)}, bf16[128,1536]{1,0:T(8,128)(2,1)S(1)}, u32[]{:S(2)}, u32[]{:S(2)}) collective-permute-start(bf16[128,1536]{1,0:T(8,128)(2,1)S(1)} %convolution_convert_fusion), channel_id=1, source_target_pairs={{4,0},{8,4},{12,8},{16,12},{20,16},{24,20},{28,24},{32,28},{36,32}... | collective-permute-start | bytes 1179656 | tf_op jit(solution)/shard_map/ppermute | solution.py:12
  177.6 9.1 %collective-permute-start.4 = (bf16[128,1536]{1,0:T(8,128)(2,1)S(1)}, bf16[128,1536]{1,0:T(8,128)(2,1)S(1)}, u32[]{:S(2)}, u32[]{:S(2)}) collective-permute-start(bf16[128,1536]{1,0:T(8,128)(2,1)S(1)} %add_convert_fusion.1), channel_id=1, source_target_pairs={{4,0},{8,4},{12,8},{16,12},{20,16},{24,20},{28,24},{32,28},{36,32}... | collective-permute-start | bytes 1179656 | tf_op jit(solution)/shard_map/ppermute | solution.py:12
  181.8 136.4 %copy-start.2 = (bf16[128,1536]{1,0:T(8,128)(2,1)S(1)}, bf16[128,1536]{1,0:T(8,128)(2,1)}, u32[]{:S(2)}) copy-start(bf16[128,1536]{1,0:T(8,128)(2,1)} %param.4) | copy-start | bytes 1179652
  186.8 20.7 %collective-permute-start.5 = (bf16[128,1536]{1,0:T(8,128)(2,1)S(1)}, bf16[128,1536]{1,0:T(8,128)(2,1)S(1)}, u32[]{:S(2)}, u32[]{:S(2)}) collective-permute-start(bf16[128,1536]{1,0:T(8,128)(2,1)S(1)} %add_convert_fusion), channel_id=1, source_target_pairs={{1020,0},{0,4},{4,8},{8,12},{12,16},{16,20},{20,24},{24,28},{28,32... | collective-permute-start | bytes 1179656 | tf_op jit(solution)/shard_map/ppermute | solution.py:12
Sparse Core Ops, SparseCore 0:
  11.3 152.0 all-gather.1
  169.7 148.4 reduce-scatter.1
where the time goes:
time: 329 us; the launch traced here: 328 us
  waiting for transfers between devices  278 us (84%)
  starting transfers between devices  19 us (6%)
  between operations  15.5 us (5%)
  other arithmetic  8.15 us (2%)
  matrix products  7.29 us (2%)
    all_gather x1, waiting for transfers between devices, local(): img_block = lax.all_gather(img_low, 'fsdp', axis=0, tiled=True)  131 us
    reduce_scatter x1, waiting for transfers between devices, local(): lax.psum_scatter(img_dir.astype(jnp.bfloat16), 'fsdp', scatter_dimension=...  109 us
    ppermute x6, waiting for transfers between devices, shifted(): return lax.ppermute(block, axis, route)  38.4 us
    ppermute x6, starting transfers between devices, shifted(): return lax.ppermute(block, axis, route)  18.9 us
  transfers between devices with their start and end apart: 8, of which 7 were waited for; matrix products, arithmetic and copies ran while one was open for 2% of the time, Pallas kernels for 0%

commit v1 on v0

v1 whole, which is shorter than its diff:
```python
import jax
import jax.numpy as jnp
from jax import lax
from jax.sharding import PartitionSpec as P

AXES = ("dp", "fsdp")
SPAN = 16


def device_of(block, role, blocks, ways):
    block = block % blocks
    return block * ways + (role + block // SPAN) % ways


def routes(blocks, ways):
    img, txt, ahead, back = [], [], [], []
    for block in range(blocks):
        for role in range(ways):
            here = device_of(block, role, blocks, ways)
            img.append((here, device_of(block, role ^ 1, blocks, ways)))
            txt.append((here, device_of(block, ways - 1 - role, blocks, ways)))
            ahead.append((here, device_of(block + 1, role, blocks, ways)))
            back.append((here, device_of(block - 1, role, blocks, ways)))
    return img, txt, ahead, back


def normalize(raw):
    values = raw.astype(jnp.float32)
    inverse = lax.rsqrt(jnp.sum(values * values, axis=-1, keepdims=True) + 1e-06)
    return (values * inverse, inverse)


def low(raw):
    return normalize(raw)[0].astype(jnp.bfloat16)


def grad_of(raw, direction):
    norm, inverse = normalize(raw)
    inner = jnp.sum(norm * direction, axis=-1, keepdims=True)
    return ((direction - norm * inner) * inverse).astype(jnp.bfloat16)


def pair_coef(img, txt, logit_scale, logit_bias, labels):
    scores = lax.dot_general(
        img, txt, (((1,), (1,)), ((), ())), preferred_element_type=jnp.float32
    )
    logits = logit_scale * scores + logit_bias
    return (-labels * jax.nn.sigmoid(-labels * logits) * logit_scale).astype(jnp.bfloat16)


def img_part(coef, txt):
    return jnp.dot(coef, txt, preferred_element_type=jnp.float32)


def txt_part(coef, img):
    return lax.dot_general(
        coef, img, (((0,), (0,)), ((), ())), preferred_element_type=jnp.float32
    )


def local(img_raw, txt_raw, logit_scale, logit_bias, moves):
    to_img, to_txt, ahead, back = moves
    rows = img_raw.shape[0]
    txt_far = lax.ppermute(txt_raw, AXES, to_txt)
    img_far = lax.ppermute(img_raw, AXES, to_img)
    prev_own = lax.ppermute(txt_raw, AXES, ahead)
    next_own = lax.ppermute(txt_raw, AXES, back)
    prev_far = lax.ppermute(txt_far, AXES, ahead)
    next_far = lax.ppermute(txt_far, AXES, back)

    img = jnp.concatenate([low(img_raw), low(img_far)])
    txt = jnp.concatenate([low(txt_raw), low(txt_far)])
    prev = jnp.concatenate([low(prev_own), low(prev_far)])
    following = jnp.concatenate([low(next_own), low(next_far)])

    shape = (2 * rows, 2 * rows)
    first = lax.broadcasted_iota(jnp.int32, shape, 0)
    positive = (first == lax.broadcasted_iota(jnp.int32, shape, 1)) & (first < rows)
    labels = jnp.where(positive, 1.0, -1.0).astype(jnp.float32)
    negative = jnp.float32(-1.0)
    coef_prev = pair_coef(img, prev, logit_scale, logit_bias, negative)
    coef_next = pair_coef(img, following, logit_scale, logit_bias, negative)
    coef_own = pair_coef(img, txt, logit_scale, logit_bias, labels)

    to_prev = txt_part(coef_prev, img).astype(jnp.bfloat16)
    to_next = txt_part(coef_next, img).astype(jnp.bfloat16)
    from_next_far = lax.ppermute(to_prev[rows:], AXES, back)
    from_prev_far = lax.ppermute(to_next[rows:], AXES, ahead)
    img_dir = img_part(coef_prev, prev) + img_part(coef_own, txt) + img_part(coef_next, following)
    img_there = lax.ppermute(img_dir[rows:].astype(jnp.bfloat16), AXES, to_img)
    from_next_own = lax.ppermute(to_prev[:rows], AXES, back)
    from_prev_own = lax.ppermute(to_next[:rows], AXES, ahead)
    own = txt_part(coef_own, img)
    far_sum = own[rows:] + from_next_far.astype(jnp.float32) + from_prev_far.astype(jnp.float32)
    txt_there = lax.ppermute(far_sum.astype(jnp.bfloat16), AXES, to_txt)
    own_sum = own[:rows] + from_next_own.astype(jnp.float32) + from_prev_own.astype(jnp.float32)

    img_grad = grad_of(img_raw, img_dir[:rows] + img_there.astype(jnp.float32))
    txt_grad = grad_of(txt_raw, own_sum + txt_there.astype(jnp.float32))
    return (img_grad, txt_grad)


def solution(mesh):
    moves = routes(mesh.shape["dp"], mesh.shape["fsdp"])
    in_specs = (P(AXES, None), P(AXES, None), P(), P())
    out_specs = (P(AXES, None), P(AXES, None))

    def step(*args):
        return local(*args, moves)

    return jax.shard_map(step, mesh=mesh, in_specs=in_specs, out_specs=out_specs, check_vma=False)
```

time: 329 us -> 228 us (0.69)
  the two profiles are of different devices: /device:TPU:52 before, /device:TPU:24 now
where the time goes in v1:
time: 228 us; the launch traced here: 226 us
  waiting for transfers between devices  137 us (60%)
  starting transfers between devices  74.8 us (33%)
  other arithmetic  8.38 us (4%)
  matrix products  3.57 us (2%)
    ppermute x1, waiting for transfers between devices, local(): img_far = lax.ppermute(img_raw, AXES, to_img)  66.3 us
    ppermute x1, waiting for transfers between devices, local(): from_prev_far = lax.ppermute(to_next[rows:], AXES, ahead)  51.8 us
    ppermute x1, starting transfers between devices, local(): txt_far = lax.ppermute(txt_raw, AXES, to_txt)  23 us
    ppermute x1, waiting for transfers between devices, local(): txt_there = lax.ppermute(far_sum.astype(jnp.bfloat16), AXES, to_txt)  9.7 us
    ppermute x1, starting transfers between devices, local(): img_far = lax.ppermute(img_raw, AXES, to_img)  8.45 us
    ppermute x1, starting transfers between devices, local(): from_next_far = lax.ppermute(to_prev[rows:], AXES, back)  8.03 us
    ppermute x1, starting transfers between devices, local(): next_own = lax.ppermute(txt_raw, AXES, back)  7.86 us
    ppermute x1, starting transfers between devices, local(): next_far = lax.ppermute(txt_far, AXES, back)  7.86 us
  transfers between devices with their start and end apart: 12, of which 6 were waited for; matrix products, arithmetic and copies ran while one was open for 4% of the time, Pallas kernels for 0%

profile of v1, /device:TPU:24, one launch (start us, length us, event | category | flops | bytes accessed | tf_op | source)
XLA Modules:
  0.0 225.9 jit_solution(1153942626600720652)
XLA Ops:
  0.6 23.0 %collective-permute-start.2 = (bf16[128,1536]{1,0:T(8,128)(2,1)}, bf16[128,1536]{1,0:T(8,128)(2,1)S(1)}, u32[]{:S(2)}, u32[]{:S(2)}) collective-permute-start(bf16[128,1536]{1,0:T(8,128)(2,1)} %param.5), channel_id=1, source_target_pairs={{0,3},{1,2},{2,1},{3,0},{4,7},{5,6},{6,5},{7,4},{8,11},{9,10},{10,... | collective-permute-start | bytes 1179656 | tf_op jit(solution)/shard_map/ppermute | solution.py:64
  23.6 1.9 collective-permute-start.1
  25.6 7.9 %collective-permute-start.4 = (bf16[128,1536]{1,0:T(8,128)(2,1)}, bf16[128,1536]{1,0:T(8,128)(2,1)S(1)}, u32[]{:S(2)}, u32[]{:S(2)}) collective-permute-start(bf16[128,1536]{1,0:T(8,128)(2,1)} %param.5), channel_id=1, source_target_pairs={{0,1023},{1,1020},{2,1021},{3,1022},{4,0},{5,1},{6,2},{7,3},{8,4},... | collective-permute-start | bytes 1179656 | tf_op jit(solution)/shard_map/ppermute | solution.py:67
  33.4 8.4 %collective-permute-start = (bf16[128,1536]{1,0:T(8,128)(2,1)}, bf16[128,1536]{1,0:T(8,128)(2,1)S(1)}, u32[]{:S(2)}, u32[]{:S(2)}) collective-permute-start(bf16[128,1536]{1,0:T(8,128)(2,1)} %param.4), channel_id=1, source_target_pairs={{0,1},{1,0},{2,3},{3,2},{4,5},{5,4},{6,7},{7,6},{8,9},{9,8},{10,11... | collective-permute-start | bytes 1179656 | tf_op jit(solution)/shard_map/ppermute | solution.py:65
  41.9 1.2 fusion.44
  43.1 1.2 fusion.33
  44.2 1.3 fusion.25
  46.9 0.2 fusion.36
  47.0 66.3 %collective-permute-done = bf16[128,1536]{1,0:T(8,128)(2,1)S(1)} collective-permute-done((bf16[128,1536]{1,0:T(8,128)(2,1)}, bf16[128,1536]{1,0:T(8,128)(2,1)S(1)}, u32[]{:S(2)}, u32[]{:S(2)}) %collective-permute-start) | collective-permute-done | bytes 393248 | tf_op jit(solution)/shard_map/ppermute | solution.py:65
  113.3 0.2 fusion.34
  113.5 0.2 fusion.45
  113.7 0.2 fusion.47
  113.9 0.1 fusion.35
  114.0 0.1 fusion.46
  114.1 0.4 fusion.21
  114.6 0.4 fusion.63
  115.0 1.9 collective-permute-start.3
  116.9 7.9 %collective-permute-start.5 = (bf16[128,1536]{1,0:T(8,128)(2,1)S(1)}, bf16[128,1536]{1,0:T(8,128)(2,1)S(1)}, u32[]{:S(2)}, u32[]{:S(2)}) collective-permute-start(bf16[128,1536]{1,0:T(8,128)(2,1)S(1)} %collective-permute-done.2), channel_id=1, source_target_pairs={{0,1023},{1,1020},{2,1021},{3,1022},{4,0},{5,1},{6,2},{7,3},{8,4},... | collective-permute-start | bytes 1179656 | tf_op jit(solution)/shard_map/ppermute | solution.py:69
  124.8 0.1 fusion.37
  124.9 0.1 fusion.48
  125.1 3.2 %collective-permute-done.3 = bf16[128,1536]{1,0:T(8,128)(2,1)S(1)} collective-permute-done((bf16[128,1536]{1,0:T(8,128)(2,1)S(1)}, bf16[128,1536]{1,0:T(8,128)(2,1)S(1)}, u32[]{:S(2)}, u32[]{:S(2)}) %collective-permute-start.3) | collective-permute-done | bytes 393248 | tf_op jit(solution)/shard_map/ppermute | solution.py:68
  128.3 0.2 fusion.38
  128.5 0.1 fusion.39
  128.6 0.4 fusion.22
  129.0 0.4 convolution_convert_fusion.1
  129.4 0.4 fusion.55
  129.8 0.2 collective-permute-done.5
  130.0 0.2 fusion.49
  130.2 0.1 fusion.50
  130.4 0.4 fusion.20
  130.8 0.4 convolution_convert_fusion
  131.2 0.1 fusion.65
  131.3 1.9 collective-permute-start.10
  133.2 8.0 %collective-permute-start.9 = (bf16[128,1536]{1,0:T(8,128)(2,1)S(1)}, bf16[128,1536]{1,0:T(8,128)(2,1)S(1)}, u32[]{:S(2)}, u32[]{:S(2)}) collective-permute-start(bf16[128,1536]{1,0:T(8,128)(2,1)S(1)} %get-tuple-element.3), channel_id=1, source_target_pairs={{0,1023},{1,1020},{2,1021},{3,1022},{4,0},{5,1},{6,2},{7,3},{8,4},... | collective-permute-start | bytes 1179656 | tf_op jit(solution)/shard_map/ppermute | solution.py:87
  141.3 0.4 convolution_add_fusion.1
  141.7 0.4 convolution_add_fusion
  142.1 2.1 collective-permute-start.6
  144.2 1.9 collective-permute-start.8
  146.1 7.9 %collective-permute-start.7 = (bf16[128,1536]{1,0:T(8,128)(2,1)S(1)}, bf16[128,1536]{1,0:T(8,128)(2,1)S(1)}, u32[]{:S(2)}, u32[]{:S(2)}) collective-permute-start(bf16[128,1536]{1,0:T(8,128)(2,1)S(1)} %get-tuple-element.2), channel_id=1, source_target_pairs={{0,1023},{1,1020},{2,1021},{3,1022},{4,0},{5,1},{6,2},{7,3},{8,4},... | collective-permute-start | bytes 1179656 | tf_op jit(solution)/shard_map/ppermute | solution.py:91
  154.0 51.8 %collective-permute-done.10 = bf16[128,1536]{1,0:T(8,128)(2,1)S(1)} collective-permute-done((bf16[128,1536]{1,0:T(8,128)(2,1)S(1)}, bf16[128,1536]{1,0:T(8,128)(2,1)S(1)}, u32[]{:S(2)}, u32[]{:S(2)}) %collective-permute-start.10) | collective-permute-done | bytes 393248 | tf_op jit(solution)/shard_map/ppermute | solution.py:88
  205.8 0.1 fusion.52
  205.9 2.1 collective-permute-start.11
  208.0 5.4 %collective-permute-done.6 = bf16[128,1536]{1,0:T(8,128)(2,1)S(1)} collective-permute-done((bf16[128,1536]{1,0:T(8,128)(2,1)S(1)}, bf16[128,1536]{1,0:T(8,128)(2,1)S(1)}, u32[]{:S(2)}, u32[]{:S(2)}) %collective-permute-start.6) | collective-permute-done | bytes 393248 | tf_op jit(solution)/shard_map/ppermute | solution.py:90
  213.4 0.3 fusion.29
  213.7 1.1 fusion.32
  214.8 9.7 %collective-permute-done.11 = bf16[128,1536]{1,0:T(8,128)(2,1)S(1)} collective-permute-done((bf16[128,1536]{1,0:T(8,128)(2,1)S(1)}, bf16[128,1536]{1,0:T(8,128)(2,1)S(1)}, u32[]{:S(2)}, u32[]{:S(2)}) %collective-permute-start.11) | collective-permute-done | bytes 393248 | tf_op jit(solution)/shard_map/ppermute | solution.py:95
  224.5 0.3 fusion.40
  224.8 1.1 fusion.43
  (21 shorter events, 0.2 us)
Async XLA Ops:
  0.6 112.9 %collective-permute-start.2 = (bf16[128,1536]{1,0:T(8,128)(2,1)}, bf16[128,1536]{1,0:T(8,128)(2,1)S(1)}, u32[]{:S(2)}, u32[]{:S(2)}) collective-permute-start(bf16[128,1536]{1,0:T(8,128)(2,1)} %param.5), channel_id=1, source_target_pairs={{0,3},{1,2},{2,1},{3,0},{4,7},{5,6},{6,5},{7,4},{8,11},{9,10},{10,... | collective-permute-start | bytes 1179656 | tf_op jit(solution)/shard_map/ppermute | solution.py:64
  23.6 23.2 %collective-permute-start.1 = (bf16[128,1536]{1,0:T(8,128)(2,1)}, bf16[128,1536]{1,0:T(8,128)(2,1)S(1)}, u32[]{:S(2)}, u32[]{:S(2)}) collective-permute-start(bf16[128,1536]{1,0:T(8,128)(2,1)} %param.5), channel_id=1, source_target_pairs={{0,4},{1,5},{2,6},{3,7},{4,8},{5,9},{6,10},{7,11},{8,12},{9,13},{1... | collective-permute-start | bytes 1179656 | tf_op jit(solution)/shard_map/ppermute | solution.py:66
  25.6 88.1 %collective-permute-start.4 = (bf16[128,1536]{1,0:T(8,128)(2,1)}, bf16[128,1536]{1,0:T(8,128)(2,1)S(1)}, u32[]{:S(2)}, u32[]{:S(2)}) collective-permute-start(bf16[128,1536]{1,0:T(8,128)(2,1)} %param.5), channel_id=1, source_target_pairs={{0,1023},{1,1020},{2,1021},{3,1022},{4,0},{5,1},{6,2},{7,3},{8,4},... | collective-permute-start | bytes 1179656 | tf_op jit(solution)/shard_map/ppermute | solution.py:67
  33.4 79.9 %collective-permute-start = (bf16[128,1536]{1,0:T(8,128)(2,1)}, bf16[128,1536]{1,0:T(8,128)(2,1)S(1)}, u32[]{:S(2)}, u32[]{:S(2)}) collective-permute-start(bf16[128,1536]{1,0:T(8,128)(2,1)} %param.4), channel_id=1, source_target_pairs={{0,1},{1,0},{2,3},{3,2},{4,5},{5,4},{6,7},{7,6},{8,9},{9,8},{10,11... | collective-permute-start | bytes 1179656 | tf_op jit(solution)/shard_map/ppermute | solution.py:65
  115.0 13.3 %collective-permute-start.3 = (bf16[128,1536]{1,0:T(8,128)(2,1)S(1)}, bf16[128,1536]{1,0:T(8,128)(2,1)S(1)}, u32[]{:S(2)}, u32[]{:S(2)}) collective-permute-start(bf16[128,1536]{1,0:T(8,128)(2,1)S(1)} %collective-permute-done.2), channel_id=1, source_target_pairs={{0,4},{1,5},{2,6},{3,7},{4,8},{5,9},{6,10},{7,11},{8,12},{9,13},{1... | collective-permute-start | bytes 1179656 | tf_op jit(solution)/shard_map/ppermute | solution.py:68
  116.9 13.1 %collective-permute-start.5 = (bf16[128,1536]{1,0:T(8,128)(2,1)S(1)}, bf16[128,1536]{1,0:T(8,128)(2,1)S(1)}, u32[]{:S(2)}, u32[]{:S(2)}) collective-permute-start(bf16[128,1536]{1,0:T(8,128)(2,1)S(1)} %collective-permute-done.2), channel_id=1, source_target_pairs={{0,1023},{1,1020},{2,1021},{3,1022},{4,0},{5,1},{6,2},{7,3},{8,4},... | collective-permute-start | bytes 1179656 | tf_op jit(solution)/shard_map/ppermute | solution.py:69
  131.3 74.5 %collective-permute-start.10 = (bf16[128,1536]{1,0:T(8,128)(2,1)S(1)}, bf16[128,1536]{1,0:T(8,128)(2,1)S(1)}, u32[]{:S(2)}, u32[]{:S(2)}) collective-permute-start(bf16[128,1536]{1,0:T(8,128)(2,1)S(1)} %get-tuple-element.5), channel_id=1, source_target_pairs={{0,4},{1,5},{2,6},{3,7},{4,8},{5,9},{6,10},{7,11},{8,12},{9,13},{1... | collective-permute-start | bytes 1179656 | tf_op jit(solution)/shard_map/ppermute | solution.py:88
  133.2 72.6 %collective-permute-start.9 = (bf16[128,1536]{1,0:T(8,128)(2,1)S(1)}, bf16[128,1536]{1,0:T(8,128)(2,1)S(1)}, u32[]{:S(2)}, u32[]{:S(2)}) collective-permute-start(bf16[128,1536]{1,0:T(8,128)(2,1)S(1)} %get-tuple-element.3), channel_id=1, source_target_pairs={{0,1023},{1,1020},{2,1021},{3,1022},{4,0},{5,1},{6,2},{7,3},{8,4},... | collective-permute-start | bytes 1179656 | tf_op jit(solution)/shard_map/ppermute | solution.py:87
  142.0 71.4 %copy-start = (bf16[128,1536]{1,0:T(8,128)(2,1)S(1)}, bf16[128,1536]{1,0:T(8,128)(2,1)}, u32[]{:S(2)}) copy-start(bf16[128,1536]{1,0:T(8,128)(2,1)} %param.4) | copy-start | bytes 1179652
  142.1 71.3 %collective-permute-start.6 = (bf16[128,1536]{1,0:T(8,128)(2,1)S(1)}, bf16[128,1536]{1,0:T(8,128)(2,1)S(1)}, u32[]{:S(2)}, u32[]{:S(2)}) collective-permute-start(bf16[128,1536]{1,0:T(8,128)(2,1)S(1)} %slice.61), channel_id=1, source_target_pairs={{0,1},{1,0},{2,3},{3,2},{4,5},{5,4},{6,7},{7,6},{8,9},{9,8},{10,11... | collective-permute-start | bytes 1179656 | tf_op jit(solution)/shard_map/ppermute | solution.py:90
  144.2 70.6 %collective-permute-start.8 = (bf16[128,1536]{1,0:T(8,128)(2,1)S(1)}, bf16[128,1536]{1,0:T(8,128)(2,1)S(1)}, u32[]{:S(2)}, u32[]{:S(2)}) collective-permute-start(bf16[128,1536]{1,0:T(8,128)(2,1)S(1)} %get-tuple-element.4), channel_id=1, source_target_pairs={{0,4},{1,5},{2,6},{3,7},{4,8},{5,9},{6,10},{7,11},{8,12},{9,13},{1... | collective-permute-start | bytes 1179656 | tf_op jit(solution)/shard_map/ppermute | solution.py:92
  146.1 68.7 %collective-permute-start.7 = (bf16[128,1536]{1,0:T(8,128)(2,1)S(1)}, bf16[128,1536]{1,0:T(8,128)(2,1)S(1)}, u32[]{:S(2)}, u32[]{:S(2)}) collective-permute-start(bf16[128,1536]{1,0:T(8,128)(2,1)S(1)} %get-tuple-element.2), channel_id=1, source_target_pairs={{0,1023},{1,1020},{2,1021},{3,1022},{4,0},{5,1},{6,2},{7,3},{8,4},... | collective-permute-start | bytes 1179656 | tf_op jit(solution)/shard_map/ppermute | solution.py:91
  205.9 18.5 %copy-start.1 = (bf16[128,1536]{1,0:T(8,128)(2,1)S(1)}, bf16[128,1536]{1,0:T(8,128)(2,1)}, u32[]{:S(2)}) copy-start(bf16[128,1536]{1,0:T(8,128)(2,1)} %param.5) | copy-start | bytes 1179652
  205.9 18.5 %collective-permute-start.11 = (bf16[128,1536]{1,0:T(8,128)(2,1)S(1)}, bf16[128,1536]{1,0:T(8,128)(2,1)S(1)}, u32[]{:S(2)}, u32[]{:S(2)}) collective-permute-start(bf16[128,1536]{1,0:T(8,128)(2,1)S(1)} %fusion.52), channel_id=1, source_target_pairs={{0,3},{1,2},{2,1},{3,0},{4,7},{5,6},{6,5},{7,4},{8,11},{9,10},{10,... | collective-permute-start | bytes 1179656 | tf_op jit(solution)/shard_map/ppermute | solution.py:95

commit v2 on v1

--- a/solution.py
+++ b/solution.py
@@ -63,40 +63,41 @@
     rows = img_raw.shape[0]
     txt_far = lax.ppermute(txt_raw, AXES, to_txt)
     img_far = lax.ppermute(img_raw, AXES, to_img)
-    prev_own = lax.ppermute(txt_raw, AXES, ahead)
-    next_own = lax.ppermute(txt_raw, AXES, back)
-    prev_far = lax.ppermute(txt_far, AXES, ahead)
-    next_far = lax.ppermute(txt_far, AXES, back)
+
+    def half(own, far, route):
+        return jnp.concatenate(
+            [low(lax.ppermute(own, AXES, route)), low(lax.ppermute(far, AXES, route))]
+        )
 
     img = jnp.concatenate([low(img_raw), low(img_far)])
     txt = jnp.concatenate([low(txt_raw), low(txt_far)])
-    prev = jnp.concatenate([low(prev_own), low(prev_far)])
-    following = jnp.concatenate([low(next_own), low(next_far)])
+    img_prev, img_next = half(img_raw, img_far, ahead), half(img_raw, img_far, back)
+    txt_prev, txt_next = half(txt_raw, txt_far, ahead), half(txt_raw, txt_far, back)
 
     shape = (2 * rows, 2 * rows)
     first = lax.broadcasted_iota(jnp.int32, shape, 0)
     positive = (first == lax.broadcasted_iota(jnp.int32, shape, 1)) & (first < rows)
     labels = jnp.where(positive, 1.0, -1.0).astype(jnp.float32)
     negative = jnp.float32(-1.0)
-    coef_prev = pair_coef(img, prev, logit_scale, logit_bias, negative)
-    coef_next = pair_coef(img, following, logit_scale, logit_bias, negative)
-    coef_own = pair_coef(img, txt, logit_scale, logit_bias, labels)
 
-    to_prev = txt_part(coef_prev, img).astype(jnp.bfloat16)
-    to_next = txt_part(coef_next, img).astype(jnp.bfloat16)
-    from_next_far = lax.ppermute(to_prev[rows:], AXES, back)
-    from_prev_far = lax.ppermute(to_next[rows:], AXES, ahead)
-    img_dir = img_part(coef_prev, prev) + img_part(coef_own, txt) + img_part(coef_next, following)
+    def coef(images, texts, signs):
+        return pair_coef(images, texts, logit_scale, logit_bias, signs)
+
+    own = coef(img, txt, labels)
+    img_dir = (
+        img_part(own, txt)
+        + img_part(coef(img, txt_prev, negative), txt_prev)
+        + img_part(coef(img, txt_next, negative), txt_next)
+    )
+    txt_dir = (
+        txt_part(own, img)
+        + txt_part(coef(img_prev, txt, negative), img_prev)
+        + txt_part(coef(img_next, txt, negative), img_next)
+    )
     img_there = lax.ppermute(img_dir[rows:].astype(jnp.bfloat16), AXES, to_img)
-    from_next_own = lax.ppermute(to_prev[:rows], AXES, back)
-    from_prev_own = lax.ppermute(to_next[:rows], AXES, ahead)
-    own = txt_part(coef_own, img)
-    far_sum = own[rows:] + from_next_far.astype(jnp.float32) + from_prev_far.astype(jnp.float32)
-    txt_there = lax.ppermute(far_sum.astype(jnp.bfloat16), AXES, to_txt)
-    own_sum = own[:rows] + from_next_own.astype(jnp.float32) + from_prev_own.astype(jnp.float32)
-
+    txt_there = lax.ppermute(txt_dir[rows:].astype(jnp.bfloat16), AXES, to_txt)
     img_grad = grad_of(img_raw, img_dir[:rows] + img_there.astype(jnp.float32))
-    txt_grad = grad_of(txt_raw, own_sum + txt_there.astype(jnp.float32))
+    txt_grad = grad_of(txt_raw, txt_dir[:rows] + txt_there.astype(jnp.float32))
     return (img_grad, txt_grad)
 
 

time: 228 us -> 239 us (1.048)
  the two profiles are of different devices: /device:TPU:24 before, /device:TPU:49 now
where the time goes in v2:
time: 239 us; the launch traced here: 238 us
  waiting for transfers between devices  119 us (50%)
  starting transfers between devices  75.2 us (31%)
  other arithmetic  25.4 us (11%)
  matrix products  15.5 us (6%)
    ppermute x1, waiting for transfers between devices, local(): txt_there = lax.ppermute(txt_dir[rows:].astype(jnp.bfloat16), AXES, to_txt)  36.6 us
    ppermute x1, waiting for transfers between devices, local(): img_far = lax.ppermute(img_raw, AXES, to_img)  33.3 us
    ppermute x1, waiting for transfers between devices, local(): img_there = lax.ppermute(img_dir[rows:].astype(jnp.bfloat16), AXES, to_img)  30.4 us
    ppermute x1, starting transfers between devices, local(): img_far = lax.ppermute(img_raw, AXES, to_img)  15.6 us
    ppermute x1, waiting for transfers between devices, local(): txt_far = lax.ppermute(txt_raw, AXES, to_txt)  14.9 us
    ppermute x4, starting transfers between devices, half(): lax.ppermute(own, AXES, route)  13.8 us
    ppermute x1, starting transfers between devices, local(): txt_far = lax.ppermute(txt_raw, AXES, to_txt)  13.6 us
    ppermute x1, starting transfers between devices, local(): txt_there = lax.ppermute(txt_dir[rows:].astype(jnp.bfloat16), AXES, to_txt)  13 us
  transfers between devices with their start and end apart: 12, of which 5 were waited for; matrix products, arithmetic and copies ran while one was open for 17% of the time, Pallas kernels for 0%

profile of v2, /device:TPU:49, one launch (start us, length us, event | category | flops | bytes accessed | tf_op | source)
XLA Modules:
  0.0 238.4 jit_solution(13108213333767252278)
XLA Ops:
  0.6 15.6 %collective-permute-start = (bf16[128,1536]{1,0:T(8,128)(2,1)}, bf16[128,1536]{1,0:T(8,128)(2,1)}, u32[]{:S(2)}, u32[]{:S(2)}) collective-permute-start(bf16[128,1536]{1,0:T(8,128)(2,1)} %param.4), channel_id=1, source_target_pairs={{0,1},{1,0},{2,3},{3,2},{4,5},{5,4},{6,7},{7,6},{8,9},{9,8},{10,11... | collective-permute-start | bytes 1179656 | tf_op jit(solution)/shard_map/ppermute | solution.py:65
  16.2 4.4 %collective-permute-start.7 = (bf16[128,1536]{1,0:T(8,128)(2,1)}, bf16[128,1536]{1,0:T(8,128)(2,1)S(1)}, u32[]{:S(2)}, u32[]{:S(2)}) collective-permute-start(bf16[128,1536]{1,0:T(8,128)(2,1)} %param.4), channel_id=1, source_target_pairs={{0,4},{1,5},{2,6},{3,7},{4,8},{5,9},{6,10},{7,11},{8,12},{9,13},{1... | collective-permute-start | bytes 1179656 | tf_op jit(solution)/shard_map/ppermute | solution.py:69
  20.6 1.9 collective-permute-start.9
  22.6 13.6 %collective-permute-start.1 = (bf16[128,1536]{1,0:T(8,128)(2,1)}, bf16[128,1536]{1,0:T(8,128)(2,1)}, u32[]{:S(2)}, u32[]{:S(2)}) collective-permute-start(bf16[128,1536]{1,0:T(8,128)(2,1)} %param.5), channel_id=1, source_target_pairs={{0,3},{1,2},{2,1},{3,0},{4,7},{5,6},{6,5},{7,4},{8,11},{9,10},{10,... | collective-permute-start | bytes 1179656 | tf_op jit(solution)/shard_map/ppermute | solution.py:64
  36.2 3.9 %collective-permute-start.2 = (bf16[128,1536]{1,0:T(8,128)(2,1)}, bf16[128,1536]{1,0:T(8,128)(2,1)S(1)}, u32[]{:S(2)}, u32[]{:S(2)}) collective-permute-start(bf16[128,1536]{1,0:T(8,128)(2,1)} %param.5), channel_id=1, source_target_pairs={{0,4},{1,5},{2,6},{3,7},{4,8},{5,9},{6,10},{7,11},{8,12},{9,13},{1... | collective-permute-start | bytes 1179656 | tf_op jit(solution)/shard_map/ppermute | solution.py:69
  40.1 1.2 fusion.47
  41.3 1.2 fusion.54
  42.5 1.3 fusion.39
  45.2 33.3 %collective-permute-done = bf16[128,1536]{1,0:T(8,128)(2,1)} collective-permute-done((bf16[128,1536]{1,0:T(8,128)(2,1)}, bf16[128,1536]{1,0:T(8,128)(2,1)}, u32[]{:S(2)}, u32[]{:S(2)}) %collective-permute-start) | collective-permute-done | bytes 393248 | tf_op jit(solution)/shard_map/ppermute | solution.py:65
  78.5 3.5 %collective-permute-start.4 = (bf16[128,1536]{1,0:T(8,128)(2,1)S(1)}, bf16[128,1536]{1,0:T(8,128)(2,1)S(1)}, u32[]{:S(2)}, u32[]{:S(2)}) collective-permute-start(bf16[128,1536]{1,0:T(8,128)(2,1)S(1)} %copy-done), channel_id=1, source_target_pairs={{0,1023},{1,1020},{2,1021},{3,1022},{4,0},{5,1},{6,2},{7,3},{8,4},... | collective-permute-start | bytes 1179656 | tf_op jit(solution)/shard_map/ppermute | solution.py:69
  82.0 1.2 fusion.48
  83.2 14.9 %collective-permute-done.1 = bf16[128,1536]{1,0:T(8,128)(2,1)} collective-permute-done((bf16[128,1536]{1,0:T(8,128)(2,1)}, bf16[128,1536]{1,0:T(8,128)(2,1)}, u32[]{:S(2)}, u32[]{:S(2)}) %collective-permute-start.1) | collective-permute-done | bytes 393248 | tf_op jit(solution)/shard_map/ppermute | solution.py:64
  98.1 1.2 fusion.55
  99.5 1.1 fusion.49
  100.6 1.3 fusion.56
  101.9 0.2 fusion.69
  102.1 0.4 fusion.36
  102.7 0.4 fusion.122
  103.1 3.9 %collective-permute-done.4 = bf16[128,1536]{1,0:T(8,128)(2,1)S(1)} collective-permute-done((bf16[128,1536]{1,0:T(8,128)(2,1)S(1)}, bf16[128,1536]{1,0:T(8,128)(2,1)S(1)}, u32[]{:S(2)}, u32[]{:S(2)}) %collective-permute-start.4) | collective-permute-done | bytes 393248 | tf_op jit(solution)/shard_map/ppermute | solution.py:69
  107.2 2.8 %collective-permute-start.8 = (bf16[128,1536]{1,0:T(8,128)(2,1)}, bf16[128,1536]{1,0:T(8,128)(2,1)S(1)}, u32[]{:S(2)}, u32[]{:S(2)}) collective-permute-start(bf16[128,1536]{1,0:T(8,128)(2,1)} %collective-permute-done), channel_id=1, source_target_pairs={{0,4},{1,5},{2,6},{3,7},{4,8},{5,9},{6,10},{7,11},{8,12},{9,13},{1... | collective-permute-start | bytes 1179656 | tf_op jit(solution)/shard_map/ppermute | solution.py:69
  110.0 2.7 %collective-permute-start.10 = (bf16[128,1536]{1,0:T(8,128)(2,1)}, bf16[128,1536]{1,0:T(8,128)(2,1)S(1)}, u32[]{:S(2)}, u32[]{:S(2)}) collective-permute-start(bf16[128,1536]{1,0:T(8,128)(2,1)} %collective-permute-done), channel_id=1, source_target_pairs={{0,1023},{1,1020},{2,1021},{3,1022},{4,0},{5,1},{6,2},{7,3},{8,4},... | collective-permute-start | bytes 1179656 | tf_op jit(solution)/shard_map/ppermute | solution.py:69
  112.6 2.9 %collective-permute-start.3 = (bf16[128,1536]{1,0:T(8,128)(2,1)}, bf16[128,1536]{1,0:T(8,128)(2,1)}, u32[]{:S(2)}, u32[]{:S(2)}) collective-permute-start(bf16[128,1536]{1,0:T(8,128)(2,1)} %collective-permute-done.1), channel_id=1, source_target_pairs={{0,4},{1,5},{2,6},{3,7},{4,8},{5,9},{6,10},{7,11},{8,12},{9,13},{1... | collective-permute-start | bytes 1179656 | tf_op jit(solution)/shard_map/ppermute | solution.py:69
  115.5 2.7 %collective-permute-start.5 = (bf16[128,1536]{1,0:T(8,128)(2,1)}, bf16[128,1536]{1,0:T(8,128)(2,1)}, u32[]{:S(2)}, u32[]{:S(2)}) collective-permute-start(bf16[128,1536]{1,0:T(8,128)(2,1)} %collective-permute-done.1), channel_id=1, source_target_pairs={{0,1023},{1,1020},{2,1021},{3,1022},{4,0},{5,1},{6,2},{7,3},{8,4},... | collective-permute-start | bytes 1179656 | tf_op jit(solution)/shard_map/ppermute | solution.py:69
  118.2 0.9 fusion.66
  119.1 0.9 fusion.58
  120.0 0.9 fusion.62
  120.9 0.9 fusion.70
  121.8 0.4 fusion.123
  122.2 0.2 fusion.67
  122.5 0.9 fusion.68
  123.4 0.9 fusion.72
  124.3 3.9 %convolution_add_fusion.1 = f32[256,1536]{1,0:T(8,128)} fusion(f32[256,1536]{1,0:T(8,128)S(1)} %fusion.123, bf16[128,1536]{1,0:T(8,128)(2,1)} %fusion.68, bf16[128,1536]{1,0:T(8,128)(2,1)} %fusion.66, f32[]{:T(128)S(6)} %copy.7, f32[]{:T(128)S(6)} %copy.6, bf16[128,1536]{1,0:T(8,128)(2,1)} %copy-done.6, bf16[128,1536]{1,0:T(8,128)(2,1)} %copy-done.5), kind=kOutput, calls=%fused_computation.1 | convolution fusion | flops 408223744 | bytes 4718600 | tf_op jit(solution)/shard_map/dot_general | solution.py:56
  128.2 3.3 %convolution_add_fusion = f32[256,1536]{1,0:T(8,128)S(1)} fusion(f32[256,1536]{1,0:T(8,128)} %convolution_add_fusion.1, bf16[128,1536]{1,0:T(8,128)(2,1)} %fusion.72, bf16[128,1536]{1,0:T(8,128)(2,1)} %fusion.70, f32[]{:T(128)S(6)} %copy.7, f32[]{:T(128)S(6)} %copy.6, bf16[128,1536]{1,0:T(8,128)(2,1)} %copy-done.6, bf16[128,1536]{1,0:T(8,128)(2,1)} %copy-done.5), kind=kOutput, calls=%fused_computation | convolution fusion | flops 408223744 | bytes 4718600 | tf_op jit(solution)/shard_map/dot_general | solution.py:56
  131.5 0.8 slice.34
  132.3 13.0 %collective-permute-start.11 = (bf16[128,1536]{1,0:T(8,128)(2,1)}, bf16[128,1536]{1,0:T(8,128)(2,1)}, u32[]{:S(2)}, u32[]{:S(2)}) collective-permute-start(bf16[128,1536]{1,0:T(8,128)(2,1)} %slice.34), channel_id=1, source_target_pairs={{0,3},{1,2},{2,1},{3,0},{4,7},{5,6},{6,5},{7,4},{8,11},{9,10},{10,... | collective-permute-start | bytes 1179656 | tf_op jit(solution)/shard_map/ppermute | solution.py:98
  145.3 1.2 fusion.59
  146.5 1.2 fusion.63
  147.6 1.9 fusion.60
  149.5 1.9 fusion.64
  151.4 3.9 %convolution_add_fusion.3 = f32[256,1536]{1,0:T(8,128)} fusion(f32[256,1536]{1,0:T(8,128)S(1)} %fusion.122, bf16[128,1536]{1,0:T(8,128)(2,1)} %fusion.60, bf16[128,1536]{1,0:T(8,128)(2,1)} %fusion.58, f32[]{:T(128)S(6)} %copy.7, f32[]{:T(128)S(6)} %copy.6, bf16[128,1536]{1,0:T(8,128)(2,1)} %copy-done.4, bf16[128,1536]{1,0:T(8,128)(2,1)} %copy-done.2), kind=kOutput, calls=%fused_computation.3 | convolution fusion | flops 408223744 | bytes 4718600 | tf_op jit(solution)/shard_map/dot_general | solution.py:52
  155.3 3.2 %convolution_add_fusion.2 = f32[256,1536]{1,0:T(8,128)S(1)} fusion(f32[256,1536]{1,0:T(8,128)} %convolution_add_fusion.3, bf16[128,1536]{1,0:T(8,128)(2,1)} %fusion.64, bf16[128,1536]{1,0:T(8,128)(2,1)} %fusion.62, f32[]{:T(128)S(6)} %copy.7, f32[]{:T(128)S(6)} %copy.6, bf16[128,1536]{1,0:T(8,128)(2,1)} %copy-done.4, bf16[128,1536]{1,0:T(8,128)(2,1)} %copy-done.2), kind=kOutput, calls=%fused_computation.2 | convolution fusion | flops 408223744 | bytes 4718600 | tf_op jit(solution)/shard_map/dot_general | solution.py:52
  158.6 8.3 %collective-permute-start.6 = (bf16[128,1536]{1,0:T(8,128)(2,1)S(1)}, bf16[128,1536]{1,0:T(8,128)(2,1)S(1)}, u32[]{:S(2)}, u32[]{:S(2)}) collective-permute-start(bf16[128,1536]{1,0:T(8,128)(2,1)S(1)} %slice.35), channel_id=1, source_target_pairs={{0,1},{1,0},{2,3},{3,2},{4,5},{5,4},{6,7},{7,6},{8,9},{9,8},{10,11... | collective-permute-start | bytes 1179656 | tf_op jit(solution)/shard_map/ppermute | solution.py:97
  166.9 36.6 %collective-permute-done.11 = bf16[128,1536]{1,0:T(8,128)(2,1)} collective-permute-done((bf16[128,1536]{1,0:T(8,128)(2,1)}, bf16[128,1536]{1,0:T(8,128)(2,1)}, u32[]{:S(2)}, u32[]{:S(2)}) %collective-permute-start.11) | collective-permute-done | bytes 393248 | tf_op jit(solution)/shard_map/ppermute | solution.py:98
  203.4 1.3 fusion.50
  204.7 2.0 fusion.53
  206.7 30.4 %collective-permute-done.6 = bf16[128,1536]{1,0:T(8,128)(2,1)S(1)} collective-permute-done((bf16[128,1536]{1,0:T(8,128)(2,1)S(1)}, bf16[128,1536]{1,0:T(8,128)(2,1)S(1)}, u32[]{:S(2)}, u32[]{:S(2)}) %collective-permute-start.6) | collective-permute-done | bytes 393248 | tf_op jit(solution)/shard_map/ppermute | solution.py:97
  237.1 0.3 fusion.43
  237.4 1.1 fusion.46
  (39 shorter events, 0.8 us)
Async XLA Ops:
  0.6 77.8 %copy-start = (bf16[128,1536]{1,0:T(8,128)(2,1)S(1)}, bf16[128,1536]{1,0:T(8,128)(2,1)}, u32[]{:S(2)}) copy-start(bf16[128,1536]{1,0:T(8,128)(2,1)} %param.5) | copy-start | bytes 1179652
  0.6 77.8 %collective-permute-start = (bf16[128,1536]{1,0:T(8,128)(2,1)}, bf16[128,1536]{1,0:T(8,128)(2,1)}, u32[]{:S(2)}, u32[]{:S(2)}) collective-permute-start(bf16[128,1536]{1,0:T(8,128)(2,1)} %param.4), channel_id=1, source_target_pairs={{0,1},{1,0},{2,3},{3,2},{4,5},{5,4},{6,7},{7,6},{8,9},{9,8},{10,11... | collective-permute-start | bytes 1179656 | tf_op jit(solution)/shard_map/ppermute | solution.py:65
  16.2 83.1 %collective-permute-start.7 = (bf16[128,1536]{1,0:T(8,128)(2,1)}, bf16[128,1536]{1,0:T(8,128)(2,1)S(1)}, u32[]{:S(2)}, u32[]{:S(2)}) collective-permute-start(bf16[128,1536]{1,0:T(8,128)(2,1)} %param.4), channel_id=1, source_target_pairs={{0,4},{1,5},{2,6},{3,7},{4,8},{5,9},{6,10},{7,11},{8,12},{9,13},{1... | collective-permute-start | bytes 1179656 | tf_op jit(solution)/shard_map/ppermute | solution.py:69
  20.6 81.3 %collective-permute-start.9 = (bf16[128,1536]{1,0:T(8,128)(2,1)}, bf16[128,1536]{1,0:T(8,128)(2,1)S(1)}, u32[]{:S(2)}, u32[]{:S(2)}) collective-permute-start(bf16[128,1536]{1,0:T(8,128)(2,1)} %param.4), channel_id=1, source_target_pairs={{0,1023},{1,1020},{2,1021},{3,1022},{4,0},{5,1},{6,2},{7,3},{8,4},... | collective-permute-start | bytes 1179656 | tf_op jit(solution)/shard_map/ppermute | solution.py:69
  22.6 75.6 %collective-permute-start.1 = (bf16[128,1536]{1,0:T(8,128)(2,1)}, bf16[128,1536]{1,0:T(8,128)(2,1)}, u32[]{:S(2)}, u32[]{:S(2)}) collective-permute-start(bf16[128,1536]{1,0:T(8,128)(2,1)} %param.5), channel_id=1, source_target_pairs={{0,3},{1,2},{2,1},{3,0},{4,7},{5,6},{6,5},{7,4},{8,11},{9,10},{10,... | collective-permute-start | bytes 1179656 | tf_op jit(solution)/shard_map/ppermute | solution.py:64
  36.2 66.3 %collective-permute-start.2 = (bf16[128,1536]{1,0:T(8,128)(2,1)}, bf16[128,1536]{1,0:T(8,128)(2,1)S(1)}, u32[]{:S(2)}, u32[]{:S(2)}) collective-permute-start(bf16[128,1536]{1,0:T(8,128)(2,1)} %param.5), channel_id=1, source_target_pairs={{0,4},{1,5},{2,6},{3,7},{4,8},{5,9},{6,10},{7,11},{8,12},{9,13},{1... | collective-permute-start | bytes 1179656 | tf_op jit(solution)/shard_map/ppermute | solution.py:69
  43.8 58.3 %copy-start.2 = (bf16[128,1536]{1,0:T(8,128)(2,1)}, bf16[128,1536]{1,0:T(8,128)(2,1)S(1)}, u32[]{:S(2)}) copy-start(bf16[128,1536]{1,0:T(8,128)(2,1)S(1)} %get-tuple-element.3) | copy-start | bytes 1179652
  43.8 58.9 %copy-start.5 = (bf16[128,1536]{1,0:T(8,128)(2,1)}, bf16[128,1536]{1,0:T(8,128)(2,1)S(1)}, u32[]{:S(2)}) copy-start(bf16[128,1536]{1,0:T(8,128)(2,1)S(1)} %get-tuple-element.2) | copy-start | bytes 1179652
  78.5 28.6 %collective-permute-start.4 = (bf16[128,1536]{1,0:T(8,128)(2,1)S(1)}, bf16[128,1536]{1,0:T(8,128)(2,1)S(1)}, u32[]{:S(2)}, u32[]{:S(2)}) collective-permute-start(bf16[128,1536]{1,0:T(8,128)(2,1)S(1)} %copy-done), channel_id=1, source_target_pairs={{0,1023},{1,1020},{2,1021},{3,1022},{4,0},{5,1},{6,2},{7,3},{8,4},... | collective-permute-start | bytes 1179656 | tf_op jit(solution)/shard_map/ppermute | solution.py:69
  100.6 21.2 %copy-start.4 = (bf16[128,1536]{1,0:T(8,128)(2,1)}, bf16[128,1536]{1,0:T(8,128)(2,1)S(1)}, u32[]{:S(2)}) copy-start(bf16[128,1536]{1,0:T(8,128)(2,1)S(1)} %fusion.49) | copy-start | bytes 1179652
  101.9 0.8 copy-start.6
  107.2 14.6 %copy-start.3 = (bf16[128,1536]{1,0:T(8,128)(2,1)S(1)}, bf16[128,1536]{1,0:T(8,128)(2,1)}, u32[]{:S(2)}) copy-start(bf16[128,1536]{1,0:T(8,128)(2,1)} %copy-done.2) | copy-start | bytes 1179652
  107.2 15.0 %collective-permute-start.8 = (bf16[128,1536]{1,0:T(8,128)(2,1)}, bf16[128,1536]{1,0:T(8,128)(2,1)S(1)}, u32[]{:S(2)}, u32[]{:S(2)}) collective-permute-start(bf16[128,1536]{1,0:T(8,128)(2,1)} %collective-permute-done), channel_id=1, source_target_pairs={{0,4},{1,5},{2,6},{3,7},{4,8},{5,9},{6,10},{7,11},{8,12},{9,13},{1... | collective-permute-start | bytes 1179656 | tf_op jit(solution)/shard_map/ppermute | solution.py:69
  110.0 12.4 %collective-permute-start.10 = (bf16[128,1536]{1,0:T(8,128)(2,1)}, bf16[128,1536]{1,0:T(8,128)(2,1)S(1)}, u32[]{:S(2)}, u32[]{:S(2)}) collective-permute-start(bf16[128,1536]{1,0:T(8,128)(2,1)} %collective-permute-done), channel_id=1, source_target_pairs={{0,1023},{1,1020},{2,1021},{3,1022},{4,0},{5,1},{6,2},{7,3},{8,4},... | collective-permute-start | bytes 1179656 | tf_op jit(solution)/shard_map/ppermute | solution.py:69
  112.6 32.7 %collective-permute-start.3 = (bf16[128,1536]{1,0:T(8,128)(2,1)}, bf16[128,1536]{1,0:T(8,128)(2,1)}, u32[]{:S(2)}, u32[]{:S(2)}) collective-permute-start(bf16[128,1536]{1,0:T(8,128)(2,1)} %collective-permute-done.1), channel_id=1, source_target_pairs={{0,4},{1,5},{2,6},{3,7},{4,8},{5,9},{6,10},{7,11},{8,12},{9,13},{1... | collective-permute-start | bytes 1179656 | tf_op jit(solution)/shard_map/ppermute | solution.py:69
  115.5 30.9 %collective-permute-start.5 = (bf16[128,1536]{1,0:T(8,128)(2,1)}, bf16[128,1536]{1,0:T(8,128)(2,1)}, u32[]{:S(2)}, u32[]{:S(2)}) collective-permute-start(bf16[128,1536]{1,0:T(8,128)(2,1)} %collective-permute-done.1), channel_id=1, source_target_pairs={{0,1023},{1,1020},{2,1021},{3,1022},{4,0},{5,1},{6,2},{7,3},{8,4},... | collective-permute-start | bytes 1179656 | tf_op jit(solution)/shard_map/ppermute | solution.py:69
  132.3 71.1 %collective-permute-start.11 = (bf16[128,1536]{1,0:T(8,128)(2,1)}, bf16[128,1536]{1,0:T(8,128)(2,1)}, u32[]{:S(2)}, u32[]{:S(2)}) collective-permute-start(bf16[128,1536]{1,0:T(8,128)(2,1)} %slice.34), channel_id=1, source_target_pairs={{0,3},{1,2},{2,1},{3,0},{4,7},{5,6},{6,5},{7,4},{8,11},{9,10},{10,... | collective-permute-start | bytes 1179656 | tf_op jit(solution)/shard_map/ppermute | solution.py:98
  158.6 78.5 %copy-start.1 = (bf16[128,1536]{1,0:T(8,128)(2,1)S(1)}, bf16[128,1536]{1,0:T(8,128)(2,1)}, u32[]{:S(2)}) copy-start(bf16[128,1536]{1,0:T(8,128)(2,1)} %param.4) | copy-start | bytes 1179652
  158.6 78.5 %collective-permute-start.6 = (bf16[128,1536]{1,0:T(8,128)(2,1)S(1)}, bf16[128,1536]{1,0:T(8,128)(2,1)S(1)}, u32[]{:S(2)}, u32[]{:S(2)}) collective-permute-start(bf16[128,1536]{1,0:T(8,128)(2,1)S(1)} %slice.35), channel_id=1, source_target_pairs={{0,1},{1,0},{2,3},{3,2},{4,5},{5,4},{6,7},{7,6},{8,9},{9,8},{10,11... | collective-permute-start | bytes 1179656 | tf_op jit(solution)/shard_map/ppermute | solution.py:97

commit v3 on v2

v3 whole, which is shorter than its diff:
```python
import jax
import jax.numpy as jnp
from jax import lax
from jax.experimental import pallas as pl
from jax.experimental.pallas import tpu as pltpu
from jax.sharding import PartitionSpec as P

AXES = ("dp", "fsdp")
SPAN = 16
STRIP = 32
VMEM_LIMIT = 32 * 1024 * 1024


def device_of(block, role, blocks, ways):
    block = block % blocks
    return block * ways + (role + block // SPAN) % ways


def routes(blocks, ways):
    img, txt, mate, cross = [], [], [], []
    for block in range(blocks):
        for role in range(ways):
            here = device_of(block, role, blocks, ways)
            across = block + 1 if block % 2 else block - 1
            img.append((here, device_of(block, role ^ 1, blocks, ways)))
            txt.append((here, device_of(block, ways - 1 - role, blocks, ways)))
            mate.append((here, device_of(block ^ 1, role, blocks, ways)))
            cross.append((here, device_of(across, role, blocks, ways)))
    return img, txt, mate, cross


def inverse_of(values):
    return lax.rsqrt(jnp.sum(values * values, axis=-1, keepdims=True) + 1e-06)


def low_kernel(img_ref, txt_ref, low_ref):
    rows = img_ref.shape[0]
    for part, ref in enumerate((img_ref, txt_ref)):
        for start in range(0, rows, STRIP):
            values = ref[start : start + STRIP, :].astype(jnp.float32)
            strip = (values * inverse_of(values)).astype(jnp.bfloat16)
            low_ref[part * rows + start : part * rows + start + STRIP, :] = strip


def scores_of(left, right):
    return lax.dot_general(left, right, (((1,), (1,)), ((), ())), preferred_element_type=jnp.float32)


def negative_coef(left, right, scale, bias):
    return (jax.nn.sigmoid(scale * scores_of(left, right) + bias) * scale).astype(jnp.bfloat16)


def columns_of(width, step=256):
    return [slice(start, start + step) for start in range(0, width, step)]


def stack(first, second, part, rows, out_ref):
    out_ref[:rows, :] = first[part * rows : (part + 1) * rows, :]
    out_ref[rows:, :] = second[part * rows : (part + 1) * rows, :]


def near_kernel(scale_ref, bias_ref, own, far, mate, cross, img_acc, txt_acc, img, txt, img_n, txt_n):
    rows = own.shape[0] // 2
    scale, bias = scale_ref[0], bias_ref[0]
    stack(own, far, 0, rows, img)
    stack(own, far, 1, rows, txt)
    stack(mate, cross, 0, rows, img_n)
    stack(mate, cross, 1, rows, txt_n)

    shape = (2 * rows, 2 * rows)
    first = lax.broadcasted_iota(jnp.int32, shape, 0)
    positive = (first == lax.broadcasted_iota(jnp.int32, shape, 1)) & (first < rows)
    logits = scale * scores_of(img[...], txt[...]) + bias
    size = jax.nn.sigmoid(jnp.where(positive, -logits, logits)) * scale
    signed = jnp.where(positive, -size, size)
    coef_own = signed.astype(jnp.bfloat16)
    coef_own_t = signed.T.astype(jnp.bfloat16)
    coef_img = negative_coef(img[...], txt_n[...], scale, bias)
    coef_txt = negative_coef(txt[...], img_n[...], scale, bias)

    def dot(coef, ref, cols):
        return jnp.dot(coef, ref[:, cols], preferred_element_type=jnp.float32)

    for cols in columns_of(own.shape[1]):
        img_acc[:, cols] = dot(coef_own, txt, cols) + dot(coef_img, txt_n, cols)
        txt_acc[:, cols] = dot(coef_own_t, img, cols) + dot(coef_txt, img_n, cols)


def far_kernel(
    scale_ref, bias_ref, own, far, mate, cross, img_acc, txt_acc,
    img_own, img_far, txt_own, txt_far, img, txt, img_n, txt_n,
):
    rows = own.shape[0] // 2
    scale, bias = scale_ref[0], bias_ref[0]
    stack(own, far, 0, rows, img)
    stack(own, far, 1, rows, txt)
    stack(mate, cross, 0, rows, img_n)
    stack(mate, cross, 1, rows, txt_n)
    coef_img = negative_coef(img[...], txt_n[...], scale, bias)
    coef_txt = negative_coef(txt[...], img_n[...], scale, bias)
    for cols in columns_of(own.shape[1]):
        total = img_acc[:, cols] + jnp.dot(
            coef_img, txt_n[:, cols], preferred_element_type=jnp.float32
        )
        img_own[:, cols] = total[:rows]
        img_far[:, cols] = total[rows:].astype(jnp.bfloat16)
        total = txt_acc[:, cols] + jnp.dot(
            coef_txt, img_n[:, cols], preferred_element_type=jnp.float32
        )
        txt_own[:, cols] = total[:rows]
        txt_far[:, cols] = total[rows:].astype(jnp.bfloat16)


def grad_kernel(raw_ref, own_ref, there_ref, out_ref):
    for start in range(0, raw_ref.shape[0], STRIP):
        here = slice(start, start + STRIP)
        values = raw_ref[here, :].astype(jnp.float32)
        inverse = inverse_of(values)
        norm = values * inverse
        direction = own_ref[here, :] + there_ref[here, :].astype(jnp.float32)
        inner = jnp.sum(norm * direction, axis=-1, keepdims=True)
        out_ref[here, :] = ((direction - norm * inner) * inverse).astype(jnp.bfloat16)


def call(kernel, outs, scalars, arrays, scratch=(), flops=0):
    moved = sum(a.size * a.dtype.itemsize for a in arrays)
    return pl.pallas_call(
        kernel,
        out_shape=outs,
        in_specs=[pl.BlockSpec(memory_space=pltpu.SMEM)] * len(scalars)
        + [pl.BlockSpec(memory_space=pltpu.VMEM)] * len(arrays),
        out_specs=jax.tree.map(lambda _: pl.BlockSpec(memory_space=pltpu.VMEM), outs),
        scratch_shapes=list(scratch),
        compiler_params=pltpu.CompilerParams(vmem_limit_bytes=VMEM_LIMIT),
        cost_estimate=pl.CostEstimate(flops=flops, bytes_accessed=moved, transcendentals=0),
    )(*scalars, *arrays)


def local(img_raw, txt_raw, logit_scale, logit_bias, moves):
    to_img, to_txt, to_mate, to_cross = moves
    rows, width = img_raw.shape
    scalars = (logit_scale.reshape(1), logit_bias.reshape(1))
    low_shape = jax.ShapeDtypeStruct((2 * rows, width), jnp.bfloat16)
    acc_shape = jax.ShapeDtypeStruct((2 * rows, width), jnp.float32)
    own_shape = jax.ShapeDtypeStruct((rows, width), jnp.float32)
    sent_shape = jax.ShapeDtypeStruct((rows, width), jnp.bfloat16)
    halves = [pltpu.VMEM((2 * rows, width), jnp.bfloat16)] * 4
    unit = 2 * (2 * rows) * (2 * rows) * width

    img_there = lax.ppermute(img_raw, AXES, to_img)
    txt_there = lax.ppermute(txt_raw, AXES, to_txt)
    own = call(low_kernel, low_shape, (), (img_raw, txt_raw))
    cross_own = lax.ppermute(own, AXES, to_cross)
    mate_own = lax.ppermute(own, AXES, to_mate)
    far = call(low_kernel, low_shape, (), (img_there, txt_there))
    cross_far = lax.ppermute(far, AXES, to_cross)
    mate_far = lax.ppermute(far, AXES, to_mate)
    img_acc, txt_acc = call(
        near_kernel, (acc_shape, acc_shape), scalars, (own, far, mate_own, cross_own), halves, 7 * unit
    )
    img_own, img_sent, txt_own, txt_sent = call(
        far_kernel,
        (own_shape, sent_shape, own_shape, sent_shape),
        scalars,
        (own, far, mate_far, cross_far, img_acc, txt_acc),
        halves,
        4 * unit,
    )
    img_back = lax.ppermute(img_sent, AXES, to_img)
    txt_back = lax.ppermute(txt_sent, AXES, to_txt)
    img_grad = call(grad_kernel, sent_shape, (), (img_raw, img_own, img_back))
    txt_grad = call(grad_kernel, sent_shape, (), (txt_raw, txt_own, txt_back))
    return (img_grad, txt_grad)


def solution(mesh):
    moves = routes(mesh.shape["dp"], mesh.shape["fsdp"])
    in_specs = (P(AXES, None), P(AXES, None), P(), P())
    out_specs = (P(AXES, None), P(AXES, None))

    def step(*args):
        return local(*args, moves)

    return jax.shard_map(step, mesh=mesh, in_specs=in_specs, out_specs=out_specs, check_vma=False)
```

time: 239 us -> 201 us (0.84)
  the two profiles are of different devices: /device:TPU:49 before, /device:TPU:24 now
where the time goes in v3:
time: 201 us; the launch traced here: 197 us
  waiting for transfers between devices  126 us (63%)
  starting transfers between devices  60.6 us (30%)
  Pallas kernels  6.96 us (3%)
  between operations  2.03 us (1%)
    ppermute x1, waiting for transfers between devices, local(): img_back = lax.ppermute(img_sent, AXES, to_img)  56.9 us
    ppermute x1, waiting for transfers between devices, local(): img_there = lax.ppermute(img_raw, AXES, to_img)  45.7 us
    ppermute x1, starting transfers between devices, local(): img_there = lax.ppermute(img_raw, AXES, to_img)  15.7 us
    ppermute x1, starting transfers between devices, local(): txt_there = lax.ppermute(txt_raw, AXES, to_txt)  15.7 us
    ppermute x1, waiting for transfers between devices, local(): txt_there = lax.ppermute(txt_raw, AXES, to_txt)  14.6 us
    ppermute x1, starting transfers between devices, local(): img_back = lax.ppermute(img_sent, AXES, to_img)  10 us
    ppermute x1, starting transfers between devices, local(): txt_back = lax.ppermute(txt_sent, AXES, to_txt)  8.59 us
    pallas_call x6, Pallas kernels, call(): pl.pallas_call(kernel, out_shape=outs, in_specs=[pl.BlockSpec(memory_spac...  6.96 us
  transfers between devices with their start and end apart: 8, of which 6 were waited for; matrix products, arithmetic and copies ran while one was open for 0% of the time, Pallas kernels for 2%

profile of v3, /device:TPU:24, one launch (start us, length us, event | category | flops | bytes accessed | tf_op | source)
XLA Modules:
  0.0 197.3 jit_solution(92653132638544878)
XLA Ops:
  0.6 15.7 %collective-permute-start = (bf16[128,1536]{1,0:T(8,128)(2,1)}, bf16[128,1536]{1,0:T(8,128)(2,1)S(1)}, u32[]{:S(2)}, u32[]{:S(2)}) collective-permute-start(bf16[128,1536]{1,0:T(8,128)(2,1)} %raw_ref.2), channel_id=1, source_target_pairs={{0,1},{1,0},{2,3},{3,2},{4,5},{5,4},{6,7},{7,6},{8,9},{9,8},{10,11... | collective-permute-start | bytes 1179656 | tf_op jit(solution)/shard_map/ppermute | solution.py:150
  16.4 15.7 %collective-permute-start.1 = (bf16[128,1536]{1,0:T(8,128)(2,1)}, bf16[128,1536]{1,0:T(8,128)(2,1)S(1)}, u32[]{:S(2)}, u32[]{:S(2)}) collective-permute-start(bf16[128,1536]{1,0:T(8,128)(2,1)} %raw_ref.3), channel_id=1, source_target_pairs={{0,3},{1,2},{2,1},{3,0},{4,7},{5,6},{6,5},{7,4},{8,11},{9,10},{10,... | collective-permute-start | bytes 1179656 | tf_op jit(solution)/shard_map/ppermute | solution.py:151
  32.1 0.0 copy-start
  32.1 1.0 copy-done
  33.1 0.0 copy-start.2
  33.1 1.0 copy-done.2
  34.1 0.2 shard_map.59.own
  34.3 3.3 %collective-permute-start.5 = (bf16[256,1536]{1,0:T(8,128)(2,1)S(1)}, bf16[256,1536]{1,0:T(8,128)(2,1)}, u32[]{:S(2)}, u32[]{:S(2)}) collective-permute-start(bf16[256,1536]{1,0:T(8,128)(2,1)S(1)} %shard_map.59.own), channel_id=1, source_target_pairs={{0,1023},{1,1020},{2,1021},{3,1022},{4,8},{5,9},{6,10},{7,11},{8,4... | collective-permute-start | bytes 2359304 | tf_op jit(solution)/shard_map/ppermute | solution.py:153
  37.6 1.9 collective-permute-start.4
  39.5 45.7 %collective-permute-done.img_ref = bf16[128,1536]{1,0:T(8,128)(2,1)S(1)} collective-permute-done((bf16[128,1536]{1,0:T(8,128)(2,1)}, bf16[128,1536]{1,0:T(8,128)(2,1)S(1)}, u32[]{:S(2)}, u32[]{:S(2)}) %collective-permute-start) | collective-permute-done | bytes 393248 | tf_op jit(solution)/shard_map/ppermute | solution.py:150
  85.2 14.6 %collective-permute-done.1.txt_ref = bf16[128,1536]{1,0:T(8,128)(2,1)S(1)} collective-permute-done((bf16[128,1536]{1,0:T(8,128)(2,1)}, bf16[128,1536]{1,0:T(8,128)(2,1)S(1)}, u32[]{:S(2)}, u32[]{:S(2)}) %collective-permute-start.1) | collective-permute-done | bytes 393248 | tf_op jit(solution)/shard_map/ppermute | solution.py:151
  99.8 0.2 shard_map.60.far
  100.0 3.4 %collective-permute-start.3 = (bf16[256,1536]{1,0:T(8,128)(2,1)S(1)}, bf16[256,1536]{1,0:T(8,128)(2,1)S(1)}, u32[]{:S(2)}, u32[]{:S(2)}) collective-permute-start(bf16[256,1536]{1,0:T(8,128)(2,1)S(1)} %shard_map.60.far), channel_id=1, source_target_pairs={{0,1023},{1,1020},{2,1021},{3,1022},{4,8},{5,9},{6,10},{7,11},{8,4... | collective-permute-start | bytes 2359304 | tf_op jit(solution)/shard_map/ppermute | solution.py:156
  103.5 1.9 collective-permute-start.2
  106.7 1.4 collective-permute-done.5.cross
  108.1 0.0 collective-permute-done.4.mate
  108.1 3.2 %shard_map.61 = (f32[256,1536]{1,0:T(8,128)S(1)}, f32[256,1536]{1,0:T(8,128)S(1)}) custom-call(f32[1]{0:T(128)} %bitcast.2.scale_ref, f32[1]{0:T(128)} %bitcast.4.bias_ref, bf16[256,1536]{1,0:T(8,128)(2,1)S(1)} %shard_map.59.own, bf16[256,1536]{1,0:T(8,128)(2,1)S(1)} %shard_map.60.far, bf16[256,1536]{1,0:T(8,128)(2,1)} %collective-permute-done.4.mate, ...), custom_call_target="tpu_custom_call" | custom-call | flops 1409286144 | bytes 3145728 | tf_op jit(solution)/shard_map/pallas_call | solution.py:127
  111.3 6.3 %collective-permute-done.3.cross = bf16[256,1536]{1,0:T(8,128)(2,1)S(1)} collective-permute-done((bf16[256,1536]{1,0:T(8,128)(2,1)S(1)}, bf16[256,1536]{1,0:T(8,128)(2,1)S(1)}, u32[]{:S(2)}, u32[]{:S(2)}) %collective-permute-start.3) | collective-permute-done | bytes 786464 | tf_op jit(solution)/shard_map/ppermute | solution.py:156
  117.5 0.0 collective-permute-done.2.mate
  117.5 0.0 copy-start.1
  117.5 1.1 shard_map.62
  118.7 0.0 copy-start.3
  118.7 10.0 %collective-permute-start.6 = (bf16[128,1536]{1,0:T(8,128)(2,1)S(1)}, bf16[128,1536]{1,0:T(8,128)(2,1)S(1)}, u32[]{:S(2)}, u32[]{:S(2)}) collective-permute-start(bf16[128,1536]{1,0:T(8,128)(2,1)S(1)} %get-tuple-element.11), channel_id=1, source_target_pairs={{0,1},{1,0},{2,3},{3,2},{4,5},{5,4},{6,7},{7,6},{8,9},{9,8},{10,11... | collective-permute-start | bytes 1179656 | tf_op jit(solution)/shard_map/ppermute | solution.py:169
  128.7 8.6 %collective-permute-start.7 = (bf16[128,1536]{1,0:T(8,128)(2,1)S(1)}, bf16[128,1536]{1,0:T(8,128)(2,1)S(1)}, u32[]{:S(2)}, u32[]{:S(2)}) collective-permute-start(bf16[128,1536]{1,0:T(8,128)(2,1)S(1)} %get-tuple-element.13), channel_id=1, source_target_pairs={{0,3},{1,2},{2,1},{3,0},{4,7},{5,6},{6,5},{7,4},{8,11},{9,10},{10,... | collective-permute-start | bytes 1179656 | tf_op jit(solution)/shard_map/ppermute | solution.py:170
  137.3 56.9 %collective-permute-done.6.there_ref = bf16[128,1536]{1,0:T(8,128)(2,1)S(1)} collective-permute-done((bf16[128,1536]{1,0:T(8,128)(2,1)S(1)}, bf16[128,1536]{1,0:T(8,128)(2,1)S(1)}, u32[]{:S(2)}, u32[]{:S(2)}) %collective-permute-start.6) | collective-permute-done | bytes 393248 | tf_op jit(solution)/shard_map/ppermute | solution.py:169
  194.2 0.0 copy-done.1
  194.2 1.1 shard_map.63
  195.3 0.9 collective-permute-done.7.there_ref
  196.2 0.0 copy-done.3
  196.2 1.1 shard_map.64
Async XLA Ops:
  0.6 84.6 %collective-permute-start = (bf16[128,1536]{1,0:T(8,128)(2,1)}, bf16[128,1536]{1,0:T(8,128)(2,1)S(1)}, u32[]{:S(2)}, u32[]{:S(2)}) collective-permute-start(bf16[128,1536]{1,0:T(8,128)(2,1)} %raw_ref.2), channel_id=1, source_target_pairs={{0,1},{1,0},{2,3},{3,2},{4,5},{5,4},{6,7},{7,6},{8,9},{9,8},{10,11... | collective-permute-start | bytes 1179656 | tf_op jit(solution)/shard_map/ppermute | solution.py:150
  16.4 83.4 %collective-permute-start.1 = (bf16[128,1536]{1,0:T(8,128)(2,1)}, bf16[128,1536]{1,0:T(8,128)(2,1)S(1)}, u32[]{:S(2)}, u32[]{:S(2)}) collective-permute-start(bf16[128,1536]{1,0:T(8,128)(2,1)} %raw_ref.3), channel_id=1, source_target_pairs={{0,3},{1,2},{2,1},{3,0},{4,7},{5,6},{6,5},{7,4},{8,11},{9,10},{10,... | collective-permute-start | bytes 1179656 | tf_op jit(solution)/shard_map/ppermute | solution.py:151
  32.1 1.0 copy-start
  33.1 1.0 copy-start.2
  34.3 73.7 %collective-permute-start.5 = (bf16[256,1536]{1,0:T(8,128)(2,1)S(1)}, bf16[256,1536]{1,0:T(8,128)(2,1)}, u32[]{:S(2)}, u32[]{:S(2)}) collective-permute-start(bf16[256,1536]{1,0:T(8,128)(2,1)S(1)} %shard_map.59.own), channel_id=1, source_target_pairs={{0,1023},{1,1020},{2,1021},{3,1022},{4,8},{5,9},{6,10},{7,11},{8,4... | collective-permute-start | bytes 2359304 | tf_op jit(solution)/shard_map/ppermute | solution.py:153
  37.6 70.4 %collective-permute-start.4 = (bf16[256,1536]{1,0:T(8,128)(2,1)S(1)}, bf16[256,1536]{1,0:T(8,128)(2,1)}, u32[]{:S(2)}, u32[]{:S(2)}) collective-permute-start(bf16[256,1536]{1,0:T(8,128)(2,1)S(1)} %shard_map.59.own), channel_id=1, source_target_pairs={{0,4},{1,5},{2,6},{3,7},{4,0},{5,1},{6,2},{7,3},{8,12},{9,13},{10,... | collective-permute-start | bytes 2359304 | tf_op jit(solution)/shard_map/ppermute | solution.py:154
  100.0 17.5 %collective-permute-start.3 = (bf16[256,1536]{1,0:T(8,128)(2,1)S(1)}, bf16[256,1536]{1,0:T(8,128)(2,1)S(1)}, u32[]{:S(2)}, u32[]{:S(2)}) collective-permute-start(bf16[256,1536]{1,0:T(8,128)(2,1)S(1)} %shard_map.60.far), channel_id=1, source_target_pairs={{0,1023},{1,1020},{2,1021},{3,1022},{4,8},{5,9},{6,10},{7,11},{8,4... | collective-permute-start | bytes 2359304 | tf_op jit(solution)/shard_map/ppermute | solution.py:156
  103.5 14.1 %collective-permute-start.2 = (bf16[256,1536]{1,0:T(8,128)(2,1)S(1)}, bf16[256,1536]{1,0:T(8,128)(2,1)S(1)}, u32[]{:S(2)}, u32[]{:S(2)}) collective-permute-start(bf16[256,1536]{1,0:T(8,128)(2,1)S(1)} %shard_map.60.far), channel_id=1, source_target_pairs={{0,4},{1,5},{2,6},{3,7},{4,0},{5,1},{6,2},{7,3},{8,12},{9,13},{10,... | collective-permute-start | bytes 2359304 | tf_op jit(solution)/shard_map/ppermute | solution.py:157
  117.5 76.7 %copy-start.1 = (bf16[128,1536]{1,0:T(8,128)(2,1)S(1)}, bf16[128,1536]{1,0:T(8,128)(2,1)}, u32[]{:S(2)}) copy-start(bf16[128,1536]{1,0:T(8,128)(2,1)} %raw_ref.2) | copy-start | bytes 1179652
  118.7 77.6 %copy-start.3 = (bf16[128,1536]{1,0:T(8,128)(2,1)S(1)}, bf16[128,1536]{1,0:T(8,128)(2,1)}, u32[]{:S(2)}) copy-start(bf16[128,1536]{1,0:T(8,128)(2,1)} %raw_ref.3) | copy-start | bytes 1179652
  118.7 75.5 %collective-permute-start.6 = (bf16[128,1536]{1,0:T(8,128)(2,1)S(1)}, bf16[128,1536]{1,0:T(8,128)(2,1)S(1)}, u32[]{:S(2)}, u32[]{:S(2)}) collective-permute-start(bf16[128,1536]{1,0:T(8,128)(2,1)S(1)} %get-tuple-element.11), channel_id=1, source_target_pairs={{0,1},{1,0},{2,3},{3,2},{4,5},{5,4},{6,7},{7,6},{8,9},{9,8},{10,11... | collective-permute-start | bytes 1179656 | tf_op jit(solution)/shard_map/ppermute | solution.py:169
  128.7 67.5 %collective-permute-start.7 = (bf16[128,1536]{1,0:T(8,128)(2,1)S(1)}, bf16[128,1536]{1,0:T(8,128)(2,1)S(1)}, u32[]{:S(2)}, u32[]{:S(2)}) collective-permute-start(bf16[128,1536]{1,0:T(8,128)(2,1)S(1)} %get-tuple-element.13), channel_id=1, source_target_pairs={{0,3},{1,2},{2,1},{3,0},{4,7},{5,6},{6,5},{7,4},{8,11},{9,10},{10,... | collective-permute-start | bytes 1179656 | tf_op jit(solution)/shard_map/ppermute | solution.py:170

commit v4 on v3

v4 whole, which is shorter than its diff:
```python
import jax
import jax.numpy as jnp
from jax import lax
from jax.experimental import pallas as pl
from jax.experimental.pallas import tpu as pltpu
from jax.sharding import PartitionSpec as P

AXES = ("dp", "fsdp")
SPAN = 16
STRIP = 32
VMEM_LIMIT = 32 * 1024 * 1024


def device_of(block, role, blocks, ways):
    block = block % blocks
    return block * ways + (role + block // SPAN) % ways


def routes(blocks, ways):
    first, second, mate, cross = [], [], [], []
    for block in range(blocks):
        for role in range(ways):
            here = device_of(block, role, blocks, ways)
            img = device_of(block, role ^ 1, blocks, ways)
            txt = device_of(block, ways - 1 - role, blocks, ways)
            across = block + 1 if block % 2 else block - 1
            first.append((here, txt if block % 2 else img))
            second.append((here, img if block % 2 else txt))
            mate.append((here, device_of(block ^ 1, role, blocks, ways)))
            cross.append((here, device_of(across, role, blocks, ways)))
    return first, second, mate, cross


def strips(rows):
    return [slice(start, start + STRIP) for start in range(0, rows, STRIP)]


def inverse_of(values):
    return lax.rsqrt(jnp.sum(values * values, axis=-1, keepdims=True) + 1e-06)


def low_of(raw):
    values = raw.astype(jnp.float32)
    return (values * inverse_of(values)).astype(jnp.bfloat16)


def start_kernel(odd_ref, img_ref, txt_ref, x_raw, y_raw, x_low, y_low, both):
    rows = img_ref.shape[0]
    odd = odd_ref[0] > 0
    for here in strips(rows):
        img, txt = img_ref[here, :], txt_ref[here, :]
        x, y = jnp.where(odd, txt, img), jnp.where(odd, img, txt)
        x_raw[here, :] = x
        y_raw[here, :] = y
        x_low[here, :] = low_of(x)
        y_low[here, :] = low_of(y)
    both[:rows, :] = x_low[...]
    both[rows:, :] = y_low[...]


def scores_of(left, right):
    return lax.dot_general(left, right, (((1,), (1,)), ((), ())), preferred_element_type=jnp.float32)


def negative_coef(left, right, scale, bias):
    return (jax.nn.sigmoid(scale * scores_of(left, right) + bias) * scale).astype(jnp.bfloat16)


def columns_of(width, step=256):
    return [slice(start, start + step) for start in range(0, width, step)]


def dot(coef, rows):
    return jnp.dot(coef, rows, preferred_element_type=jnp.float32)


def stack(out_ref, *pieces):
    rows = out_ref.shape[0] // len(pieces)
    for place, piece in enumerate(pieces):
        out_ref[place * rows : (place + 1) * rows, :] = piece


def side_kernel(scale_ref, bias_ref, own, far, mate, cross, mate_far, cross_far, acc, x, near):
    rows = own.shape[0]
    stack(x, own[...], far[...])
    stack(near, mate[:rows, :], mate_far[...], cross[:rows, :], cross_far[...])
    coef = negative_coef(x[...], near[...], scale_ref[0], bias_ref[0])
    for cols in columns_of(own.shape[1]):
        acc[:, cols] = dot(coef, near[:, cols])


def block_kernel(scale_ref, bias_ref, x_own, x_far, y_own, y_far, acc, kept, sent, coef_t, x, y):
    rows = x_own.shape[0]
    scale, bias = scale_ref[0], bias_ref[0]
    stack(x, x_own[...], x_far[...])
    stack(y, y_own[...], y_far[...])
    shape = (2 * rows, 2 * rows)
    first = lax.broadcasted_iota(jnp.int32, shape, 0)
    positive = (first == lax.broadcasted_iota(jnp.int32, shape, 1)) & (first < rows)
    logits = scale * scores_of(x[...], y[...]) + bias
    size = jax.nn.sigmoid(jnp.where(positive, -logits, logits)) * scale
    signed = jnp.where(positive, -size, size)
    coef = signed.astype(jnp.bfloat16)
    coef_t[...] = signed.T.astype(jnp.bfloat16)
    for cols in columns_of(x_own.shape[1]):
        total = acc[:, cols] + dot(coef, y[:, cols])
        kept[:, cols] = total[:rows]
        sent[:, cols] = total[rows:].astype(jnp.bfloat16)


def last_kernel(
    scale_ref, bias_ref, x_own, x_far, y_own, y_far, coef_t, mate, cross, mate_far, cross_far,
    kept, sent, x, y, near,
):
    rows = x_own.shape[0]
    stack(x, x_own[...], x_far[...])
    stack(y, y_own[...], y_far[...])
    stack(near, mate[rows:, :], mate_far[...], cross[rows:, :], cross_far[...])
    coef = negative_coef(y[...], near[...], scale_ref[0], bias_ref[0])
    for cols in columns_of(x_own.shape[1]):
        total = dot(coef_t[...], x[:, cols]) + dot(coef, near[:, cols])
        kept[:, cols] = total[:rows]
        sent[:, cols] = total[rows:].astype(jnp.bfloat16)


def grad_strip(raw, direction):
    values = raw.astype(jnp.float32)
    inverse = inverse_of(values)
    norm = values * inverse
    inner = jnp.sum(norm * direction, axis=-1, keepdims=True)
    return ((direction - norm * inner) * inverse).astype(jnp.bfloat16)


def first_grad_kernel(raw, kept, there, out):
    for here in strips(raw.shape[0]):
        out[here, :] = grad_strip(raw[here, :], kept[here, :] + there[here, :].astype(jnp.float32))


def second_grad_kernel(odd_ref, raw, kept, there, x_grad, img_grad, txt_grad):
    odd = odd_ref[0] > 0
    for here in strips(raw.shape[0]):
        y = grad_strip(raw[here, :], kept[here, :] + there[here, :].astype(jnp.float32))
        x = x_grad[here, :]
        img_grad[here, :] = jnp.where(odd, y, x)
        txt_grad[here, :] = jnp.where(odd, x, y)


def call(kernel, outs, scalars, arrays, scratch=(), flops=0):
    moved = sum(a.size * a.dtype.itemsize for a in arrays)
    return pl.pallas_call(
        kernel,
        out_shape=outs,
        in_specs=[pl.BlockSpec(memory_space=pltpu.SMEM)] * len(scalars)
        + [pl.BlockSpec(memory_space=pltpu.VMEM)] * len(arrays),
        out_specs=jax.tree.map(lambda _: pl.BlockSpec(memory_space=pltpu.VMEM), outs),
        scratch_shapes=list(scratch),
        compiler_params=pltpu.CompilerParams(vmem_limit_bytes=VMEM_LIMIT),
        cost_estimate=pl.CostEstimate(flops=flops, bytes_accessed=moved, transcendentals=0),
    )(*scalars, *arrays)


def local(img_raw, txt_raw, logit_scale, logit_bias, moves):
    first, second, to_mate, to_cross = moves
    rows, width = img_raw.shape
    odd = (lax.axis_index("dp") % 2).astype(jnp.int32).reshape(1)
    scalars = (logit_scale.reshape(1), logit_bias.reshape(1))

    def shape(count, kind):
        return jax.ShapeDtypeStruct((count * rows, width), kind)

    def space(count):
        return pltpu.VMEM((count * rows, width), jnp.bfloat16)

    piece, kept = shape(1, jnp.bfloat16), shape(1, jnp.float32)
    coef_shape = jax.ShapeDtypeStruct((2 * rows, 2 * rows), jnp.bfloat16)
    unit = 2 * (2 * rows) * (2 * rows) * width

    x_raw, y_raw, x, y, both = call(
        start_kernel, (piece,) * 4 + (shape(2, jnp.bfloat16),), (odd,), (img_raw, txt_raw)
    )
    x_far = lax.ppermute(x, AXES, first)
    y_far = lax.ppermute(y, AXES, second)
    cross = lax.ppermute(both, AXES, to_cross)
    mate = lax.ppermute(both, AXES, to_mate)
    x_cross = lax.ppermute(x_far, AXES, to_cross)
    x_mate = lax.ppermute(x_far, AXES, to_mate)
    acc = call(
        side_kernel,
        shape(2, jnp.float32),
        scalars,
        (x, x_far, mate, cross, x_mate, x_cross),
        (space(2), space(4)),
        4 * unit,
    )
    y_cross = lax.ppermute(y_far, AXES, to_cross)
    y_mate = lax.ppermute(y_far, AXES, to_mate)
    x_kept, x_sent, coef_t = call(
        block_kernel,
        (kept, piece, coef_shape),
        scalars,
        (x, x_far, y, y_far, acc),
        (space(2), space(2)),
        2 * unit,
    )
    x_back = lax.ppermute(x_sent, AXES, first)
    y_kept, y_sent = call(
        last_kernel,
        (kept, piece),
        scalars,
        (x, x_far, y, y_far, coef_t, mate, cross, y_mate, y_cross),
        (space(2), space(2), space(4)),
        5 * unit,
    )
    y_back = lax.ppermute(y_sent, AXES, second)
    x_grad = call(first_grad_kernel, piece, (), (x_raw, x_kept, x_back))
    return call(
        second_grad_kernel, (piece, piece), (odd,), (y_raw, y_kept, y_back, x_grad)
    )


def solution(mesh):
    moves = routes(mesh.shape["dp"], mesh.shape["fsdp"])
    in_specs = (P(AXES, None), P(AXES, None), P(), P())
    out_specs = (P(AXES, None), P(AXES, None))

    def step(*args):
        return local(*args, moves)

    return jax.shard_map(step, mesh=mesh, in_specs=in_specs, out_specs=out_specs, check_vma=False)
```

time: 201 us -> 199 us (0.990)
  the two profiles are of different devices: /device:TPU:24 before, /device:TPU:50 now
where the time goes in v4:
time: 199 us
  waiting for transfers between devices  105 us (53%)
  starting transfers between devices  77.7 us (39%)
  Pallas kernels  8.3 us (4%)
  local copies, waits for them, and re-layouts  5.24 us (3%)
  between operations  2.16 us (1%)
    ppermute x1, waiting for transfers between devices, local(): x_back = lax.ppermute(x_sent, AXES, first)  58.6 us
    ppermute x1, waiting for transfers between devices, local(): x_far = lax.ppermute(x, AXES, first)  46.6 us
    ppermute x1, starting transfers between devices, local(): x_far = lax.ppermute(x, AXES, first)  22.1 us
    ppermute x1, starting transfers between devices, local(): y_back = lax.ppermute(y_sent, AXES, second)  12.9 us
    ppermute x1, starting transfers between devices, local(): y_cross = lax.ppermute(y_far, AXES, to_cross)  11.6 us
    ppermute x1, starting transfers between devices, local(): y_far = lax.ppermute(y, AXES, second)  8.45 us
    pallas_call x6, Pallas kernels, call(): pl.pallas_call(kernel, out_shape=outs, in_specs=[pl.BlockSpec(memory_spac...  8.3 us
    ppermute x1, starting transfers between devices, local(): x_back = lax.ppermute(x_sent, AXES, first)  7.12 us
  transfers between devices with their start and end apart: 10, of which 2 were waited for; matrix products, arithmetic and copies ran while one was open for 0% of the time, Pallas kernels for 3%

profile of v4, /device:TPU:50, one launch (start us, length us, event | category | flops | bytes accessed | tf_op | source)
XLA Modules:
  0.0 198.6 jit_solution(2637302329541956714)
XLA Ops:
  0.6 0.0 copy-start.2
  0.7 1.0 copy-done.2
  1.6 0.0 copy-start.3
  1.6 1.0 copy-done.3
  2.6 1.2 shard_map.59
  3.8 0.0 copy-start.4
  3.8 0.7 copy-done.4
  4.6 0.0 copy-start.6
  4.6 0.8 copy-done.6
  5.3 22.1 %collective-permute-start = (bf16[128,1536]{1,0:T(8,128)(2,1)S(1)}, bf16[128,1536]{1,0:T(8,128)(2,1)S(1)}, u32[]{:S(2)}, u32[]{:S(2)}) collective-permute-start(bf16[128,1536]{1,0:T(8,128)(2,1)S(1)} %get-tuple-element.13.own.x_own), channel_id=1, source_target_pairs={{0,1},{1,0},{2,3},{3,2},{4,7},{5,6},{6,5},{7,4},{8,9},{9,8},{10,11... | collective-permute-start | bytes 1179656 | tf_op jit(solution)/shard_map/ppermute | solution.py:181
  27.4 1.9 collective-permute-start.2
  29.4 3.0 %collective-permute-start.3 = (bf16[256,1536]{1,0:T(8,128)(2,1)}, bf16[256,1536]{1,0:T(8,128)(2,1)S(1)}, u32[]{:S(2)}, u32[]{:S(2)}) collective-permute-start(bf16[256,1536]{1,0:T(8,128)(2,1)} %get-tuple-element.15), channel_id=1, source_target_pairs={{0,1023},{1,1020},{2,1021},{3,1022},{4,8},{5,9},{6,10},{7,11},{8,4... | collective-permute-start | bytes 2359304 | tf_op jit(solution)/shard_map/ppermute | solution.py:183
  32.4 8.4 %collective-permute-start.1 = (bf16[128,1536]{1,0:T(8,128)(2,1)S(1)}, bf16[128,1536]{1,0:T(8,128)(2,1)S(1)}, u32[]{:S(2)}, u32[]{:S(2)}) collective-permute-start(bf16[128,1536]{1,0:T(8,128)(2,1)S(1)} %get-tuple-element.14.y_own), channel_id=1, source_target_pairs={{0,3},{1,2},{2,1},{3,0},{4,5},{5,4},{6,7},{7,6},{8,11},{9,10},{10,... | collective-permute-start | bytes 1179656 | tf_op jit(solution)/shard_map/ppermute | solution.py:182
  40.8 46.6 %collective-permute-done.far.x_far = bf16[128,1536]{1,0:T(8,128)(2,1)S(1)} collective-permute-done((bf16[128,1536]{1,0:T(8,128)(2,1)S(1)}, bf16[128,1536]{1,0:T(8,128)(2,1)S(1)}, u32[]{:S(2)}, u32[]{:S(2)}) %collective-permute-start) | collective-permute-done | bytes 393248 | tf_op jit(solution)/shard_map/ppermute | solution.py:181
  87.5 1.9 collective-permute-start.4
  89.4 6.8 %collective-permute-start.5 = (bf16[128,1536]{1,0:T(8,128)(2,1)S(1)}, bf16[128,1536]{1,0:T(8,128)(2,1)}, u32[]{:S(2)}, u32[]{:S(2)}) collective-permute-start(bf16[128,1536]{1,0:T(8,128)(2,1)S(1)} %collective-permute-done.far.x_far), channel_id=1, source_target_pairs={{0,1023},{1,1020},{2,1021},{3,1022},{4,8},{5,9},{6,10},{7,11},{8,4... | collective-permute-start | bytes 1179656 | tf_op jit(solution)/shard_map/ppermute | solution.py:185
  96.2 0.0 collective-permute-done.1.y_far
  96.2 1.9 collective-permute-start.6
  98.1 0.0 collective-permute-done.4.mate_far
  98.1 0.0 copy-start
  98.1 0.7 copy-done
  98.9 11.6 %collective-permute-start.7 = (bf16[128,1536]{1,0:T(8,128)(2,1)S(1)}, bf16[128,1536]{1,0:T(8,128)(2,1)}, u32[]{:S(2)}, u32[]{:S(2)}) collective-permute-start(bf16[128,1536]{1,0:T(8,128)(2,1)S(1)} %collective-permute-done.1.y_far), channel_id=1, source_target_pairs={{0,1023},{1,1020},{2,1021},{3,1022},{4,8},{5,9},{6,10},{7,11},{8,4... | collective-permute-start | bytes 1179656 | tf_op jit(solution)/shard_map/ppermute | solution.py:195
  111.8 0.0 collective-permute-done.5.cross_far
  111.8 0.0 collective-permute-done.2.mate
  111.8 0.0 collective-permute-done.3.cross
  111.8 0.0 copy-start.1
  111.8 1.0 copy-done.1
  112.8 2.1 %shard_map.60.acc = f32[256,1536]{1,0:T(8,128)S(1)} custom-call(f32[1]{0:T(128)} %bitcast.3.scale_ref, f32[1]{0:T(128)} %bitcast.6.bias_ref, bf16[128,1536]{1,0:T(8,128)(2,1)S(1)} %get-tuple-element.13.own.x_own, bf16[128,1536]{1,0:T(8,128)(2,1)S(1)} %collective-permute-done.far.x_far, bf16[256,1536]{1,0:T(8,128)(2,1)S(1)} %collective-permute-done.2.mate, ...), custom_call_target="tpu_custom_call" | custom-call | flops 805306368 | bytes 3145728 | tf_op jit(solution)/shard_map/pallas_call | solution.py:150
  114.9 1.1 shard_map.61
  116.0 7.1 %collective-permute-start.9 = (bf16[128,1536]{1,0:T(8,128)(2,1)S(1)}, bf16[128,1536]{1,0:T(8,128)(2,1)S(1)}, u32[]{:S(2)}, u32[]{:S(2)}) collective-permute-start(bf16[128,1536]{1,0:T(8,128)(2,1)S(1)} %get-tuple-element.21), channel_id=1, source_target_pairs={{0,1},{1,0},{2,3},{3,2},{4,7},{5,6},{6,5},{7,4},{8,9},{9,8},{10,11... | collective-permute-start | bytes 1179656 | tf_op jit(solution)/shard_map/ppermute | solution.py:205
  123.1 0.0 collective-permute-done.6.mate_far
  123.1 0.0 collective-permute-done.7.cross_far
  123.1 0.0 copy-start.7
  123.1 2.4 %shard_map.62 = (f32[128,1536]{1,0:T(8,128)S(1)}, bf16[128,1536]{1,0:T(8,128)(2,1)S(1)}) custom-call(f32[1]{0:T(128)} %bitcast.5.scale_ref, f32[1]{0:T(128)} %bitcast.8.bias_ref, bf16[128,1536]{1,0:T(8,128)(2,1)S(1)} %get-tuple-element.13.own.x_own, bf16[128,1536]{1,0:T(8,128)(2,1)S(1)} %collective-permute-done.far.x_far, ...), custom_call_target="tpu_custom_call" | custom-call | flops 1006632960 | bytes 4063232 | tf_op jit(solution)/shard_map/pallas_call | solution.py:150
  125.5 0.0 copy-start.5
  125.5 12.9 %collective-permute-start.8 = (bf16[128,1536]{1,0:T(8,128)(2,1)S(1)}, bf16[128,1536]{1,0:T(8,128)(2,1)S(1)}, u32[]{:S(2)}, u32[]{:S(2)}) collective-permute-start(bf16[128,1536]{1,0:T(8,128)(2,1)S(1)} %get-tuple-element.18), channel_id=1, source_target_pairs={{0,3},{1,2},{2,1},{3,0},{4,5},{5,4},{6,7},{7,6},{8,11},{9,10},{10,... | collective-permute-start | bytes 1179656 | tf_op jit(solution)/shard_map/ppermute | solution.py:214
  138.4 58.6 %collective-permute-done.9.there = bf16[128,1536]{1,0:T(8,128)(2,1)S(1)} collective-permute-done((bf16[128,1536]{1,0:T(8,128)(2,1)S(1)}, bf16[128,1536]{1,0:T(8,128)(2,1)S(1)}, u32[]{:S(2)}, u32[]{:S(2)}) %collective-permute-start.9) | collective-permute-done | bytes 393248 | tf_op jit(solution)/shard_map/ppermute | solution.py:205
  197.0 0.0 copy-done.7
  197.0 0.3 shard_map.63.x_grad
  197.3 0.0 collective-permute-done.8.there
  197.3 0.0 copy-done.5
  197.3 1.3 shard_map.64
Async XLA Ops:
  0.6 1.0 copy-start.2
  1.6 1.0 copy-start.3
  3.8 0.7 copy-start.4
  4.6 0.8 copy-start.6
  5.3 82.1 %collective-permute-start = (bf16[128,1536]{1,0:T(8,128)(2,1)S(1)}, bf16[128,1536]{1,0:T(8,128)(2,1)S(1)}, u32[]{:S(2)}, u32[]{:S(2)}) collective-permute-start(bf16[128,1536]{1,0:T(8,128)(2,1)S(1)} %get-tuple-element.13.own.x_own), channel_id=1, source_target_pairs={{0,1},{1,0},{2,3},{3,2},{4,7},{5,6},{6,5},{7,4},{8,9},{9,8},{10,11... | collective-permute-start | bytes 1179656 | tf_op jit(solution)/shard_map/ppermute | solution.py:181
  27.4 84.3 %collective-permute-start.2 = (bf16[256,1536]{1,0:T(8,128)(2,1)}, bf16[256,1536]{1,0:T(8,128)(2,1)S(1)}, u32[]{:S(2)}, u32[]{:S(2)}) collective-permute-start(bf16[256,1536]{1,0:T(8,128)(2,1)} %get-tuple-element.15), channel_id=1, source_target_pairs={{0,4},{1,5},{2,6},{3,7},{4,0},{5,1},{6,2},{7,3},{8,12},{9,13},{10,... | collective-permute-start | bytes 2359304 | tf_op jit(solution)/shard_map/ppermute | solution.py:184
  29.4 82.4 %collective-permute-start.3 = (bf16[256,1536]{1,0:T(8,128)(2,1)}, bf16[256,1536]{1,0:T(8,128)(2,1)S(1)}, u32[]{:S(2)}, u32[]{:S(2)}) collective-permute-start(bf16[256,1536]{1,0:T(8,128)(2,1)} %get-tuple-element.15), channel_id=1, source_target_pairs={{0,1023},{1,1020},{2,1021},{3,1022},{4,8},{5,9},{6,10},{7,11},{8,4... | collective-permute-start | bytes 2359304 | tf_op jit(solution)/shard_map/ppermute | solution.py:183
  32.4 63.8 %collective-permute-start.1 = (bf16[128,1536]{1,0:T(8,128)(2,1)S(1)}, bf16[128,1536]{1,0:T(8,128)(2,1)S(1)}, u32[]{:S(2)}, u32[]{:S(2)}) collective-permute-start(bf16[128,1536]{1,0:T(8,128)(2,1)S(1)} %get-tuple-element.14.y_own), channel_id=1, source_target_pairs={{0,3},{1,2},{2,1},{3,0},{4,5},{5,4},{6,7},{7,6},{8,11},{9,10},{10,... | collective-permute-start | bytes 1179656 | tf_op jit(solution)/shard_map/ppermute | solution.py:182
  87.5 10.6 %collective-permute-start.4 = (bf16[128,1536]{1,0:T(8,128)(2,1)S(1)}, bf16[128,1536]{1,0:T(8,128)(2,1)S(1)}, u32[]{:S(2)}, u32[]{:S(2)}) collective-permute-start(bf16[128,1536]{1,0:T(8,128)(2,1)S(1)} %collective-permute-done.far.x_far), channel_id=1, source_target_pairs={{0,4},{1,5},{2,6},{3,7},{4,0},{5,1},{6,2},{7,3},{8,12},{9,13},{10,... | collective-permute-start | bytes 1179656 | tf_op jit(solution)/shard_map/ppermute | solution.py:186
  89.4 22.4 %collective-permute-start.5 = (bf16[128,1536]{1,0:T(8,128)(2,1)S(1)}, bf16[128,1536]{1,0:T(8,128)(2,1)}, u32[]{:S(2)}, u32[]{:S(2)}) collective-permute-start(bf16[128,1536]{1,0:T(8,128)(2,1)S(1)} %collective-permute-done.far.x_far), channel_id=1, source_target_pairs={{0,1023},{1,1020},{2,1021},{3,1022},{4,8},{5,9},{6,10},{7,11},{8,4... | collective-permute-start | bytes 1179656 | tf_op jit(solution)/shard_map/ppermute | solution.py:185
  96.2 26.9 %collective-permute-start.6 = (bf16[128,1536]{1,0:T(8,128)(2,1)S(1)}, bf16[128,1536]{1,0:T(8,128)(2,1)S(1)}, u32[]{:S(2)}, u32[]{:S(2)}) collective-permute-start(bf16[128,1536]{1,0:T(8,128)(2,1)S(1)} %collective-permute-done.1.y_far), channel_id=1, source_target_pairs={{0,4},{1,5},{2,6},{3,7},{4,0},{5,1},{6,2},{7,3},{8,12},{9,13},{10,... | collective-permute-start | bytes 1179656 | tf_op jit(solution)/shard_map/ppermute | solution.py:196
  98.1 0.7 copy-start
  98.9 24.2 %collective-permute-start.7 = (bf16[128,1536]{1,0:T(8,128)(2,1)S(1)}, bf16[128,1536]{1,0:T(8,128)(2,1)}, u32[]{:S(2)}, u32[]{:S(2)}) collective-permute-start(bf16[128,1536]{1,0:T(8,128)(2,1)S(1)} %collective-permute-done.1.y_far), channel_id=1, source_target_pairs={{0,1023},{1,1020},{2,1021},{3,1022},{4,8},{5,9},{6,10},{7,11},{8,4... | collective-permute-start | bytes 1179656 | tf_op jit(solution)/shard_map/ppermute | solution.py:195
  111.8 1.0 copy-start.1
  116.0 81.0 %collective-permute-start.9 = (bf16[128,1536]{1,0:T(8,128)(2,1)S(1)}, bf16[128,1536]{1,0:T(8,128)(2,1)S(1)}, u32[]{:S(2)}, u32[]{:S(2)}) collective-permute-start(bf16[128,1536]{1,0:T(8,128)(2,1)S(1)} %get-tuple-element.21), channel_id=1, source_target_pairs={{0,1},{1,0},{2,3},{3,2},{4,7},{5,6},{6,5},{7,4},{8,9},{9,8},{10,11... | collective-permute-start | bytes 1179656 | tf_op jit(solution)/shard_map/ppermute | solution.py:205
  123.1 73.8 %copy-start.7 = (bf16[128,1536]{1,0:T(8,128)(2,1)S(1)}, bf16[128,1536]{1,0:T(8,128)(2,1)}, u32[]{:S(2)}) copy-start(bf16[128,1536]{1,0:T(8,128)(2,1)} %copy-done.6) | copy-start | bytes 1179652
  125.5 71.8 %copy-start.5 = (bf16[128,1536]{1,0:T(8,128)(2,1)S(1)}, bf16[128,1536]{1,0:T(8,128)(2,1)}, u32[]{:S(2)}) copy-start(bf16[128,1536]{1,0:T(8,128)(2,1)} %copy-done.4) | copy-start | bytes 1179652
  125.5 71.8 %collective-permute-start.8 = (bf16[128,1536]{1,0:T(8,128)(2,1)S(1)}, bf16[128,1536]{1,0:T(8,128)(2,1)S(1)}, u32[]{:S(2)}, u32[]{:S(2)}) collective-permute-start(bf16[128,1536]{1,0:T(8,128)(2,1)S(1)} %get-tuple-element.18), channel_id=1, source_target_pairs={{0,3},{1,2},{2,1},{3,0},{4,5},{5,4},{6,7},{7,6},{8,11},{9,10},{10,... | collective-permute-start | bytes 1179656 | tf_op jit(solution)/shard_map/ppermute | solution.py:214

commit v5 on v4

v5 whole, which is shorter than its diff:
```python
import jax
import jax.numpy as jnp
from jax import lax
from jax.experimental import pallas as pl
from jax.experimental.pallas import tpu as pltpu
from jax.sharding import PartitionSpec as P

AXES = ("dp", "fsdp")
SPAN = 16
STRIP = 32
VMEM_LIMIT = 16 * 1024 * 1024


def device_of(block, role, blocks, ways):
    block = block % blocks
    return block * ways + (role + block // SPAN) % ways


def routes(blocks, ways):
    first, second, mate, cross = [], [], [], []
    for block in range(blocks):
        for role in range(ways):
            here = device_of(block, role, blocks, ways)
            img = device_of(block, role ^ 1, blocks, ways)
            txt = device_of(block, ways - 1 - role, blocks, ways)
            ahead = device_of(block + 1, role, blocks, ways)
            first.append((here, txt if block % 2 else img))
            second.append((here, img if block % 2 else txt))
            (cross if block % 2 else mate).append((here, ahead))
    return first, second, mate, cross


def swaps(pairs):
    return [*pairs, *((second, first) for first, second in pairs)]


def strips(rows):
    return [slice(start, start + STRIP) for start in range(0, rows, STRIP)]


def inverse_of(values):
    return lax.rsqrt(jnp.sum(values * values, axis=-1, keepdims=True) + 1e-06)


def low_of(raw):
    values = raw.astype(jnp.float32)
    return (values * inverse_of(values)).astype(jnp.bfloat16)


def start_kernel(odd_ref, img_ref, txt_ref, x_low, y_low, both):
    odd = odd_ref[0] > 0
    img, txt = low_of(img_ref[...]), low_of(txt_ref[...])
    x, y = jnp.where(odd, txt, img), jnp.where(odd, img, txt)
    x_low[...] = x
    y_low[...] = y
    both[0] = x
    both[1] = y


def scores_of(left, right):
    return lax.dot_general(left, right, (((1,), (1,)), ((), ())), preferred_element_type=jnp.float32)


def negative_coef(left, right, scale, bias):
    return (jax.nn.sigmoid(scale * scores_of(left, right) + bias) * scale).astype(jnp.bfloat16)


def columns_of(width, step=256):
    return [slice(start, start + step) for start in range(0, width, step)]


def dot(coef, rows):
    return jnp.dot(coef, rows, preferred_element_type=jnp.float32)


def stack(out_ref, *pieces):
    rows = out_ref.shape[0] // len(pieces)
    for place, piece in enumerate(pieces):
        out_ref[place * rows : (place + 1) * rows, :] = piece


def other(ref, place, pieces, piece, rows):
    begin = pl.multiple_of((place * pieces + piece) * rows, rows)
    return ref.at[pl.ds(begin, rows), :]


def fetch(sources, out_ref, sems):
    rows = out_ref.shape[0] // len(sources)
    copies = []
    for place, source in enumerate(sources):
        part = out_ref.at[pl.ds(place * rows, rows), :]
        copies.append(pltpu.make_async_copy(source, part, sems.at[place]))
    for copy in copies:
        copy.start()
    for copy in copies:
        copy.wait()


def near_kernel(
    scale_ref, bias_ref, odd_ref, own, far, mate, cross, acc, y_near, x, near, sems
):
    rows = own.shape[0]
    odd = odd_ref[0]
    stack(x, own[...], far[...])
    places = ((mate, 1 - odd), (cross, odd))
    fetch([other(ref, place, 2, 0, rows) for ref, place in places], near, sems)
    fetch([other(ref, place, 2, 1, rows) for ref, place in places], y_near, sems)
    coef = negative_coef(x[...], near[...], scale_ref[0], bias_ref[0])
    for cols in columns_of(own.shape[1]):
        acc[:, cols] = dot(coef, near[:, cols])


def block_kernel(scale_ref, bias_ref, x_own, x_far, y_own, y_far, acc, out, coef_t, x, y):
    rows = x_own.shape[0]
    scale, bias = scale_ref[0], bias_ref[0]
    stack(x, x_own[...], x_far[...])
    stack(y, y_own[...], y_far[...])
    shape = (2 * rows, 2 * rows)
    first = lax.broadcasted_iota(jnp.int32, shape, 0)
    positive = (first == lax.broadcasted_iota(jnp.int32, shape, 1)) & (first < rows)
    logits = scale * scores_of(x[...], y[...]) + bias
    size = jax.nn.sigmoid(jnp.where(positive, -logits, logits)) * scale
    signed = jnp.where(positive, -size, size)
    coef = signed.astype(jnp.bfloat16)
    coef_t[...] = signed.T.astype(jnp.bfloat16)
    for cols in columns_of(x_own.shape[1]):
        out[:, cols] = acc[:, cols] + dot(coef, y[:, cols])


def far_kernel(
    scale_ref, bias_ref, odd_ref, own, far, acc, mate, cross, kept, sent, side, near, sems
):
    rows = own.shape[0]
    odd = odd_ref[0]
    stack(side, own[...], far[...])
    if mate.shape[0] > rows:
        mate, cross = other(mate, 1 - odd, 1, 0, rows), other(cross, odd, 1, 0, rows)
    fetch([mate, cross], near, sems)
    coef = negative_coef(side[...], near[...], scale_ref[0], bias_ref[0])
    for cols in columns_of(own.shape[1]):
        total = acc[:, cols] + dot(coef, near[:, cols])
        kept[:, cols] = total[:rows]
        sent[:, cols] = total[rows:].astype(jnp.bfloat16)


def far_pass_kernel(
    scale_ref, bias_ref, odd_ref, own, far, acc, held, mate, cross, kept, sent, passed, side, near, sems
):
    passed[...] = held[...]
    far_kernel(
        scale_ref, bias_ref, odd_ref, own, far, acc, mate, cross, kept, sent, side, near, sems
    )


def second_kernel(scale_ref, bias_ref, x_own, x_far, y_own, y_far, coef_t, near, acc, x, y):
    stack(x, x_own[...], x_far[...])
    stack(y, y_own[...], y_far[...])
    coef = negative_coef(y[...], near[...], scale_ref[0], bias_ref[0])
    for cols in columns_of(x_own.shape[1]):
        acc[:, cols] = dot(coef_t[...], x[:, cols]) + dot(coef, near[:, cols])


def grad_strip(raw, direction):
    values = raw.astype(jnp.float32)
    inverse = inverse_of(values)
    norm = values * inverse
    inner = jnp.sum(norm * direction, axis=-1, keepdims=True)
    return ((direction - norm * inner) * inverse).astype(jnp.bfloat16)


def first_grad_kernel(odd_ref, img_raw, txt_raw, kept, there, out):
    odd = odd_ref[0] > 0
    for here in strips(img_raw.shape[0]):
        raw = jnp.where(odd, txt_raw[here, :], img_raw[here, :])
        out[here, :] = grad_strip(raw, kept[here, :] + there[here, :].astype(jnp.float32))


def second_grad_kernel(odd_ref, img_raw, txt_raw, kept, there, x_grad, img_grad, txt_grad):
    odd = odd_ref[0] > 0
    for here in strips(img_raw.shape[0]):
        raw = jnp.where(odd, img_raw[here, :], txt_raw[here, :])
        y = grad_strip(raw, kept[here, :] + there[here, :].astype(jnp.float32))
        x = x_grad[here, :]
        img_grad[here, :] = jnp.where(odd, y, x)
        txt_grad[here, :] = jnp.where(odd, x, y)


def start(odd, img_raw, txt_raw):
    rows, width = img_raw.shape
    strip = pl.BlockSpec((STRIP, width), lambda i: (i, 0))
    piece = jax.ShapeDtypeStruct((rows, width), jnp.bfloat16)
    x, y, both = pl.pallas_call(
        start_kernel,
        grid=(rows // STRIP,),
        out_shape=(piece, piece, jax.ShapeDtypeStruct((2, rows, width), jnp.bfloat16)),
        in_specs=[pl.BlockSpec(memory_space=pltpu.SMEM), strip, strip],
        out_specs=(strip, strip, pl.BlockSpec((2, STRIP, width), lambda i: (0, i, 0))),
        compiler_params=pltpu.CompilerParams(vmem_limit_bytes=VMEM_LIMIT),
    )(odd, img_raw, txt_raw)
    return x, y, both.reshape(2 * rows, width)


def call(kernel, outs, scalars, arrays, there=(), scratch=(), flops=0):
    moved = sum(a.size * a.dtype.itemsize for a in arrays)
    return pl.pallas_call(
        kernel,
        out_shape=outs,
        in_specs=[pl.BlockSpec(memory_space=pltpu.SMEM)] * len(scalars)
        + [pl.BlockSpec(memory_space=pltpu.VMEM)] * len(arrays)
        + [pl.BlockSpec(memory_space=pl.ANY)] * len(there),
        out_specs=jax.tree.map(lambda _: pl.BlockSpec(memory_space=pltpu.VMEM), outs),
        scratch_shapes=list(scratch),
        compiler_params=pltpu.CompilerParams(vmem_limit_bytes=VMEM_LIMIT),
        cost_estimate=pl.CostEstimate(flops=flops, bytes_accessed=moved, transcendentals=0),
    )(*scalars, *arrays, *there)


def local(img_raw, txt_raw, logit_scale, logit_bias, moves):
    first, second, mates, across = moves
    rows, width = img_raw.shape
    odd = (lax.axis_index("dp") & 1).astype(jnp.int32).reshape(1)
    scalars = (logit_scale.reshape(1), logit_bias.reshape(1))

    def shape(count, kind):
        return jax.ShapeDtypeStruct((count * rows, width), kind)

    def gathered(array, groups):
        return lax.all_gather(array, AXES, axis=0, tiled=True, axis_index_groups=[list(group) for group in groups])

    pair, sems = pltpu.VMEM((2 * rows, width), jnp.bfloat16), pltpu.SemaphoreType.DMA((2,))
    piece, kept, acc = shape(1, jnp.bfloat16), shape(1, jnp.float32), shape(2, jnp.float32)
    coef_shape = jax.ShapeDtypeStruct((2 * rows, 2 * rows), jnp.bfloat16)
    unit = 2 * (2 * rows) * (2 * rows) * width

    x, y, both = start(odd, img_raw, txt_raw)
    mate, cross = gathered(both, mates), gathered(both, across)
    x_far = lax.ppermute(x, AXES, first)
    y_far = lax.ppermute(y, AXES, second)
    x_cross = lax.ppermute(x_far, AXES, swaps(across))
    x_mate = lax.ppermute(x_far, AXES, swaps(mates))
    x_acc, y_near = call(
        near_kernel,
        (acc, shape(2, jnp.bfloat16)),
        (*scalars, odd),
        (x, x_far),
        (mate, cross),
        (pair, pair, sems),
        2 * unit,
    )
    x_acc, coef_t = call(
        block_kernel, (acc, coef_shape), scalars, (x, x_far, y, y_far, x_acc), (), (pair, pair), 4 * unit
    )
    x_kept, x_sent, y_passed = call(
        far_pass_kernel,
        (kept, piece, piece),
        (*scalars, odd),
        (x, x_far, x_acc, y_far),
        (x_mate, x_cross),
        (pair, pair, sems),
        2 * unit,
    )
    y_cross, y_mate = gathered(y_passed, across), gathered(y_passed, mates)
    x_back = lax.ppermute(x_sent, AXES, first)
    y_acc = call(
        second_kernel, acc, scalars, (x, x_far, y, y_far, coef_t, y_near), (), (pair, pair), 3 * unit
    )
    y_kept, y_sent = call(
        far_kernel,
        (kept, piece),
        (*scalars, odd),
        (y, y_far, y_acc),
        (y_mate, y_cross),
        (pair, pair, sems),
        2 * unit,
    )
    y_back = lax.ppermute(y_sent, AXES, second)
    x_grad = call(first_grad_kernel, piece, (odd,), (img_raw, txt_raw, x_kept, x_back))
    return call(
        second_grad_kernel,
        (piece, piece),
        (odd,),
        (img_raw, txt_raw, y_kept, y_back, x_grad),
    )


def solution(mesh):
    moves = routes(mesh.shape["dp"], mesh.shape["fsdp"])
    in_specs = (P(AXES, None), P(AXES, None), P(), P())
    out_specs = (P(AXES, None), P(AXES, None))

    def step(*args):
        return local(*args, moves)

    return jax.shard_map(step, mesh=mesh, in_specs=in_specs, out_specs=out_specs, check_vma=False)
```

time: 199 us -> 227 us (1.14)
  the two profiles are of different devices: /device:TPU:50 before, /device:TPU:1 now
where the time goes in v5:
time: 227 us
  waiting for transfers between devices  127 us (56%)
  starting transfers between devices  55.4 us (24%)
  between operations  15.5 us (7%)
  blocking collectives  12.7 us (6%)
  Pallas kernels  10.8 us (5%)
  local copies, waits for them, and re-layouts  4.81 us (2%)
    ppermute x1, waiting for transfers between devices, local(): x_back = lax.ppermute(x_sent, AXES, first)  59.3 us
    ppermute x1, waiting for transfers between devices, local(): x_far = lax.ppermute(x, AXES, first)  55.6 us
    ppermute x1, starting transfers between devices, local(): x_far = lax.ppermute(x, AXES, first)  23.5 us
    all_gather x2, blocking collectives, gathered(): lax.all_gather(array, AXES, axis=0, tiled=True, axis_index_groups=[list(g...  12.7 us
    ppermute x1, starting transfers between devices, local(): y_back = lax.ppermute(y_sent, AXES, second)  12.4 us
    all_gather x2, waiting for transfers between devices, gathered(): lax.all_gather(array, AXES, axis=0, tiled=True, axis_index_groups=[list(g...  11.6 us
    pallas_call x7, Pallas kernels, call(): pl.pallas_call(kernel, out_shape=outs, in_specs=[pl.BlockSpec(memory_spac...  8.95 us
    ppermute x1, starting transfers between devices, local(): y_far = lax.ppermute(y, AXES, second)  8.17 us
  transfers between devices with their start and end apart: 8, of which 3 were waited for; matrix products, arithmetic and copies ran while one was open for 0% of the time, Pallas kernels for 3%

profile of v5, /device:TPU:1, one launch (start us, length us, event | category | flops | bytes accessed | tf_op | source)
XLA Modules:
  0.0 226.6 jit_solution(16678317060406187999)
XLA Ops:
  7.2 0.0 all-gather.3.cloned.1.call-start
  7.2 0.0 copy-start
  7.2 1.0 copy-done
  8.2 0.0 copy-start.2
  8.2 1.0 copy-done.2
  9.2 1.9 shard_map.59
  11.1 0.0 all-gather.3.cloned.1.call-update
  11.1 0.0 all-gather.5.cloned.1.call-start
  11.1 0.7 all-gather.5.cloned.1.call-update
  11.8 23.5 %collective-permute-start.1 = (bf16[128,1536]{1,0:T(8,128)(2,1)S(1)}, bf16[128,1536]{1,0:T(8,128)(2,1)S(1)}, u32[]{:S(2)}, u32[]{:S(2)}) collective-permute-start(bf16[128,1536]{1,0:T(8,128)(2,1)S(1)} %get-tuple-element.15.own.x_own), channel_id=1, source_target_pairs={{0,1},{1,0},{2,3},{3,2},{4,7},{5,6},{6,5},{7,4},{8,9},{9,8},{10,11... | collective-permute-start | bytes 1179656 | tf_op jit(solution)/shard_map/ppermute | solution.py:237
  35.4 8.2 %collective-permute-start = (bf16[128,1536]{1,0:T(8,128)(2,1)S(1)}, bf16[128,1536]{1,0:T(8,128)(2,1)S(1)}, u32[]{:S(2)}, u32[]{:S(2)}) collective-permute-start(bf16[128,1536]{1,0:T(8,128)(2,1)S(1)} %get-tuple-element.14.y_own.own), channel_id=1, source_target_pairs={{0,3},{1,2},{2,1},{3,0},{4,5},{5,4},{6,7},{7,6},{8,11},{9,10},{10,... | collective-permute-start | bytes 1179656 | tf_op jit(solution)/shard_map/ppermute | solution.py:238
  43.6 55.6 %collective-permute-done.1.far.x_far = bf16[128,1536]{1,0:T(8,128)(2,1)S(1)} collective-permute-done((bf16[128,1536]{1,0:T(8,128)(2,1)S(1)}, bf16[128,1536]{1,0:T(8,128)(2,1)S(1)}, u32[]{:S(2)}, u32[]{:S(2)}) %collective-permute-start.1) | collective-permute-done | bytes 393248 | tf_op jit(solution)/shard_map/ppermute | solution.py:237
  99.2 3.3 %collective-permute-start.2 = (bf16[128,1536]{1,0:T(8,128)(2,1)S(1)}, bf16[128,1536]{1,0:T(8,128)(2,1)S(1)}, u32[]{:S(2)}, u32[]{:S(2)}) collective-permute-start(bf16[128,1536]{1,0:T(8,128)(2,1)S(1)} %collective-permute-done.1.far.x_far), channel_id=1, source_target_pairs={{0,4},{1,5},{2,6},{3,7},{8,12},{9,13},{10,14},{11,15},{16,20},{17,... | collective-permute-start | bytes 1179656 | tf_op jit(solution)/shard_map/ppermute | solution.py:240
  102.5 1.9 collective-permute-start.3
  105.8 0.0 all-gather.3.cloned.1.call-done.mate
  105.8 11.6 %all-gather.5.cloned.1.call-done.cross = bf16[512,1536]{1,0:T(8,128)(2,1)} async-done(((bf16[256,1536]{1,0:T(8,128)(2,1)}), bf16[512,1536]{1,0:T(8,128)(2,1)}) %all-gather.5.cloned.1.call-update) | async-done | bytes 1572880 | tf_op jit(solution)/shard_map/all_gather | solution.py:228
  117.4 0.0 copy-start.4
  117.4 1.4 copy-done.4
  118.8 0.0 copy-start.5
  118.8 1.4 copy-done.5
  120.2 1.9 shard_map.60
  122.1 0.0 collective-permute-done.y_far.held.far
  122.1 1.1 shard_map.61
  123.2 0.0 collective-permute-done.2.mate
  123.2 0.0 collective-permute-done.3.cross
  123.2 1.5 shard_map.63
  124.8 4.6 %all_gather.14.mate = bf16[256,1536]{1,0:T(8,128)(2,1)S(1)} all-gather(bf16[128,1536]{1,0:T(8,128)(2,1)S(1)} %get-tuple-element.21), channel_id=1, replica_groups={{0,4},{1,5},{2,6},{3,7},{8,12},{9,13},{10,14},{11,15},{16,20},{17,21},{..., dimensions={0}, use_global_device_ids=true | all-gather | bytes 1179648 | tf_op jit(solution)/shard_map/all_gather | solution.py:228
  129.4 8.2 %all_gather.15.cross = bf16[256,1536]{1,0:T(8,128)(2,1)S(1)} all-gather(bf16[128,1536]{1,0:T(8,128)(2,1)S(1)} %get-tuple-element.21), channel_id=1, replica_groups={{4,8},{5,9},{6,10},{7,11},{12,16},{13,17},{14,18},{15,19},{20,24},{21,2..., dimensions={0}, use_global_device_ids=true | all-gather | bytes 1179648 | tf_op jit(solution)/shard_map/all_gather | solution.py:228
  137.5 6.0 %collective-permute-start.5 = (bf16[128,1536]{1,0:T(8,128)(2,1)S(1)}, bf16[128,1536]{1,0:T(8,128)(2,1)S(1)}, u32[]{:S(2)}, u32[]{:S(2)}) collective-permute-start(bf16[128,1536]{1,0:T(8,128)(2,1)S(1)} %get-tuple-element.25), channel_id=1, source_target_pairs={{0,1},{1,0},{2,3},{3,2},{4,7},{5,6},{6,5},{7,4},{8,9},{9,8},{10,11... | collective-permute-start | bytes 1179656 | tf_op jit(solution)/shard_map/ppermute | solution.py:263
  143.5 1.3 shard_map.62.acc
  144.9 0.0 copy-start.1
  144.9 0.0 copy-start.3
  144.9 1.5 shard_map.64
  146.4 12.4 %collective-permute-start.4 = (bf16[128,1536]{1,0:T(8,128)(2,1)S(1)}, bf16[128,1536]{1,0:T(8,128)(2,1)S(1)}, u32[]{:S(2)}, u32[]{:S(2)}) collective-permute-start(bf16[128,1536]{1,0:T(8,128)(2,1)S(1)} %get-tuple-element.23), channel_id=1, source_target_pairs={{0,3},{1,2},{2,1},{3,0},{4,5},{5,4},{6,7},{7,6},{8,11},{9,10},{10,... | collective-permute-start | bytes 1179656 | tf_op jit(solution)/shard_map/ppermute | solution.py:276
  158.8 59.3 %collective-permute-done.5.there = bf16[128,1536]{1,0:T(8,128)(2,1)S(1)} collective-permute-done((bf16[128,1536]{1,0:T(8,128)(2,1)S(1)}, bf16[128,1536]{1,0:T(8,128)(2,1)S(1)}, u32[]{:S(2)}, u32[]{:S(2)}) %collective-permute-start.5) | collective-permute-done | bytes 393248 | tf_op jit(solution)/shard_map/ppermute | solution.py:263
  218.1 0.0 copy-done.1
  218.1 0.0 copy-done.3
  218.1 0.3 shard_map.65.x_grad
  218.4 0.0 collective-permute-done.4.there
  218.4 1.3 shard_map.66
Async XLA Ops:
  7.2 98.6 %all-gather.3.cloned.1.call-start = ((), (), s32[]{:S(2)}) async-start(), calls=%async_computation | async-start | bytes 2359296 | tf_op jit(solution)/shard_map/all_gather | solution.py:228
  7.2 1.0 copy-start
  8.2 1.0 copy-start.2
  11.1 106.3 %all-gather.5.cloned.1.call-start = ((), (), s32[]{:S(2)}) async-start(), calls=%async_computation.1 | async-start | bytes 2359296 | tf_op jit(solution)/shard_map/all_gather | solution.py:228
  11.8 87.4 %collective-permute-start.1 = (bf16[128,1536]{1,0:T(8,128)(2,1)S(1)}, bf16[128,1536]{1,0:T(8,128)(2,1)S(1)}, u32[]{:S(2)}, u32[]{:S(2)}) collective-permute-start(bf16[128,1536]{1,0:T(8,128)(2,1)S(1)} %get-tuple-element.15.own.x_own), channel_id=1, source_target_pairs={{0,1},{1,0},{2,3},{3,2},{4,7},{5,6},{6,5},{7,4},{8,9},{9,8},{10,11... | collective-permute-start | bytes 1179656 | tf_op jit(solution)/shard_map/ppermute | solution.py:237
  35.4 86.7 %collective-permute-start = (bf16[128,1536]{1,0:T(8,128)(2,1)S(1)}, bf16[128,1536]{1,0:T(8,128)(2,1)S(1)}, u32[]{:S(2)}, u32[]{:S(2)}) collective-permute-start(bf16[128,1536]{1,0:T(8,128)(2,1)S(1)} %get-tuple-element.14.y_own.own), channel_id=1, source_target_pairs={{0,3},{1,2},{2,1},{3,0},{4,5},{5,4},{6,7},{7,6},{8,11},{9,10},{10,... | collective-permute-start | bytes 1179656 | tf_op jit(solution)/shard_map/ppermute | solution.py:238
  99.2 24.0 %collective-permute-start.2 = (bf16[128,1536]{1,0:T(8,128)(2,1)S(1)}, bf16[128,1536]{1,0:T(8,128)(2,1)S(1)}, u32[]{:S(2)}, u32[]{:S(2)}) collective-permute-start(bf16[128,1536]{1,0:T(8,128)(2,1)S(1)} %collective-permute-done.1.far.x_far), channel_id=1, source_target_pairs={{0,4},{1,5},{2,6},{3,7},{8,12},{9,13},{10,14},{11,15},{16,20},{17,... | collective-permute-start | bytes 1179656 | tf_op jit(solution)/shard_map/ppermute | solution.py:240
  102.5 20.7 %collective-permute-start.3 = (bf16[128,1536]{1,0:T(8,128)(2,1)S(1)}, bf16[128,1536]{1,0:T(8,128)(2,1)S(1)}, u32[]{:S(2)}, u32[]{:S(2)}) collective-permute-start(bf16[128,1536]{1,0:T(8,128)(2,1)S(1)} %collective-permute-done.1.far.x_far), channel_id=1, source_target_pairs={{4,8},{5,9},{6,10},{7,11},{12,16},{13,17},{14,18},{15,19},{20,24},... | collective-permute-start | bytes 1179656 | tf_op jit(solution)/shard_map/ppermute | solution.py:239
  117.4 1.4 copy-start.4
  118.8 1.4 copy-start.5
  137.5 80.5 %collective-permute-start.5 = (bf16[128,1536]{1,0:T(8,128)(2,1)S(1)}, bf16[128,1536]{1,0:T(8,128)(2,1)S(1)}, u32[]{:S(2)}, u32[]{:S(2)}) collective-permute-start(bf16[128,1536]{1,0:T(8,128)(2,1)S(1)} %get-tuple-element.25), channel_id=1, source_target_pairs={{0,1},{1,0},{2,3},{3,2},{4,7},{5,6},{6,5},{7,4},{8,9},{9,8},{10,11... | collective-permute-start | bytes 1179656 | tf_op jit(solution)/shard_map/ppermute | solution.py:263
  144.9 73.2 %copy-start.1 = (bf16[128,1536]{1,0:T(8,128)(2,1)S(1)}, bf16[128,1536]{1,0:T(8,128)(2,1)}, u32[]{:S(2)}) copy-start(bf16[128,1536]{1,0:T(8,128)(2,1)} %img_raw.3) | copy-start | bytes 1179652
  144.9 73.2 %copy-start.3 = (bf16[128,1536]{1,0:T(8,128)(2,1)S(1)}, bf16[128,1536]{1,0:T(8,128)(2,1)}, u32[]{:S(2)}) copy-start(bf16[128,1536]{1,0:T(8,128)(2,1)} %txt_raw.3) | copy-start | bytes 1179652
  146.4 72.0 %collective-permute-start.4 = (bf16[128,1536]{1,0:T(8,128)(2,1)S(1)}, bf16[128,1536]{1,0:T(8,128)(2,1)S(1)}, u32[]{:S(2)}, u32[]{:S(2)}) collective-permute-start(bf16[128,1536]{1,0:T(8,128)(2,1)S(1)} %get-tuple-element.23), channel_id=1, source_target_pairs={{0,3},{1,2},{2,1},{3,0},{4,5},{5,4},{6,7},{7,6},{8,11},{9,10},{10,... | collective-permute-start | bytes 1179656 | tf_op jit(solution)/shard_map/ppermute | solution.py:276
Sparse Core Ops, SparseCore 0:
  11.2 41.7 all-gather.2
  55.7 61.7 all-gather.4

commit v6 on v3

--- a/solution.py
+++ b/solution.py
@@ -17,13 +17,14 @@
 
 
 def routes(blocks, ways):
-    img, txt, mate, cross = [], [], [], []
+    img, txt, mate, cross = ([], []), ([], []), [], []
     for block in range(blocks):
         for role in range(ways):
             here = device_of(block, role, blocks, ways)
             across = block + 1 if block % 2 else block - 1
-            img.append((here, device_of(block, role ^ 1, blocks, ways)))
-            txt.append((here, device_of(block, ways - 1 - role, blocks, ways)))
+            group = block % SPAN * 2 // SPAN
+            img[group].append((here, device_of(block, role ^ 1, blocks, ways)))
+            txt[group].append((here, device_of(block, ways - 1 - role, blocks, ways)))
             mate.append((here, device_of(block ^ 1, role, blocks, ways)))
             cross.append((here, device_of(across, role, blocks, ways)))
     return img, txt, mate, cross
@@ -38,6 +39,21 @@
     for part, ref in enumerate((img_ref, txt_ref)):
         for start in range(0, rows, STRIP):
             values = ref[start : start + STRIP, :].astype(jnp.float32)
+            strip = (values * inverse_of(values)).astype(jnp.bfloat16)
+            low_ref[part * rows + start : part * rows + start + STRIP, :] = strip
+
+
+def pass_kernel(img_ref, txt_ref, mate_ref, cross_ref, img_out, txt_out):
+    del mate_ref, cross_ref
+    img_out[...] = img_ref[...]
+    txt_out[...] = txt_ref[...]
+
+
+def sum_kernel(img_a, img_b, txt_a, txt_b, low_ref):
+    rows = img_a.shape[0]
+    for part, refs in enumerate(((img_a, img_b), (txt_a, txt_b))):
+        for start in range(0, rows, STRIP):
+            values = sum(ref[start : start + STRIP, :].astype(jnp.float32) for ref in refs)
             strip = (values * inverse_of(values)).astype(jnp.bfloat16)
             low_ref[part * rows + start : part * rows + start + STRIP, :] = strip
 
@@ -87,7 +103,7 @@
 
 
 def far_kernel(
-    scale_ref, bias_ref, own, far, mate, cross, img_acc, txt_acc,
+    scale_ref, bias_ref, own, far, cross, mate, img_acc, txt_acc,
     img_own, img_far, txt_own, txt_far, img, txt, img_n, txt_n,
 ):
     rows = own.shape[0] // 2
@@ -122,18 +138,19 @@
         out_ref[here, :] = ((direction - norm * inner) * inverse).astype(jnp.bfloat16)
 
 
-def call(kernel, outs, scalars, arrays, scratch=(), flops=0):
+def call(kernel, outs, scalars, arrays, there=(), scratch=(), flops=0):
     moved = sum(a.size * a.dtype.itemsize for a in arrays)
     return pl.pallas_call(
         kernel,
         out_shape=outs,
         in_specs=[pl.BlockSpec(memory_space=pltpu.SMEM)] * len(scalars)
-        + [pl.BlockSpec(memory_space=pltpu.VMEM)] * len(arrays),
+        + [pl.BlockSpec(memory_space=pltpu.VMEM)] * len(arrays)
+        + [pl.BlockSpec(memory_space=pl.ANY)] * len(there),
         out_specs=jax.tree.map(lambda _: pl.BlockSpec(memory_space=pltpu.VMEM), outs),
         scratch_shapes=list(scratch),
         compiler_params=pltpu.CompilerParams(vmem_limit_bytes=VMEM_LIMIT),
         cost_estimate=pl.CostEstimate(flops=flops, bytes_accessed=moved, transcendentals=0),
-    )(*scalars, *arrays)
+    )(*scalars, *arrays, *there)
 
 
 def local(img_raw, txt_raw, logit_scale, logit_bias, moves):
@@ -147,27 +164,39 @@
     halves = [pltpu.VMEM((2 * rows, width), jnp.bfloat16)] * 4
     unit = 2 * (2 * rows) * (2 * rows) * width
 
-    img_there = lax.ppermute(img_raw, AXES, to_img)
-    txt_there = lax.ppermute(txt_raw, AXES, to_txt)
+    img_a = lax.ppermute(img_raw, AXES, to_img[0])
+    txt_a = lax.ppermute(txt_raw, AXES, to_txt[0])
     own = call(low_kernel, low_shape, (), (img_raw, txt_raw))
+    mate_own = lax.ppermute(own, AXES, to_mate)
     cross_own = lax.ppermute(own, AXES, to_cross)
-    mate_own = lax.ppermute(own, AXES, to_mate)
-    far = call(low_kernel, low_shape, (), (img_there, txt_there))
+    img_late, txt_late = call(
+        pass_kernel, (sent_shape, sent_shape), (), (img_raw, txt_raw), (mate_own, cross_own)
+    )
+    img_b = lax.ppermute(img_late, AXES, to_img[1])
+    txt_b = lax.ppermute(txt_late, AXES, to_txt[1])
+    far = call(sum_kernel, low_shape, (), (img_a, img_b, txt_a, txt_b))
+    mate_far = lax.ppermute(far, AXES, to_mate)
     cross_far = lax.ppermute(far, AXES, to_cross)
-    mate_far = lax.ppermute(far, AXES, to_mate)
     img_acc, txt_acc = call(
-        near_kernel, (acc_shape, acc_shape), scalars, (own, far, mate_own, cross_own), halves, 7 * unit
+        near_kernel,
+        (acc_shape, acc_shape),
+        scalars,
+        (own, far, mate_own, cross_own),
+        (),
+        halves,
+        7 * unit,
     )
     img_own, img_sent, txt_own, txt_sent = call(
         far_kernel,
         (own_shape, sent_shape, own_shape, sent_shape),
         scalars,
-        (own, far, mate_far, cross_far, img_acc, txt_acc),
+        (own, far, cross_far, mate_far, img_acc, txt_acc),
+        (),
         halves,
         4 * unit,
     )
-    img_back = lax.ppermute(img_sent, AXES, to_img)
-    txt_back = lax.ppermute(txt_sent, AXES, to_txt)
+    img_back = lax.ppermute(img_sent, AXES, to_img[0] + to_img[1])
+    txt_back = lax.ppermute(txt_sent, AXES, to_txt[0] + to_txt[1])
     img_grad = call(grad_kernel, sent_shape, (), (img_raw, img_own, img_back))
     txt_grad = call(grad_kernel, sent_shape, (), (txt_raw, txt_own, txt_back))
     return (img_grad, txt_grad)

time: 201 us -> 214 us (1.065)
  the two profiles are of different devices: /device:TPU:24 before, /device:TPU:6 now
where the time goes in v6:
time: 214 us
  waiting for transfers between devices  155 us (72%)
  starting transfers between devices  47.6 us (22%)
  Pallas kernels  7.17 us (3%)
    ppermute x1, waiting for transfers between devices, local(): img_back = lax.ppermute(img_sent, AXES, to_img[0] + to_img[1])  73.6 us
    ppermute x1, waiting for transfers between devices, local(): txt_a = lax.ppermute(txt_raw, AXES, to_txt[0])  45.5 us
    ppermute x1, waiting for transfers between devices, local(): img_a = lax.ppermute(img_raw, AXES, to_img[0])  25.6 us
    ppermute x1, starting transfers between devices, local(): cross_own = lax.ppermute(own, AXES, to_cross)  18.4 us
    ppermute x1, waiting for transfers between devices, local(): cross_far = lax.ppermute(far, AXES, to_cross)  10.4 us
    ppermute x1, starting transfers between devices, local(): img_a = lax.ppermute(img_raw, AXES, to_img[0])  8.45 us
    ppermute x1, starting transfers between devices, local(): txt_a = lax.ppermute(txt_raw, AXES, to_txt[0])  7.65 us
    pallas_call x7, Pallas kernels, call(): pl.pallas_call(kernel, out_shape=outs, in_specs=[pl.BlockSpec(memory_spac...  7.17 us
  transfers between devices with their start and end apart: 10, of which 4 were waited for; matrix products, arithmetic and copies ran while one was open for 0% of the time, Pallas kernels for 1%

profile of v6, /device:TPU:6, one launch (start us, length us, event | category | flops | bytes accessed | tf_op | source)
XLA Modules:
  0.0 214.0 jit_solution(10036590311277887485)
XLA Ops:
  0.6 0.0 copy-start
  0.6 1.0 copy-done
  1.6 0.0 copy-start.2
  1.6 1.0 copy-done.2
  2.6 0.2 shard_map.59.own
  2.9 18.4 %collective-permute-start.2 = (bf16[256,1536]{1,0:T(8,128)(2,1)S(1)}, bf16[256,1536]{1,0:T(8,128)(2,1)S(1)}, u32[]{:S(2)}, u32[]{:S(2)}) collective-permute-start(bf16[256,1536]{1,0:T(8,128)(2,1)S(1)} %shard_map.59.own), channel_id=1, source_target_pairs={{0,1023},{1,1020},{2,1021},{3,1022},{4,8},{5,9},{6,10},{7,11},{8,4... | collective-permute-start | bytes 2359304 | tf_op jit(solution)/shard_map/ppermute | solution.py:171
  21.3 1.9 collective-permute-start.1
  23.2 8.4 %collective-permute-start = (bf16[128,1536]{1,0:T(8,128)(2,1)S(1)}, bf16[128,1536]{1,0:T(8,128)(2,1)S(1)}, u32[]{:S(2)}, u32[]{:S(2)}) collective-permute-start(bf16[128,1536]{1,0:T(8,128)(2,1)S(1)} %copy-done), channel_id=1, source_target_pairs={{0,1},{1,0},{2,3},{3,2},{4,5},{5,4},{6,7},{7,6},{8,9},{9,8},{10,11... | collective-permute-start | bytes 1179656 | tf_op jit(solution)/shard_map/ppermute | solution.py:167
  31.6 7.6 %collective-permute-start.4 = (bf16[128,1536]{1,0:T(8,128)(2,1)S(1)}, bf16[128,1536]{1,0:T(8,128)(2,1)S(1)}, u32[]{:S(2)}, u32[]{:S(2)}) collective-permute-start(bf16[128,1536]{1,0:T(8,128)(2,1)S(1)} %copy-done.2), channel_id=1, source_target_pairs={{0,3},{1,2},{2,1},{3,0},{4,7},{5,6},{6,5},{7,4},{8,11},{9,10},{10,... | collective-permute-start | bytes 1179656 | tf_op jit(solution)/shard_map/ppermute | solution.py:168
  39.3 0.0 collective-permute-done.2.cross_ref.cross
  39.3 0.0 collective-permute-done.1.mate_ref.mate
  39.3 0.1 shard_map.60
  39.4 0.7 collective-permute-start.3
  40.1 0.7 collective-permute-start.5
  40.8 25.6 %collective-permute-done.img_a = bf16[128,1536]{1,0:T(8,128)(2,1)S(1)} collective-permute-done((bf16[128,1536]{1,0:T(8,128)(2,1)S(1)}, bf16[128,1536]{1,0:T(8,128)(2,1)S(1)}, u32[]{:S(2)}, u32[]{:S(2)}) %collective-permute-start) | collective-permute-done | bytes 393248 | tf_op jit(solution)/shard_map/ppermute | solution.py:167
  66.4 45.5 %collective-permute-done.4.txt_a = bf16[128,1536]{1,0:T(8,128)(2,1)S(1)} collective-permute-done((bf16[128,1536]{1,0:T(8,128)(2,1)S(1)}, bf16[128,1536]{1,0:T(8,128)(2,1)S(1)}, u32[]{:S(2)}, u32[]{:S(2)}) %collective-permute-start.4) | collective-permute-done | bytes 393248 | tf_op jit(solution)/shard_map/ppermute | solution.py:168
  111.9 0.0 collective-permute-done.3.img_b
  111.9 0.0 collective-permute-done.5.txt_b
  111.9 0.3 shard_map.61.far
  112.3 1.9 collective-permute-start.7
  114.2 1.9 collective-permute-start.6
  117.5 1.9 shard_map.62
  119.3 0.0 collective-permute-done.7.mate
  119.3 10.4 %collective-permute-done.6.cross = bf16[256,1536]{1,0:T(8,128)(2,1)} collective-permute-done((bf16[256,1536]{1,0:T(8,128)(2,1)S(1)}, bf16[256,1536]{1,0:T(8,128)(2,1)}, u32[]{:S(2)}, u32[]{:S(2)}) %collective-permute-start.6) | collective-permute-done | bytes 786464 | tf_op jit(solution)/shard_map/ppermute | solution.py:179
  129.8 0.0 copy-start.1
  129.8 2.5 %shard_map.63 = (f32[128,1536]{1,0:T(8,128)S(1)}, bf16[128,1536]{1,0:T(8,128)(2,1)S(1)}, f32[128,1536]{1,0:T(8,128)S(1)}, bf16[128,1536]{1,0:T(8,128)(2,1)S(1)}) custom-call(f32[1]{0:T(128)} %bitcast.3.scale_ref, f32[1]{0:T(128)} %bitcast.5.bias_ref, bf16[256,1536]{1,0:T(8,128)(2,1)S(1)} %shard_map.59.own, bf16[256,1536]{1,0:T(8,128)(2,1)S(1)} %shard_map.61.far, ...), custom_call_target="tpu_custom_call" | custom-call | flops 805306368 | bytes 6291456 | tf_op jit(solution)/shard_map/pallas_call | solution.py:143
  132.3 0.0 copy-start.3
  132.3 2.1 collective-permute-start.8
  134.4 3.9 %collective-permute-start.9 = (bf16[128,1536]{1,0:T(8,128)(2,1)S(1)}, bf16[128,1536]{1,0:T(8,128)(2,1)S(1)}, u32[]{:S(2)}, u32[]{:S(2)}) collective-permute-start(bf16[128,1536]{1,0:T(8,128)(2,1)S(1)} %get-tuple-element.17), channel_id=1, source_target_pairs={{0,3},{1,2},{2,1},{3,0},{4,7},{5,6},{6,5},{7,4},{8,11},{9,10},{10,... | collective-permute-start | bytes 1179656 | tf_op jit(solution)/shard_map/ppermute | solution.py:199
  138.3 73.6 %collective-permute-done.8.there_ref = bf16[128,1536]{1,0:T(8,128)(2,1)S(1)} collective-permute-done((bf16[128,1536]{1,0:T(8,128)(2,1)S(1)}, bf16[128,1536]{1,0:T(8,128)(2,1)S(1)}, u32[]{:S(2)}, u32[]{:S(2)}) %collective-permute-start.8) | collective-permute-done | bytes 393248 | tf_op jit(solution)/shard_map/ppermute | solution.py:198
  211.9 0.0 copy-done.1
  211.9 1.1 shard_map.64
  212.9 0.0 collective-permute-done.9.there_ref
  212.9 0.0 copy-done.3
  212.9 1.1 shard_map.65
Async XLA Ops:
  0.6 1.0 copy-start
  1.6 1.0 copy-start.2
  2.9 36.4 %collective-permute-start.2 = (bf16[256,1536]{1,0:T(8,128)(2,1)S(1)}, bf16[256,1536]{1,0:T(8,128)(2,1)S(1)}, u32[]{:S(2)}, u32[]{:S(2)}) collective-permute-start(bf16[256,1536]{1,0:T(8,128)(2,1)S(1)} %shard_map.59.own), channel_id=1, source_target_pairs={{0,1023},{1,1020},{2,1021},{3,1022},{4,8},{5,9},{6,10},{7,11},{8,4... | collective-permute-start | bytes 2359304 | tf_op jit(solution)/shard_map/ppermute | solution.py:171
  21.3 18.0 %collective-permute-start.1 = (bf16[256,1536]{1,0:T(8,128)(2,1)S(1)}, bf16[256,1536]{1,0:T(8,128)(2,1)S(1)}, u32[]{:S(2)}, u32[]{:S(2)}) collective-permute-start(bf16[256,1536]{1,0:T(8,128)(2,1)S(1)} %shard_map.59.own), channel_id=1, source_target_pairs={{0,4},{1,5},{2,6},{3,7},{4,0},{5,1},{6,2},{7,3},{8,12},{9,13},{10,... | collective-permute-start | bytes 2359304 | tf_op jit(solution)/shard_map/ppermute | solution.py:170
  23.2 43.2 %collective-permute-start = (bf16[128,1536]{1,0:T(8,128)(2,1)S(1)}, bf16[128,1536]{1,0:T(8,128)(2,1)S(1)}, u32[]{:S(2)}, u32[]{:S(2)}) collective-permute-start(bf16[128,1536]{1,0:T(8,128)(2,1)S(1)} %copy-done), channel_id=1, source_target_pairs={{0,1},{1,0},{2,3},{3,2},{4,5},{5,4},{6,7},{7,6},{8,9},{9,8},{10,11... | collective-permute-start | bytes 1179656 | tf_op jit(solution)/shard_map/ppermute | solution.py:167
  31.6 80.3 %collective-permute-start.4 = (bf16[128,1536]{1,0:T(8,128)(2,1)S(1)}, bf16[128,1536]{1,0:T(8,128)(2,1)S(1)}, u32[]{:S(2)}, u32[]{:S(2)}) collective-permute-start(bf16[128,1536]{1,0:T(8,128)(2,1)S(1)} %copy-done.2), channel_id=1, source_target_pairs={{0,3},{1,2},{2,1},{3,0},{4,7},{5,6},{6,5},{7,4},{8,11},{9,10},{10,... | collective-permute-start | bytes 1179656 | tf_op jit(solution)/shard_map/ppermute | solution.py:168
  39.4 72.5 %collective-permute-start.3 = (bf16[128,1536]{1,0:T(8,128)(2,1)S(1)}, bf16[128,1536]{1,0:T(8,128)(2,1)S(1)}, u32[]{:S(2)}, u32[]{:S(2)}) collective-permute-start(bf16[128,1536]{1,0:T(8,128)(2,1)S(1)} %get-tuple-element.10), channel_id=1, source_target_pairs={{32,33},{33,32},{34,35},{35,34},{36,37},{37,36},{38,39},{39,38},{4... | collective-permute-start | bytes 1179656 | tf_op jit(solution)/shard_map/ppermute | solution.py:175
  40.1 71.8 %collective-permute-start.5 = (bf16[128,1536]{1,0:T(8,128)(2,1)S(1)}, bf16[128,1536]{1,0:T(8,128)(2,1)S(1)}, u32[]{:S(2)}, u32[]{:S(2)}) collective-permute-start(bf16[128,1536]{1,0:T(8,128)(2,1)S(1)} %get-tuple-element.11), channel_id=1, source_target_pairs={{32,35},{33,34},{34,33},{35,32},{36,39},{37,38},{38,37},{39,36},{4... | collective-permute-start | bytes 1179656 | tf_op jit(solution)/shard_map/ppermute | solution.py:176
  112.3 7.0 %collective-permute-start.7 = (bf16[256,1536]{1,0:T(8,128)(2,1)S(1)}, bf16[256,1536]{1,0:T(8,128)(2,1)}, u32[]{:S(2)}, u32[]{:S(2)}) collective-permute-start(bf16[256,1536]{1,0:T(8,128)(2,1)S(1)} %shard_map.61.far), channel_id=1, source_target_pairs={{0,4},{1,5},{2,6},{3,7},{4,0},{5,1},{6,2},{7,3},{8,12},{9,13},{10,... | collective-permute-start | bytes 2359304 | tf_op jit(solution)/shard_map/ppermute | solution.py:178
  114.2 15.5 %collective-permute-start.6 = (bf16[256,1536]{1,0:T(8,128)(2,1)S(1)}, bf16[256,1536]{1,0:T(8,128)(2,1)}, u32[]{:S(2)}, u32[]{:S(2)}) collective-permute-start(bf16[256,1536]{1,0:T(8,128)(2,1)S(1)} %shard_map.61.far), channel_id=1, source_target_pairs={{0,1023},{1,1020},{2,1021},{3,1022},{4,8},{5,9},{6,10},{7,11},{8,4... | collective-permute-start | bytes 2359304 | tf_op jit(solution)/shard_map/ppermute | solution.py:179
  129.8 82.1 %copy-start.1 = (bf16[128,1536]{1,0:T(8,128)(2,1)S(1)}, bf16[128,1536]{1,0:T(8,128)(2,1)}, u32[]{:S(2)}) copy-start(bf16[128,1536]{1,0:T(8,128)(2,1)} %raw_ref.2) | copy-start | bytes 1179652
  132.3 80.6 %copy-start.3 = (bf16[128,1536]{1,0:T(8,128)(2,1)S(1)}, bf16[128,1536]{1,0:T(8,128)(2,1)}, u32[]{:S(2)}) copy-start(bf16[128,1536]{1,0:T(8,128)(2,1)} %raw_ref.3) | copy-start | bytes 1179652
  132.3 79.6 %collective-permute-start.8 = (bf16[128,1536]{1,0:T(8,128)(2,1)S(1)}, bf16[128,1536]{1,0:T(8,128)(2,1)S(1)}, u32[]{:S(2)}, u32[]{:S(2)}) collective-permute-start(bf16[128,1536]{1,0:T(8,128)(2,1)S(1)} %get-tuple-element.15), channel_id=1, source_target_pairs={{0,1},{1,0},{2,3},{3,2},{4,5},{5,4},{6,7},{7,6},{8,9},{9,8},{10,11... | collective-permute-start | bytes 1179656 | tf_op jit(solution)/shard_map/ppermute | solution.py:198
  134.4 78.6 %collective-permute-start.9 = (bf16[128,1536]{1,0:T(8,128)(2,1)S(1)}, bf16[128,1536]{1,0:T(8,128)(2,1)S(1)}, u32[]{:S(2)}, u32[]{:S(2)}) collective-permute-start(bf16[128,1536]{1,0:T(8,128)(2,1)S(1)} %get-tuple-element.17), channel_id=1, source_target_pairs={{0,3},{1,2},{2,1},{3,0},{4,7},{5,6},{6,5},{7,4},{8,11},{9,10},{10,... | collective-permute-start | bytes 1179656 | tf_op jit(solution)/shard_map/ppermute | solution.py:199

commit v7 on v6

--- a/solution.py
+++ b/solution.py
@@ -8,6 +8,7 @@
 AXES = ("dp", "fsdp")
 SPAN = 16
 STRIP = 32
+TOKEN = 16
 VMEM_LIMIT = 32 * 1024 * 1024
 
 
@@ -17,7 +18,7 @@
 
 
 def routes(blocks, ways):
-    img, txt, mate, cross = ([], []), ([], []), [], []
+    img, txt, mate, cross, token = ([], []), ([], []), [], [], []
     for block in range(blocks):
         for role in range(ways):
             here = device_of(block, role, blocks, ways)
@@ -25,9 +26,11 @@
             group = block % SPAN * 2 // SPAN
             img[group].append((here, device_of(block, role ^ 1, blocks, ways)))
             txt[group].append((here, device_of(block, ways - 1 - role, blocks, ways)))
+            if group == 0:
+                token.append((here, device_of(block + SPAN // 2, role, blocks, ways)))
             mate.append((here, device_of(block ^ 1, role, blocks, ways)))
             cross.append((here, device_of(across, role, blocks, ways)))
-    return img, txt, mate, cross
+    return img, txt, mate, cross, token
 
 
 def inverse_of(values):
@@ -43,8 +46,8 @@
             low_ref[part * rows + start : part * rows + start + STRIP, :] = strip
 
 
-def pass_kernel(img_ref, txt_ref, mate_ref, cross_ref, img_out, txt_out):
-    del mate_ref, cross_ref
+def pass_kernel(img_ref, txt_ref, token_ref, img_done, txt_done, img_out, txt_out):
+    del token_ref, img_done, txt_done
     img_out[...] = img_ref[...]
     txt_out[...] = txt_ref[...]
 
@@ -154,7 +157,7 @@
 
 
 def local(img_raw, txt_raw, logit_scale, logit_bias, moves):
-    to_img, to_txt, to_mate, to_cross = moves
+    to_img, to_txt, to_mate, to_cross, to_late = moves
     rows, width = img_raw.shape
     scalars = (logit_scale.reshape(1), logit_bias.reshape(1))
     low_shape = jax.ShapeDtypeStruct((2 * rows, width), jnp.bfloat16)
@@ -169,8 +172,9 @@
     own = call(low_kernel, low_shape, (), (img_raw, txt_raw))
     mate_own = lax.ppermute(own, AXES, to_mate)
     cross_own = lax.ppermute(own, AXES, to_cross)
+    token = lax.ppermute(cross_own[:TOKEN, :128] + mate_own[:TOKEN, :128], AXES, to_late)
     img_late, txt_late = call(
-        pass_kernel, (sent_shape, sent_shape), (), (img_raw, txt_raw), (mate_own, cross_own)
+        pass_kernel, (sent_shape, sent_shape), (), (img_raw, txt_raw), (token, img_a, txt_a)
     )
     img_b = lax.ppermute(img_late, AXES, to_img[1])
     txt_b = lax.ppermute(txt_late, AXES, to_txt[1])

time: 214 us -> 243 us (1.14)
  the two profiles are of different devices: /device:TPU:6 before, /device:TPU:113 now
where the time goes in v7:
time: 243 us; the launch traced here: 242 us
  starting transfers between devices  165 us (68%)
  waiting for transfers between devices  63.7 us (26%)
  local copies, waits for them, and re-layouts  6.04 us (2%)
  Pallas kernels  5.74 us (2%)
    ppermute x1, starting transfers between devices, local(): cross_far = lax.ppermute(far, AXES, to_cross)  74.7 us
    ppermute x1, starting transfers between devices, local(): txt_back = lax.ppermute(txt_sent, AXES, to_txt[0] + to_txt[1])  33.3 us
    ppermute x1, waiting for transfers between devices, local(): txt_back = lax.ppermute(txt_sent, AXES, to_txt[0] + to_txt[1])  23.3 us
    ppermute x1, starting transfers between devices, local(): img_back = lax.ppermute(img_sent, AXES, to_img[0] + to_img[1])  18.4 us
    ppermute x1, waiting for transfers between devices, local(): img_a = lax.ppermute(img_raw, AXES, to_img[0])  17.8 us
    ppermute x1, starting transfers between devices, local(): img_a = lax.ppermute(img_raw, AXES, to_img[0])  15.4 us
    ppermute x1, waiting for transfers between devices, local(): txt_a = lax.ppermute(txt_raw, AXES, to_txt[0])  14.7 us
    ppermute x1, starting transfers between devices, local(): txt_a = lax.ppermute(txt_raw, AXES, to_txt[0])  10.6 us
  transfers between devices with their start and end apart: 11, of which 4 were waited for; matrix products, arithmetic and copies ran while one was open for 0% of the time, Pallas kernels for 1%

profile of v7, /device:TPU:113, one launch (start us, length us, event | category | flops | bytes accessed | tf_op | source)
XLA Modules:
  0.0 242.4 jit_solution(12943041439571262514)
XLA Ops:
  0.6 0.0 copy-start
  0.6 1.0 copy-done
  1.6 0.0 copy-start.2
  1.6 1.0 copy-done.2
  2.6 0.2 shard_map.59.own
  2.9 2.6 %collective-permute-start.2 = (bf16[256,1536]{1,0:T(8,128)(2,1)S(1)}, bf16[256,1536]{1,0:T(8,128)(2,1)S(1)}, u32[]{:S(2)}, u32[]{:S(2)}) collective-permute-start(bf16[256,1536]{1,0:T(8,128)(2,1)S(1)} %shard_map.59.own), channel_id=1, source_target_pairs={{0,4},{1,5},{2,6},{3,7},{4,0},{5,1},{6,2},{7,3},{8,12},{9,13},{10,... | collective-permute-start | bytes 2359304 | tf_op jit(solution)/shard_map/ppermute | solution.py:173
  5.5 4.7 %collective-permute-start.1 = (bf16[256,1536]{1,0:T(8,128)(2,1)S(1)}, bf16[256,1536]{1,0:T(8,128)(2,1)S(1)}, u32[]{:S(2)}, u32[]{:S(2)}) collective-permute-start(bf16[256,1536]{1,0:T(8,128)(2,1)S(1)} %shard_map.59.own), channel_id=1, source_target_pairs={{0,1023},{1,1020},{2,1021},{3,1022},{4,8},{5,9},{6,10},{7,11},{8,4... | collective-permute-start | bytes 2359304 | tf_op jit(solution)/shard_map/ppermute | solution.py:174
  10.1 15.4 %collective-permute-start = (bf16[128,1536]{1,0:T(8,128)(2,1)S(1)}, bf16[128,1536]{1,0:T(8,128)(2,1)S(1)}, u32[]{:S(2)}, u32[]{:S(2)}) collective-permute-start(bf16[128,1536]{1,0:T(8,128)(2,1)S(1)} %copy-done), channel_id=1, source_target_pairs={{0,1},{1,0},{2,3},{3,2},{4,5},{5,4},{6,7},{7,6},{8,9},{9,8},{10,11... | collective-permute-start | bytes 1179656 | tf_op jit(solution)/shard_map/ppermute | solution.py:170
  25.6 10.6 %collective-permute-start.4 = (bf16[128,1536]{1,0:T(8,128)(2,1)S(1)}, bf16[128,1536]{1,0:T(8,128)(2,1)S(1)}, u32[]{:S(2)}, u32[]{:S(2)}) collective-permute-start(bf16[128,1536]{1,0:T(8,128)(2,1)S(1)} %copy-done.2), channel_id=1, source_target_pairs={{0,3},{1,2},{2,1},{3,0},{4,7},{5,6},{6,5},{7,4},{8,11},{9,10},{10,... | collective-permute-start | bytes 1179656 | tf_op jit(solution)/shard_map/ppermute | solution.py:171
  36.2 0.0 collective-permute-done.2.mate
  36.2 0.0 collective-permute-done.1.cross
  36.3 0.0 copy-start.4
  36.3 0.9 copy-done.4
  37.1 0.0 copy-start.6
  37.1 0.9 copy-done.6
  38.0 1.3 collective-permute-start.3
  39.3 17.8 %collective-permute-done.img_done.img_a = bf16[128,1536]{1,0:T(8,128)(2,1)S(1)} collective-permute-done((bf16[128,1536]{1,0:T(8,128)(2,1)S(1)}, bf16[128,1536]{1,0:T(8,128)(2,1)S(1)}, u32[]{:S(2)}, u32[]{:S(2)}) %collective-permute-start) | collective-permute-done | bytes 393248 | tf_op jit(solution)/shard_map/ppermute | solution.py:170
  57.2 14.7 %collective-permute-done.4.txt_done.txt_a = bf16[128,1536]{1,0:T(8,128)(2,1)S(1)} collective-permute-done((bf16[128,1536]{1,0:T(8,128)(2,1)S(1)}, bf16[128,1536]{1,0:T(8,128)(2,1)S(1)}, u32[]{:S(2)}, u32[]{:S(2)}) %collective-permute-start.4) | collective-permute-done | bytes 393248 | tf_op jit(solution)/shard_map/ppermute | solution.py:171
  71.9 0.0 collective-permute-done.3.token_ref
  71.9 0.1 shard_map.60
  71.9 0.7 collective-permute-start.5
  72.6 0.7 collective-permute-start.6
  73.3 0.0 collective-permute-done.5.img_b
  73.3 0.0 collective-permute-done.6.txt_b
  73.3 0.4 shard_map.61.far
  73.7 2.3 collective-permute-start.8
  76.1 74.7 %collective-permute-start.7 = (bf16[256,1536]{1,0:T(8,128)(2,1)S(1)}, bf16[256,1536]{1,0:T(8,128)(2,1)S(1)}, u32[]{:S(2)}, u32[]{:S(2)}) collective-permute-start(bf16[256,1536]{1,0:T(8,128)(2,1)S(1)} %shard_map.61.far), channel_id=1, source_target_pairs={{0,1023},{1,1020},{2,1021},{3,1022},{4,8},{5,9},{6,10},{7,11},{8,4... | collective-permute-start | bytes 2359304 | tf_op jit(solution)/shard_map/ppermute | solution.py:183
  152.0 0.0 copy-start.5
  152.0 1.1 copy-done.5
  153.2 0.0 copy-start.7
  153.2 1.1 copy-done.7
  154.3 1.8 shard_map.62
  156.2 0.0 collective-permute-done.8.mate
  156.2 7.9 %collective-permute-done.7.cross = bf16[256,1536]{1,0:T(8,128)(2,1)S(1)} collective-permute-done((bf16[256,1536]{1,0:T(8,128)(2,1)S(1)}, bf16[256,1536]{1,0:T(8,128)(2,1)S(1)}, u32[]{:S(2)}, u32[]{:S(2)}) %collective-permute-start.7) | collective-permute-done | bytes 786464 | tf_op jit(solution)/shard_map/ppermute | solution.py:183
  164.0 0.0 copy-start.1
  164.0 1.1 shard_map.63
  165.2 0.0 copy-start.3
  165.2 18.4 %collective-permute-start.9 = (bf16[128,1536]{1,0:T(8,128)(2,1)S(1)}, bf16[128,1536]{1,0:T(8,128)(2,1)S(1)}, u32[]{:S(2)}, u32[]{:S(2)}) collective-permute-start(bf16[128,1536]{1,0:T(8,128)(2,1)S(1)} %get-tuple-element.15), channel_id=1, source_target_pairs={{0,1},{1,0},{2,3},{3,2},{4,5},{5,4},{6,7},{7,6},{8,9},{9,8},{10,11... | collective-permute-start | bytes 1179656 | tf_op jit(solution)/shard_map/ppermute | solution.py:202
  183.6 33.3 %collective-permute-start.10 = (bf16[128,1536]{1,0:T(8,128)(2,1)S(1)}, bf16[128,1536]{1,0:T(8,128)(2,1)S(1)}, u32[]{:S(2)}, u32[]{:S(2)}) collective-permute-start(bf16[128,1536]{1,0:T(8,128)(2,1)S(1)} %get-tuple-element.17), channel_id=1, source_target_pairs={{0,3},{1,2},{2,1},{3,0},{4,7},{5,6},{6,5},{7,4},{8,11},{9,10},{10,... | collective-permute-start | bytes 1179656 | tf_op jit(solution)/shard_map/ppermute | solution.py:203
  216.9 0.0 collective-permute-done.9.there_ref
  216.9 0.0 copy-done.1
  216.9 1.1 shard_map.64
  218.0 23.3 %collective-permute-done.10.there_ref = bf16[128,1536]{1,0:T(8,128)(2,1)S(1)} collective-permute-done((bf16[128,1536]{1,0:T(8,128)(2,1)S(1)}, bf16[128,1536]{1,0:T(8,128)(2,1)S(1)}, u32[]{:S(2)}, u32[]{:S(2)}) %collective-permute-start.10) | collective-permute-done | bytes 393248 | tf_op jit(solution)/shard_map/ppermute | solution.py:203
  241.3 0.0 copy-done.3
  241.3 1.1 shard_map.65
  (1 shorter events, 0.0 us)
Async XLA Ops:
  0.6 1.0 copy-start
  1.6 1.0 copy-start.2
  2.9 33.4 %collective-permute-start.2 = (bf16[256,1536]{1,0:T(8,128)(2,1)S(1)}, bf16[256,1536]{1,0:T(8,128)(2,1)S(1)}, u32[]{:S(2)}, u32[]{:S(2)}) collective-permute-start(bf16[256,1536]{1,0:T(8,128)(2,1)S(1)} %shard_map.59.own), channel_id=1, source_target_pairs={{0,4},{1,5},{2,6},{3,7},{4,0},{5,1},{6,2},{7,3},{8,12},{9,13},{10,... | collective-permute-start | bytes 2359304 | tf_op jit(solution)/shard_map/ppermute | solution.py:173
  5.5 30.8 %collective-permute-start.1 = (bf16[256,1536]{1,0:T(8,128)(2,1)S(1)}, bf16[256,1536]{1,0:T(8,128)(2,1)S(1)}, u32[]{:S(2)}, u32[]{:S(2)}) collective-permute-start(bf16[256,1536]{1,0:T(8,128)(2,1)S(1)} %shard_map.59.own), channel_id=1, source_target_pairs={{0,1023},{1,1020},{2,1021},{3,1022},{4,8},{5,9},{6,10},{7,11},{8,4... | collective-permute-start | bytes 2359304 | tf_op jit(solution)/shard_map/ppermute | solution.py:174
  10.1 47.0 %collective-permute-start = (bf16[128,1536]{1,0:T(8,128)(2,1)S(1)}, bf16[128,1536]{1,0:T(8,128)(2,1)S(1)}, u32[]{:S(2)}, u32[]{:S(2)}) collective-permute-start(bf16[128,1536]{1,0:T(8,128)(2,1)S(1)} %copy-done), channel_id=1, source_target_pairs={{0,1},{1,0},{2,3},{3,2},{4,5},{5,4},{6,7},{7,6},{8,9},{9,8},{10,11... | collective-permute-start | bytes 1179656 | tf_op jit(solution)/shard_map/ppermute | solution.py:170
  25.6 46.3 %collective-permute-start.4 = (bf16[128,1536]{1,0:T(8,128)(2,1)S(1)}, bf16[128,1536]{1,0:T(8,128)(2,1)S(1)}, u32[]{:S(2)}, u32[]{:S(2)}) collective-permute-start(bf16[128,1536]{1,0:T(8,128)(2,1)S(1)} %copy-done.2), channel_id=1, source_target_pairs={{0,3},{1,2},{2,1},{3,0},{4,7},{5,6},{6,5},{7,4},{8,11},{9,10},{10,... | collective-permute-start | bytes 1179656 | tf_op jit(solution)/shard_map/ppermute | solution.py:171
  36.3 0.9 copy-start.4
  37.1 0.9 copy-start.6
  38.0 33.8 %collective-permute-start.3 = (bf16[16,128]{1,0:T(8,128)(2,1)S(1)}, bf16[16,128]{1,0:T(8,128)(2,1)S(1)}, u32[]{:S(2)}, u32[]{:S(2)}) collective-permute-start(bf16[16,128]{1,0:T(8,128)(2,1)S(1)} %slice_add_fusion), channel_id=1, source_target_pairs={{0,32},{1,33},{2,34},{3,35},{4,36},{5,37},{6,38},{7,39},{8,40},{9,... | collective-permute-start | bytes 12296 | tf_op jit(solution)/shard_map/ppermute | solution.py:175
  71.9 1.4 collective-permute-start.5
  72.6 0.7 collective-permute-start.6
  73.7 82.5 %collective-permute-start.8 = (bf16[256,1536]{1,0:T(8,128)(2,1)S(1)}, bf16[256,1536]{1,0:T(8,128)(2,1)S(1)}, u32[]{:S(2)}, u32[]{:S(2)}) collective-permute-start(bf16[256,1536]{1,0:T(8,128)(2,1)S(1)} %shard_map.61.far), channel_id=1, source_target_pairs={{0,4},{1,5},{2,6},{3,7},{4,0},{5,1},{6,2},{7,3},{8,12},{9,13},{10,... | collective-permute-start | bytes 2359304 | tf_op jit(solution)/shard_map/ppermute | solution.py:182
  76.1 88.0 %collective-permute-start.7 = (bf16[256,1536]{1,0:T(8,128)(2,1)S(1)}, bf16[256,1536]{1,0:T(8,128)(2,1)S(1)}, u32[]{:S(2)}, u32[]{:S(2)}) collective-permute-start(bf16[256,1536]{1,0:T(8,128)(2,1)S(1)} %shard_map.61.far), channel_id=1, source_target_pairs={{0,1023},{1,1020},{2,1021},{3,1022},{4,8},{5,9},{6,10},{7,11},{8,4... | collective-permute-start | bytes 2359304 | tf_op jit(solution)/shard_map/ppermute | solution.py:183
  152.0 1.1 copy-start.5
  153.2 1.1 copy-start.7
  164.0 52.9 %copy-start.1 = (bf16[128,1536]{1,0:T(8,128)(2,1)S(1)}, bf16[128,1536]{1,0:T(8,128)(2,1)}, u32[]{:S(2)}) copy-start(bf16[128,1536]{1,0:T(8,128)(2,1)} %raw_ref.2) | copy-start | bytes 1179652
  165.2 76.1 %copy-start.3 = (bf16[128,1536]{1,0:T(8,128)(2,1)S(1)}, bf16[128,1536]{1,0:T(8,128)(2,1)}, u32[]{:S(2)}) copy-start(bf16[128,1536]{1,0:T(8,128)(2,1)} %raw_ref.3) | copy-start | bytes 1179652
  165.2 51.7 %collective-permute-start.9 = (bf16[128,1536]{1,0:T(8,128)(2,1)S(1)}, bf16[128,1536]{1,0:T(8,128)(2,1)S(1)}, u32[]{:S(2)}, u32[]{:S(2)}) collective-permute-start(bf16[128,1536]{1,0:T(8,128)(2,1)S(1)} %get-tuple-element.15), channel_id=1, source_target_pairs={{0,1},{1,0},{2,3},{3,2},{4,5},{5,4},{6,7},{7,6},{8,9},{9,8},{10,11... | collective-permute-start | bytes 1179656 | tf_op jit(solution)/shard_map/ppermute | solution.py:202
  183.6 57.7 %collective-permute-start.10 = (bf16[128,1536]{1,0:T(8,128)(2,1)S(1)}, bf16[128,1536]{1,0:T(8,128)(2,1)S(1)}, u32[]{:S(2)}, u32[]{:S(2)}) collective-permute-start(bf16[128,1536]{1,0:T(8,128)(2,1)S(1)} %get-tuple-element.17), channel_id=1, source_target_pairs={{0,3},{1,2},{2,1},{3,0},{4,7},{5,6},{6,5},{7,4},{8,11},{9,10},{10,... | collective-permute-start | bytes 1179656 | tf_op jit(solution)/shard_map/ppermute | solution.py:203

commit v8 on v3

v8 whole, which is shorter than its diff:
```python
import jax
import jax.numpy as jnp
from jax import lax
from jax.experimental import pallas as pl
from jax.experimental.pallas import tpu as pltpu
from jax.sharding import PartitionSpec as P

AXES = ("dp", "fsdp")
SPAN = 16
STRIP = 32
VMEM_LIMIT = 16 * 1024 * 1024
PICK_LIMIT = 56 * 1024 * 1024


def device_of(block, role, blocks, ways):
    block = block % blocks
    return block * ways + (role + block // SPAN) % ways


def routes(blocks, ways):
    first, second, mate, cross = [], [], [], []
    for block in range(blocks):
        for role in range(ways):
            here = device_of(block, role, blocks, ways)
            img = device_of(block, role ^ 1, blocks, ways)
            txt = device_of(block, ways - 1 - role, blocks, ways)
            across = block + 1 if block % 2 else block - 1
            first.append((here, txt if block % 2 else img))
            second.append((here, img if block % 2 else txt))
            mate.append((here, device_of(block ^ 1, role, blocks, ways)))
            cross.append((here, device_of(across, role, blocks, ways)))
    return first, second, mate, cross


def inverse_of(values):
    return lax.rsqrt(jnp.sum(values * values, axis=-1, keepdims=True) + 1e-06)


def pick_kernel(odd_ref, img_ref, txt_ref, x_ref, y_ref, sems):
    def move(x_from, y_from):
        copies = [
            pltpu.make_async_copy(x_from, x_ref, sems.at[0]),
            pltpu.make_async_copy(y_from, y_ref, sems.at[1]),
        ]
        for copy in copies:
            copy.start()
        for copy in copies:
            copy.wait()

    @pl.when(odd_ref[0] == 0)
    def _():
        move(img_ref, txt_ref)

    @pl.when(odd_ref[0] != 0)
    def _():
        move(txt_ref, img_ref)


def low_kernel(x_ref, y_ref, low_ref):
    rows = x_ref.shape[0]
    for part, ref in enumerate((x_ref, y_ref)):
        for start in range(0, rows, STRIP):
            values = ref[start : start + STRIP, :].astype(jnp.float32)
            strip = (values * inverse_of(values)).astype(jnp.bfloat16)
            low_ref[part * rows + start : part * rows + start + STRIP, :] = strip


def scores_of(left, right):
    return lax.dot_general(left, right, (((1,), (1,)), ((), ())), preferred_element_type=jnp.float32)


def negative_coef(left, right, scale, bias):
    return (jax.nn.sigmoid(scale * scores_of(left, right) + bias) * scale).astype(jnp.bfloat16)


def columns_of(width, step=256):
    return [slice(start, start + step) for start in range(0, width, step)]


def stack(first, second, part, rows, out_ref):
    out_ref[:rows, :] = first[part * rows : (part + 1) * rows, :]
    out_ref[rows:, :] = second[part * rows : (part + 1) * rows, :]


def near_kernel(scale_ref, bias_ref, own, far, mate, cross, x_acc, y_acc, x, y, x_n, y_n):
    rows = own.shape[0] // 2
    scale, bias = scale_ref[0], bias_ref[0]
    stack(own, far, 0, rows, x)
    stack(own, far, 1, rows, y)
    stack(mate, cross, 0, rows, x_n)
    stack(mate, cross, 1, rows, y_n)

    shape = (2 * rows, 2 * rows)
    first = lax.broadcasted_iota(jnp.int32, shape, 0)
    positive = (first == lax.broadcasted_iota(jnp.int32, shape, 1)) & (first < rows)
    logits = scale * scores_of(x[...], y[...]) + bias
    size = jax.nn.sigmoid(jnp.where(positive, -logits, logits)) * scale
    signed = jnp.where(positive, -size, size)
    coef_own = signed.astype(jnp.bfloat16)
    coef_own_t = signed.T.astype(jnp.bfloat16)
    coef_x = negative_coef(x[...], x_n[...], scale, bias)
    coef_y = negative_coef(y[...], y_n[...], scale, bias)

    def dot(coef, ref, cols):
        return jnp.dot(coef, ref[:, cols], preferred_element_type=jnp.float32)

    for cols in columns_of(own.shape[1]):
        x_acc[:, cols] = dot(coef_own, y, cols) + dot(coef_x, x_n, cols)
        y_acc[:, cols] = dot(coef_own_t, x, cols) + dot(coef_y, y_n, cols)


def far_kernel(
    scale_ref, bias_ref, own, far, mate, cross, x_acc, y_acc,
    x_own, x_far, y_own, y_far, x, y, x_n, y_n,
):
    rows = own.shape[0] // 2
    scale, bias = scale_ref[0], bias_ref[0]
    stack(own, far, 0, rows, x)
    stack(own, far, 1, rows, y)
    stack(mate, cross, 0, rows, x_n)
    stack(mate, cross, 1, rows, y_n)
    coef_x = negative_coef(x[...], x_n[...], scale, bias)
    coef_y = negative_coef(y[...], y_n[...], scale, bias)
    for cols in columns_of(own.shape[1]):
        total = x_acc[:, cols] + jnp.dot(
            coef_x, x_n[:, cols], preferred_element_type=jnp.float32
        )
        x_own[:, cols] = total[:rows]
        x_far[:, cols] = total[rows:].astype(jnp.bfloat16)
        total = y_acc[:, cols] + jnp.dot(
            coef_y, y_n[:, cols], preferred_element_type=jnp.float32
        )
        y_own[:, cols] = total[:rows]
        y_far[:, cols] = total[rows:].astype(jnp.bfloat16)


def grad_strip(raw, direction):
    values = raw.astype(jnp.float32)
    inverse = inverse_of(values)
    norm = values * inverse
    inner = jnp.sum(norm * direction, axis=-1, keepdims=True)
    return ((direction - norm * inner) * inverse).astype(jnp.bfloat16)


def first_grad_kernel(odd_ref, img_raw, txt_raw, kept, there, out):
    odd = odd_ref[0] > 0
    for start in range(0, img_raw.shape[0], STRIP):
        here = slice(start, start + STRIP)
        raw = jnp.where(odd, txt_raw[here, :], img_raw[here, :])
        out[here, :] = grad_strip(raw, kept[here, :] + there[here, :].astype(jnp.float32))


def second_grad_kernel(odd_ref, img_raw, txt_raw, kept, there, x_grad, img_grad, txt_grad):
    odd = odd_ref[0] > 0
    for start in range(0, img_raw.shape[0], STRIP):
        here = slice(start, start + STRIP)
        raw = jnp.where(odd, img_raw[here, :], txt_raw[here, :])
        y = grad_strip(raw, kept[here, :] + there[here, :].astype(jnp.float32))
        x = x_grad[here, :]
        img_grad[here, :] = jnp.where(odd, y, x)
        txt_grad[here, :] = jnp.where(odd, x, y)


def pick(odd, img_raw, txt_raw):
    piece = jax.ShapeDtypeStruct(img_raw.shape, img_raw.dtype)
    return pl.pallas_call(
        pick_kernel,
        out_shape=(piece, piece),
        in_specs=[pl.BlockSpec(memory_space=pltpu.SMEM)] + [pl.BlockSpec(memory_space=pl.ANY)] * 2,
        out_specs=(pl.BlockSpec(memory_space=pltpu.VMEM),) * 2,
        scratch_shapes=[pltpu.SemaphoreType.DMA((2,))],
        compiler_params=pltpu.CompilerParams(vmem_limit_bytes=PICK_LIMIT),
    )(odd, img_raw, txt_raw)


def call(kernel, outs, scalars, arrays, scratch=(), flops=0):
    moved = sum(a.size * a.dtype.itemsize for a in arrays)
    return pl.pallas_call(
        kernel,
        out_shape=outs,
        in_specs=[pl.BlockSpec(memory_space=pltpu.SMEM)] * len(scalars)
        + [pl.BlockSpec(memory_space=pltpu.VMEM)] * len(arrays),
        out_specs=jax.tree.map(lambda _: pl.BlockSpec(memory_space=pltpu.VMEM), outs),
        scratch_shapes=list(scratch),
        compiler_params=pltpu.CompilerParams(vmem_limit_bytes=VMEM_LIMIT),
        cost_estimate=pl.CostEstimate(flops=flops, bytes_accessed=moved, transcendentals=0),
    )(*scalars, *arrays)


def local(img_raw, txt_raw, logit_scale, logit_bias, moves):
    first, second, to_mate, to_cross = moves
    rows, width = img_raw.shape
    odd = (lax.axis_index("dp") & 1).astype(jnp.int32).reshape(1)
    scalars = (logit_scale.reshape(1), logit_bias.reshape(1))
    low_shape = jax.ShapeDtypeStruct((2 * rows, width), jnp.bfloat16)
    acc_shape = jax.ShapeDtypeStruct((2 * rows, width), jnp.float32)
    own_shape = jax.ShapeDtypeStruct((rows, width), jnp.float32)
    sent_shape = jax.ShapeDtypeStruct((rows, width), jnp.bfloat16)
    halves = [pltpu.VMEM((2 * rows, width), jnp.bfloat16)] * 4
    unit = 2 * (2 * rows) * (2 * rows) * width

    x, y = pick(odd, img_raw, txt_raw)
    x_there = lax.ppermute(x, AXES, first)
    y_there = lax.ppermute(y, AXES, second)
    own = call(low_kernel, low_shape, (), (x, y))
    cross_own = lax.ppermute(own, AXES, to_cross)
    mate_own = lax.ppermute(own, AXES, to_mate)
    far = call(low_kernel, low_shape, (), (x_there, y_there))
    cross_far = lax.ppermute(far, AXES, to_cross)
    mate_far = lax.ppermute(far, AXES, to_mate)
    x_acc, y_acc = call(
        near_kernel, (acc_shape, acc_shape), scalars, (own, far, mate_own, cross_own), halves, 7 * unit
    )
    x_kept, x_sent, y_kept, y_sent = call(
        far_kernel,
        (own_shape, sent_shape, own_shape, sent_shape),
        scalars,
        (own, far, mate_far, cross_far, x_acc, y_acc),
        halves,
        4 * unit,
    )
    x_back = lax.ppermute(x_sent, AXES, first)
    y_back = lax.ppermute(y_sent, AXES, second)
    x_grad = call(first_grad_kernel, sent_shape, (odd,), (img_raw, txt_raw, x_kept, x_back))
    return call(
        second_grad_kernel,
        (sent_shape, sent_shape),
        (odd,),
        (img_raw, txt_raw, y_kept, y_back, x_grad),
    )


def solution(mesh):
    moves = routes(mesh.shape["dp"], mesh.shape["fsdp"])
    in_specs = (P(AXES, None), P(AXES, None), P(), P())
    out_specs = (P(AXES, None), P(AXES, None))

    def step(*args):
        return local(*args, moves)

    return jax.shard_map(step, mesh=mesh, in_specs=in_specs, out_specs=out_specs, check_vma=False)
```

time: 201 us -> 197 us (0.980)
  starting transfers between devices: 60.6 us -> 57.5 us
  waiting for transfers between devices: 126 us -> 123 us
    ppermute x4, waiting for transfers between devices: 118 us -> 114 us  [the longest x1 55.6 us: local(): x_back = lax.ppermute(x_sent, AXES, first)]
    ppermute x1, waiting for transfers between devices: 6.26 us -> 9.13 us  [local(): cross_far = lax.ppermute(far, AXES, to_cross)]
    pallas_call x0 -> x1, Pallas kernels: none -> 2.01 us  [pick(): pl.pallas_call(pick_kernel, out_shape=(piece, piece), in_specs=[pl.BlockS...]
  transfers between devices with their start and end apart: 8 -> 8, of which waited for: 6 -> 4; matrix products, arithmetic and copies ran while one was open for 0% -> 0% of each run, Pallas kernels for 2% -> 2%
where the time goes in v8:
time: 197 us; the launch traced here: 193 us
  waiting for transfers between devices  123 us (62%)
  starting transfers between devices  57.5 us (29%)
  Pallas kernels  8.47 us (4%)
  between operations  2.07 us (1%)
  local copies, waits for them, and re-layouts  2 us (1%)
    ppermute x1, waiting for transfers between devices, local(): x_back = lax.ppermute(x_sent, AXES, first)  55.6 us
    ppermute x1, waiting for transfers between devices, local(): x_there = lax.ppermute(x, AXES, first)  43.3 us
    ppermute x1, starting transfers between devices, local(): x_there = lax.ppermute(x, AXES, first)  15.7 us
    ppermute x1, starting transfers between devices, local(): y_there = lax.ppermute(y, AXES, second)  15.7 us
    ppermute x1, waiting for transfers between devices, local(): y_there = lax.ppermute(y, AXES, second)  15.3 us
    ppermute x1, starting transfers between devices, local(): y_back = lax.ppermute(y_sent, AXES, second)  13 us
    ppermute x1, waiting for transfers between devices, local(): cross_far = lax.ppermute(far, AXES, to_cross)  9.13 us
    pallas_call x6, Pallas kernels, call(): pl.pallas_call(kernel, out_shape=outs, in_specs=[pl.BlockSpec(memory_spac...  6.46 us
  transfers between devices with their start and end apart: 8, of which 4 were waited for; matrix products, arithmetic and copies ran while one was open for 0% of the time, Pallas kernels for 2%

profile of v8, /device:TPU:24, one launch (start us, length us, event | category | flops | bytes accessed | tf_op | source)
XLA Modules:
  0.0 193.3 jit_solution(12524288908638729948)
XLA Ops:
  0.6 2.0 %shard_map.59 = (bf16[128,1536]{1,0:T(8,128)(2,1)}, bf16[128,1536]{1,0:T(8,128)(2,1)}) custom-call(s32[1]{0:T(128)} %bitcast.odd_ref, bf16[128,1536]{1,0:T(8,128)(2,1)} %img_raw.3, bf16[128,1536]{1,0:T(8,128)(2,1)} %txt_raw.3), custom_call_target="tpu_custom_call" | custom-call | tf_op jit(solution)/shard_map/pallas_call | solution.py:166
  2.7 15.7 %collective-permute-start = (bf16[128,1536]{1,0:T(8,128)(2,1)}, bf16[128,1536]{1,0:T(8,128)(2,1)S(1)}, u32[]{:S(2)}, u32[]{:S(2)}) collective-permute-start(bf16[128,1536]{1,0:T(8,128)(2,1)} %get-tuple-element.10.x_ref), channel_id=1, source_target_pairs={{0,1},{1,0},{2,3},{3,2},{4,7},{5,6},{6,5},{7,4},{8,9},{9,8},{10,11... | collective-permute-start | bytes 1179656 | tf_op jit(solution)/shard_map/ppermute | solution.py:203
  18.4 15.7 %collective-permute-start.1 = (bf16[128,1536]{1,0:T(8,128)(2,1)}, bf16[128,1536]{1,0:T(8,128)(2,1)S(1)}, u32[]{:S(2)}, u32[]{:S(2)}) collective-permute-start(bf16[128,1536]{1,0:T(8,128)(2,1)} %get-tuple-element.11.y_ref), channel_id=1, source_target_pairs={{0,3},{1,2},{2,1},{3,0},{4,5},{5,4},{6,7},{7,6},{8,11},{9,10},{10,... | collective-permute-start | bytes 1179656 | tf_op jit(solution)/shard_map/ppermute | solution.py:204
  34.1 0.0 copy-start.2
  34.1 1.0 copy-done.2
  35.1 0.0 copy-start.3
  35.1 1.0 copy-done.3
  36.1 0.2 shard_map.60.own
  36.4 3.3 %collective-permute-start.5 = (bf16[256,1536]{1,0:T(8,128)(2,1)S(1)}, bf16[256,1536]{1,0:T(8,128)(2,1)}, u32[]{:S(2)}, u32[]{:S(2)}) collective-permute-start(bf16[256,1536]{1,0:T(8,128)(2,1)S(1)} %shard_map.60.own), channel_id=1, source_target_pairs={{0,1023},{1,1020},{2,1021},{3,1022},{4,8},{5,9},{6,10},{7,11},{8,4... | collective-permute-start | bytes 2359304 | tf_op jit(solution)/shard_map/ppermute | solution.py:206
  39.7 1.9 collective-permute-start.4
  41.6 43.3 %collective-permute-done.x_ref = bf16[128,1536]{1,0:T(8,128)(2,1)S(1)} collective-permute-done((bf16[128,1536]{1,0:T(8,128)(2,1)}, bf16[128,1536]{1,0:T(8,128)(2,1)S(1)}, u32[]{:S(2)}, u32[]{:S(2)}) %collective-permute-start) | collective-permute-done | bytes 393248 | tf_op jit(solution)/shard_map/ppermute | solution.py:203
  84.9 15.3 %collective-permute-done.1.y_ref = bf16[128,1536]{1,0:T(8,128)(2,1)S(1)} collective-permute-done((bf16[128,1536]{1,0:T(8,128)(2,1)}, bf16[128,1536]{1,0:T(8,128)(2,1)S(1)}, u32[]{:S(2)}, u32[]{:S(2)}) %collective-permute-start.1) | collective-permute-done | bytes 393248 | tf_op jit(solution)/shard_map/ppermute | solution.py:204
  100.2 0.2 shard_map.61.far
  100.4 1.9 collective-permute-start.3
  102.4 1.9 collective-permute-start.2
  105.6 0.0 collective-permute-done.5.cross
  105.6 0.0 collective-permute-done.4.mate
  105.6 3.2 %shard_map.62 = (f32[256,1536]{1,0:T(8,128)S(1)}, f32[256,1536]{1,0:T(8,128)S(1)}) custom-call(f32[1]{0:T(128)} %bitcast.3.scale_ref, f32[1]{0:T(128)} %bitcast.5.bias_ref, bf16[256,1536]{1,0:T(8,128)(2,1)S(1)} %shard_map.60.own, bf16[256,1536]{1,0:T(8,128)(2,1)S(1)} %shard_map.61.far, bf16[256,1536]{1,0:T(8,128)(2,1)} %collective-permute-done.4.mate, ...), custom_call_target="tpu_custom_call" | custom-call | flops 1409286144 | bytes 3145728 | tf_op jit(solution)/shard_map/pallas_call | solution.py:178
  108.8 9.1 %collective-permute-done.3.cross = bf16[256,1536]{1,0:T(8,128)(2,1)S(1)} collective-permute-done((bf16[256,1536]{1,0:T(8,128)(2,1)S(1)}, bf16[256,1536]{1,0:T(8,128)(2,1)S(1)}, u32[]{:S(2)}, u32[]{:S(2)}) %collective-permute-start.3) | collective-permute-done | bytes 786464 | tf_op jit(solution)/shard_map/ppermute | solution.py:209
  118.0 0.0 collective-permute-done.2.mate
  118.0 0.0 copy-start
  118.0 0.0 copy-start.1
  118.0 1.1 shard_map.63
  119.1 4.0 %collective-permute-start.7 = (bf16[128,1536]{1,0:T(8,128)(2,1)S(1)}, bf16[128,1536]{1,0:T(8,128)(2,1)S(1)}, u32[]{:S(2)}, u32[]{:S(2)}) collective-permute-start(bf16[128,1536]{1,0:T(8,128)(2,1)S(1)} %get-tuple-element.17), channel_id=1, source_target_pairs={{0,1},{1,0},{2,3},{3,2},{4,7},{5,6},{6,5},{7,4},{8,9},{9,8},{10,11... | collective-permute-start | bytes 1179656 | tf_op jit(solution)/shard_map/ppermute | solution.py:222
  123.1 13.0 %collective-permute-start.6 = (bf16[128,1536]{1,0:T(8,128)(2,1)S(1)}, bf16[128,1536]{1,0:T(8,128)(2,1)S(1)}, u32[]{:S(2)}, u32[]{:S(2)}) collective-permute-start(bf16[128,1536]{1,0:T(8,128)(2,1)S(1)} %get-tuple-element.15), channel_id=1, source_target_pairs={{0,3},{1,2},{2,1},{3,0},{4,5},{5,4},{6,7},{7,6},{8,11},{9,10},{10,... | collective-permute-start | bytes 1179656 | tf_op jit(solution)/shard_map/ppermute | solution.py:223
  136.1 55.6 %collective-permute-done.7.there = bf16[128,1536]{1,0:T(8,128)(2,1)S(1)} collective-permute-done((bf16[128,1536]{1,0:T(8,128)(2,1)S(1)}, bf16[128,1536]{1,0:T(8,128)(2,1)S(1)}, u32[]{:S(2)}, u32[]{:S(2)}) %collective-permute-start.7) | collective-permute-done | bytes 393248 | tf_op jit(solution)/shard_map/ppermute | solution.py:222
  191.7 0.0 copy-done
  191.7 0.0 copy-done.1
  191.7 0.3 shard_map.64.x_grad
  192.0 0.0 collective-permute-done.6.there
  192.0 1.3 shard_map.65
Async XLA Ops:
  2.7 82.2 %collective-permute-start = (bf16[128,1536]{1,0:T(8,128)(2,1)}, bf16[128,1536]{1,0:T(8,128)(2,1)S(1)}, u32[]{:S(2)}, u32[]{:S(2)}) collective-permute-start(bf16[128,1536]{1,0:T(8,128)(2,1)} %get-tuple-element.10.x_ref), channel_id=1, source_target_pairs={{0,1},{1,0},{2,3},{3,2},{4,7},{5,6},{6,5},{7,4},{8,9},{9,8},{10,11... | collective-permute-start | bytes 1179656 | tf_op jit(solution)/shard_map/ppermute | solution.py:203
  18.4 81.8 %collective-permute-start.1 = (bf16[128,1536]{1,0:T(8,128)(2,1)}, bf16[128,1536]{1,0:T(8,128)(2,1)S(1)}, u32[]{:S(2)}, u32[]{:S(2)}) collective-permute-start(bf16[128,1536]{1,0:T(8,128)(2,1)} %get-tuple-element.11.y_ref), channel_id=1, source_target_pairs={{0,3},{1,2},{2,1},{3,0},{4,5},{5,4},{6,7},{7,6},{8,11},{9,10},{10,... | collective-permute-start | bytes 1179656 | tf_op jit(solution)/shard_map/ppermute | solution.py:204
  34.1 1.0 copy-start.2
  35.1 1.0 copy-start.3
  36.4 69.2 %collective-permute-start.5 = (bf16[256,1536]{1,0:T(8,128)(2,1)S(1)}, bf16[256,1536]{1,0:T(8,128)(2,1)}, u32[]{:S(2)}, u32[]{:S(2)}) collective-permute-start(bf16[256,1536]{1,0:T(8,128)(2,1)S(1)} %shard_map.60.own), channel_id=1, source_target_pairs={{0,1023},{1,1020},{2,1021},{3,1022},{4,8},{5,9},{6,10},{7,11},{8,4... | collective-permute-start | bytes 2359304 | tf_op jit(solution)/shard_map/ppermute | solution.py:206
  39.7 66.0 %collective-permute-start.4 = (bf16[256,1536]{1,0:T(8,128)(2,1)S(1)}, bf16[256,1536]{1,0:T(8,128)(2,1)}, u32[]{:S(2)}, u32[]{:S(2)}) collective-permute-start(bf16[256,1536]{1,0:T(8,128)(2,1)S(1)} %shard_map.60.own), channel_id=1, source_target_pairs={{0,4},{1,5},{2,6},{3,7},{4,0},{5,1},{6,2},{7,3},{8,12},{9,13},{10,... | collective-permute-start | bytes 2359304 | tf_op jit(solution)/shard_map/ppermute | solution.py:207
  100.4 17.5 %collective-permute-start.3 = (bf16[256,1536]{1,0:T(8,128)(2,1)S(1)}, bf16[256,1536]{1,0:T(8,128)(2,1)S(1)}, u32[]{:S(2)}, u32[]{:S(2)}) collective-permute-start(bf16[256,1536]{1,0:T(8,128)(2,1)S(1)} %shard_map.61.far), channel_id=1, source_target_pairs={{0,1023},{1,1020},{2,1021},{3,1022},{4,8},{5,9},{6,10},{7,11},{8,4... | collective-permute-start | bytes 2359304 | tf_op jit(solution)/shard_map/ppermute | solution.py:209
  102.4 15.6 %collective-permute-start.2 = (bf16[256,1536]{1,0:T(8,128)(2,1)S(1)}, bf16[256,1536]{1,0:T(8,128)(2,1)S(1)}, u32[]{:S(2)}, u32[]{:S(2)}) collective-permute-start(bf16[256,1536]{1,0:T(8,128)(2,1)S(1)} %shard_map.61.far), channel_id=1, source_target_pairs={{0,4},{1,5},{2,6},{3,7},{4,0},{5,1},{6,2},{7,3},{8,12},{9,13},{10,... | collective-permute-start | bytes 2359304 | tf_op jit(solution)/shard_map/ppermute | solution.py:210
  118.0 73.7 %copy-start = (bf16[128,1536]{1,0:T(8,128)(2,1)S(1)}, bf16[128,1536]{1,0:T(8,128)(2,1)}, u32[]{:S(2)}) copy-start(bf16[128,1536]{1,0:T(8,128)(2,1)} %img_raw.3) | copy-start | bytes 1179652
  118.0 73.7 %copy-start.1 = (bf16[128,1536]{1,0:T(8,128)(2,1)S(1)}, bf16[128,1536]{1,0:T(8,128)(2,1)}, u32[]{:S(2)}) copy-start(bf16[128,1536]{1,0:T(8,128)(2,1)} %txt_raw.3) | copy-start | bytes 1179652
  119.1 72.6 %collective-permute-start.7 = (bf16[128,1536]{1,0:T(8,128)(2,1)S(1)}, bf16[128,1536]{1,0:T(8,128)(2,1)S(1)}, u32[]{:S(2)}, u32[]{:S(2)}) collective-permute-start(bf16[128,1536]{1,0:T(8,128)(2,1)S(1)} %get-tuple-element.17), channel_id=1, source_target_pairs={{0,1},{1,0},{2,3},{3,2},{4,7},{5,6},{6,5},{7,4},{8,9},{9,8},{10,11... | collective-permute-start | bytes 1179656 | tf_op jit(solution)/shard_map/ppermute | solution.py:222
  123.1 68.9 %collective-permute-start.6 = (bf16[128,1536]{1,0:T(8,128)(2,1)S(1)}, bf16[128,1536]{1,0:T(8,128)(2,1)S(1)}, u32[]{:S(2)}, u32[]{:S(2)}) collective-permute-start(bf16[128,1536]{1,0:T(8,128)(2,1)S(1)} %get-tuple-element.15), channel_id=1, source_target_pairs={{0,3},{1,2},{2,1},{3,0},{4,5},{5,4},{6,7},{7,6},{8,11},{9,10},{10,... | collective-permute-start | bytes 1179656 | tf_op jit(solution)/shard_map/ppermute | solution.py:223

commit v9 on v8

--- a/solution.py
+++ b/solution.py
@@ -1,3 +1,5 @@
+import functools
+
 import jax
 import jax.numpy as jnp
 from jax import lax
@@ -9,6 +11,7 @@
 SPAN = 16
 STRIP = 32
 VMEM_LIMIT = 16 * 1024 * 1024
+PIECES = 4
 PICK_LIMIT = 56 * 1024 * 1024
 
 
@@ -38,10 +41,13 @@
 
 def pick_kernel(odd_ref, img_ref, txt_ref, x_ref, y_ref, sems):
     def move(x_from, y_from):
-        copies = [
-            pltpu.make_async_copy(x_from, x_ref, sems.at[0]),
-            pltpu.make_async_copy(y_from, y_ref, sems.at[1]),
-        ]
+        copies = []
+        rows = x_ref.shape[0] // PIECES
+        for place in range(PIECES):
+            here = pl.ds(place * rows, rows)
+            for side, (source, out) in enumerate(((x_from, x_ref), (y_from, y_ref))):
+                sem = sems.at[side, place]
+                copies.append(pltpu.make_async_copy(source.at[here, :], out.at[here, :], sem))
         for copy in copies:
             copy.start()
         for copy in copies:
@@ -65,6 +71,13 @@
             low_ref[part * rows + start : part * rows + start + STRIP, :] = strip
 
 
+def split_low_kernel(x_ref, y_ref, low_ref, x_low, y_low):
+    rows = x_ref.shape[0]
+    low_kernel(x_ref, y_ref, low_ref)
+    x_low[...] = low_ref[:rows, :]
+    y_low[...] = low_ref[rows:, :]
+
+
 def scores_of(left, right):
     return lax.dot_general(left, right, (((1,), (1,)), ((), ())), preferred_element_type=jnp.float32)
 
@@ -77,19 +90,27 @@
     return [slice(start, start + step) for start in range(0, width, step)]
 
 
-def stack(first, second, part, rows, out_ref):
-    out_ref[:rows, :] = first[part * rows : (part + 1) * rows, :]
-    out_ref[rows:, :] = second[part * rows : (part + 1) * rows, :]
-
-
-def near_kernel(scale_ref, bias_ref, own, far, mate, cross, x_acc, y_acc, x, y, x_n, y_n):
+def dot(coef, rows):
+    return jnp.dot(coef, rows, preferred_element_type=jnp.float32)
+
+
+def stack(out_ref, first, second):
+    rows = first.shape[0]
+    out_ref[:rows, :] = first
+    out_ref[rows:, :] = second
+
+
+def half(ref, part):
+    rows = ref.shape[0] // 2
+    return ref[part * rows : (part + 1) * rows, :]
+
+
+def near_x_kernel(scale_ref, bias_ref, own, far, mate, cross, acc, coef_t, x, y, near):
     rows = own.shape[0] // 2
     scale, bias = scale_ref[0], bias_ref[0]
-    stack(own, far, 0, rows, x)
-    stack(own, far, 1, rows, y)
-    stack(mate, cross, 0, rows, x_n)
-    stack(mate, cross, 1, rows, y_n)
-
+    stack(x, half(own, 0), half(far, 0))
+    stack(y, half(own, 1), half(far, 1))
+    stack(near, half(mate, 0), half(cross, 0))
     shape = (2 * rows, 2 * rows)
     first = lax.broadcasted_iota(jnp.int32, shape, 0)
     positive = (first == lax.broadcasted_iota(jnp.int32, shape, 1)) & (first < rows)
@@ -97,41 +118,35 @@
     size = jax.nn.sigmoid(jnp.where(positive, -logits, logits)) * scale
     signed = jnp.where(positive, -size, size)
     coef_own = signed.astype(jnp.bfloat16)
-    coef_own_t = signed.T.astype(jnp.bfloat16)
-    coef_x = negative_coef(x[...], x_n[...], scale, bias)
-    coef_y = negative_coef(y[...], y_n[...], scale, bias)
-
-    def dot(coef, ref, cols):
-        return jnp.dot(coef, ref[:, cols], preferred_element_type=jnp.float32)
-
+    coef_t[...] = signed.T.astype(jnp.bfloat16)
+    coef = negative_coef(x[...], near[...], scale, bias)
     for cols in columns_of(own.shape[1]):
-        x_acc[:, cols] = dot(coef_own, y, cols) + dot(coef_x, x_n, cols)
-        y_acc[:, cols] = dot(coef_own_t, x, cols) + dot(coef_y, y_n, cols)
-
-
-def far_kernel(
-    scale_ref, bias_ref, own, far, mate, cross, x_acc, y_acc,
-    x_own, x_far, y_own, y_far, x, y, x_n, y_n,
-):
+        acc[:, cols] = dot(coef_own, y[:, cols]) + dot(coef, near[:, cols])
+
+
+def near_y_kernel(scale_ref, bias_ref, own, far, mate, cross, coef_t, acc, x, y, near):
+    stack(x, half(own, 0), half(far, 0))
+    stack(y, half(own, 1), half(far, 1))
+    stack(near, half(mate, 1), half(cross, 1))
+    coef = negative_coef(y[...], near[...], scale_ref[0], bias_ref[0])
+    for cols in columns_of(own.shape[1]):
+        acc[:, cols] = dot(coef_t[...], x[:, cols]) + dot(coef, near[:, cols])
+
+
+def far_kernel(part, scale_ref, bias_ref, own, far, cross, mate, acc, kept, sent, side, near):
     rows = own.shape[0] // 2
-    scale, bias = scale_ref[0], bias_ref[0]
-    stack(own, far, 0, rows, x)
-    stack(own, far, 1, rows, y)
-    stack(mate, cross, 0, rows, x_n)
-    stack(mate, cross, 1, rows, y_n)
-    coef_x = negative_coef(x[...], x_n[...], scale, bias)
-    coef_y = negative_coef(y[...], y_n[...], scale, bias)
+    stack(side, half(own, part), half(far, part))
+    stack(near, half(mate, part), cross[...])
+    coef = negative_coef(side[...], near[...], scale_ref[0], bias_ref[0])
     for cols in columns_of(own.shape[1]):
-        total = x_acc[:, cols] + jnp.dot(
-            coef_x, x_n[:, cols], preferred_element_type=jnp.float32
-        )
-        x_own[:, cols] = total[:rows]
-        x_far[:, cols] = total[rows:].astype(jnp.bfloat16)
-        total = y_acc[:, cols] + jnp.dot(
-            coef_y, y_n[:, cols], preferred_element_type=jnp.float32
-        )
-        y_own[:, cols] = total[:rows]
-        y_far[:, cols] = total[rows:].astype(jnp.bfloat16)
+        total = acc[:, cols] + dot(coef, near[:, cols])
+        kept[:, cols] = total[:rows]
+        sent[:, cols] = total[rows:].astype(jnp.bfloat16)
+
+
+def far_x_kernel(scale_ref, bias_ref, own, far, cross, mate, acc, coef, kept, sent, passed, *scratch):
+    passed[...] = coef[...]
+    far_kernel(0, scale_ref, bias_ref, own, far, cross, mate, acc, kept, sent, *scratch)
 
 
 def grad_strip(raw, direction):
@@ -168,7 +183,7 @@
         out_shape=(piece, piece),
         in_specs=[pl.BlockSpec(memory_space=pltpu.SMEM)] + [pl.BlockSpec(memory_space=pl.ANY)] * 2,
         out_specs=(pl.BlockSpec(memory_space=pltpu.VMEM),) * 2,
-        scratch_shapes=[pltpu.SemaphoreType.DMA((2,))],
+        scratch_shapes=[pltpu.SemaphoreType.DMA((2, PIECES))],
         compiler_params=pltpu.CompilerParams(vmem_limit_bytes=PICK_LIMIT),
     )(odd, img_raw, txt_raw)
 
@@ -196,7 +211,8 @@
     acc_shape = jax.ShapeDtypeStruct((2 * rows, width), jnp.float32)
     own_shape = jax.ShapeDtypeStruct((rows, width), jnp.float32)
     sent_shape = jax.ShapeDtypeStruct((rows, width), jnp.bfloat16)
-    halves = [pltpu.VMEM((2 * rows, width), jnp.bfloat16)] * 4
+    coef_shape = jax.ShapeDtypeStruct((2 * rows, 2 * rows), jnp.bfloat16)
+    pair = pltpu.VMEM((2 * rows, width), jnp.bfloat16)
     unit = 2 * (2 * rows) * (2 * rows) * width
 
     x, y = pick(odd, img_raw, txt_raw)
@@ -205,19 +221,43 @@
     own = call(low_kernel, low_shape, (), (x, y))
     cross_own = lax.ppermute(own, AXES, to_cross)
     mate_own = lax.ppermute(own, AXES, to_mate)
-    far = call(low_kernel, low_shape, (), (x_there, y_there))
-    cross_far = lax.ppermute(far, AXES, to_cross)
+    far, x_far, y_far = call(
+        split_low_kernel, (low_shape, sent_shape, sent_shape), (), (x_there, y_there)
+    )
+    x_cross = lax.ppermute(x_far, AXES, to_cross)
     mate_far = lax.ppermute(far, AXES, to_mate)
-    x_acc, y_acc = call(
-        near_kernel, (acc_shape, acc_shape), scalars, (own, far, mate_own, cross_own), halves, 7 * unit
-    )
-    x_kept, x_sent, y_kept, y_sent = call(
-        far_kernel,
-        (own_shape, sent_shape, own_shape, sent_shape),
-        scalars,
-        (own, far, mate_far, cross_far, x_acc, y_acc),
-        halves,
+    y_cross = lax.ppermute(y_far, AXES, to_cross)
+    x_acc, coef_t = call(
+        near_x_kernel,
+        (acc_shape, coef_shape),
+        scalars,
+        (own, far, mate_own, cross_own),
+        [pair] * 3,
         4 * unit,
+    )
+    x_kept, x_sent, coef_t = call(
+        far_x_kernel,
+        (own_shape, sent_shape, coef_shape),
+        scalars,
+        (own, far, x_cross, mate_far, x_acc, coef_t),
+        [pair] * 2,
+        2 * unit,
+    )
+    y_acc = call(
+        near_y_kernel,
+        acc_shape,
+        scalars,
+        (own, far, mate_own, cross_own, coef_t),
+        [pair] * 3,
+        3 * unit,
+    )
+    y_kept, y_sent = call(
+        functools.partial(far_kernel, 1),
+        (own_shape, sent_shape),
+        scalars,
+        (own, far, y_cross, mate_far, y_acc),
+        [pair] * 2,
+        2 * unit,
     )
     x_back = lax.ppermute(x_sent, AXES, first)
     y_back = lax.ppermute(y_sent, AXES, second)

time: 197 us -> 195 us (0.990); the launches traced: 193 us -> 194 us
  Pallas kernels: 8.47 us -> 12.9 us
  starting transfers between devices: 57.5 us -> 54.4 us
    ppermute x1, waiting for transfers between devices: 55.6 us -> 10.3 us  [local(): x_back = lax.ppermute(x_sent, AXES, first)]
    ppermute x1 -> x2, waiting for transfers between devices: 9.13 us -> 44.3 us  [the longest x1 44.1 us: local(): y_cross = lax.ppermute(y_far, AXES, to_cross)]
    ppermute x1, starting transfers between devices: 13 us -> 1.92 us  [local(): y_back = lax.ppermute(y_sent, AXES, second)]
    ppermute x1, waiting for transfers between devices: 0.01 us -> 9.68 us  [local(): y_back = lax.ppermute(y_sent, AXES, second)]
    ppermute x1 -> x2, starting transfers between devices: 1.92 us -> 9.78 us  [the longest x1 7.02 us: local(): y_cross = lax.ppermute(y_far, AXES, to_cross)]
    pallas_call x6 -> x8, Pallas kernels: 6.46 us -> 10.8 us  [call(): pl.pallas_call(kernel, out_shape=outs, in_specs=[pl.BlockSpec(memory_spac...]
  transfers between devices with their start and end apart: 8 -> 9, of which waited for: 4 -> 6; matrix products, arithmetic and copies ran while one was open for 0% -> 0% of each run, Pallas kernels for 2% -> 5%
where the time goes in v9:
time: 195 us; the launch traced here: 194 us
  waiting for transfers between devices  123 us (63%)
  starting transfers between devices  54.4 us (28%)
  Pallas kernels  12.9 us (7%)
  between operations  2.06 us (1%)
  local copies, waits for them, and re-layouts  2 us (1%)
    ppermute x1, waiting for transfers between devices, local(): y_cross = lax.ppermute(y_far, AXES, to_cross)  44.1 us
    ppermute x1, waiting for transfers between devices, local(): x_there = lax.ppermute(x, AXES, first)  43.2 us
    ppermute x1, starting transfers between devices, local(): x_there = lax.ppermute(x, AXES, first)  15.7 us
    ppermute x1, starting transfers between devices, local(): y_there = lax.ppermute(y, AXES, second)  15.7 us
    ppermute x1, waiting for transfers between devices, local(): y_there = lax.ppermute(y, AXES, second)  15.2 us
    pallas_call x8, Pallas kernels, call(): pl.pallas_call(kernel, out_shape=outs, in_specs=[pl.BlockSpec(memory_spac...  10.8 us
    ppermute x1, waiting for transfers between devices, local(): x_back = lax.ppermute(x_sent, AXES, first)  10.3 us
    ppermute x1, waiting for transfers between devices, local(): y_back = lax.ppermute(y_sent, AXES, second)  9.68 us
  transfers between devices with their start and end apart: 9, of which 6 were waited for; matrix products, arithmetic and copies ran while one was open for 0% of the time, Pallas kernels for 5%

profile of v9, /device:TPU:24, one launch (start us, length us, event | category | flops | bytes accessed | tf_op | source)
XLA Modules:
  0.0 194.1 jit_solution(15421283251051589210)
XLA Ops:
  0.6 2.2 %shard_map.59 = (bf16[128,1536]{1,0:T(8,128)(2,1)}, bf16[128,1536]{1,0:T(8,128)(2,1)}) custom-call(s32[1]{0:T(128)} %bitcast.odd_ref, bf16[128,1536]{1,0:T(8,128)(2,1)} %img_raw.3, bf16[128,1536]{1,0:T(8,128)(2,1)} %txt_raw.3), custom_call_target="tpu_custom_call" | custom-call | tf_op jit(solution)/shard_map/pallas_call | solution.py:181
  2.8 15.7 %collective-permute-start = (bf16[128,1536]{1,0:T(8,128)(2,1)}, bf16[128,1536]{1,0:T(8,128)(2,1)S(1)}, u32[]{:S(2)}, u32[]{:S(2)}) collective-permute-start(bf16[128,1536]{1,0:T(8,128)(2,1)} %get-tuple-element.14.x_ref), channel_id=1, source_target_pairs={{0,1},{1,0},{2,3},{3,2},{4,7},{5,6},{6,5},{7,4},{8,9},{9,8},{10,11... | collective-permute-start | bytes 1179656 | tf_op jit(solution)/shard_map/ppermute | solution.py:219
  18.5 15.7 %collective-permute-start.1 = (bf16[128,1536]{1,0:T(8,128)(2,1)}, bf16[128,1536]{1,0:T(8,128)(2,1)S(1)}, u32[]{:S(2)}, u32[]{:S(2)}) collective-permute-start(bf16[128,1536]{1,0:T(8,128)(2,1)} %get-tuple-element.15.y_ref), channel_id=1, source_target_pairs={{0,3},{1,2},{2,1},{3,0},{4,5},{5,4},{6,7},{7,6},{8,11},{9,10},{10,... | collective-permute-start | bytes 1179656 | tf_op jit(solution)/shard_map/ppermute | solution.py:220
  34.3 0.0 copy-start.2
  34.3 1.0 copy-done.2
  35.3 0.0 copy-start.3
  35.3 1.0 copy-done.3
  36.3 0.2 shard_map.60.own
  36.5 3.3 %collective-permute-start.5 = (bf16[256,1536]{1,0:T(8,128)(2,1)S(1)}, bf16[256,1536]{1,0:T(8,128)(2,1)S(1)}, u32[]{:S(2)}, u32[]{:S(2)}) collective-permute-start(bf16[256,1536]{1,0:T(8,128)(2,1)S(1)} %shard_map.60.own), channel_id=1, source_target_pairs={{0,1023},{1,1020},{2,1021},{3,1022},{4,8},{5,9},{6,10},{7,11},{8,4... | collective-permute-start | bytes 2359304 | tf_op jit(solution)/shard_map/ppermute | solution.py:222
  39.8 1.9 collective-permute-start.4
  41.7 43.2 %collective-permute-done.x_ref = bf16[128,1536]{1,0:T(8,128)(2,1)S(1)} collective-permute-done((bf16[128,1536]{1,0:T(8,128)(2,1)}, bf16[128,1536]{1,0:T(8,128)(2,1)S(1)}, u32[]{:S(2)}, u32[]{:S(2)}) %collective-permute-start) | collective-permute-done | bytes 393248 | tf_op jit(solution)/shard_map/ppermute | solution.py:219
  85.0 15.2 %collective-permute-done.1.y_ref = bf16[128,1536]{1,0:T(8,128)(2,1)S(1)} collective-permute-done((bf16[128,1536]{1,0:T(8,128)(2,1)}, bf16[128,1536]{1,0:T(8,128)(2,1)S(1)}, u32[]{:S(2)}, u32[]{:S(2)}) %collective-permute-start.1) | collective-permute-done | bytes 393248 | tf_op jit(solution)/shard_map/ppermute | solution.py:220
  100.2 1.1 shard_map.61
  101.3 1.9 collective-permute-start.3
  103.2 2.8 %collective-permute-start.6 = (bf16[128,1536]{1,0:T(8,128)(2,1)}, bf16[128,1536]{1,0:T(8,128)(2,1)}, u32[]{:S(2)}, u32[]{:S(2)}) collective-permute-start(bf16[128,1536]{1,0:T(8,128)(2,1)} %get-tuple-element.18), channel_id=1, source_target_pairs={{0,1023},{1,1020},{2,1021},{3,1022},{4,8},{5,9},{6,10},{7,11},{8,4... | collective-permute-start | bytes 1179656 | tf_op jit(solution)/shard_map/ppermute | solution.py:227
  106.0 7.0 %collective-permute-start.2 = (bf16[128,1536]{1,0:T(8,128)(2,1)}, bf16[128,1536]{1,0:T(8,128)(2,1)S(1)}, u32[]{:S(2)}, u32[]{:S(2)}) collective-permute-start(bf16[128,1536]{1,0:T(8,128)(2,1)} %get-tuple-element.17), channel_id=1, source_target_pairs={{0,1023},{1,1020},{2,1021},{3,1022},{4,8},{5,9},{6,10},{7,11},{8,4... | collective-permute-start | bytes 1179656 | tf_op jit(solution)/shard_map/ppermute | solution.py:229
  114.3 0.0 collective-permute-done.5.cross
  114.3 0.0 collective-permute-done.4.mate
  114.3 2.3 %shard_map.62 = (f32[256,1536]{1,0:T(8,128)S(1)}, bf16[256,256]{1,0:T(8,128)(2,1)S(1)}) custom-call(f32[1]{0:T(128)} %bitcast.3.scale_ref, f32[1]{0:T(128)} %bitcast.7.bias_ref, bf16[256,1536]{1,0:T(8,128)(2,1)S(1)} %shard_map.60.own, bf16[256,1536]{1,0:T(8,128)(2,1)S(1)} %get-tuple-element.16.far, bf16[256,1536]{1,0:T(8,128)(2,1)} %collective-permute-done.4.mate, ...), custom_call_target="tpu_custom_call" | custom-call | flops 805306368 | bytes 3145728 | tf_op jit(solution)/shard_map/pallas_call | solution.py:193
  116.6 0.3 collective-permute-done.6.cross
  116.8 0.0 collective-permute-done.3.mate
  116.8 2.1 %shard_map.63 = (f32[128,1536]{1,0:T(8,128)S(1)}, bf16[128,1536]{1,0:T(8,128)(2,1)S(1)}, bf16[256,256]{1,0:T(8,128)(2,1)S(1)}) custom-call(f32[1]{0:T(128)} %bitcast.4.scale_ref, f32[1]{0:T(128)} %bitcast.8.bias_ref, bf16[256,1536]{1,0:T(8,128)(2,1)S(1)} %shard_map.60.own, bf16[256,1536]{1,0:T(8,128)(2,1)S(1)} %get-tuple-element.16.far, ...), custom_call_target="tpu_custom_call" | custom-call | flops 402653184 | bytes 4456448 | tf_op jit(solution)/shard_map/pallas_call | solution.py:193
  118.9 4.1 %collective-permute-start.8 = (bf16[128,1536]{1,0:T(8,128)(2,1)S(1)}, bf16[128,1536]{1,0:T(8,128)(2,1)S(1)}, u32[]{:S(2)}, u32[]{:S(2)}) collective-permute-start(bf16[128,1536]{1,0:T(8,128)(2,1)S(1)} %get-tuple-element.25), channel_id=1, source_target_pairs={{0,1},{1,0},{2,3},{3,2},{4,7},{5,6},{6,5},{7,4},{8,9},{9,8},{10,11... | collective-permute-start | bytes 1179656 | tf_op jit(solution)/shard_map/ppermute | solution.py:262
  123.0 2.4 %shard_map.64.acc = f32[256,1536]{1,0:T(8,128)S(1)} custom-call(f32[1]{0:T(128)} %bitcast.5.scale_ref, f32[1]{0:T(128)} %bitcast.9.bias_ref, bf16[256,1536]{1,0:T(8,128)(2,1)S(1)} %shard_map.60.own, bf16[256,1536]{1,0:T(8,128)(2,1)S(1)} %get-tuple-element.16.far, bf16[256,1536]{1,0:T(8,128)(2,1)} %collective-permute-done.4.mate, ...), custom_call_target="tpu_custom_call" | custom-call | flops 603979776 | bytes 3276800 | tf_op jit(solution)/shard_map/pallas_call | solution.py:193
  125.5 44.1 %collective-permute-done.2.cross = bf16[128,1536]{1,0:T(8,128)(2,1)S(1)} collective-permute-done((bf16[128,1536]{1,0:T(8,128)(2,1)}, bf16[128,1536]{1,0:T(8,128)(2,1)S(1)}, u32[]{:S(2)}, u32[]{:S(2)}) %collective-permute-start.2) | collective-permute-done | bytes 393248 | tf_op jit(solution)/shard_map/ppermute | solution.py:229
  169.5 0.0 copy-start
  169.5 0.0 copy-start.1
  169.5 1.1 shard_map.65
  170.6 1.9 collective-permute-start.7
  172.5 10.3 %collective-permute-done.8.there = bf16[128,1536]{1,0:T(8,128)(2,1)S(1)} collective-permute-done((bf16[128,1536]{1,0:T(8,128)(2,1)S(1)}, bf16[128,1536]{1,0:T(8,128)(2,1)S(1)}, u32[]{:S(2)}, u32[]{:S(2)}) %collective-permute-start.8) | collective-permute-done | bytes 393248 | tf_op jit(solution)/shard_map/ppermute | solution.py:262
  182.8 0.0 copy-done
  182.8 0.0 copy-done.1
  182.8 0.3 shard_map.66.x_grad
  183.1 9.7 %collective-permute-done.7.there = bf16[128,1536]{1,0:T(8,128)(2,1)S(1)} collective-permute-done((bf16[128,1536]{1,0:T(8,128)(2,1)S(1)}, bf16[128,1536]{1,0:T(8,128)(2,1)S(1)}, u32[]{:S(2)}, u32[]{:S(2)}) %collective-permute-start.7) | collective-permute-done | bytes 393248 | tf_op jit(solution)/shard_map/ppermute | solution.py:263
  192.8 1.3 shard_map.67
Async XLA Ops:
  2.8 82.2 %collective-permute-start = (bf16[128,1536]{1,0:T(8,128)(2,1)}, bf16[128,1536]{1,0:T(8,128)(2,1)S(1)}, u32[]{:S(2)}, u32[]{:S(2)}) collective-permute-start(bf16[128,1536]{1,0:T(8,128)(2,1)} %get-tuple-element.14.x_ref), channel_id=1, source_target_pairs={{0,1},{1,0},{2,3},{3,2},{4,7},{5,6},{6,5},{7,4},{8,9},{9,8},{10,11... | collective-permute-start | bytes 1179656 | tf_op jit(solution)/shard_map/ppermute | solution.py:219
  18.5 81.7 %collective-permute-start.1 = (bf16[128,1536]{1,0:T(8,128)(2,1)}, bf16[128,1536]{1,0:T(8,128)(2,1)S(1)}, u32[]{:S(2)}, u32[]{:S(2)}) collective-permute-start(bf16[128,1536]{1,0:T(8,128)(2,1)} %get-tuple-element.15.y_ref), channel_id=1, source_target_pairs={{0,3},{1,2},{2,1},{3,0},{4,5},{5,4},{6,7},{7,6},{8,11},{9,10},{10,... | collective-permute-start | bytes 1179656 | tf_op jit(solution)/shard_map/ppermute | solution.py:220
  34.3 1.0 copy-start.2
  35.3 1.0 copy-start.3
  36.5 77.8 %collective-permute-start.5 = (bf16[256,1536]{1,0:T(8,128)(2,1)S(1)}, bf16[256,1536]{1,0:T(8,128)(2,1)S(1)}, u32[]{:S(2)}, u32[]{:S(2)}) collective-permute-start(bf16[256,1536]{1,0:T(8,128)(2,1)S(1)} %shard_map.60.own), channel_id=1, source_target_pairs={{0,1023},{1,1020},{2,1021},{3,1022},{4,8},{5,9},{6,10},{7,11},{8,4... | collective-permute-start | bytes 2359304 | tf_op jit(solution)/shard_map/ppermute | solution.py:222
  39.8 74.5 %collective-permute-start.4 = (bf16[256,1536]{1,0:T(8,128)(2,1)S(1)}, bf16[256,1536]{1,0:T(8,128)(2,1)}, u32[]{:S(2)}, u32[]{:S(2)}) collective-permute-start(bf16[256,1536]{1,0:T(8,128)(2,1)S(1)} %shard_map.60.own), channel_id=1, source_target_pairs={{0,4},{1,5},{2,6},{3,7},{4,0},{5,1},{6,2},{7,3},{8,12},{9,13},{10,... | collective-permute-start | bytes 2359304 | tf_op jit(solution)/shard_map/ppermute | solution.py:223
  101.3 15.6 %collective-permute-start.3 = (bf16[256,1536]{1,0:T(8,128)(2,1)S(1)}, bf16[256,1536]{1,0:T(8,128)(2,1)S(1)}, u32[]{:S(2)}, u32[]{:S(2)}) collective-permute-start(bf16[256,1536]{1,0:T(8,128)(2,1)S(1)} %get-tuple-element.16.far), channel_id=1, source_target_pairs={{0,4},{1,5},{2,6},{3,7},{4,0},{5,1},{6,2},{7,3},{8,12},{9,13},{10,... | collective-permute-start | bytes 2359304 | tf_op jit(solution)/shard_map/ppermute | solution.py:228
  103.2 13.6 %collective-permute-start.6 = (bf16[128,1536]{1,0:T(8,128)(2,1)}, bf16[128,1536]{1,0:T(8,128)(2,1)}, u32[]{:S(2)}, u32[]{:S(2)}) collective-permute-start(bf16[128,1536]{1,0:T(8,128)(2,1)} %get-tuple-element.18), channel_id=1, source_target_pairs={{0,1023},{1,1020},{2,1021},{3,1022},{4,8},{5,9},{6,10},{7,11},{8,4... | collective-permute-start | bytes 1179656 | tf_op jit(solution)/shard_map/ppermute | solution.py:227
  106.0 63.6 %collective-permute-start.2 = (bf16[128,1536]{1,0:T(8,128)(2,1)}, bf16[128,1536]{1,0:T(8,128)(2,1)S(1)}, u32[]{:S(2)}, u32[]{:S(2)}) collective-permute-start(bf16[128,1536]{1,0:T(8,128)(2,1)} %get-tuple-element.17), channel_id=1, source_target_pairs={{0,1023},{1,1020},{2,1021},{3,1022},{4,8},{5,9},{6,10},{7,11},{8,4... | collective-permute-start | bytes 1179656 | tf_op jit(solution)/shard_map/ppermute | solution.py:229
  118.9 63.9 %collective-permute-start.8 = (bf16[128,1536]{1,0:T(8,128)(2,1)S(1)}, bf16[128,1536]{1,0:T(8,128)(2,1)S(1)}, u32[]{:S(2)}, u32[]{:S(2)}) collective-permute-start(bf16[128,1536]{1,0:T(8,128)(2,1)S(1)} %get-tuple-element.25), channel_id=1, source_target_pairs={{0,1},{1,0},{2,3},{3,2},{4,7},{5,6},{6,5},{7,4},{8,9},{9,8},{10,11... | collective-permute-start | bytes 1179656 | tf_op jit(solution)/shard_map/ppermute | solution.py:262
  169.5 13.3 %copy-start = (bf16[128,1536]{1,0:T(8,128)(2,1)S(1)}, bf16[128,1536]{1,0:T(8,128)(2,1)}, u32[]{:S(2)}) copy-start(bf16[128,1536]{1,0:T(8,128)(2,1)} %img_raw.3) | copy-start | bytes 1179652
  169.5 13.3 %copy-start.1 = (bf16[128,1536]{1,0:T(8,128)(2,1)S(1)}, bf16[128,1536]{1,0:T(8,128)(2,1)}, u32[]{:S(2)}) copy-start(bf16[128,1536]{1,0:T(8,128)(2,1)} %txt_raw.3) | copy-start | bytes 1179652
  170.6 22.2 %collective-permute-start.7 = (bf16[128,1536]{1,0:T(8,128)(2,1)S(1)}, bf16[128,1536]{1,0:T(8,128)(2,1)S(1)}, u32[]{:S(2)}, u32[]{:S(2)}) collective-permute-start(bf16[128,1536]{1,0:T(8,128)(2,1)S(1)} %get-tuple-element.23), channel_id=1, source_target_pairs={{0,3},{1,2},{2,1},{3,0},{4,5},{5,4},{6,7},{7,6},{8,11},{9,10},{10,... | collective-permute-start | bytes 1179656 | tf_op jit(solution)/shard_map/ppermute | solution.py:263

commit v10 on v9

--- a/solution.py
+++ b/solution.py
@@ -124,7 +124,8 @@
         acc[:, cols] = dot(coef_own, y[:, cols]) + dot(coef, near[:, cols])
 
 
-def near_y_kernel(scale_ref, bias_ref, own, far, mate, cross, coef_t, acc, x, y, near):
+def near_y_kernel(scale_ref, bias_ref, own, far, mate, cross, coef_t, after, acc, x, y, near):
+    del after
     stack(x, half(own, 0), half(far, 0))
     stack(y, half(own, 1), half(far, 1))
     stack(near, half(mate, 1), half(cross, 1))
@@ -144,11 +145,6 @@
         sent[:, cols] = total[rows:].astype(jnp.bfloat16)
 
 
-def far_x_kernel(scale_ref, bias_ref, own, far, cross, mate, acc, coef, kept, sent, passed, *scratch):
-    passed[...] = coef[...]
-    far_kernel(0, scale_ref, bias_ref, own, far, cross, mate, acc, kept, sent, *scratch)
-
-
 def grad_strip(raw, direction):
     values = raw.astype(jnp.float32)
     inverse = inverse_of(values)
@@ -182,24 +178,25 @@
         pick_kernel,
         out_shape=(piece, piece),
         in_specs=[pl.BlockSpec(memory_space=pltpu.SMEM)] + [pl.BlockSpec(memory_space=pl.ANY)] * 2,
-        out_specs=(pl.BlockSpec(memory_space=pltpu.VMEM),) * 2,
+        out_specs=(pl.BlockSpec(memory_space=pl.ANY),) * 2,
         scratch_shapes=[pltpu.SemaphoreType.DMA((2, PIECES))],
         compiler_params=pltpu.CompilerParams(vmem_limit_bytes=PICK_LIMIT),
     )(odd, img_raw, txt_raw)
 
 
-def call(kernel, outs, scalars, arrays, scratch=(), flops=0):
+def call(kernel, outs, scalars, arrays, scratch=(), flops=0, there=()):
     moved = sum(a.size * a.dtype.itemsize for a in arrays)
     return pl.pallas_call(
         kernel,
         out_shape=outs,
         in_specs=[pl.BlockSpec(memory_space=pltpu.SMEM)] * len(scalars)
-        + [pl.BlockSpec(memory_space=pltpu.VMEM)] * len(arrays),
+        + [pl.BlockSpec(memory_space=pltpu.VMEM)] * len(arrays)
+        + [pl.BlockSpec(memory_space=pl.ANY)] * len(there),
         out_specs=jax.tree.map(lambda _: pl.BlockSpec(memory_space=pltpu.VMEM), outs),
         scratch_shapes=list(scratch),
         compiler_params=pltpu.CompilerParams(vmem_limit_bytes=VMEM_LIMIT),
         cost_estimate=pl.CostEstimate(flops=flops, bytes_accessed=moved, transcendentals=0),
-    )(*scalars, *arrays)
+    )(*scalars, *arrays, *there)
 
 
 def local(img_raw, txt_raw, logit_scale, logit_bias, moves):
@@ -235,11 +232,11 @@
         [pair] * 3,
         4 * unit,
     )
-    x_kept, x_sent, coef_t = call(
-        far_x_kernel,
-        (own_shape, sent_shape, coef_shape),
-        scalars,
-        (own, far, x_cross, mate_far, x_acc, coef_t),
+    x_kept, x_sent = call(
+        functools.partial(far_kernel, 0),
+        (own_shape, sent_shape),
+        scalars,
+        (own, far, x_cross, mate_far, x_acc),
         [pair] * 2,
         2 * unit,
     )
@@ -250,6 +247,7 @@
         (own, far, mate_own, cross_own, coef_t),
         [pair] * 3,
         3 * unit,
+        (x_sent,),
     )
     y_kept, y_sent = call(
         functools.partial(far_kernel, 1),

time: 195 us -> 218 us (1.12)
  Pallas kernels: 12.9 us -> 35.7 us
    pallas_call x1, Pallas kernels: 2.16 us -> 25 us  [pick(): pl.pallas_call(pick_kernel, out_shape=(piece, piece), in_specs=[pl.BlockS...]
  transfers between devices with their start and end apart: 9 -> 9, of which waited for: 6 -> 6; matrix products, arithmetic and copies ran while one was open for 0% -> 0% of each run, Pallas kernels for 5% -> 4%
where the time goes in v10:
time: 218 us; the launch traced here: 217 us
  waiting for transfers between devices  123 us (56%)
  starting transfers between devices  54.4 us (25%)
  Pallas kernels  35.7 us (16%)
    ppermute x1, waiting for transfers between devices, local(): y_cross = lax.ppermute(y_far, AXES, to_cross)  44.1 us
    ppermute x1, waiting for transfers between devices, local(): x_there = lax.ppermute(x, AXES, first)  43.2 us
    pallas_call x1, Pallas kernels, pick(): pl.pallas_call(pick_kernel, out_shape=(piece, piece), in_specs=[pl.BlockS...  25 us
    ppermute x1, starting transfers between devices, local(): x_there = lax.ppermute(x, AXES, first)  15.7 us
    ppermute x1, starting transfers between devices, local(): y_there = lax.ppermute(y, AXES, second)  15.7 us
    ppermute x1, waiting for transfers between devices, local(): y_there = lax.ppermute(y, AXES, second)  15.2 us
    pallas_call x8, Pallas kernels, call(): pl.pallas_call(kernel, out_shape=outs, in_specs=[pl.BlockSpec(memory_spac...  10.7 us
    ppermute x1, waiting for transfers between devices, local(): x_back = lax.ppermute(x_sent, AXES, first)  10.3 us
  transfers between devices with their start and end apart: 9, of which 6 were waited for; matrix products, arithmetic and copies ran while one was open for 0% of the time, Pallas kernels for 4%

profile of v10, /device:TPU:24, one launch (start us, length us, event | category | flops | bytes accessed | tf_op | source)
XLA Modules:
  0.0 217.0 jit_solution(3809478668854674936)
XLA Ops:
  0.6 25.0 %shard_map.59 = (bf16[128,1536]{1,0:T(8,128)(2,1)}, bf16[128,1536]{1,0:T(8,128)(2,1)}) custom-call(s32[1]{0:T(128)} %bitcast.odd_ref, bf16[128,1536]{1,0:T(8,128)(2,1)} %img_raw.3, bf16[128,1536]{1,0:T(8,128)(2,1)} %txt_raw.3), custom_call_target="tpu_custom_call" | custom-call | tf_op jit(solution)/shard_map/pallas_call | solution.py:177
  25.6 15.7 %collective-permute-start = (bf16[128,1536]{1,0:T(8,128)(2,1)}, bf16[128,1536]{1,0:T(8,128)(2,1)S(1)}, u32[]{:S(2)}, u32[]{:S(2)}) collective-permute-start(bf16[128,1536]{1,0:T(8,128)(2,1)} %get-tuple-element.13.x_ref), channel_id=1, source_target_pairs={{0,1},{1,0},{2,3},{3,2},{4,7},{5,6},{6,5},{7,4},{8,9},{9,8},{10,11... | collective-permute-start | bytes 1179656 | tf_op jit(solution)/shard_map/ppermute | solution.py:216
  41.4 15.7 %collective-permute-start.1 = (bf16[128,1536]{1,0:T(8,128)(2,1)}, bf16[128,1536]{1,0:T(8,128)(2,1)S(1)}, u32[]{:S(2)}, u32[]{:S(2)}) collective-permute-start(bf16[128,1536]{1,0:T(8,128)(2,1)} %get-tuple-element.14.y_ref), channel_id=1, source_target_pairs={{0,3},{1,2},{2,1},{3,0},{4,5},{5,4},{6,7},{7,6},{8,11},{9,10},{10,... | collective-permute-start | bytes 1179656 | tf_op jit(solution)/shard_map/ppermute | solution.py:217
  57.1 0.0 copy-start.2
  57.1 1.0 copy-done.2
  58.1 0.0 copy-start.3
  58.1 1.0 copy-done.3
  59.1 0.2 shard_map.60.own
  59.4 3.3 %collective-permute-start.5 = (bf16[256,1536]{1,0:T(8,128)(2,1)S(1)}, bf16[256,1536]{1,0:T(8,128)(2,1)S(1)}, u32[]{:S(2)}, u32[]{:S(2)}) collective-permute-start(bf16[256,1536]{1,0:T(8,128)(2,1)S(1)} %shard_map.60.own), channel_id=1, source_target_pairs={{0,1023},{1,1020},{2,1021},{3,1022},{4,8},{5,9},{6,10},{7,11},{8,4... | collective-permute-start | bytes 2359304 | tf_op jit(solution)/shard_map/ppermute | solution.py:219
  62.7 1.9 collective-permute-start.4
  64.6 43.2 %collective-permute-done.x_ref = bf16[128,1536]{1,0:T(8,128)(2,1)S(1)} collective-permute-done((bf16[128,1536]{1,0:T(8,128)(2,1)}, bf16[128,1536]{1,0:T(8,128)(2,1)S(1)}, u32[]{:S(2)}, u32[]{:S(2)}) %collective-permute-start) | collective-permute-done | bytes 393248 | tf_op jit(solution)/shard_map/ppermute | solution.py:216
  107.8 15.2 %collective-permute-done.1.y_ref = bf16[128,1536]{1,0:T(8,128)(2,1)S(1)} collective-permute-done((bf16[128,1536]{1,0:T(8,128)(2,1)}, bf16[128,1536]{1,0:T(8,128)(2,1)S(1)}, u32[]{:S(2)}, u32[]{:S(2)}) %collective-permute-start.1) | collective-permute-done | bytes 393248 | tf_op jit(solution)/shard_map/ppermute | solution.py:217
  123.0 1.1 shard_map.61
  124.1 1.9 collective-permute-start.3
  126.0 2.8 %collective-permute-start.6 = (bf16[128,1536]{1,0:T(8,128)(2,1)}, bf16[128,1536]{1,0:T(8,128)(2,1)}, u32[]{:S(2)}, u32[]{:S(2)}) collective-permute-start(bf16[128,1536]{1,0:T(8,128)(2,1)} %get-tuple-element.18), channel_id=1, source_target_pairs={{0,1023},{1,1020},{2,1021},{3,1022},{4,8},{5,9},{6,10},{7,11},{8,4... | collective-permute-start | bytes 1179656 | tf_op jit(solution)/shard_map/ppermute | solution.py:224
  128.8 7.0 %collective-permute-start.2 = (bf16[128,1536]{1,0:T(8,128)(2,1)}, bf16[128,1536]{1,0:T(8,128)(2,1)S(1)}, u32[]{:S(2)}, u32[]{:S(2)}) collective-permute-start(bf16[128,1536]{1,0:T(8,128)(2,1)} %get-tuple-element.16), channel_id=1, source_target_pairs={{0,1023},{1,1020},{2,1021},{3,1022},{4,8},{5,9},{6,10},{7,11},{8,4... | collective-permute-start | bytes 1179656 | tf_op jit(solution)/shard_map/ppermute | solution.py:226
  137.1 0.0 collective-permute-done.5.cross
  137.1 0.0 collective-permute-done.4.mate
  137.1 2.3 %shard_map.62 = (f32[256,1536]{1,0:T(8,128)S(1)}, bf16[256,256]{1,0:T(8,128)(2,1)S(1)}) custom-call(f32[1]{0:T(128)} %bitcast.3.scale_ref, f32[1]{0:T(128)} %bitcast.7.bias_ref, bf16[256,1536]{1,0:T(8,128)(2,1)S(1)} %shard_map.60.own, bf16[256,1536]{1,0:T(8,128)(2,1)S(1)} %get-tuple-element.15.far, bf16[256,1536]{1,0:T(8,128)(2,1)} %collective-permute-done.4.mate, ...), custom_call_target="tpu_custom_call" | custom-call | flops 805306368 | bytes 3145728 | tf_op jit(solution)/shard_map/pallas_call | solution.py:189
  139.4 0.3 collective-permute-done.6.cross
  139.7 0.0 collective-permute-done.3.mate
  139.7 2.1 shard_map.63
  141.7 4.1 %collective-permute-start.8 = (bf16[128,1536]{1,0:T(8,128)(2,1)S(1)}, bf16[128,1536]{1,0:T(8,128)(2,1)S(1)}, u32[]{:S(2)}, u32[]{:S(2)}) collective-permute-start(bf16[128,1536]{1,0:T(8,128)(2,1)S(1)} %get-tuple-element.20.after), channel_id=1, source_target_pairs={{0,1},{1,0},{2,3},{3,2},{4,7},{5,6},{6,5},{7,4},{8,9},{9,8},{10,11... | collective-permute-start | bytes 1179656 | tf_op jit(solution)/shard_map/ppermute | solution.py:260
  145.8 2.4 %shard_map.64.acc = f32[256,1536]{1,0:T(8,128)S(1)} custom-call(f32[1]{0:T(128)} %bitcast.5.scale_ref, f32[1]{0:T(128)} %bitcast.9.bias_ref, bf16[256,1536]{1,0:T(8,128)(2,1)S(1)} %shard_map.60.own, bf16[256,1536]{1,0:T(8,128)(2,1)S(1)} %get-tuple-element.15.far, bf16[256,1536]{1,0:T(8,128)(2,1)} %collective-permute-done.4.mate, ...), custom_call_target="tpu_custom_call" | custom-call | flops 603979776 | bytes 3276800 | tf_op jit(solution)/shard_map/pallas_call | solution.py:189
  148.3 44.1 %collective-permute-done.2.cross = bf16[128,1536]{1,0:T(8,128)(2,1)S(1)} collective-permute-done((bf16[128,1536]{1,0:T(8,128)(2,1)}, bf16[128,1536]{1,0:T(8,128)(2,1)S(1)}, u32[]{:S(2)}, u32[]{:S(2)}) %collective-permute-start.2) | collective-permute-done | bytes 393248 | tf_op jit(solution)/shard_map/ppermute | solution.py:226
  192.3 0.0 copy-start
  192.3 0.0 copy-start.1
  192.3 1.1 shard_map.65
  193.4 1.9 collective-permute-start.7
  195.3 10.3 %collective-permute-done.8.there = bf16[128,1536]{1,0:T(8,128)(2,1)S(1)} collective-permute-done((bf16[128,1536]{1,0:T(8,128)(2,1)S(1)}, bf16[128,1536]{1,0:T(8,128)(2,1)S(1)}, u32[]{:S(2)}, u32[]{:S(2)}) %collective-permute-start.8) | collective-permute-done | bytes 393248 | tf_op jit(solution)/shard_map/ppermute | solution.py:260
  205.6 0.0 copy-done
  205.6 0.0 copy-done.1
  205.6 0.3 shard_map.66.x_grad
  206.0 9.7 %collective-permute-done.7.there = bf16[128,1536]{1,0:T(8,128)(2,1)S(1)} collective-permute-done((bf16[128,1536]{1,0:T(8,128)(2,1)S(1)}, bf16[128,1536]{1,0:T(8,128)(2,1)S(1)}, u32[]{:S(2)}, u32[]{:S(2)}) %collective-permute-start.7) | collective-permute-done | bytes 393248 | tf_op jit(solution)/shard_map/ppermute | solution.py:261
  215.7 1.3 shard_map.67
Async XLA Ops:
  25.6 82.1 %collective-permute-start = (bf16[128,1536]{1,0:T(8,128)(2,1)}, bf16[128,1536]{1,0:T(8,128)(2,1)S(1)}, u32[]{:S(2)}, u32[]{:S(2)}) collective-permute-start(bf16[128,1536]{1,0:T(8,128)(2,1)} %get-tuple-element.13.x_ref), channel_id=1, source_target_pairs={{0,1},{1,0},{2,3},{3,2},{4,7},{5,6},{6,5},{7,4},{8,9},{9,8},{10,11... | collective-permute-start | bytes 1179656 | tf_op jit(solution)/shard_map/ppermute | solution.py:216
  41.4 81.7 %collective-permute-start.1 = (bf16[128,1536]{1,0:T(8,128)(2,1)}, bf16[128,1536]{1,0:T(8,128)(2,1)S(1)}, u32[]{:S(2)}, u32[]{:S(2)}) collective-permute-start(bf16[128,1536]{1,0:T(8,128)(2,1)} %get-tuple-element.14.y_ref), channel_id=1, source_target_pairs={{0,3},{1,2},{2,1},{3,0},{4,5},{5,4},{6,7},{7,6},{8,11},{9,10},{10,... | collective-permute-start | bytes 1179656 | tf_op jit(solution)/shard_map/ppermute | solution.py:217
  57.1 1.0 copy-start.2
  58.1 1.0 copy-start.3
  59.4 77.8 %collective-permute-start.5 = (bf16[256,1536]{1,0:T(8,128)(2,1)S(1)}, bf16[256,1536]{1,0:T(8,128)(2,1)S(1)}, u32[]{:S(2)}, u32[]{:S(2)}) collective-permute-start(bf16[256,1536]{1,0:T(8,128)(2,1)S(1)} %shard_map.60.own), channel_id=1, source_target_pairs={{0,1023},{1,1020},{2,1021},{3,1022},{4,8},{5,9},{6,10},{7,11},{8,4... | collective-permute-start | bytes 2359304 | tf_op jit(solution)/shard_map/ppermute | solution.py:219
  62.7 74.5 %collective-permute-start.4 = (bf16[256,1536]{1,0:T(8,128)(2,1)S(1)}, bf16[256,1536]{1,0:T(8,128)(2,1)}, u32[]{:S(2)}, u32[]{:S(2)}) collective-permute-start(bf16[256,1536]{1,0:T(8,128)(2,1)S(1)} %shard_map.60.own), channel_id=1, source_target_pairs={{0,4},{1,5},{2,6},{3,7},{4,0},{5,1},{6,2},{7,3},{8,12},{9,13},{10,... | collective-permute-start | bytes 2359304 | tf_op jit(solution)/shard_map/ppermute | solution.py:220
  124.1 15.6 %collective-permute-start.3 = (bf16[256,1536]{1,0:T(8,128)(2,1)S(1)}, bf16[256,1536]{1,0:T(8,128)(2,1)S(1)}, u32[]{:S(2)}, u32[]{:S(2)}) collective-permute-start(bf16[256,1536]{1,0:T(8,128)(2,1)S(1)} %get-tuple-element.15.far), channel_id=1, source_target_pairs={{0,4},{1,5},{2,6},{3,7},{4,0},{5,1},{6,2},{7,3},{8,12},{9,13},{10,... | collective-permute-start | bytes 2359304 | tf_op jit(solution)/shard_map/ppermute | solution.py:225
  126.0 13.6 %collective-permute-start.6 = (bf16[128,1536]{1,0:T(8,128)(2,1)}, bf16[128,1536]{1,0:T(8,128)(2,1)}, u32[]{:S(2)}, u32[]{:S(2)}) collective-permute-start(bf16[128,1536]{1,0:T(8,128)(2,1)} %get-tuple-element.18), channel_id=1, source_target_pairs={{0,1023},{1,1020},{2,1021},{3,1022},{4,8},{5,9},{6,10},{7,11},{8,4... | collective-permute-start | bytes 1179656 | tf_op jit(solution)/shard_map/ppermute | solution.py:224
  128.8 63.5 %collective-permute-start.2 = (bf16[128,1536]{1,0:T(8,128)(2,1)}, bf16[128,1536]{1,0:T(8,128)(2,1)S(1)}, u32[]{:S(2)}, u32[]{:S(2)}) collective-permute-start(bf16[128,1536]{1,0:T(8,128)(2,1)} %get-tuple-element.16), channel_id=1, source_target_pairs={{0,1023},{1,1020},{2,1021},{3,1022},{4,8},{5,9},{6,10},{7,11},{8,4... | collective-permute-start | bytes 1179656 | tf_op jit(solution)/shard_map/ppermute | solution.py:226
  141.7 63.9 %collective-permute-start.8 = (bf16[128,1536]{1,0:T(8,128)(2,1)S(1)}, bf16[128,1536]{1,0:T(8,128)(2,1)S(1)}, u32[]{:S(2)}, u32[]{:S(2)}) collective-permute-start(bf16[128,1536]{1,0:T(8,128)(2,1)S(1)} %get-tuple-element.20.after), channel_id=1, source_target_pairs={{0,1},{1,0},{2,3},{3,2},{4,7},{5,6},{6,5},{7,4},{8,9},{9,8},{10,11... | collective-permute-start | bytes 1179656 | tf_op jit(solution)/shard_map/ppermute | solution.py:260
  192.3 13.3 %copy-start = (bf16[128,1536]{1,0:T(8,128)(2,1)S(1)}, bf16[128,1536]{1,0:T(8,128)(2,1)}, u32[]{:S(2)}) copy-start(bf16[128,1536]{1,0:T(8,128)(2,1)} %img_raw.3) | copy-start | bytes 1179652
  192.3 13.3 %copy-start.1 = (bf16[128,1536]{1,0:T(8,128)(2,1)S(1)}, bf16[128,1536]{1,0:T(8,128)(2,1)}, u32[]{:S(2)}) copy-start(bf16[128,1536]{1,0:T(8,128)(2,1)} %txt_raw.3) | copy-start | bytes 1179652
  193.4 22.3 %collective-permute-start.7 = (bf16[128,1536]{1,0:T(8,128)(2,1)S(1)}, bf16[128,1536]{1,0:T(8,128)(2,1)S(1)}, u32[]{:S(2)}, u32[]{:S(2)}) collective-permute-start(bf16[128,1536]{1,0:T(8,128)(2,1)S(1)} %get-tuple-element.22), channel_id=1, source_target_pairs={{0,3},{1,2},{2,1},{3,0},{4,5},{5,4},{6,7},{7,6},{8,11},{9,10},{10,... | collective-permute-start | bytes 1179656 | tf_op jit(solution)/shard_map/ppermute | solution.py:261

commit v11 on v10

--- a/solution.py
+++ b/solution.py
@@ -11,8 +11,6 @@
 SPAN = 16
 STRIP = 32
 VMEM_LIMIT = 16 * 1024 * 1024
-PIECES = 4
-PICK_LIMIT = 56 * 1024 * 1024
 
 
 def device_of(block, role, blocks, ways):
@@ -39,29 +37,6 @@
     return lax.rsqrt(jnp.sum(values * values, axis=-1, keepdims=True) + 1e-06)
 
 
-def pick_kernel(odd_ref, img_ref, txt_ref, x_ref, y_ref, sems):
-    def move(x_from, y_from):
-        copies = []
-        rows = x_ref.shape[0] // PIECES
-        for place in range(PIECES):
-            here = pl.ds(place * rows, rows)
-            for side, (source, out) in enumerate(((x_from, x_ref), (y_from, y_ref))):
-                sem = sems.at[side, place]
-                copies.append(pltpu.make_async_copy(source.at[here, :], out.at[here, :], sem))
-        for copy in copies:
-            copy.start()
-        for copy in copies:
-            copy.wait()
-
-    @pl.when(odd_ref[0] == 0)
-    def _():
-        move(img_ref, txt_ref)
-
-    @pl.when(odd_ref[0] != 0)
-    def _():
-        move(txt_ref, img_ref)
-
-
 def low_kernel(x_ref, y_ref, low_ref):
     rows = x_ref.shape[0]
     for part, ref in enumerate((x_ref, y_ref)):
@@ -86,8 +61,12 @@
     return (jax.nn.sigmoid(scale * scores_of(left, right) + bias) * scale).astype(jnp.bfloat16)
 
 
-def columns_of(width, step=256):
-    return [slice(start, start + step) for start in range(0, width, step)]
+def each_columns(width, body, step=256):
+    def run(place, carry):
+        body(pl.ds(pl.multiple_of(place * step, step), step))
+        return carry
+
+    lax.fori_loop(0, width // step, run, 0)
 
 
 def dot(coef, rows):
@@ -120,29 +99,35 @@
     coef_own = signed.astype(jnp.bfloat16)
     coef_t[...] = signed.T.astype(jnp.bfloat16)
     coef = negative_coef(x[...], near[...], scale, bias)
-    for cols in columns_of(own.shape[1]):
+
+    def body(cols):
         acc[:, cols] = dot(coef_own, y[:, cols]) + dot(coef, near[:, cols])
 
-
-def near_y_kernel(scale_ref, bias_ref, own, far, mate, cross, coef_t, after, acc, x, y, near):
+    each_columns(own.shape[1], body)
+
+
+def near_y_kernel(scale_ref, bias_ref, x, y, mate, cross, coef_t, after, acc, near):
     del after
-    stack(x, half(own, 0), half(far, 0))
-    stack(y, half(own, 1), half(far, 1))
     stack(near, half(mate, 1), half(cross, 1))
     coef = negative_coef(y[...], near[...], scale_ref[0], bias_ref[0])
-    for cols in columns_of(own.shape[1]):
+
+    def body(cols):
         acc[:, cols] = dot(coef_t[...], x[:, cols]) + dot(coef, near[:, cols])
 
-
-def far_kernel(part, scale_ref, bias_ref, own, far, cross, mate, acc, kept, sent, side, near):
-    rows = own.shape[0] // 2
-    stack(side, half(own, part), half(far, part))
+    each_columns(x.shape[1], body)
+
+
+def far_kernel(part, scale_ref, bias_ref, side, cross, mate, acc, kept, sent, near):
+    rows = kept.shape[0]
     stack(near, half(mate, part), cross[...])
     coef = negative_coef(side[...], near[...], scale_ref[0], bias_ref[0])
-    for cols in columns_of(own.shape[1]):
+
+    def body(cols):
         total = acc[:, cols] + dot(coef, near[:, cols])
         kept[:, cols] = total[:rows]
         sent[:, cols] = total[rows:].astype(jnp.bfloat16)
+
+    each_columns(side.shape[1], body)
 
 
 def grad_strip(raw, direction):
@@ -170,18 +155,6 @@
         x = x_grad[here, :]
         img_grad[here, :] = jnp.where(odd, y, x)
         txt_grad[here, :] = jnp.where(odd, x, y)
-
-
-def pick(odd, img_raw, txt_raw):
-    piece = jax.ShapeDtypeStruct(img_raw.shape, img_raw.dtype)
-    return pl.pallas_call(
-        pick_kernel,
-        out_shape=(piece, piece),
-        in_specs=[pl.BlockSpec(memory_space=pltpu.SMEM)] + [pl.BlockSpec(memory_space=pl.ANY)] * 2,
-        out_specs=(pl.BlockSpec(memory_space=pl.ANY),) * 2,
-        scratch_shapes=[pltpu.SemaphoreType.DMA((2, PIECES))],
-        compiler_params=pltpu.CompilerParams(vmem_limit_bytes=PICK_LIMIT),
-    )(odd, img_raw, txt_raw)
 
 
 def call(kernel, outs, scalars, arrays, scratch=(), flops=0, there=()):
@@ -212,7 +185,8 @@
     pair = pltpu.VMEM((2 * rows, width), jnp.bfloat16)
     unit = 2 * (2 * rows) * (2 * rows) * width
 
-    x, y = pick(odd, img_raw, txt_raw)
+    x = jnp.where(odd > 0, txt_raw, img_raw)
+    y = jnp.where(odd > 0, img_raw, txt_raw)
     x_there = lax.ppermute(x, AXES, first)
     y_there = lax.ppermute(y, AXES, second)
     own = call(low_kernel, low_shape, (), (x, y))
@@ -224,28 +198,28 @@
     x_cross = lax.ppermute(x_far, AXES, to_cross)
     mate_far = lax.ppermute(far, AXES, to_mate)
     y_cross = lax.ppermute(y_far, AXES, to_cross)
-    x_acc, coef_t = call(
+    x_acc, coef_t, x_half, y_half = call(
         near_x_kernel,
-        (acc_shape, coef_shape),
+        (acc_shape, coef_shape, low_shape, low_shape),
         scalars,
         (own, far, mate_own, cross_own),
-        [pair] * 3,
+        [pair],
         4 * unit,
     )
     x_kept, x_sent = call(
         functools.partial(far_kernel, 0),
         (own_shape, sent_shape),
         scalars,
-        (own, far, x_cross, mate_far, x_acc),
-        [pair] * 2,
+        (x_half, x_cross, mate_far, x_acc),
+        [pair],
         2 * unit,
     )
     y_acc = call(
         near_y_kernel,
         acc_shape,
         scalars,
-        (own, far, mate_own, cross_own, coef_t),
-        [pair] * 3,
+        (x_half, y_half, mate_own, cross_own, coef_t),
+        [pair],
         3 * unit,
         (x_sent,),
     )
@@ -253,8 +227,8 @@
         functools.partial(far_kernel, 1),
         (own_shape, sent_shape),
         scalars,
-        (own, far, y_cross, mate_far, y_acc),
-        [pair] * 2,
+        (y_half, y_cross, mate_far, y_acc),
+        [pair],
         2 * unit,
     )
     x_back = lax.ppermute(x_sent, AXES, first)

time: 218 us -> 196 us (0.90)
  Pallas kernels: 35.7 us -> 12.4 us
    pallas_call x1 -> x0, Pallas kernels: 25 us -> none  [pick(): pl.pallas_call(pick_kernel, out_shape=(piece, piece), in_specs=[pl.BlockS...]
    ppermute x1, waiting for transfers between devices: 44.1 us -> 33.6 us  [local(): y_cross = lax.ppermute(y_far, AXES, to_cross)]
    ppermute x1, waiting for transfers between devices: 10.3 us -> 19.8 us  [local(): x_back = lax.ppermute(x_sent, AXES, first)]
  transfers between devices with their start and end apart: 9 -> 9, of which waited for: 6 -> 5; matrix products, arithmetic and copies ran while one was open for 0% -> 0% of each run, Pallas kernels for 4% -> 6%
where the time goes in v11:
time: 196 us; the launch traced here: 195 us
  waiting for transfers between devices  124 us (63%)
  starting transfers between devices  55.5 us (28%)
  Pallas kernels  12.4 us (6%)
  between operations  2.09 us (1%)
    ppermute x1, waiting for transfers between devices, local(): x_there = lax.ppermute(x, AXES, first)  44 us
    ppermute x1, waiting for transfers between devices, local(): y_cross = lax.ppermute(y_far, AXES, to_cross)  33.6 us
    ppermute x1, waiting for transfers between devices, local(): x_back = lax.ppermute(x_sent, AXES, first)  19.8 us
    ppermute x1, starting transfers between devices, local(): x_there = lax.ppermute(x, AXES, first)  15.7 us
    ppermute x1, starting transfers between devices, local(): y_there = lax.ppermute(y, AXES, second)  15.7 us
    ppermute x1, waiting for transfers between devices, local(): y_there = lax.ppermute(y, AXES, second)  15.1 us
    pallas_call x8, Pallas kernels, call(): pl.pallas_call(kernel, out_shape=outs, in_specs=[pl.BlockSpec(memory_spac...  12.4 us
    ppermute x1, waiting for transfers between devices, local(): y_back = lax.ppermute(y_sent, AXES, second)  11.6 us
  transfers between devices with their start and end apart: 9, of which 5 were waited for; matrix products, arithmetic and copies ran while one was open for 0% of the time, Pallas kernels for 6%

profile of v11, /device:TPU:24, one launch (start us, length us, event | category | flops | bytes accessed | tf_op | source)
XLA Modules:
  0.0 195.3 jit_solution(2702558078158715108)
XLA Ops:
  0.6 1.2 broadcast_select_fusion
  1.8 15.7 %collective-permute-start = (bf16[128,1536]{1,0:T(8,128)(2,1)S(1)}, bf16[128,1536]{1,0:T(8,128)(2,1)S(1)}, u32[]{:S(2)}, u32[]{:S(2)}) collective-permute-start(bf16[128,1536]{1,0:T(8,128)(2,1)S(1)} %get-tuple-element.25.x_ref), channel_id=1, source_target_pairs={{0,1},{1,0},{2,3},{3,2},{4,7},{5,6},{6,5},{7,4},{8,9},{9,8},{10,11... | collective-permute-start | bytes 1179656 | tf_op jit(solution)/shard_map/ppermute | solution.py:190
  17.5 15.7 %collective-permute-start.1 = (bf16[128,1536]{1,0:T(8,128)(2,1)S(1)}, bf16[128,1536]{1,0:T(8,128)(2,1)S(1)}, u32[]{:S(2)}, u32[]{:S(2)}) collective-permute-start(bf16[128,1536]{1,0:T(8,128)(2,1)S(1)} %get-tuple-element.24.y_ref), channel_id=1, source_target_pairs={{0,3},{1,2},{2,1},{3,0},{4,5},{5,4},{6,7},{7,6},{8,11},{9,10},{10,... | collective-permute-start | bytes 1179656 | tf_op jit(solution)/shard_map/ppermute | solution.py:191
  33.3 0.2 shard_map.59.own
  33.5 1.9 collective-permute-start.2
  35.5 4.5 %collective-permute-start.3 = (bf16[256,1536]{1,0:T(8,128)(2,1)S(1)}, bf16[256,1536]{1,0:T(8,128)(2,1)S(1)}, u32[]{:S(2)}, u32[]{:S(2)}) collective-permute-start(bf16[256,1536]{1,0:T(8,128)(2,1)S(1)} %shard_map.59.own), channel_id=1, source_target_pairs={{0,1023},{1,1020},{2,1021},{3,1022},{4,8},{5,9},{6,10},{7,11},{8,4... | collective-permute-start | bytes 2359304 | tf_op jit(solution)/shard_map/ppermute | solution.py:193
  40.0 44.0 %collective-permute-done.x_ref = bf16[128,1536]{1,0:T(8,128)(2,1)S(1)} collective-permute-done((bf16[128,1536]{1,0:T(8,128)(2,1)S(1)}, bf16[128,1536]{1,0:T(8,128)(2,1)S(1)}, u32[]{:S(2)}, u32[]{:S(2)}) %collective-permute-start) | collective-permute-done | bytes 393248 | tf_op jit(solution)/shard_map/ppermute | solution.py:190
  84.0 15.1 %collective-permute-done.1.y_ref = bf16[128,1536]{1,0:T(8,128)(2,1)S(1)} collective-permute-done((bf16[128,1536]{1,0:T(8,128)(2,1)S(1)}, bf16[128,1536]{1,0:T(8,128)(2,1)S(1)}, u32[]{:S(2)}, u32[]{:S(2)}) %collective-permute-start.1) | collective-permute-done | bytes 393248 | tf_op jit(solution)/shard_map/ppermute | solution.py:191
  99.1 1.3 shard_map.60
  100.5 1.9 collective-permute-start.5
  102.4 2.6 %collective-permute-start.6 = (bf16[128,1536]{1,0:T(8,128)(2,1)}, bf16[128,1536]{1,0:T(8,128)(2,1)}, u32[]{:S(2)}, u32[]{:S(2)}) collective-permute-start(bf16[128,1536]{1,0:T(8,128)(2,1)} %get-tuple-element.18), channel_id=1, source_target_pairs={{0,1023},{1,1020},{2,1021},{3,1022},{4,8},{5,9},{6,10},{7,11},{8,4... | collective-permute-start | bytes 1179656 | tf_op jit(solution)/shard_map/ppermute | solution.py:198
  105.0 7.2 %collective-permute-start.4 = (bf16[128,1536]{1,0:T(8,128)(2,1)}, bf16[128,1536]{1,0:T(8,128)(2,1)S(1)}, u32[]{:S(2)}, u32[]{:S(2)}) collective-permute-start(bf16[128,1536]{1,0:T(8,128)(2,1)} %get-tuple-element.15), channel_id=1, source_target_pairs={{0,1023},{1,1020},{2,1021},{3,1022},{4,8},{5,9},{6,10},{7,11},{8,4... | collective-permute-start | bytes 1179656 | tf_op jit(solution)/shard_map/ppermute | solution.py:200
  113.5 0.0 collective-permute-done.2.mate
  113.5 0.0 collective-permute-done.3.cross
  113.5 3.3 %shard_map.61 = (f32[256,1536]{1,0:T(8,128)S(1)}, bf16[256,256]{1,0:T(8,128)(2,1)S(1)}, bf16[256,1536]{1,0:T(8,128)(2,1)S(1)}, bf16[256,1536]{1,0:T(8,128)(2,1)S(1)}) custom-call(f32[1]{0:T(128)} %bitcast.4.scale_ref, f32[1]{0:T(128)} %bitcast.8.bias_ref, bf16[256,1536]{1,0:T(8,128)(2,1)S(1)} %shard_map.59.own, bf16[256,1536]{1,0:T(8,128)(2,1)} %get-tuple-element.13.far, ...), custom_call_target="tpu_custom_call" | custom-call | flops 805306368 | bytes 3145728 | tf_op jit(solution)/shard_map/pallas_call | solution.py:162
  116.8 0.0 collective-permute-done.6.cross
  116.8 0.0 collective-permute-done.5.mate
  116.8 2.6 %shard_map.62 = (f32[128,1536]{1,0:T(8,128)S(1)}, bf16[128,1536]{1,0:T(8,128)(2,1)S(1)}) custom-call(f32[1]{0:T(128)} %bitcast.5.scale_ref, f32[1]{0:T(128)} %bitcast.9.bias_ref, bf16[256,1536]{1,0:T(8,128)(2,1)S(1)} %get-tuple-element.16.side.x, bf16[128,1536]{1,0:T(8,128)(2,1)} %collective-permute-done.6.cross, ...), custom_call_target="tpu_custom_call" | custom-call | flops 402653184 | bytes 3538944 | tf_op jit(solution)/shard_map/pallas_call | solution.py:162
  119.4 4.0 %collective-permute-start.8 = (bf16[128,1536]{1,0:T(8,128)(2,1)S(1)}, bf16[128,1536]{1,0:T(8,128)(2,1)S(1)}, u32[]{:S(2)}, u32[]{:S(2)}) collective-permute-start(bf16[128,1536]{1,0:T(8,128)(2,1)S(1)} %get-tuple-element.20.after), channel_id=1, source_target_pairs={{0,1},{1,0},{2,3},{3,2},{4,7},{5,6},{6,5},{7,4},{8,9},{9,8},{10,11... | collective-permute-start | bytes 1179656 | tf_op jit(solution)/shard_map/ppermute | solution.py:234
  123.4 1.8 shard_map.63.acc
  125.2 33.6 %collective-permute-done.4.cross = bf16[128,1536]{1,0:T(8,128)(2,1)S(1)} collective-permute-done((bf16[128,1536]{1,0:T(8,128)(2,1)}, bf16[128,1536]{1,0:T(8,128)(2,1)S(1)}, u32[]{:S(2)}, u32[]{:S(2)}) %collective-permute-start.4) | collective-permute-done | bytes 393248 | tf_op jit(solution)/shard_map/ppermute | solution.py:200
  158.7 0.0 copy-start
  158.7 0.0 copy-start.1
  158.7 1.6 shard_map.64
  160.3 1.9 collective-permute-start.7
  162.2 19.8 %collective-permute-done.8.there = bf16[128,1536]{1,0:T(8,128)(2,1)S(1)} collective-permute-done((bf16[128,1536]{1,0:T(8,128)(2,1)S(1)}, bf16[128,1536]{1,0:T(8,128)(2,1)S(1)}, u32[]{:S(2)}, u32[]{:S(2)}) %collective-permute-start.8) | collective-permute-done | bytes 393248 | tf_op jit(solution)/shard_map/ppermute | solution.py:234
  182.1 0.0 copy-done
  182.1 0.0 copy-done.1
  182.1 0.3 shard_map.65.x_grad
  182.4 11.6 %collective-permute-done.7.there = bf16[128,1536]{1,0:T(8,128)(2,1)S(1)} collective-permute-done((bf16[128,1536]{1,0:T(8,128)(2,1)S(1)}, bf16[128,1536]{1,0:T(8,128)(2,1)S(1)}, u32[]{:S(2)}, u32[]{:S(2)}) %collective-permute-start.7) | collective-permute-done | bytes 393248 | tf_op jit(solution)/shard_map/ppermute | solution.py:235
  194.0 1.3 shard_map.66
Async XLA Ops:
  1.8 82.2 %collective-permute-start = (bf16[128,1536]{1,0:T(8,128)(2,1)S(1)}, bf16[128,1536]{1,0:T(8,128)(2,1)S(1)}, u32[]{:S(2)}, u32[]{:S(2)}) collective-permute-start(bf16[128,1536]{1,0:T(8,128)(2,1)S(1)} %get-tuple-element.25.x_ref), channel_id=1, source_target_pairs={{0,1},{1,0},{2,3},{3,2},{4,7},{5,6},{6,5},{7,4},{8,9},{9,8},{10,11... | collective-permute-start | bytes 1179656 | tf_op jit(solution)/shard_map/ppermute | solution.py:190
  17.5 81.6 %collective-permute-start.1 = (bf16[128,1536]{1,0:T(8,128)(2,1)S(1)}, bf16[128,1536]{1,0:T(8,128)(2,1)S(1)}, u32[]{:S(2)}, u32[]{:S(2)}) collective-permute-start(bf16[128,1536]{1,0:T(8,128)(2,1)S(1)} %get-tuple-element.24.y_ref), channel_id=1, source_target_pairs={{0,3},{1,2},{2,1},{3,0},{4,5},{5,4},{6,7},{7,6},{8,11},{9,10},{10,... | collective-permute-start | bytes 1179656 | tf_op jit(solution)/shard_map/ppermute | solution.py:191
  33.5 79.9 %collective-permute-start.2 = (bf16[256,1536]{1,0:T(8,128)(2,1)S(1)}, bf16[256,1536]{1,0:T(8,128)(2,1)S(1)}, u32[]{:S(2)}, u32[]{:S(2)}) collective-permute-start(bf16[256,1536]{1,0:T(8,128)(2,1)S(1)} %shard_map.59.own), channel_id=1, source_target_pairs={{0,4},{1,5},{2,6},{3,7},{4,0},{5,1},{6,2},{7,3},{8,12},{9,13},{10,... | collective-permute-start | bytes 2359304 | tf_op jit(solution)/shard_map/ppermute | solution.py:194
  35.5 78.0 %collective-permute-start.3 = (bf16[256,1536]{1,0:T(8,128)(2,1)S(1)}, bf16[256,1536]{1,0:T(8,128)(2,1)S(1)}, u32[]{:S(2)}, u32[]{:S(2)}) collective-permute-start(bf16[256,1536]{1,0:T(8,128)(2,1)S(1)} %shard_map.59.own), channel_id=1, source_target_pairs={{0,1023},{1,1020},{2,1021},{3,1022},{4,8},{5,9},{6,10},{7,11},{8,4... | collective-permute-start | bytes 2359304 | tf_op jit(solution)/shard_map/ppermute | solution.py:193
  100.5 16.3 %collective-permute-start.5 = (bf16[256,1536]{1,0:T(8,128)(2,1)}, bf16[256,1536]{1,0:T(8,128)(2,1)S(1)}, u32[]{:S(2)}, u32[]{:S(2)}) collective-permute-start(bf16[256,1536]{1,0:T(8,128)(2,1)} %get-tuple-element.13.far), channel_id=1, source_target_pairs={{0,4},{1,5},{2,6},{3,7},{4,0},{5,1},{6,2},{7,3},{8,12},{9,13},{10,... | collective-permute-start | bytes 2359304 | tf_op jit(solution)/shard_map/ppermute | solution.py:199
  102.4 14.4 %collective-permute-start.6 = (bf16[128,1536]{1,0:T(8,128)(2,1)}, bf16[128,1536]{1,0:T(8,128)(2,1)}, u32[]{:S(2)}, u32[]{:S(2)}) collective-permute-start(bf16[128,1536]{1,0:T(8,128)(2,1)} %get-tuple-element.18), channel_id=1, source_target_pairs={{0,1023},{1,1020},{2,1021},{3,1022},{4,8},{5,9},{6,10},{7,11},{8,4... | collective-permute-start | bytes 1179656 | tf_op jit(solution)/shard_map/ppermute | solution.py:198
  105.0 53.7 %collective-permute-start.4 = (bf16[128,1536]{1,0:T(8,128)(2,1)}, bf16[128,1536]{1,0:T(8,128)(2,1)S(1)}, u32[]{:S(2)}, u32[]{:S(2)}) collective-permute-start(bf16[128,1536]{1,0:T(8,128)(2,1)} %get-tuple-element.15), channel_id=1, source_target_pairs={{0,1023},{1,1020},{2,1021},{3,1022},{4,8},{5,9},{6,10},{7,11},{8,4... | collective-permute-start | bytes 1179656 | tf_op jit(solution)/shard_map/ppermute | solution.py:200
  119.4 62.7 %collective-permute-start.8 = (bf16[128,1536]{1,0:T(8,128)(2,1)S(1)}, bf16[128,1536]{1,0:T(8,128)(2,1)S(1)}, u32[]{:S(2)}, u32[]{:S(2)}) collective-permute-start(bf16[128,1536]{1,0:T(8,128)(2,1)S(1)} %get-tuple-element.20.after), channel_id=1, source_target_pairs={{0,1},{1,0},{2,3},{3,2},{4,7},{5,6},{6,5},{7,4},{8,9},{9,8},{10,11... | collective-permute-start | bytes 1179656 | tf_op jit(solution)/shard_map/ppermute | solution.py:234
  158.7 23.3 %copy-start = (bf16[128,1536]{1,0:T(8,128)(2,1)S(1)}, bf16[128,1536]{1,0:T(8,128)(2,1)}, u32[]{:S(2)}) copy-start(bf16[128,1536]{1,0:T(8,128)(2,1)} %img_raw.3) | copy-start | bytes 1179652
  158.7 23.3 %copy-start.1 = (bf16[128,1536]{1,0:T(8,128)(2,1)S(1)}, bf16[128,1536]{1,0:T(8,128)(2,1)}, u32[]{:S(2)}) copy-start(bf16[128,1536]{1,0:T(8,128)(2,1)} %txt_raw.3) | copy-start | bytes 1179652
  160.3 33.7 %collective-permute-start.7 = (bf16[128,1536]{1,0:T(8,128)(2,1)S(1)}, bf16[128,1536]{1,0:T(8,128)(2,1)S(1)}, u32[]{:S(2)}, u32[]{:S(2)}) collective-permute-start(bf16[128,1536]{1,0:T(8,128)(2,1)S(1)} %get-tuple-element.22), channel_id=1, source_target_pairs={{0,3},{1,2},{2,1},{3,0},{4,5},{5,4},{6,7},{7,6},{8,11},{9,10},{10,... | collective-permute-start | bytes 1179656 | tf_op jit(solution)/shard_map/ppermute | solution.py:235

commit v12 on v11

--- a/solution.py
+++ b/solution.py
@@ -62,11 +62,8 @@
 
 
 def each_columns(width, body, step=256):
-    def run(place, carry):
-        body(pl.ds(pl.multiple_of(place * step, step), step))
-        return carry
-
-    lax.fori_loop(0, width // step, run, 0)
+    for start in range(0, width, step):
+        body(slice(start, start + step))
 
 
 def dot(coef, rows):

time: 196 us -> 194 us (0.990)
  Pallas kernels: 12.4 us -> 9.89 us
    ppermute x1, waiting for transfers between devices: 33.6 us -> 37.8 us  [local(): y_cross = lax.ppermute(y_far, AXES, to_cross)]
    pallas_call x8, Pallas kernels: 12.4 us -> 9.89 us  [call(): pl.pallas_call(kernel, out_shape=outs, in_specs=[pl.BlockSpec(memory_spac...]
    ppermute x1, waiting for transfers between devices: 19.8 us -> 17.6 us  [local(): x_back = lax.ppermute(x_sent, AXES, first)]
  transfers between devices with their start and end apart: 9 -> 9, of which waited for: 5 -> 6; matrix products, arithmetic and copies ran while one was open for 0% -> 0% of each run, Pallas kernels for 6% -> 4%
where the time goes in v12:
time: 194 us; the launch traced here: 193 us
  waiting for transfers between devices  124 us (64%)
  starting transfers between devices  55.5 us (29%)
  Pallas kernels  9.89 us (5%)
  between operations  2.06 us (1%)
    ppermute x1, waiting for transfers between devices, local(): x_there = lax.ppermute(x, AXES, first)  44 us
    ppermute x1, waiting for transfers between devices, local(): y_cross = lax.ppermute(y_far, AXES, to_cross)  37.8 us
    ppermute x1, waiting for transfers between devices, local(): x_back = lax.ppermute(x_sent, AXES, first)  17.6 us
    ppermute x1, starting transfers between devices, local(): x_there = lax.ppermute(x, AXES, first)  15.7 us
    ppermute x1, starting transfers between devices, local(): y_there = lax.ppermute(y, AXES, second)  15.7 us
    ppermute x1, waiting for transfers between devices, local(): y_there = lax.ppermute(y, AXES, second)  15.1 us
    pallas_call x8, Pallas kernels, call(): pl.pallas_call(kernel, out_shape=outs, in_specs=[pl.BlockSpec(memory_spac...  9.89 us
    ppermute x1, waiting for transfers between devices, local(): y_back = lax.ppermute(y_sent, AXES, second)  9.64 us
  transfers between devices with their start and end apart: 9, of which 6 were waited for; matrix products, arithmetic and copies ran while one was open for 0% of the time, Pallas kernels for 4%

profile of v12, /device:TPU:24, one launch (start us, length us, event | category | flops | bytes accessed | tf_op | source)
XLA Modules:
  0.0 193.1 jit_solution(628353592368880836)
XLA Ops:
  0.6 1.2 broadcast_select_fusion
  1.8 15.7 %collective-permute-start = (bf16[128,1536]{1,0:T(8,128)(2,1)S(1)}, bf16[128,1536]{1,0:T(8,128)(2,1)S(1)}, u32[]{:S(2)}, u32[]{:S(2)}) collective-permute-start(bf16[128,1536]{1,0:T(8,128)(2,1)S(1)} %get-tuple-element.25.x_ref), channel_id=1, source_target_pairs={{0,1},{1,0},{2,3},{3,2},{4,7},{5,6},{6,5},{7,4},{8,9},{9,8},{10,11... | collective-permute-start | bytes 1179656 | tf_op jit(solution)/shard_map/ppermute | solution.py:187
  17.5 15.7 %collective-permute-start.1 = (bf16[128,1536]{1,0:T(8,128)(2,1)S(1)}, bf16[128,1536]{1,0:T(8,128)(2,1)S(1)}, u32[]{:S(2)}, u32[]{:S(2)}) collective-permute-start(bf16[128,1536]{1,0:T(8,128)(2,1)S(1)} %get-tuple-element.24.y_ref), channel_id=1, source_target_pairs={{0,3},{1,2},{2,1},{3,0},{4,5},{5,4},{6,7},{7,6},{8,11},{9,10},{10,... | collective-permute-start | bytes 1179656 | tf_op jit(solution)/shard_map/ppermute | solution.py:188
  33.3 0.2 shard_map.59.own
  33.5 1.9 collective-permute-start.2
  35.5 4.5 %collective-permute-start.3 = (bf16[256,1536]{1,0:T(8,128)(2,1)S(1)}, bf16[256,1536]{1,0:T(8,128)(2,1)S(1)}, u32[]{:S(2)}, u32[]{:S(2)}) collective-permute-start(bf16[256,1536]{1,0:T(8,128)(2,1)S(1)} %shard_map.59.own), channel_id=1, source_target_pairs={{0,1023},{1,1020},{2,1021},{3,1022},{4,8},{5,9},{6,10},{7,11},{8,4... | collective-permute-start | bytes 2359304 | tf_op jit(solution)/shard_map/ppermute | solution.py:190
  40.0 44.0 %collective-permute-done.x_ref = bf16[128,1536]{1,0:T(8,128)(2,1)S(1)} collective-permute-done((bf16[128,1536]{1,0:T(8,128)(2,1)S(1)}, bf16[128,1536]{1,0:T(8,128)(2,1)S(1)}, u32[]{:S(2)}, u32[]{:S(2)}) %collective-permute-start) | collective-permute-done | bytes 393248 | tf_op jit(solution)/shard_map/ppermute | solution.py:187
  84.0 15.1 %collective-permute-done.1.y_ref = bf16[128,1536]{1,0:T(8,128)(2,1)S(1)} collective-permute-done((bf16[128,1536]{1,0:T(8,128)(2,1)S(1)}, bf16[128,1536]{1,0:T(8,128)(2,1)S(1)}, u32[]{:S(2)}, u32[]{:S(2)}) %collective-permute-start.1) | collective-permute-done | bytes 393248 | tf_op jit(solution)/shard_map/ppermute | solution.py:188
  99.1 1.3 shard_map.60
  100.5 1.9 collective-permute-start.5
  102.4 2.6 %collective-permute-start.6 = (bf16[128,1536]{1,0:T(8,128)(2,1)}, bf16[128,1536]{1,0:T(8,128)(2,1)}, u32[]{:S(2)}, u32[]{:S(2)}) collective-permute-start(bf16[128,1536]{1,0:T(8,128)(2,1)} %get-tuple-element.18), channel_id=1, source_target_pairs={{0,1023},{1,1020},{2,1021},{3,1022},{4,8},{5,9},{6,10},{7,11},{8,4... | collective-permute-start | bytes 1179656 | tf_op jit(solution)/shard_map/ppermute | solution.py:195
  105.0 7.2 %collective-permute-start.4 = (bf16[128,1536]{1,0:T(8,128)(2,1)}, bf16[128,1536]{1,0:T(8,128)(2,1)S(1)}, u32[]{:S(2)}, u32[]{:S(2)}) collective-permute-start(bf16[128,1536]{1,0:T(8,128)(2,1)} %get-tuple-element.15), channel_id=1, source_target_pairs={{0,1023},{1,1020},{2,1021},{3,1022},{4,8},{5,9},{6,10},{7,11},{8,4... | collective-permute-start | bytes 1179656 | tf_op jit(solution)/shard_map/ppermute | solution.py:197
  113.5 0.0 collective-permute-done.2.mate
  113.5 0.0 collective-permute-done.3.cross
  113.5 2.3 %shard_map.61 = (f32[256,1536]{1,0:T(8,128)S(1)}, bf16[256,256]{1,0:T(8,128)(2,1)S(1)}, bf16[256,1536]{1,0:T(8,128)(2,1)S(1)}, bf16[256,1536]{1,0:T(8,128)(2,1)S(1)}) custom-call(f32[1]{0:T(128)} %bitcast.4.scale_ref, f32[1]{0:T(128)} %bitcast.8.bias_ref, bf16[256,1536]{1,0:T(8,128)(2,1)S(1)} %shard_map.59.own, bf16[256,1536]{1,0:T(8,128)(2,1)} %get-tuple-element.13.far, ...), custom_call_target="tpu_custom_call" | custom-call | flops 805306368 | bytes 3145728 | tf_op jit(solution)/shard_map/pallas_call | solution.py:159
  115.8 0.2 collective-permute-done.6.cross
  116.0 0.0 collective-permute-done.5.mate
  116.0 2.1 %shard_map.62 = (f32[128,1536]{1,0:T(8,128)S(1)}, bf16[128,1536]{1,0:T(8,128)(2,1)S(1)}) custom-call(f32[1]{0:T(128)} %bitcast.5.scale_ref, f32[1]{0:T(128)} %bitcast.9.bias_ref, bf16[256,1536]{1,0:T(8,128)(2,1)S(1)} %get-tuple-element.16.side.x, bf16[128,1536]{1,0:T(8,128)(2,1)} %collective-permute-done.6.cross, ...), custom_call_target="tpu_custom_call" | custom-call | flops 402653184 | bytes 3538944 | tf_op jit(solution)/shard_map/pallas_call | solution.py:159
  118.1 4.0 %collective-permute-start.8 = (bf16[128,1536]{1,0:T(8,128)(2,1)S(1)}, bf16[128,1536]{1,0:T(8,128)(2,1)S(1)}, u32[]{:S(2)}, u32[]{:S(2)}) collective-permute-start(bf16[128,1536]{1,0:T(8,128)(2,1)S(1)} %get-tuple-element.20.after), channel_id=1, source_target_pairs={{0,1},{1,0},{2,3},{3,2},{4,7},{5,6},{6,5},{7,4},{8,9},{9,8},{10,11... | collective-permute-start | bytes 1179656 | tf_op jit(solution)/shard_map/ppermute | solution.py:231
  122.1 1.3 shard_map.63.acc
  123.4 37.8 %collective-permute-done.4.cross = bf16[128,1536]{1,0:T(8,128)(2,1)S(1)} collective-permute-done((bf16[128,1536]{1,0:T(8,128)(2,1)}, bf16[128,1536]{1,0:T(8,128)(2,1)S(1)}, u32[]{:S(2)}, u32[]{:S(2)}) %collective-permute-start.4) | collective-permute-done | bytes 393248 | tf_op jit(solution)/shard_map/ppermute | solution.py:197
  161.2 0.0 copy-start
  161.2 0.0 copy-start.1
  161.2 1.1 shard_map.64
  162.3 1.9 collective-permute-start.7
  164.2 17.6 %collective-permute-done.8.there = bf16[128,1536]{1,0:T(8,128)(2,1)S(1)} collective-permute-done((bf16[128,1536]{1,0:T(8,128)(2,1)S(1)}, bf16[128,1536]{1,0:T(8,128)(2,1)S(1)}, u32[]{:S(2)}, u32[]{:S(2)}) %collective-permute-start.8) | collective-permute-done | bytes 393248 | tf_op jit(solution)/shard_map/ppermute | solution.py:231
  181.8 0.0 copy-done
  181.8 0.0 copy-done.1
  181.8 0.3 shard_map.65.x_grad
  182.1 9.6 %collective-permute-done.7.there = bf16[128,1536]{1,0:T(8,128)(2,1)S(1)} collective-permute-done((bf16[128,1536]{1,0:T(8,128)(2,1)S(1)}, bf16[128,1536]{1,0:T(8,128)(2,1)S(1)}, u32[]{:S(2)}, u32[]{:S(2)}) %collective-permute-start.7) | collective-permute-done | bytes 393248 | tf_op jit(solution)/shard_map/ppermute | solution.py:232
  191.8 1.3 shard_map.66
Async XLA Ops:
  1.8 82.2 %collective-permute-start = (bf16[128,1536]{1,0:T(8,128)(2,1)S(1)}, bf16[128,1536]{1,0:T(8,128)(2,1)S(1)}, u32[]{:S(2)}, u32[]{:S(2)}) collective-permute-start(bf16[128,1536]{1,0:T(8,128)(2,1)S(1)} %get-tuple-element.25.x_ref), channel_id=1, source_target_pairs={{0,1},{1,0},{2,3},{3,2},{4,7},{5,6},{6,5},{7,4},{8,9},{9,8},{10,11... | collective-permute-start | bytes 1179656 | tf_op jit(solution)/shard_map/ppermute | solution.py:187
  17.5 81.6 %collective-permute-start.1 = (bf16[128,1536]{1,0:T(8,128)(2,1)S(1)}, bf16[128,1536]{1,0:T(8,128)(2,1)S(1)}, u32[]{:S(2)}, u32[]{:S(2)}) collective-permute-start(bf16[128,1536]{1,0:T(8,128)(2,1)S(1)} %get-tuple-element.24.y_ref), channel_id=1, source_target_pairs={{0,3},{1,2},{2,1},{3,0},{4,5},{5,4},{6,7},{7,6},{8,11},{9,10},{10,... | collective-permute-start | bytes 1179656 | tf_op jit(solution)/shard_map/ppermute | solution.py:188
  33.5 79.9 %collective-permute-start.2 = (bf16[256,1536]{1,0:T(8,128)(2,1)S(1)}, bf16[256,1536]{1,0:T(8,128)(2,1)S(1)}, u32[]{:S(2)}, u32[]{:S(2)}) collective-permute-start(bf16[256,1536]{1,0:T(8,128)(2,1)S(1)} %shard_map.59.own), channel_id=1, source_target_pairs={{0,4},{1,5},{2,6},{3,7},{4,0},{5,1},{6,2},{7,3},{8,12},{9,13},{10,... | collective-permute-start | bytes 2359304 | tf_op jit(solution)/shard_map/ppermute | solution.py:191
  35.5 78.0 %collective-permute-start.3 = (bf16[256,1536]{1,0:T(8,128)(2,1)S(1)}, bf16[256,1536]{1,0:T(8,128)(2,1)S(1)}, u32[]{:S(2)}, u32[]{:S(2)}) collective-permute-start(bf16[256,1536]{1,0:T(8,128)(2,1)S(1)} %shard_map.59.own), channel_id=1, source_target_pairs={{0,1023},{1,1020},{2,1021},{3,1022},{4,8},{5,9},{6,10},{7,11},{8,4... | collective-permute-start | bytes 2359304 | tf_op jit(solution)/shard_map/ppermute | solution.py:190
  100.5 15.6 %collective-permute-start.5 = (bf16[256,1536]{1,0:T(8,128)(2,1)}, bf16[256,1536]{1,0:T(8,128)(2,1)S(1)}, u32[]{:S(2)}, u32[]{:S(2)}) collective-permute-start(bf16[256,1536]{1,0:T(8,128)(2,1)} %get-tuple-element.13.far), channel_id=1, source_target_pairs={{0,4},{1,5},{2,6},{3,7},{4,0},{5,1},{6,2},{7,3},{8,12},{9,13},{10,... | collective-permute-start | bytes 2359304 | tf_op jit(solution)/shard_map/ppermute | solution.py:196
  102.4 13.6 %collective-permute-start.6 = (bf16[128,1536]{1,0:T(8,128)(2,1)}, bf16[128,1536]{1,0:T(8,128)(2,1)}, u32[]{:S(2)}, u32[]{:S(2)}) collective-permute-start(bf16[128,1536]{1,0:T(8,128)(2,1)} %get-tuple-element.18), channel_id=1, source_target_pairs={{0,1023},{1,1020},{2,1021},{3,1022},{4,8},{5,9},{6,10},{7,11},{8,4... | collective-permute-start | bytes 1179656 | tf_op jit(solution)/shard_map/ppermute | solution.py:195
  105.0 56.2 %collective-permute-start.4 = (bf16[128,1536]{1,0:T(8,128)(2,1)}, bf16[128,1536]{1,0:T(8,128)(2,1)S(1)}, u32[]{:S(2)}, u32[]{:S(2)}) collective-permute-start(bf16[128,1536]{1,0:T(8,128)(2,1)} %get-tuple-element.15), channel_id=1, source_target_pairs={{0,1023},{1,1020},{2,1021},{3,1022},{4,8},{5,9},{6,10},{7,11},{8,4... | collective-permute-start | bytes 1179656 | tf_op jit(solution)/shard_map/ppermute | solution.py:197
  118.1 63.7 %collective-permute-start.8 = (bf16[128,1536]{1,0:T(8,128)(2,1)S(1)}, bf16[128,1536]{1,0:T(8,128)(2,1)S(1)}, u32[]{:S(2)}, u32[]{:S(2)}) collective-permute-start(bf16[128,1536]{1,0:T(8,128)(2,1)S(1)} %get-tuple-element.20.after), channel_id=1, source_target_pairs={{0,1},{1,0},{2,3},{3,2},{4,7},{5,6},{6,5},{7,4},{8,9},{9,8},{10,11... | collective-permute-start | bytes 1179656 | tf_op jit(solution)/shard_map/ppermute | solution.py:231
  161.2 20.6 %copy-start = (bf16[128,1536]{1,0:T(8,128)(2,1)S(1)}, bf16[128,1536]{1,0:T(8,128)(2,1)}, u32[]{:S(2)}) copy-start(bf16[128,1536]{1,0:T(8,128)(2,1)} %img_raw.3) | copy-start | bytes 1179652
  161.2 20.6 %copy-start.1 = (bf16[128,1536]{1,0:T(8,128)(2,1)S(1)}, bf16[128,1536]{1,0:T(8,128)(2,1)}, u32[]{:S(2)}) copy-start(bf16[128,1536]{1,0:T(8,128)(2,1)} %txt_raw.3) | copy-start | bytes 1179652
  162.3 29.5 %collective-permute-start.7 = (bf16[128,1536]{1,0:T(8,128)(2,1)S(1)}, bf16[128,1536]{1,0:T(8,128)(2,1)S(1)}, u32[]{:S(2)}, u32[]{:S(2)}) collective-permute-start(bf16[128,1536]{1,0:T(8,128)(2,1)S(1)} %get-tuple-element.22), channel_id=1, source_target_pairs={{0,3},{1,2},{2,1},{3,0},{4,5},{5,4},{6,7},{7,6},{8,11},{9,10},{10,... | collective-permute-start | bytes 1179656 | tf_op jit(solution)/shard_map/ppermute | solution.py:232

commit v13 on v12

--- a/solution.py
+++ b/solution.py
@@ -1,5 +1,3 @@
-import functools
-
 import jax
 import jax.numpy as jnp
 from jax import lax
@@ -46,11 +44,11 @@
             low_ref[part * rows + start : part * rows + start + STRIP, :] = strip
 
 
-def split_low_kernel(x_ref, y_ref, low_ref, x_low, y_low):
-    rows = x_ref.shape[0]
-    low_kernel(x_ref, y_ref, low_ref)
-    x_low[...] = low_ref[:rows, :]
-    y_low[...] = low_ref[rows:, :]
+def one_low_kernel(raw_ref, low_ref):
+    for start in range(0, raw_ref.shape[0], STRIP):
+        here = slice(start, start + STRIP)
+        values = raw_ref[here, :].astype(jnp.float32)
+        low_ref[here, :] = (values * inverse_of(values)).astype(jnp.bfloat16)
 
 
 def scores_of(left, right):
@@ -81,11 +79,13 @@
     return ref[part * rows : (part + 1) * rows, :]
 
 
-def near_x_kernel(scale_ref, bias_ref, own, far, mate, cross, acc, coef_t, x, y, near):
+def near_x_kernel(
+    scale_ref, bias_ref, own, x_far, y_far, mate, cross, acc, coef_t, x, y, near
+):
     rows = own.shape[0] // 2
     scale, bias = scale_ref[0], bias_ref[0]
-    stack(x, half(own, 0), half(far, 0))
-    stack(y, half(own, 1), half(far, 1))
+    stack(x, half(own, 0), x_far[...])
+    stack(y, half(own, 1), y_far[...])
     stack(near, half(mate, 0), half(cross, 0))
     shape = (2 * rows, 2 * rows)
     first = lax.broadcasted_iota(jnp.int32, shape, 0)
@@ -114,9 +114,9 @@
     each_columns(x.shape[1], body)
 
 
-def far_kernel(part, scale_ref, bias_ref, side, cross, mate, acc, kept, sent, near):
+def far_kernel(scale_ref, bias_ref, side, cross, mate, acc, kept, sent, near):
     rows = kept.shape[0]
-    stack(near, half(mate, part), cross[...])
+    stack(near, mate[...], cross[...])
     coef = negative_coef(side[...], near[...], scale_ref[0], bias_ref[0])
 
     def body(cols):
@@ -189,25 +189,25 @@
     own = call(low_kernel, low_shape, (), (x, y))
     cross_own = lax.ppermute(own, AXES, to_cross)
     mate_own = lax.ppermute(own, AXES, to_mate)
-    far, x_far, y_far = call(
-        split_low_kernel, (low_shape, sent_shape, sent_shape), (), (x_there, y_there)
-    )
+    x_far = call(one_low_kernel, sent_shape, (), (x_there,))
     x_cross = lax.ppermute(x_far, AXES, to_cross)
-    mate_far = lax.ppermute(far, AXES, to_mate)
+    x_mate = lax.ppermute(x_far, AXES, to_mate)
+    y_far = call(one_low_kernel, sent_shape, (), (y_there,))
     y_cross = lax.ppermute(y_far, AXES, to_cross)
+    y_mate = lax.ppermute(y_far, AXES, to_mate)
     x_acc, coef_t, x_half, y_half = call(
         near_x_kernel,
         (acc_shape, coef_shape, low_shape, low_shape),
         scalars,
-        (own, far, mate_own, cross_own),
+        (own, x_far, y_far, mate_own, cross_own),
         [pair],
         4 * unit,
     )
     x_kept, x_sent = call(
-        functools.partial(far_kernel, 0),
+        far_kernel,
         (own_shape, sent_shape),
         scalars,
-        (x_half, x_cross, mate_far, x_acc),
+        (x_half, x_cross, x_mate, x_acc),
         [pair],
         2 * unit,
     )
@@ -221,10 +221,10 @@
         (x_sent,),
     )
     y_kept, y_sent = call(
-        functools.partial(far_kernel, 1),
+        far_kernel,
         (own_shape, sent_shape),
         scalars,
-        (y_half, y_cross, mate_far, y_acc),
+        (y_half, y_cross, y_mate, y_acc),
         [pair],
         2 * unit,
     )

time: 194 us -> 203 us (1.046); the launches traced: 193 us -> 199 us
  starting transfers between devices: 55.5 us -> 66.5 us
  waiting for transfers between devices: 124 us -> 120 us
    ppermute x1, starting transfers between devices: 4.49 us -> 21.2 us  [local(): cross_own = lax.ppermute(own, AXES, to_cross)]
    ppermute x1, starting transfers between devices: 2.62 us -> 18.5 us  [local(): x_cross = lax.ppermute(x_far, AXES, to_cross)]
    ppermute x1, waiting for transfers between devices: 15.1 us -> 0.01 us  [local(): y_there = lax.ppermute(y, AXES, second)]
    ppermute x1, starting transfers between devices: 15.7 us -> 1.92 us  [local(): x_there = lax.ppermute(x, AXES, first)]
    ppermute x1, waiting for transfers between devices: 9.64 us -> 19 us  [local(): y_back = lax.ppermute(y_sent, AXES, second)]
    ppermute x1, waiting for transfers between devices: 17.6 us -> 8.37 us  [local(): x_back = lax.ppermute(x_sent, AXES, first)]
    ppermute x1, waiting for transfers between devices: 44 us -> 53.2 us  [local(): x_there = lax.ppermute(x, AXES, first)]
    ppermute x1, starting transfers between devices: 7.16 us -> 1.92 us  [local(): y_cross = lax.ppermute(y_far, AXES, to_cross)]
  transfers between devices with their start and end apart: 9 -> 10, of which waited for: 6 -> 4; matrix products, arithmetic and copies ran while one was open for 0% -> 0% of each run, Pallas kernels for 4% -> 4%
where the time goes in v13:
time: 203 us; the launch traced here: 199 us
  waiting for transfers between devices  120 us (59%)
  starting transfers between devices  66.5 us (33%)
  Pallas kernels  8.95 us (4%)
  between operations  2.1 us (1%)
    ppermute x1, waiting for transfers between devices, local(): x_there = lax.ppermute(x, AXES, first)  53.2 us
    ppermute x1, waiting for transfers between devices, local(): y_cross = lax.ppermute(y_far, AXES, to_cross)  39.9 us
    ppermute x1, starting transfers between devices, local(): cross_own = lax.ppermute(own, AXES, to_cross)  21.2 us
    ppermute x1, waiting for transfers between devices, local(): y_back = lax.ppermute(y_sent, AXES, second)  19 us
    ppermute x1, starting transfers between devices, local(): x_cross = lax.ppermute(x_far, AXES, to_cross)  18.5 us
    ppermute x1, starting transfers between devices, local(): y_there = lax.ppermute(y, AXES, second)  12.9 us
    pallas_call x9, Pallas kernels, call(): pl.pallas_call(kernel, out_shape=outs, in_specs=[pl.BlockSpec(memory_spac...  8.95 us
    ppermute x1, waiting for transfers between devices, local(): x_back = lax.ppermute(x_sent, AXES, first)  8.37 us
  transfers between devices with their start and end apart: 10, of which 4 were waited for; matrix products, arithmetic and copies ran while one was open for 0% of the time, Pallas kernels for 4%

profile of v13, /device:TPU:24, one launch (start us, length us, event | category | flops | bytes accessed | tf_op | source)
XLA Modules:
  0.0 199.2 jit_solution(1350348455677538678)
XLA Ops:
  0.6 1.2 broadcast_select_fusion
  1.8 0.2 shard_map.59.own
  2.1 1.9 collective-permute-start.2
  4.0 21.2 %collective-permute-start.3 = (bf16[256,1536]{1,0:T(8,128)(2,1)S(1)}, bf16[256,1536]{1,0:T(8,128)(2,1)S(1)}, u32[]{:S(2)}, u32[]{:S(2)}) collective-permute-start(bf16[256,1536]{1,0:T(8,128)(2,1)S(1)} %shard_map.59.own), channel_id=1, source_target_pairs={{0,1023},{1,1020},{2,1021},{3,1022},{4,8},{5,9},{6,10},{7,11},{8,4... | collective-permute-start | bytes 2359304 | tf_op jit(solution)/shard_map/ppermute | solution.py:190
  25.2 1.9 collective-permute-start
  27.1 12.9 %collective-permute-start.1 = (bf16[128,1536]{1,0:T(8,128)(2,1)S(1)}, bf16[128,1536]{1,0:T(8,128)(2,1)S(1)}, u32[]{:S(2)}, u32[]{:S(2)}) collective-permute-start(bf16[128,1536]{1,0:T(8,128)(2,1)S(1)} %get-tuple-element.18.y_ref), channel_id=1, source_target_pairs={{0,3},{1,2},{2,1},{3,0},{4,5},{5,4},{6,7},{7,6},{8,11},{9,10},{10,... | collective-permute-start | bytes 1179656 | tf_op jit(solution)/shard_map/ppermute | solution.py:188
  40.0 53.2 %collective-permute-done.raw_ref = bf16[128,1536]{1,0:T(8,128)(2,1)S(1)} collective-permute-done((bf16[128,1536]{1,0:T(8,128)(2,1)S(1)}, bf16[128,1536]{1,0:T(8,128)(2,1)S(1)}, u32[]{:S(2)}, u32[]{:S(2)}) %collective-permute-start) | collective-permute-done | bytes 393248 | tf_op jit(solution)/shard_map/ppermute | solution.py:187
  93.1 0.2 shard_map.60.x_far
  93.3 18.5 %collective-permute-start.6 = (bf16[128,1536]{1,0:T(8,128)(2,1)S(1)}, bf16[128,1536]{1,0:T(8,128)(2,1)}, u32[]{:S(2)}, u32[]{:S(2)}) collective-permute-start(bf16[128,1536]{1,0:T(8,128)(2,1)S(1)} %shard_map.60.x_far), channel_id=1, source_target_pairs={{0,1023},{1,1020},{2,1021},{3,1022},{4,8},{5,9},{6,10},{7,11},{8,4... | collective-permute-start | bytes 1179656 | tf_op jit(solution)/shard_map/ppermute | solution.py:193
  111.9 1.9 collective-permute-start.7
  113.8 0.0 collective-permute-done.1.raw_ref
  113.8 0.2 shard_map.61.y_far
  114.0 1.9 collective-permute-start.4
  115.9 0.0 collective-permute-done.2.mate
  115.9 2.4 %collective-permute-start.5 = (bf16[128,1536]{1,0:T(8,128)(2,1)S(1)}, bf16[128,1536]{1,0:T(8,128)(2,1)}, u32[]{:S(2)}, u32[]{:S(2)}) collective-permute-start(bf16[128,1536]{1,0:T(8,128)(2,1)S(1)} %shard_map.61.y_far), channel_id=1, source_target_pairs={{0,4},{1,5},{2,6},{3,7},{4,0},{5,1},{6,2},{7,3},{8,12},{9,13},{10,... | collective-permute-start | bytes 1179656 | tf_op jit(solution)/shard_map/ppermute | solution.py:197
  119.6 0.0 collective-permute-done.3.cross
  119.6 1.1 shard_map.62
  120.8 0.0 collective-permute-done.6.cross
  120.8 0.0 collective-permute-done.7.mate
  120.8 2.2 %shard_map.63 = (f32[128,1536]{1,0:T(8,128)S(1)}, bf16[128,1536]{1,0:T(8,128)(2,1)S(1)}) custom-call(f32[1]{0:T(128)} %bitcast.5.scale_ref, f32[1]{0:T(128)} %bitcast.9.bias_ref, bf16[256,1536]{1,0:T(8,128)(2,1)S(1)} %get-tuple-element.11.side.x, bf16[128,1536]{1,0:T(8,128)(2,1)} %collective-permute-done.6.cross, ...), custom_call_target="tpu_custom_call" | custom-call | flops 402653184 | bytes 3145728 | tf_op jit(solution)/shard_map/pallas_call | solution.py:159
  123.0 1.9 collective-permute-start.9
  124.9 1.3 shard_map.64.acc
  126.2 39.9 %collective-permute-done.4.cross = bf16[128,1536]{1,0:T(8,128)(2,1)S(1)} collective-permute-done((bf16[128,1536]{1,0:T(8,128)(2,1)S(1)}, bf16[128,1536]{1,0:T(8,128)(2,1)S(1)}, u32[]{:S(2)}, u32[]{:S(2)}) %collective-permute-start.4) | collective-permute-done | bytes 393248 | tf_op jit(solution)/shard_map/ppermute | solution.py:196
  166.1 0.0 collective-permute-done.5.mate
  166.1 0.0 copy-start
  166.1 0.0 copy-start.1
  166.1 2.1 %shard_map.65 = (f32[128,1536]{1,0:T(8,128)S(1)}, bf16[128,1536]{1,0:T(8,128)(2,1)S(1)}) custom-call(f32[1]{0:T(128)} %bitcast.7.scale_ref, f32[1]{0:T(128)} %bitcast.11.bias_ref, bf16[256,1536]{1,0:T(8,128)(2,1)S(1)} %get-tuple-element.10.y.side, bf16[128,1536]{1,0:T(8,128)(2,1)S(1)} %collective-permute-done.4.cross, ...), custom_call_target="tpu_custom_call" | custom-call | flops 402653184 | bytes 3145728 | tf_op jit(solution)/shard_map/pallas_call | solution.py:159
  168.2 1.9 collective-permute-start.8
  170.2 8.4 %collective-permute-done.9.there = bf16[128,1536]{1,0:T(8,128)(2,1)S(1)} collective-permute-done((bf16[128,1536]{1,0:T(8,128)(2,1)S(1)}, bf16[128,1536]{1,0:T(8,128)(2,1)S(1)}, u32[]{:S(2)}, u32[]{:S(2)}) %collective-permute-start.9) | collective-permute-done | bytes 393248 | tf_op jit(solution)/shard_map/ppermute | solution.py:231
  178.5 0.0 copy-done
  178.5 0.0 copy-done.1
  178.5 0.3 shard_map.66.x_grad
  178.9 19.0 %collective-permute-done.8.there = bf16[128,1536]{1,0:T(8,128)(2,1)S(1)} collective-permute-done((bf16[128,1536]{1,0:T(8,128)(2,1)S(1)}, bf16[128,1536]{1,0:T(8,128)(2,1)S(1)}, u32[]{:S(2)}, u32[]{:S(2)}) %collective-permute-start.8) | collective-permute-done | bytes 393248 | tf_op jit(solution)/shard_map/ppermute | solution.py:232
  197.9 1.3 shard_map.67
Async XLA Ops:
  2.1 113.8 %collective-permute-start.2 = (bf16[256,1536]{1,0:T(8,128)(2,1)S(1)}, bf16[256,1536]{1,0:T(8,128)(2,1)S(1)}, u32[]{:S(2)}, u32[]{:S(2)}) collective-permute-start(bf16[256,1536]{1,0:T(8,128)(2,1)S(1)} %shard_map.59.own), channel_id=1, source_target_pairs={{0,4},{1,5},{2,6},{3,7},{4,0},{5,1},{6,2},{7,3},{8,12},{9,13},{10,... | collective-permute-start | bytes 2359304 | tf_op jit(solution)/shard_map/ppermute | solution.py:191
  4.0 115.6 %collective-permute-start.3 = (bf16[256,1536]{1,0:T(8,128)(2,1)S(1)}, bf16[256,1536]{1,0:T(8,128)(2,1)S(1)}, u32[]{:S(2)}, u32[]{:S(2)}) collective-permute-start(bf16[256,1536]{1,0:T(8,128)(2,1)S(1)} %shard_map.59.own), channel_id=1, source_target_pairs={{0,1023},{1,1020},{2,1021},{3,1022},{4,8},{5,9},{6,10},{7,11},{8,4... | collective-permute-start | bytes 2359304 | tf_op jit(solution)/shard_map/ppermute | solution.py:190
  25.2 68.0 %collective-permute-start = (bf16[128,1536]{1,0:T(8,128)(2,1)S(1)}, bf16[128,1536]{1,0:T(8,128)(2,1)S(1)}, u32[]{:S(2)}, u32[]{:S(2)}) collective-permute-start(bf16[128,1536]{1,0:T(8,128)(2,1)S(1)} %get-tuple-element.19.x_ref), channel_id=1, source_target_pairs={{0,1},{1,0},{2,3},{3,2},{4,7},{5,6},{6,5},{7,4},{8,9},{9,8},{10,11... | collective-permute-start | bytes 1179656 | tf_op jit(solution)/shard_map/ppermute | solution.py:187
  27.1 86.7 %collective-permute-start.1 = (bf16[128,1536]{1,0:T(8,128)(2,1)S(1)}, bf16[128,1536]{1,0:T(8,128)(2,1)S(1)}, u32[]{:S(2)}, u32[]{:S(2)}) collective-permute-start(bf16[128,1536]{1,0:T(8,128)(2,1)S(1)} %get-tuple-element.18.y_ref), channel_id=1, source_target_pairs={{0,3},{1,2},{2,1},{3,0},{4,5},{5,4},{6,7},{7,6},{8,11},{9,10},{10,... | collective-permute-start | bytes 1179656 | tf_op jit(solution)/shard_map/ppermute | solution.py:188
  93.3 27.5 %collective-permute-start.6 = (bf16[128,1536]{1,0:T(8,128)(2,1)S(1)}, bf16[128,1536]{1,0:T(8,128)(2,1)}, u32[]{:S(2)}, u32[]{:S(2)}) collective-permute-start(bf16[128,1536]{1,0:T(8,128)(2,1)S(1)} %shard_map.60.x_far), channel_id=1, source_target_pairs={{0,1023},{1,1020},{2,1021},{3,1022},{4,8},{5,9},{6,10},{7,11},{8,4... | collective-permute-start | bytes 1179656 | tf_op jit(solution)/shard_map/ppermute | solution.py:193
  111.9 8.9 %collective-permute-start.7 = (bf16[128,1536]{1,0:T(8,128)(2,1)S(1)}, bf16[128,1536]{1,0:T(8,128)(2,1)}, u32[]{:S(2)}, u32[]{:S(2)}) collective-permute-start(bf16[128,1536]{1,0:T(8,128)(2,1)S(1)} %shard_map.60.x_far), channel_id=1, source_target_pairs={{0,4},{1,5},{2,6},{3,7},{4,0},{5,1},{6,2},{7,3},{8,12},{9,13},{10,... | collective-permute-start | bytes 1179656 | tf_op jit(solution)/shard_map/ppermute | solution.py:194
  114.0 52.1 %collective-permute-start.4 = (bf16[128,1536]{1,0:T(8,128)(2,1)S(1)}, bf16[128,1536]{1,0:T(8,128)(2,1)S(1)}, u32[]{:S(2)}, u32[]{:S(2)}) collective-permute-start(bf16[128,1536]{1,0:T(8,128)(2,1)S(1)} %shard_map.61.y_far), channel_id=1, source_target_pairs={{0,1023},{1,1020},{2,1021},{3,1022},{4,8},{5,9},{6,10},{7,11},{8,4... | collective-permute-start | bytes 1179656 | tf_op jit(solution)/shard_map/ppermute | solution.py:196
  115.9 50.2 %collective-permute-start.5 = (bf16[128,1536]{1,0:T(8,128)(2,1)S(1)}, bf16[128,1536]{1,0:T(8,128)(2,1)}, u32[]{:S(2)}, u32[]{:S(2)}) collective-permute-start(bf16[128,1536]{1,0:T(8,128)(2,1)S(1)} %shard_map.61.y_far), channel_id=1, source_target_pairs={{0,4},{1,5},{2,6},{3,7},{4,0},{5,1},{6,2},{7,3},{8,12},{9,13},{10,... | collective-permute-start | bytes 1179656 | tf_op jit(solution)/shard_map/ppermute | solution.py:197
  123.0 55.5 %collective-permute-start.9 = (bf16[128,1536]{1,0:T(8,128)(2,1)S(1)}, bf16[128,1536]{1,0:T(8,128)(2,1)S(1)}, u32[]{:S(2)}, u32[]{:S(2)}) collective-permute-start(bf16[128,1536]{1,0:T(8,128)(2,1)S(1)} %get-tuple-element.14.after), channel_id=1, source_target_pairs={{0,1},{1,0},{2,3},{3,2},{4,7},{5,6},{6,5},{7,4},{8,9},{9,8},{10,11... | collective-permute-start | bytes 1179656 | tf_op jit(solution)/shard_map/ppermute | solution.py:231
  166.1 12.4 %copy-start = (bf16[128,1536]{1,0:T(8,128)(2,1)S(1)}, bf16[128,1536]{1,0:T(8,128)(2,1)}, u32[]{:S(2)}) copy-start(bf16[128,1536]{1,0:T(8,128)(2,1)} %img_raw.3) | copy-start | bytes 1179652
  166.1 12.4 %copy-start.1 = (bf16[128,1536]{1,0:T(8,128)(2,1)S(1)}, bf16[128,1536]{1,0:T(8,128)(2,1)}, u32[]{:S(2)}) copy-start(bf16[128,1536]{1,0:T(8,128)(2,1)} %txt_raw.3) | copy-start | bytes 1179652
  168.2 29.7 %collective-permute-start.8 = (bf16[128,1536]{1,0:T(8,128)(2,1)S(1)}, bf16[128,1536]{1,0:T(8,128)(2,1)S(1)}, u32[]{:S(2)}, u32[]{:S(2)}) collective-permute-start(bf16[128,1536]{1,0:T(8,128)(2,1)S(1)} %get-tuple-element.16), channel_id=1, source_target_pairs={{0,3},{1,2},{2,1},{3,0},{4,5},{5,4},{6,7},{7,6},{8,11},{9,10},{10,... | collective-permute-start | bytes 1179656 | tf_op jit(solution)/shard_map/ppermute | solution.py:232

commit v14 on v12

--- a/solution.py
+++ b/solution.py
@@ -10,7 +10,7 @@
 AXES = ("dp", "fsdp")
 SPAN = 16
 STRIP = 32
-VMEM_LIMIT = 16 * 1024 * 1024
+VMEM_LIMIT = 10 * 1024 * 1024
 
 
 def device_of(block, role, blocks, ways):
@@ -44,13 +44,6 @@
             values = ref[start : start + STRIP, :].astype(jnp.float32)
             strip = (values * inverse_of(values)).astype(jnp.bfloat16)
             low_ref[part * rows + start : part * rows + start + STRIP, :] = strip
-
-
-def split_low_kernel(x_ref, y_ref, low_ref, x_low, y_low):
-    rows = x_ref.shape[0]
-    low_kernel(x_ref, y_ref, low_ref)
-    x_low[...] = low_ref[:rows, :]
-    y_low[...] = low_ref[rows:, :]
 
 
 def scores_of(left, right):
@@ -189,9 +182,8 @@
     own = call(low_kernel, low_shape, (), (x, y))
     cross_own = lax.ppermute(own, AXES, to_cross)
     mate_own = lax.ppermute(own, AXES, to_mate)
-    far, x_far, y_far = call(
-        split_low_kernel, (low_shape, sent_shape, sent_shape), (), (x_there, y_there)
-    )
+    far = call(low_kernel, low_shape, (), (x_there, y_there))
+    x_far, y_far = far[:rows], far[rows:]
     x_cross = lax.ppermute(x_far, AXES, to_cross)
     mate_far = lax.ppermute(far, AXES, to_mate)
     y_cross = lax.ppermute(y_far, AXES, to_cross)

time: 194 us -> 194 us (level)
  no operation moved by 1% of the time
where the time goes in v14:
time: 194 us; the launch traced here: 193 us
  waiting for transfers between devices  124 us (64%)
  starting transfers between devices  55.5 us (29%)
  Pallas kernels  9.13 us (5%)
  between operations  2.06 us (1%)
    ppermute x1, waiting for transfers between devices, local(): x_there = lax.ppermute(x, AXES, first)  44 us
    ppermute x1, waiting for transfers between devices, local(): y_cross = lax.ppermute(y_far, AXES, to_cross)  37.7 us
    ppermute x1, waiting for transfers between devices, local(): x_back = lax.ppermute(x_sent, AXES, first)  16.5 us
    ppermute x1, starting transfers between devices, local(): x_there = lax.ppermute(x, AXES, first)  15.7 us
    ppermute x1, starting transfers between devices, local(): y_there = lax.ppermute(y, AXES, second)  15.7 us
    ppermute x1, waiting for transfers between devices, local(): y_there = lax.ppermute(y, AXES, second)  15.1 us
    ppermute x1, waiting for transfers between devices, local(): y_back = lax.ppermute(y_sent, AXES, second)  9.72 us
    pallas_call x8, Pallas kernels, call(): pl.pallas_call(kernel, out_shape=outs, in_specs=[pl.BlockSpec(memory_spac...  9.13 us
  transfers between devices with their start and end apart: 9, of which 6 were waited for; matrix products, arithmetic and copies ran while one was open for 0% of the time, Pallas kernels for 4%

profile of v14, /device:TPU:24, one launch (start us, length us, event | category | flops | bytes accessed | tf_op | source)
XLA Modules:
  0.0 193.2 jit_solution(1984255083976325276)
XLA Ops:
  0.6 1.2 broadcast_select_fusion
  1.8 15.7 %collective-permute-start = (bf16[128,1536]{1,0:T(8,128)(2,1)S(1)}, bf16[128,1536]{1,0:T(8,128)(2,1)S(1)}, u32[]{:S(2)}, u32[]{:S(2)}) collective-permute-start(bf16[128,1536]{1,0:T(8,128)(2,1)S(1)} %get-tuple-element.21.x_ref), channel_id=1, source_target_pairs={{0,1},{1,0},{2,3},{3,2},{4,7},{5,6},{6,5},{7,4},{8,9},{9,8},{10,11... | collective-permute-start | bytes 1179656 | tf_op jit(solution)/shard_map/ppermute | solution.py:180
  17.5 15.7 %collective-permute-start.1 = (bf16[128,1536]{1,0:T(8,128)(2,1)S(1)}, bf16[128,1536]{1,0:T(8,128)(2,1)S(1)}, u32[]{:S(2)}, u32[]{:S(2)}) collective-permute-start(bf16[128,1536]{1,0:T(8,128)(2,1)S(1)} %get-tuple-element.20.y_ref), channel_id=1, source_target_pairs={{0,3},{1,2},{2,1},{3,0},{4,5},{5,4},{6,7},{7,6},{8,11},{9,10},{10,... | collective-permute-start | bytes 1179656 | tf_op jit(solution)/shard_map/ppermute | solution.py:181
  33.3 0.2 shard_map.59.own
  33.5 1.9 collective-permute-start.2
  35.5 4.5 %collective-permute-start.3 = (bf16[256,1536]{1,0:T(8,128)(2,1)S(1)}, bf16[256,1536]{1,0:T(8,128)(2,1)S(1)}, u32[]{:S(2)}, u32[]{:S(2)}) collective-permute-start(bf16[256,1536]{1,0:T(8,128)(2,1)S(1)} %shard_map.59.own), channel_id=1, source_target_pairs={{0,1023},{1,1020},{2,1021},{3,1022},{4,8},{5,9},{6,10},{7,11},{8,4... | collective-permute-start | bytes 2359304 | tf_op jit(solution)/shard_map/ppermute | solution.py:183
  40.0 44.0 %collective-permute-done.x_ref = bf16[128,1536]{1,0:T(8,128)(2,1)S(1)} collective-permute-done((bf16[128,1536]{1,0:T(8,128)(2,1)S(1)}, bf16[128,1536]{1,0:T(8,128)(2,1)S(1)}, u32[]{:S(2)}, u32[]{:S(2)}) %collective-permute-start) | collective-permute-done | bytes 393248 | tf_op jit(solution)/shard_map/ppermute | solution.py:180
  84.0 15.1 %collective-permute-done.1.y_ref = bf16[128,1536]{1,0:T(8,128)(2,1)S(1)} collective-permute-done((bf16[128,1536]{1,0:T(8,128)(2,1)S(1)}, bf16[128,1536]{1,0:T(8,128)(2,1)S(1)}, u32[]{:S(2)}, u32[]{:S(2)}) %collective-permute-start.1) | collective-permute-done | bytes 393248 | tf_op jit(solution)/shard_map/ppermute | solution.py:181
  99.1 0.2 shard_map.60.far
  99.4 1.9 collective-permute-start.5
  101.3 0.9 fusion
  102.2 2.6 %collective-permute-start.6 = (bf16[128,1536]{1,0:T(8,128)(2,1)}, bf16[128,1536]{1,0:T(8,128)(2,1)}, u32[]{:S(2)}, u32[]{:S(2)}) collective-permute-start(bf16[128,1536]{1,0:T(8,128)(2,1)} %get-tuple-element.18), channel_id=1, source_target_pairs={{0,1023},{1,1020},{2,1021},{3,1022},{4,8},{5,9},{6,10},{7,11},{8,4... | collective-permute-start | bytes 1179656 | tf_op jit(solution)/shard_map/ppermute | solution.py:187
  104.8 7.2 %collective-permute-start.4 = (bf16[128,1536]{1,0:T(8,128)(2,1)}, bf16[128,1536]{1,0:T(8,128)(2,1)S(1)}, u32[]{:S(2)}, u32[]{:S(2)}) collective-permute-start(bf16[128,1536]{1,0:T(8,128)(2,1)} %get-tuple-element.19), channel_id=1, source_target_pairs={{0,1023},{1,1020},{2,1021},{3,1022},{4,8},{5,9},{6,10},{7,11},{8,4... | collective-permute-start | bytes 1179656 | tf_op jit(solution)/shard_map/ppermute | solution.py:189
  113.3 0.0 collective-permute-done.2.mate
  113.3 0.0 collective-permute-done.3.cross
  113.3 1.1 shard_map.61
  114.5 1.4 collective-permute-done.6.cross
  115.8 0.0 collective-permute-done.5.mate
  115.8 2.3 %shard_map.62 = (f32[128,1536]{1,0:T(8,128)S(1)}, bf16[128,1536]{1,0:T(8,128)(2,1)S(1)}) custom-call(f32[1]{0:T(128)} %bitcast.5.scale_ref, f32[1]{0:T(128)} %bitcast.9.bias_ref, bf16[256,1536]{1,0:T(8,128)(2,1)S(1)} %get-tuple-element.11.side.x, bf16[128,1536]{1,0:T(8,128)(2,1)} %collective-permute-done.6.cross, ...), custom_call_target="tpu_custom_call" | custom-call | flops 402653184 | bytes 3538944 | tf_op jit(solution)/shard_map/pallas_call | solution.py:152
  118.2 4.0 %collective-permute-start.8 = (bf16[128,1536]{1,0:T(8,128)(2,1)S(1)}, bf16[128,1536]{1,0:T(8,128)(2,1)S(1)}, u32[]{:S(2)}, u32[]{:S(2)}) collective-permute-start(bf16[128,1536]{1,0:T(8,128)(2,1)S(1)} %get-tuple-element.14.after), channel_id=1, source_target_pairs={{0,1},{1,0},{2,3},{3,2},{4,7},{5,6},{6,5},{7,4},{8,9},{9,8},{10,11... | collective-permute-start | bytes 1179656 | tf_op jit(solution)/shard_map/ppermute | solution.py:223
  122.2 1.3 shard_map.63.acc
  123.5 37.7 %collective-permute-done.4.cross = bf16[128,1536]{1,0:T(8,128)(2,1)S(1)} collective-permute-done((bf16[128,1536]{1,0:T(8,128)(2,1)}, bf16[128,1536]{1,0:T(8,128)(2,1)S(1)}, u32[]{:S(2)}, u32[]{:S(2)}) %collective-permute-start.4) | collective-permute-done | bytes 393248 | tf_op jit(solution)/shard_map/ppermute | solution.py:189
  161.1 0.0 copy-start
  161.1 0.0 copy-start.1
  161.1 2.3 %shard_map.64 = (f32[128,1536]{1,0:T(8,128)S(1)}, bf16[128,1536]{1,0:T(8,128)(2,1)S(1)}) custom-call(f32[1]{0:T(128)} %bitcast.7.scale_ref, f32[1]{0:T(128)} %bitcast.11.bias_ref, bf16[256,1536]{1,0:T(8,128)(2,1)S(1)} %get-tuple-element.10.y.side, bf16[128,1536]{1,0:T(8,128)(2,1)S(1)} %collective-permute-done.4.cross, ...), custom_call_target="tpu_custom_call" | custom-call | flops 402653184 | bytes 3538944 | tf_op jit(solution)/shard_map/pallas_call | solution.py:152
  163.4 1.9 collective-permute-start.7
  165.3 16.5 %collective-permute-done.8.there = bf16[128,1536]{1,0:T(8,128)(2,1)S(1)} collective-permute-done((bf16[128,1536]{1,0:T(8,128)(2,1)S(1)}, bf16[128,1536]{1,0:T(8,128)(2,1)S(1)}, u32[]{:S(2)}, u32[]{:S(2)}) %collective-permute-start.8) | collective-permute-done | bytes 393248 | tf_op jit(solution)/shard_map/ppermute | solution.py:223
  181.8 0.0 copy-done
  181.8 0.0 copy-done.1
  181.8 0.3 shard_map.65.x_grad
  182.2 9.7 %collective-permute-done.7.there = bf16[128,1536]{1,0:T(8,128)(2,1)S(1)} collective-permute-done((bf16[128,1536]{1,0:T(8,128)(2,1)S(1)}, bf16[128,1536]{1,0:T(8,128)(2,1)S(1)}, u32[]{:S(2)}, u32[]{:S(2)}) %collective-permute-start.7) | collective-permute-done | bytes 393248 | tf_op jit(solution)/shard_map/ppermute | solution.py:224
  191.9 1.3 shard_map.66
Async XLA Ops:
  1.8 82.2 %collective-permute-start = (bf16[128,1536]{1,0:T(8,128)(2,1)S(1)}, bf16[128,1536]{1,0:T(8,128)(2,1)S(1)}, u32[]{:S(2)}, u32[]{:S(2)}) collective-permute-start(bf16[128,1536]{1,0:T(8,128)(2,1)S(1)} %get-tuple-element.21.x_ref), channel_id=1, source_target_pairs={{0,1},{1,0},{2,3},{3,2},{4,7},{5,6},{6,5},{7,4},{8,9},{9,8},{10,11... | collective-permute-start | bytes 1179656 | tf_op jit(solution)/shard_map/ppermute | solution.py:180
  17.5 81.6 %collective-permute-start.1 = (bf16[128,1536]{1,0:T(8,128)(2,1)S(1)}, bf16[128,1536]{1,0:T(8,128)(2,1)S(1)}, u32[]{:S(2)}, u32[]{:S(2)}) collective-permute-start(bf16[128,1536]{1,0:T(8,128)(2,1)S(1)} %get-tuple-element.20.y_ref), channel_id=1, source_target_pairs={{0,3},{1,2},{2,1},{3,0},{4,5},{5,4},{6,7},{7,6},{8,11},{9,10},{10,... | collective-permute-start | bytes 1179656 | tf_op jit(solution)/shard_map/ppermute | solution.py:181
  33.5 79.8 %collective-permute-start.2 = (bf16[256,1536]{1,0:T(8,128)(2,1)S(1)}, bf16[256,1536]{1,0:T(8,128)(2,1)S(1)}, u32[]{:S(2)}, u32[]{:S(2)}) collective-permute-start(bf16[256,1536]{1,0:T(8,128)(2,1)S(1)} %shard_map.59.own), channel_id=1, source_target_pairs={{0,4},{1,5},{2,6},{3,7},{4,0},{5,1},{6,2},{7,3},{8,12},{9,13},{10,... | collective-permute-start | bytes 2359304 | tf_op jit(solution)/shard_map/ppermute | solution.py:184
  35.5 77.9 %collective-permute-start.3 = (bf16[256,1536]{1,0:T(8,128)(2,1)S(1)}, bf16[256,1536]{1,0:T(8,128)(2,1)S(1)}, u32[]{:S(2)}, u32[]{:S(2)}) collective-permute-start(bf16[256,1536]{1,0:T(8,128)(2,1)S(1)} %shard_map.59.own), channel_id=1, source_target_pairs={{0,1023},{1,1020},{2,1021},{3,1022},{4,8},{5,9},{6,10},{7,11},{8,4... | collective-permute-start | bytes 2359304 | tf_op jit(solution)/shard_map/ppermute | solution.py:183
  99.4 16.5 %collective-permute-start.5 = (bf16[256,1536]{1,0:T(8,128)(2,1)S(1)}, bf16[256,1536]{1,0:T(8,128)(2,1)}, u32[]{:S(2)}, u32[]{:S(2)}) collective-permute-start(bf16[256,1536]{1,0:T(8,128)(2,1)S(1)} %shard_map.60.far), channel_id=1, source_target_pairs={{0,4},{1,5},{2,6},{3,7},{4,0},{5,1},{6,2},{7,3},{8,12},{9,13},{10,... | collective-permute-start | bytes 2359304 | tf_op jit(solution)/shard_map/ppermute | solution.py:188
  102.2 13.6 %collective-permute-start.6 = (bf16[128,1536]{1,0:T(8,128)(2,1)}, bf16[128,1536]{1,0:T(8,128)(2,1)}, u32[]{:S(2)}, u32[]{:S(2)}) collective-permute-start(bf16[128,1536]{1,0:T(8,128)(2,1)} %get-tuple-element.18), channel_id=1, source_target_pairs={{0,1023},{1,1020},{2,1021},{3,1022},{4,8},{5,9},{6,10},{7,11},{8,4... | collective-permute-start | bytes 1179656 | tf_op jit(solution)/shard_map/ppermute | solution.py:187
  104.8 56.3 %collective-permute-start.4 = (bf16[128,1536]{1,0:T(8,128)(2,1)}, bf16[128,1536]{1,0:T(8,128)(2,1)S(1)}, u32[]{:S(2)}, u32[]{:S(2)}) collective-permute-start(bf16[128,1536]{1,0:T(8,128)(2,1)} %get-tuple-element.19), channel_id=1, source_target_pairs={{0,1023},{1,1020},{2,1021},{3,1022},{4,8},{5,9},{6,10},{7,11},{8,4... | collective-permute-start | bytes 1179656 | tf_op jit(solution)/shard_map/ppermute | solution.py:189
  118.2 63.7 %collective-permute-start.8 = (bf16[128,1536]{1,0:T(8,128)(2,1)S(1)}, bf16[128,1536]{1,0:T(8,128)(2,1)S(1)}, u32[]{:S(2)}, u32[]{:S(2)}) collective-permute-start(bf16[128,1536]{1,0:T(8,128)(2,1)S(1)} %get-tuple-element.14.after), channel_id=1, source_target_pairs={{0,1},{1,0},{2,3},{3,2},{4,7},{5,6},{6,5},{7,4},{8,9},{9,8},{10,11... | collective-permute-start | bytes 1179656 | tf_op jit(solution)/shard_map/ppermute | solution.py:223
  161.1 20.7 %copy-start = (bf16[128,1536]{1,0:T(8,128)(2,1)S(1)}, bf16[128,1536]{1,0:T(8,128)(2,1)}, u32[]{:S(2)}) copy-start(bf16[128,1536]{1,0:T(8,128)(2,1)} %img_raw.3) | copy-start | bytes 1179652
  161.1 20.7 %copy-start.1 = (bf16[128,1536]{1,0:T(8,128)(2,1)S(1)}, bf16[128,1536]{1,0:T(8,128)(2,1)}, u32[]{:S(2)}) copy-start(bf16[128,1536]{1,0:T(8,128)(2,1)} %txt_raw.3) | copy-start | bytes 1179652
  163.4 28.5 %collective-permute-start.7 = (bf16[128,1536]{1,0:T(8,128)(2,1)S(1)}, bf16[128,1536]{1,0:T(8,128)(2,1)S(1)}, u32[]{:S(2)}, u32[]{:S(2)}) collective-permute-start(bf16[128,1536]{1,0:T(8,128)(2,1)S(1)} %get-tuple-element.16), channel_id=1, source_target_pairs={{0,3},{1,2},{2,1},{3,0},{4,5},{5,4},{6,7},{7,6},{8,11},{9,10},{10,... | collective-permute-start | bytes 1179656 | tf_op jit(solution)/shard_map/ppermute | solution.py:224

commit v15 on v14

--- a/solution.py
+++ b/solution.py
@@ -107,9 +107,16 @@
     each_columns(x.shape[1], body)
 
 
-def far_kernel(part, scale_ref, bias_ref, side, cross, mate, acc, kept, sent, near):
+def far_kernel(part, scale_ref, bias_ref, side, acc, cross, mate, kept, sent, near, sems):
     rows = kept.shape[0]
-    stack(near, half(mate, part), cross[...])
+    copies = [
+        pltpu.make_async_copy(mate.at[pl.ds(part * rows, rows), :], near.at[pl.ds(0, rows), :], sems.at[0]),
+        pltpu.make_async_copy(cross, near.at[pl.ds(rows, rows), :], sems.at[1]),
+    ]
+    for copy in copies:
+        copy.start()
+    for copy in copies:
+        copy.wait()
     coef = negative_coef(side[...], near[...], scale_ref[0], bias_ref[0])
 
     def body(cols):
@@ -172,7 +179,7 @@
     own_shape = jax.ShapeDtypeStruct((rows, width), jnp.float32)
     sent_shape = jax.ShapeDtypeStruct((rows, width), jnp.bfloat16)
     coef_shape = jax.ShapeDtypeStruct((2 * rows, 2 * rows), jnp.bfloat16)
-    pair = pltpu.VMEM((2 * rows, width), jnp.bfloat16)
+    pair, sems = pltpu.VMEM((2 * rows, width), jnp.bfloat16), pltpu.SemaphoreType.DMA((2,))
     unit = 2 * (2 * rows) * (2 * rows) * width
 
     x = jnp.where(odd > 0, txt_raw, img_raw)
@@ -199,9 +206,10 @@
         functools.partial(far_kernel, 0),
         (own_shape, sent_shape),
         scalars,
-        (x_half, x_cross, mate_far, x_acc),
-        [pair],
+        (x_half, x_acc),
+        [pair, sems],
         2 * unit,
+        (x_cross, mate_far),
     )
     y_acc = call(
         near_y_kernel,
@@ -216,9 +224,10 @@
         functools.partial(far_kernel, 1),
         (own_shape, sent_shape),
         scalars,
-        (y_half, y_cross, mate_far, y_acc),
-        [pair],
+        (y_half, y_acc),
+        [pair, sems],
         2 * unit,
+        (y_cross, mate_far),
     )
     x_back = lax.ppermute(x_sent, AXES, first)
     y_back = lax.ppermute(y_sent, AXES, second)

time: 194 us -> 194 us (level)
  no operation moved by 1% of the time
where the time goes in v15:
time: 194 us; the launch traced here: 193 us
  waiting for transfers between devices  125 us (64%)
  starting transfers between devices  55.5 us (29%)
  Pallas kernels  8.89 us (5%)
  between operations  2.07 us (1%)
    ppermute x1, waiting for transfers between devices, local(): x_there = lax.ppermute(x, AXES, first)  44 us
    ppermute x1, waiting for transfers between devices, local(): y_cross = lax.ppermute(y_far, AXES, to_cross)  37.9 us
    ppermute x1, waiting for transfers between devices, local(): x_back = lax.ppermute(x_sent, AXES, first)  16.6 us
    ppermute x1, starting transfers between devices, local(): x_there = lax.ppermute(x, AXES, first)  15.7 us
    ppermute x1, starting transfers between devices, local(): y_there = lax.ppermute(y, AXES, second)  15.7 us
    ppermute x1, waiting for transfers between devices, local(): y_there = lax.ppermute(y, AXES, second)  15.1 us
    ppermute x1, waiting for transfers between devices, local(): y_back = lax.ppermute(y_sent, AXES, second)  9.51 us
    pallas_call x8, Pallas kernels, call(): pl.pallas_call(kernel, out_shape=outs, in_specs=[pl.BlockSpec(memory_spac...  8.89 us
  transfers between devices with their start and end apart: 9, of which 6 were waited for; matrix products, arithmetic and copies ran while one was open for 0% of the time, Pallas kernels for 4%

profile of v15, /device:TPU:24, one launch (start us, length us, event | category | flops | bytes accessed | tf_op | source)
XLA Modules:
  0.0 193.1 jit_solution(8768697352312184274)
XLA Ops:
  0.6 1.2 broadcast_select_fusion
  1.8 15.7 %collective-permute-start = (bf16[128,1536]{1,0:T(8,128)(2,1)S(1)}, bf16[128,1536]{1,0:T(8,128)(2,1)S(1)}, u32[]{:S(2)}, u32[]{:S(2)}) collective-permute-start(bf16[128,1536]{1,0:T(8,128)(2,1)S(1)} %get-tuple-element.21.x_ref), channel_id=1, source_target_pairs={{0,1},{1,0},{2,3},{3,2},{4,7},{5,6},{6,5},{7,4},{8,9},{9,8},{10,11... | collective-permute-start | bytes 1179656 | tf_op jit(solution)/shard_map/ppermute | solution.py:187
  17.5 15.7 %collective-permute-start.1 = (bf16[128,1536]{1,0:T(8,128)(2,1)S(1)}, bf16[128,1536]{1,0:T(8,128)(2,1)S(1)}, u32[]{:S(2)}, u32[]{:S(2)}) collective-permute-start(bf16[128,1536]{1,0:T(8,128)(2,1)S(1)} %get-tuple-element.20.y_ref), channel_id=1, source_target_pairs={{0,3},{1,2},{2,1},{3,0},{4,5},{5,4},{6,7},{7,6},{8,11},{9,10},{10,... | collective-permute-start | bytes 1179656 | tf_op jit(solution)/shard_map/ppermute | solution.py:188
  33.3 0.2 shard_map.59.own
  33.5 1.9 collective-permute-start.2
  35.5 4.5 %collective-permute-start.3 = (bf16[256,1536]{1,0:T(8,128)(2,1)S(1)}, bf16[256,1536]{1,0:T(8,128)(2,1)S(1)}, u32[]{:S(2)}, u32[]{:S(2)}) collective-permute-start(bf16[256,1536]{1,0:T(8,128)(2,1)S(1)} %shard_map.59.own), channel_id=1, source_target_pairs={{0,1023},{1,1020},{2,1021},{3,1022},{4,8},{5,9},{6,10},{7,11},{8,4... | collective-permute-start | bytes 2359304 | tf_op jit(solution)/shard_map/ppermute | solution.py:190
  40.0 44.0 %collective-permute-done.x_ref = bf16[128,1536]{1,0:T(8,128)(2,1)S(1)} collective-permute-done((bf16[128,1536]{1,0:T(8,128)(2,1)S(1)}, bf16[128,1536]{1,0:T(8,128)(2,1)S(1)}, u32[]{:S(2)}, u32[]{:S(2)}) %collective-permute-start) | collective-permute-done | bytes 393248 | tf_op jit(solution)/shard_map/ppermute | solution.py:187
  84.0 15.1 %collective-permute-done.1.y_ref = bf16[128,1536]{1,0:T(8,128)(2,1)S(1)} collective-permute-done((bf16[128,1536]{1,0:T(8,128)(2,1)S(1)}, bf16[128,1536]{1,0:T(8,128)(2,1)S(1)}, u32[]{:S(2)}, u32[]{:S(2)}) %collective-permute-start.1) | collective-permute-done | bytes 393248 | tf_op jit(solution)/shard_map/ppermute | solution.py:188
  99.1 0.2 shard_map.60.far
  99.4 1.9 collective-permute-start.5
  101.3 0.9 fusion
  102.2 2.6 %collective-permute-start.4 = (bf16[128,1536]{1,0:T(8,128)(2,1)}, bf16[128,1536]{1,0:T(8,128)(2,1)}, u32[]{:S(2)}, u32[]{:S(2)}) collective-permute-start(bf16[128,1536]{1,0:T(8,128)(2,1)} %get-tuple-element.19), channel_id=1, source_target_pairs={{0,1023},{1,1020},{2,1021},{3,1022},{4,8},{5,9},{6,10},{7,11},{8,4... | collective-permute-start | bytes 1179656 | tf_op jit(solution)/shard_map/ppermute | solution.py:194
  104.8 7.2 %collective-permute-start.6 = (bf16[128,1536]{1,0:T(8,128)(2,1)}, bf16[128,1536]{1,0:T(8,128)(2,1)S(1)}, u32[]{:S(2)}, u32[]{:S(2)}) collective-permute-start(bf16[128,1536]{1,0:T(8,128)(2,1)} %get-tuple-element.18), channel_id=1, source_target_pairs={{0,1023},{1,1020},{2,1021},{3,1022},{4,8},{5,9},{6,10},{7,11},{8,4... | collective-permute-start | bytes 1179656 | tf_op jit(solution)/shard_map/ppermute | solution.py:196
  113.3 0.0 collective-permute-done.2.mate
  113.3 0.0 collective-permute-done.3.cross
  113.3 1.1 shard_map.61
  114.5 1.4 collective-permute-done.4.cross
  115.8 0.0 collective-permute-done.5.mate
  115.8 2.2 %shard_map.62 = (f32[128,1536]{1,0:T(8,128)S(1)}, bf16[128,1536]{1,0:T(8,128)(2,1)S(1)}) custom-call(f32[1]{0:T(128)} %bitcast.5.scale_ref, f32[1]{0:T(128)} %bitcast.9.bias_ref, bf16[256,1536]{1,0:T(8,128)(2,1)S(1)} %get-tuple-element.11.side.x, f32[256,1536]{1,0:T(8,128)S(1)} %get-tuple-element.13.acc, bf16[128,1536]{1,0:T(8,128)(2,1)} %collective-permute-done.4.cross, ...), custom_call_target="tpu_custom_call" | custom-call | flops 402653184 | bytes 2359296 | tf_op jit(solution)/shard_map/pallas_call | solution.py:159
  118.0 4.0 %collective-permute-start.8 = (bf16[128,1536]{1,0:T(8,128)(2,1)S(1)}, bf16[128,1536]{1,0:T(8,128)(2,1)S(1)}, u32[]{:S(2)}, u32[]{:S(2)}) collective-permute-start(bf16[128,1536]{1,0:T(8,128)(2,1)S(1)} %get-tuple-element.14.after), channel_id=1, source_target_pairs={{0,1},{1,0},{2,3},{3,2},{4,7},{5,6},{6,5},{7,4},{8,9},{9,8},{10,11... | collective-permute-start | bytes 1179656 | tf_op jit(solution)/shard_map/ppermute | solution.py:232
  122.0 1.3 shard_map.63.acc
  123.4 37.9 %collective-permute-done.6.cross = bf16[128,1536]{1,0:T(8,128)(2,1)S(1)} collective-permute-done((bf16[128,1536]{1,0:T(8,128)(2,1)}, bf16[128,1536]{1,0:T(8,128)(2,1)S(1)}, u32[]{:S(2)}, u32[]{:S(2)}) %collective-permute-start.6) | collective-permute-done | bytes 393248 | tf_op jit(solution)/shard_map/ppermute | solution.py:196
  161.2 0.0 copy-start
  161.2 0.0 copy-start.1
  161.2 2.1 %shard_map.64 = (f32[128,1536]{1,0:T(8,128)S(1)}, bf16[128,1536]{1,0:T(8,128)(2,1)S(1)}) custom-call(f32[1]{0:T(128)} %bitcast.7.scale_ref, f32[1]{0:T(128)} %bitcast.11.bias_ref, bf16[256,1536]{1,0:T(8,128)(2,1)S(1)} %get-tuple-element.10.y.side, f32[256,1536]{1,0:T(8,128)S(1)} %shard_map.63.acc, bf16[128,1536]{1,0:T(8,128)(2,1)S(1)} %collective-permute-done.6.cross, ...), custom_call_target="tpu_custom_call" | custom-call | flops 402653184 | bytes 2359296 | tf_op jit(solution)/shard_map/pallas_call | solution.py:159
  163.4 1.9 collective-permute-start.7
  165.3 16.6 %collective-permute-done.8.there = bf16[128,1536]{1,0:T(8,128)(2,1)S(1)} collective-permute-done((bf16[128,1536]{1,0:T(8,128)(2,1)S(1)}, bf16[128,1536]{1,0:T(8,128)(2,1)S(1)}, u32[]{:S(2)}, u32[]{:S(2)}) %collective-permute-start.8) | collective-permute-done | bytes 393248 | tf_op jit(solution)/shard_map/ppermute | solution.py:232
  181.9 0.0 copy-done
  181.9 0.0 copy-done.1
  181.9 0.3 shard_map.65.x_grad
  182.3 9.5 %collective-permute-done.7.there = bf16[128,1536]{1,0:T(8,128)(2,1)S(1)} collective-permute-done((bf16[128,1536]{1,0:T(8,128)(2,1)S(1)}, bf16[128,1536]{1,0:T(8,128)(2,1)S(1)}, u32[]{:S(2)}, u32[]{:S(2)}) %collective-permute-start.7) | collective-permute-done | bytes 393248 | tf_op jit(solution)/shard_map/ppermute | solution.py:233
  191.8 1.3 shard_map.66
Async XLA Ops:
  1.8 82.2 %collective-permute-start = (bf16[128,1536]{1,0:T(8,128)(2,1)S(1)}, bf16[128,1536]{1,0:T(8,128)(2,1)S(1)}, u32[]{:S(2)}, u32[]{:S(2)}) collective-permute-start(bf16[128,1536]{1,0:T(8,128)(2,1)S(1)} %get-tuple-element.21.x_ref), channel_id=1, source_target_pairs={{0,1},{1,0},{2,3},{3,2},{4,7},{5,6},{6,5},{7,4},{8,9},{9,8},{10,11... | collective-permute-start | bytes 1179656 | tf_op jit(solution)/shard_map/ppermute | solution.py:187
  17.5 81.6 %collective-permute-start.1 = (bf16[128,1536]{1,0:T(8,128)(2,1)S(1)}, bf16[128,1536]{1,0:T(8,128)(2,1)S(1)}, u32[]{:S(2)}, u32[]{:S(2)}) collective-permute-start(bf16[128,1536]{1,0:T(8,128)(2,1)S(1)} %get-tuple-element.20.y_ref), channel_id=1, source_target_pairs={{0,3},{1,2},{2,1},{3,0},{4,5},{5,4},{6,7},{7,6},{8,11},{9,10},{10,... | collective-permute-start | bytes 1179656 | tf_op jit(solution)/shard_map/ppermute | solution.py:188
  33.5 79.8 %collective-permute-start.2 = (bf16[256,1536]{1,0:T(8,128)(2,1)S(1)}, bf16[256,1536]{1,0:T(8,128)(2,1)S(1)}, u32[]{:S(2)}, u32[]{:S(2)}) collective-permute-start(bf16[256,1536]{1,0:T(8,128)(2,1)S(1)} %shard_map.59.own), channel_id=1, source_target_pairs={{0,4},{1,5},{2,6},{3,7},{4,0},{5,1},{6,2},{7,3},{8,12},{9,13},{10,... | collective-permute-start | bytes 2359304 | tf_op jit(solution)/shard_map/ppermute | solution.py:191
  35.5 77.9 %collective-permute-start.3 = (bf16[256,1536]{1,0:T(8,128)(2,1)S(1)}, bf16[256,1536]{1,0:T(8,128)(2,1)S(1)}, u32[]{:S(2)}, u32[]{:S(2)}) collective-permute-start(bf16[256,1536]{1,0:T(8,128)(2,1)S(1)} %shard_map.59.own), channel_id=1, source_target_pairs={{0,1023},{1,1020},{2,1021},{3,1022},{4,8},{5,9},{6,10},{7,11},{8,4... | collective-permute-start | bytes 2359304 | tf_op jit(solution)/shard_map/ppermute | solution.py:190
  99.4 16.5 %collective-permute-start.5 = (bf16[256,1536]{1,0:T(8,128)(2,1)S(1)}, bf16[256,1536]{1,0:T(8,128)(2,1)}, u32[]{:S(2)}, u32[]{:S(2)}) collective-permute-start(bf16[256,1536]{1,0:T(8,128)(2,1)S(1)} %shard_map.60.far), channel_id=1, source_target_pairs={{0,4},{1,5},{2,6},{3,7},{4,0},{5,1},{6,2},{7,3},{8,12},{9,13},{10,... | collective-permute-start | bytes 2359304 | tf_op jit(solution)/shard_map/ppermute | solution.py:195
  102.2 13.6 %collective-permute-start.4 = (bf16[128,1536]{1,0:T(8,128)(2,1)}, bf16[128,1536]{1,0:T(8,128)(2,1)}, u32[]{:S(2)}, u32[]{:S(2)}) collective-permute-start(bf16[128,1536]{1,0:T(8,128)(2,1)} %get-tuple-element.19), channel_id=1, source_target_pairs={{0,1023},{1,1020},{2,1021},{3,1022},{4,8},{5,9},{6,10},{7,11},{8,4... | collective-permute-start | bytes 1179656 | tf_op jit(solution)/shard_map/ppermute | solution.py:194
  104.8 56.4 %collective-permute-start.6 = (bf16[128,1536]{1,0:T(8,128)(2,1)}, bf16[128,1536]{1,0:T(8,128)(2,1)S(1)}, u32[]{:S(2)}, u32[]{:S(2)}) collective-permute-start(bf16[128,1536]{1,0:T(8,128)(2,1)} %get-tuple-element.18), channel_id=1, source_target_pairs={{0,1023},{1,1020},{2,1021},{3,1022},{4,8},{5,9},{6,10},{7,11},{8,4... | collective-permute-start | bytes 1179656 | tf_op jit(solution)/shard_map/ppermute | solution.py:196
  118.0 63.9 %collective-permute-start.8 = (bf16[128,1536]{1,0:T(8,128)(2,1)S(1)}, bf16[128,1536]{1,0:T(8,128)(2,1)S(1)}, u32[]{:S(2)}, u32[]{:S(2)}) collective-permute-start(bf16[128,1536]{1,0:T(8,128)(2,1)S(1)} %get-tuple-element.14.after), channel_id=1, source_target_pairs={{0,1},{1,0},{2,3},{3,2},{4,7},{5,6},{6,5},{7,4},{8,9},{9,8},{10,11... | collective-permute-start | bytes 1179656 | tf_op jit(solution)/shard_map/ppermute | solution.py:232
  161.2 20.7 %copy-start = (bf16[128,1536]{1,0:T(8,128)(2,1)S(1)}, bf16[128,1536]{1,0:T(8,128)(2,1)}, u32[]{:S(2)}) copy-start(bf16[128,1536]{1,0:T(8,128)(2,1)} %img_raw.3) | copy-start | bytes 1179652
  161.2 20.7 %copy-start.1 = (bf16[128,1536]{1,0:T(8,128)(2,1)S(1)}, bf16[128,1536]{1,0:T(8,128)(2,1)}, u32[]{:S(2)}) copy-start(bf16[128,1536]{1,0:T(8,128)(2,1)} %txt_raw.3) | copy-start | bytes 1179652
  163.4 28.4 %collective-permute-start.7 = (bf16[128,1536]{1,0:T(8,128)(2,1)S(1)}, bf16[128,1536]{1,0:T(8,128)(2,1)S(1)}, u32[]{:S(2)}, u32[]{:S(2)}) collective-permute-start(bf16[128,1536]{1,0:T(8,128)(2,1)S(1)} %get-tuple-element.16), channel_id=1, source_target_pairs={{0,3},{1,2},{2,1},{3,0},{4,5},{5,4},{6,7},{7,6},{8,11},{9,10},{10,... | collective-permute-start | bytes 1179656 | tf_op jit(solution)/shard_map/ppermute | solution.py:233

commit v16 on v14

--- a/solution.py
+++ b/solution.py
@@ -136,15 +136,47 @@
         out[here, :] = grad_strip(raw, kept[here, :] + there[here, :].astype(jnp.float32))
 
 
-def second_grad_kernel(odd_ref, img_raw, txt_raw, kept, there, x_grad, img_grad, txt_grad):
-    odd = odd_ref[0] > 0
-    for start in range(0, img_raw.shape[0], STRIP):
-        here = slice(start, start + STRIP)
-        raw = jnp.where(odd, img_raw[here, :], txt_raw[here, :])
-        y = grad_strip(raw, kept[here, :] + there[here, :].astype(jnp.float32))
-        x = x_grad[here, :]
-        img_grad[here, :] = jnp.where(odd, y, x)
-        txt_grad[here, :] = jnp.where(odd, x, y)
+def second_grad_kernel(
+    odd_ref, img_raw, txt_raw, kept, there, x_grad, img_grad, txt_grad, y_grad, sems
+):
+    def run(raw, x_out, y_out):
+        copies = [pltpu.make_async_copy(x_grad, x_out, sems.at[0])]
+        copies[0].start()
+        for place in range(raw.shape[0] // STRIP):
+            here = slice(place * STRIP, (place + 1) * STRIP)
+            y = grad_strip(raw[here, :], kept[here, :] + there[here, :].astype(jnp.float32))
+            y_grad[here, :] = y
+            strip = pl.ds(place * STRIP, STRIP)
+            source, out = y_grad.at[strip, :], y_out.at[strip, :]
+            copies.append(pltpu.make_async_copy(source, out, sems.at[place + 1]))
+            copies[-1].start()
+        for copy in copies:
+            copy.wait()
+
+    @pl.when(odd_ref[0] == 0)
+    def _():
+        run(txt_raw, img_grad, txt_grad)
+
+    @pl.when(odd_ref[0] != 0)
+    def _():
+        run(img_raw, txt_grad, img_grad)
+
+
+def last(odd, *arrays):
+    shape = arrays[0].shape
+    out = jax.ShapeDtypeStruct(shape, jnp.bfloat16)
+    return pl.pallas_call(
+        second_grad_kernel,
+        out_shape=(out, out),
+        in_specs=[pl.BlockSpec(memory_space=pltpu.SMEM)]
+        + [pl.BlockSpec(memory_space=pltpu.VMEM)] * len(arrays),
+        out_specs=(pl.BlockSpec(memory_space=pl.ANY),) * 2,
+        scratch_shapes=[
+            pltpu.VMEM(shape, jnp.bfloat16),
+            pltpu.SemaphoreType.DMA((1 + shape[0] // STRIP,)),
+        ],
+        compiler_params=pltpu.CompilerParams(vmem_limit_bytes=VMEM_LIMIT),
+    )(odd, *arrays)
 
 
 def call(kernel, outs, scalars, arrays, scratch=(), flops=0, there=()):
@@ -223,12 +255,7 @@
     x_back = lax.ppermute(x_sent, AXES, first)
     y_back = lax.ppermute(y_sent, AXES, second)
     x_grad = call(first_grad_kernel, sent_shape, (odd,), (img_raw, txt_raw, x_kept, x_back))
-    return call(
-        second_grad_kernel,
-        (sent_shape, sent_shape),
-        (odd,),
-        (img_raw, txt_raw, y_kept, y_back, x_grad),
-    )
+    return last(odd, img_raw, txt_raw, y_kept, y_back, x_grad)
 
 
 def solution(mesh):

time: 194 us -> 193 us (level)
    pallas_call x8 -> x7, Pallas kernels: 9.13 us -> 7.85 us  [call(): pl.pallas_call(kernel, out_shape=outs, in_specs=[pl.BlockSpec(memory_spac...]
where the time goes in v16:
time: 193 us
  waiting for transfers between devices  124 us (64%)
  starting transfers between devices  55.5 us (29%)
  Pallas kernels  8.88 us (5%)
  between operations  2.06 us (1%)
    ppermute x1, waiting for transfers between devices, local(): x_there = lax.ppermute(x, AXES, first)  44 us
    ppermute x1, waiting for transfers between devices, local(): y_cross = lax.ppermute(y_far, AXES, to_cross)  37.7 us
    ppermute x1, waiting for transfers between devices, local(): x_back = lax.ppermute(x_sent, AXES, first)  16.5 us
    ppermute x1, starting transfers between devices, local(): x_there = lax.ppermute(x, AXES, first)  15.7 us
    ppermute x1, starting transfers between devices, local(): y_there = lax.ppermute(y, AXES, second)  15.7 us
    ppermute x1, waiting for transfers between devices, local(): y_there = lax.ppermute(y, AXES, second)  15.1 us
    ppermute x1, waiting for transfers between devices, local(): y_back = lax.ppermute(y_sent, AXES, second)  9.72 us
    pallas_call x7, Pallas kernels, call(): pl.pallas_call(kernel, out_shape=outs, in_specs=[pl.BlockSpec(memory_spac...  7.85 us
  transfers between devices with their start and end apart: 9, of which 6 were waited for; matrix products, arithmetic and copies ran while one was open for 0% of the time, Pallas kernels for 4%

profile of v16, /device:TPU:24, one launch (start us, length us, event | category | flops | bytes accessed | tf_op | source)
XLA Modules:
  0.0 192.9 jit_solution(13664270280634975614)
XLA Ops:
  0.6 1.2 broadcast_select_fusion
  1.8 15.7 %collective-permute-start = (bf16[128,1536]{1,0:T(8,128)(2,1)S(1)}, bf16[128,1536]{1,0:T(8,128)(2,1)S(1)}, u32[]{:S(2)}, u32[]{:S(2)}) collective-permute-start(bf16[128,1536]{1,0:T(8,128)(2,1)S(1)} %get-tuple-element.21.x_ref), channel_id=1, source_target_pairs={{0,1},{1,0},{2,3},{3,2},{4,7},{5,6},{6,5},{7,4},{8,9},{9,8},{10,11... | collective-permute-start | bytes 1179656 | tf_op jit(solution)/shard_map/ppermute | solution.py:212
  17.5 15.7 %collective-permute-start.1 = (bf16[128,1536]{1,0:T(8,128)(2,1)S(1)}, bf16[128,1536]{1,0:T(8,128)(2,1)S(1)}, u32[]{:S(2)}, u32[]{:S(2)}) collective-permute-start(bf16[128,1536]{1,0:T(8,128)(2,1)S(1)} %get-tuple-element.20.y_ref), channel_id=1, source_target_pairs={{0,3},{1,2},{2,1},{3,0},{4,5},{5,4},{6,7},{7,6},{8,11},{9,10},{10,... | collective-permute-start | bytes 1179656 | tf_op jit(solution)/shard_map/ppermute | solution.py:213
  33.3 0.2 shard_map.59.own
  33.5 1.9 collective-permute-start.2
  35.5 4.5 %collective-permute-start.3 = (bf16[256,1536]{1,0:T(8,128)(2,1)S(1)}, bf16[256,1536]{1,0:T(8,128)(2,1)S(1)}, u32[]{:S(2)}, u32[]{:S(2)}) collective-permute-start(bf16[256,1536]{1,0:T(8,128)(2,1)S(1)} %shard_map.59.own), channel_id=1, source_target_pairs={{0,1023},{1,1020},{2,1021},{3,1022},{4,8},{5,9},{6,10},{7,11},{8,4... | collective-permute-start | bytes 2359304 | tf_op jit(solution)/shard_map/ppermute | solution.py:215
  40.0 44.0 %collective-permute-done.x_ref = bf16[128,1536]{1,0:T(8,128)(2,1)S(1)} collective-permute-done((bf16[128,1536]{1,0:T(8,128)(2,1)S(1)}, bf16[128,1536]{1,0:T(8,128)(2,1)S(1)}, u32[]{:S(2)}, u32[]{:S(2)}) %collective-permute-start) | collective-permute-done | bytes 393248 | tf_op jit(solution)/shard_map/ppermute | solution.py:212
  84.0 15.1 %collective-permute-done.1.y_ref = bf16[128,1536]{1,0:T(8,128)(2,1)S(1)} collective-permute-done((bf16[128,1536]{1,0:T(8,128)(2,1)S(1)}, bf16[128,1536]{1,0:T(8,128)(2,1)S(1)}, u32[]{:S(2)}, u32[]{:S(2)}) %collective-permute-start.1) | collective-permute-done | bytes 393248 | tf_op jit(solution)/shard_map/ppermute | solution.py:213
  99.1 0.2 shard_map.60.far
  99.4 1.9 collective-permute-start.5
  101.3 0.9 fusion
  102.2 2.6 %collective-permute-start.6 = (bf16[128,1536]{1,0:T(8,128)(2,1)}, bf16[128,1536]{1,0:T(8,128)(2,1)}, u32[]{:S(2)}, u32[]{:S(2)}) collective-permute-start(bf16[128,1536]{1,0:T(8,128)(2,1)} %get-tuple-element.18), channel_id=1, source_target_pairs={{0,1023},{1,1020},{2,1021},{3,1022},{4,8},{5,9},{6,10},{7,11},{8,4... | collective-permute-start | bytes 1179656 | tf_op jit(solution)/shard_map/ppermute | solution.py:219
  104.8 7.2 %collective-permute-start.4 = (bf16[128,1536]{1,0:T(8,128)(2,1)}, bf16[128,1536]{1,0:T(8,128)(2,1)S(1)}, u32[]{:S(2)}, u32[]{:S(2)}) collective-permute-start(bf16[128,1536]{1,0:T(8,128)(2,1)} %get-tuple-element.19), channel_id=1, source_target_pairs={{0,1023},{1,1020},{2,1021},{3,1022},{4,8},{5,9},{6,10},{7,11},{8,4... | collective-permute-start | bytes 1179656 | tf_op jit(solution)/shard_map/ppermute | solution.py:221
  113.3 0.0 collective-permute-done.2.mate
  113.3 0.0 collective-permute-done.3.cross
  113.3 1.1 shard_map.61
  114.5 1.4 collective-permute-done.6.cross
  115.8 0.0 collective-permute-done.5.mate
  115.8 2.3 %shard_map.62 = (f32[128,1536]{1,0:T(8,128)S(1)}, bf16[128,1536]{1,0:T(8,128)(2,1)S(1)}) custom-call(f32[1]{0:T(128)} %bitcast.5.scale_ref, f32[1]{0:T(128)} %bitcast.9.bias_ref, bf16[256,1536]{1,0:T(8,128)(2,1)S(1)} %get-tuple-element.11.side.x, bf16[128,1536]{1,0:T(8,128)(2,1)} %collective-permute-done.6.cross, ...), custom_call_target="tpu_custom_call" | custom-call | flops 402653184 | bytes 3538944 | tf_op jit(solution)/shard_map/pallas_call | solution.py:184
  118.2 4.0 %collective-permute-start.8 = (bf16[128,1536]{1,0:T(8,128)(2,1)S(1)}, bf16[128,1536]{1,0:T(8,128)(2,1)S(1)}, u32[]{:S(2)}, u32[]{:S(2)}) collective-permute-start(bf16[128,1536]{1,0:T(8,128)(2,1)S(1)} %get-tuple-element.14.after), channel_id=1, source_target_pairs={{0,1},{1,0},{2,3},{3,2},{4,7},{5,6},{6,5},{7,4},{8,9},{9,8},{10,11... | collective-permute-start | bytes 1179656 | tf_op jit(solution)/shard_map/ppermute | solution.py:255
  122.2 1.3 shard_map.63.acc
  123.5 37.7 %collective-permute-done.4.cross = bf16[128,1536]{1,0:T(8,128)(2,1)S(1)} collective-permute-done((bf16[128,1536]{1,0:T(8,128)(2,1)}, bf16[128,1536]{1,0:T(8,128)(2,1)S(1)}, u32[]{:S(2)}, u32[]{:S(2)}) %collective-permute-start.4) | collective-permute-done | bytes 393248 | tf_op jit(solution)/shard_map/ppermute | solution.py:221
  161.1 0.0 copy-start
  161.1 0.0 copy-start.1
  161.1 2.3 %shard_map.64 = (f32[128,1536]{1,0:T(8,128)S(1)}, bf16[128,1536]{1,0:T(8,128)(2,1)S(1)}) custom-call(f32[1]{0:T(128)} %bitcast.7.scale_ref, f32[1]{0:T(128)} %bitcast.11.bias_ref, bf16[256,1536]{1,0:T(8,128)(2,1)S(1)} %get-tuple-element.10.y.side, bf16[128,1536]{1,0:T(8,128)(2,1)S(1)} %collective-permute-done.4.cross, ...), custom_call_target="tpu_custom_call" | custom-call | flops 402653184 | bytes 3538944 | tf_op jit(solution)/shard_map/pallas_call | solution.py:184
  163.4 1.9 collective-permute-start.7
  165.3 16.5 %collective-permute-done.8.there = bf16[128,1536]{1,0:T(8,128)(2,1)S(1)} collective-permute-done((bf16[128,1536]{1,0:T(8,128)(2,1)S(1)}, bf16[128,1536]{1,0:T(8,128)(2,1)S(1)}, u32[]{:S(2)}, u32[]{:S(2)}) %collective-permute-start.8) | collective-permute-done | bytes 393248 | tf_op jit(solution)/shard_map/ppermute | solution.py:255
  181.8 0.0 copy-done
  181.8 0.0 copy-done.1
  181.8 0.3 shard_map.65.x_grad
  182.2 9.7 %collective-permute-done.7.there = bf16[128,1536]{1,0:T(8,128)(2,1)S(1)} collective-permute-done((bf16[128,1536]{1,0:T(8,128)(2,1)S(1)}, bf16[128,1536]{1,0:T(8,128)(2,1)S(1)}, u32[]{:S(2)}, u32[]{:S(2)}) %collective-permute-start.7) | collective-permute-done | bytes 393248 | tf_op jit(solution)/shard_map/ppermute | solution.py:256
  191.9 1.0 shard_map.66
Async XLA Ops:
  1.8 82.2 %collective-permute-start = (bf16[128,1536]{1,0:T(8,128)(2,1)S(1)}, bf16[128,1536]{1,0:T(8,128)(2,1)S(1)}, u32[]{:S(2)}, u32[]{:S(2)}) collective-permute-start(bf16[128,1536]{1,0:T(8,128)(2,1)S(1)} %get-tuple-element.21.x_ref), channel_id=1, source_target_pairs={{0,1},{1,0},{2,3},{3,2},{4,7},{5,6},{6,5},{7,4},{8,9},{9,8},{10,11... | collective-permute-start | bytes 1179656 | tf_op jit(solution)/shard_map/ppermute | solution.py:212
  17.5 81.6 %collective-permute-start.1 = (bf16[128,1536]{1,0:T(8,128)(2,1)S(1)}, bf16[128,1536]{1,0:T(8,128)(2,1)S(1)}, u32[]{:S(2)}, u32[]{:S(2)}) collective-permute-start(bf16[128,1536]{1,0:T(8,128)(2,1)S(1)} %get-tuple-element.20.y_ref), channel_id=1, source_target_pairs={{0,3},{1,2},{2,1},{3,0},{4,5},{5,4},{6,7},{7,6},{8,11},{9,10},{10,... | collective-permute-start | bytes 1179656 | tf_op jit(solution)/shard_map/ppermute | solution.py:213
  33.5 79.8 %collective-permute-start.2 = (bf16[256,1536]{1,0:T(8,128)(2,1)S(1)}, bf16[256,1536]{1,0:T(8,128)(2,1)S(1)}, u32[]{:S(2)}, u32[]{:S(2)}) collective-permute-start(bf16[256,1536]{1,0:T(8,128)(2,1)S(1)} %shard_map.59.own), channel_id=1, source_target_pairs={{0,4},{1,5},{2,6},{3,7},{4,0},{5,1},{6,2},{7,3},{8,12},{9,13},{10,... | collective-permute-start | bytes 2359304 | tf_op jit(solution)/shard_map/ppermute | solution.py:216
  35.5 77.9 %collective-permute-start.3 = (bf16[256,1536]{1,0:T(8,128)(2,1)S(1)}, bf16[256,1536]{1,0:T(8,128)(2,1)S(1)}, u32[]{:S(2)}, u32[]{:S(2)}) collective-permute-start(bf16[256,1536]{1,0:T(8,128)(2,1)S(1)} %shard_map.59.own), channel_id=1, source_target_pairs={{0,1023},{1,1020},{2,1021},{3,1022},{4,8},{5,9},{6,10},{7,11},{8,4... | collective-permute-start | bytes 2359304 | tf_op jit(solution)/shard_map/ppermute | solution.py:215
  99.4 16.5 %collective-permute-start.5 = (bf16[256,1536]{1,0:T(8,128)(2,1)S(1)}, bf16[256,1536]{1,0:T(8,128)(2,1)}, u32[]{:S(2)}, u32[]{:S(2)}) collective-permute-start(bf16[256,1536]{1,0:T(8,128)(2,1)S(1)} %shard_map.60.far), channel_id=1, source_target_pairs={{0,4},{1,5},{2,6},{3,7},{4,0},{5,1},{6,2},{7,3},{8,12},{9,13},{10,... | collective-permute-start | bytes 2359304 | tf_op jit(solution)/shard_map/ppermute | solution.py:220
  102.2 13.6 %collective-permute-start.6 = (bf16[128,1536]{1,0:T(8,128)(2,1)}, bf16[128,1536]{1,0:T(8,128)(2,1)}, u32[]{:S(2)}, u32[]{:S(2)}) collective-permute-start(bf16[128,1536]{1,0:T(8,128)(2,1)} %get-tuple-element.18), channel_id=1, source_target_pairs={{0,1023},{1,1020},{2,1021},{3,1022},{4,8},{5,9},{6,10},{7,11},{8,4... | collective-permute-start | bytes 1179656 | tf_op jit(solution)/shard_map/ppermute | solution.py:219
  104.8 56.3 %collective-permute-start.4 = (bf16[128,1536]{1,0:T(8,128)(2,1)}, bf16[128,1536]{1,0:T(8,128)(2,1)S(1)}, u32[]{:S(2)}, u32[]{:S(2)}) collective-permute-start(bf16[128,1536]{1,0:T(8,128)(2,1)} %get-tuple-element.19), channel_id=1, source_target_pairs={{0,1023},{1,1020},{2,1021},{3,1022},{4,8},{5,9},{6,10},{7,11},{8,4... | collective-permute-start | bytes 1179656 | tf_op jit(solution)/shard_map/ppermute | solution.py:221
  118.2 63.7 %collective-permute-start.8 = (bf16[128,1536]{1,0:T(8,128)(2,1)S(1)}, bf16[128,1536]{1,0:T(8,128)(2,1)S(1)}, u32[]{:S(2)}, u32[]{:S(2)}) collective-permute-start(bf16[128,1536]{1,0:T(8,128)(2,1)S(1)} %get-tuple-element.14.after), channel_id=1, source_target_pairs={{0,1},{1,0},{2,3},{3,2},{4,7},{5,6},{6,5},{7,4},{8,9},{9,8},{10,11... | collective-permute-start | bytes 1179656 | tf_op jit(solution)/shard_map/ppermute | solution.py:255
  161.1 20.7 %copy-start = (bf16[128,1536]{1,0:T(8,128)(2,1)S(1)}, bf16[128,1536]{1,0:T(8,128)(2,1)}, u32[]{:S(2)}) copy-start(bf16[128,1536]{1,0:T(8,128)(2,1)} %img_raw.3) | copy-start | bytes 1179652
  161.1 20.7 %copy-start.1 = (bf16[128,1536]{1,0:T(8,128)(2,1)S(1)}, bf16[128,1536]{1,0:T(8,128)(2,1)}, u32[]{:S(2)}) copy-start(bf16[128,1536]{1,0:T(8,128)(2,1)} %txt_raw.3) | copy-start | bytes 1179652
  163.4 28.5 %collective-permute-start.7 = (bf16[128,1536]{1,0:T(8,128)(2,1)S(1)}, bf16[128,1536]{1,0:T(8,128)(2,1)S(1)}, u32[]{:S(2)}, u32[]{:S(2)}) collective-permute-start(bf16[128,1536]{1,0:T(8,128)(2,1)S(1)} %get-tuple-element.16), channel_id=1, source_target_pairs={{0,3},{1,2},{2,1},{3,0},{4,5},{5,4},{6,7},{7,6},{8,11},{9,10},{10,... | collective-permute-start | bytes 1179656 | tf_op jit(solution)/shard_map/ppermute | solution.py:256

commit v17 on v16

--- a/solution.py
+++ b/solution.py
@@ -107,9 +107,16 @@
     each_columns(x.shape[1], body)
 
 
-def far_kernel(part, scale_ref, bias_ref, side, cross, mate, acc, kept, sent, near):
+def far_kernel(part, scale_ref, bias_ref, side, acc, cross, mate, kept, sent, near, sems):
     rows = kept.shape[0]
-    stack(near, half(mate, part), cross[...])
+    copies = [
+        pltpu.make_async_copy(mate.at[pl.ds(part * rows, rows), :], near.at[pl.ds(0, rows), :], sems.at[0]),
+        pltpu.make_async_copy(cross, near.at[pl.ds(rows, rows), :], sems.at[1]),
+    ]
+    for copy in copies:
+        copy.start()
+    for copy in copies:
+        copy.wait()
     coef = negative_coef(side[...], near[...], scale_ref[0], bias_ref[0])
 
     def body(cols):
@@ -204,7 +211,7 @@
     own_shape = jax.ShapeDtypeStruct((rows, width), jnp.float32)
     sent_shape = jax.ShapeDtypeStruct((rows, width), jnp.bfloat16)
     coef_shape = jax.ShapeDtypeStruct((2 * rows, 2 * rows), jnp.bfloat16)
-    pair = pltpu.VMEM((2 * rows, width), jnp.bfloat16)
+    pair, sems = pltpu.VMEM((2 * rows, width), jnp.bfloat16), pltpu.SemaphoreType.DMA((2,))
     unit = 2 * (2 * rows) * (2 * rows) * width
 
     x = jnp.where(odd > 0, txt_raw, img_raw)
@@ -231,9 +238,10 @@
         functools.partial(far_kernel, 0),
         (own_shape, sent_shape),
         scalars,
-        (x_half, x_cross, mate_far, x_acc),
-        [pair],
+        (x_half, x_acc),
+        [pair, sems],
         2 * unit,
+        (x_cross, mate_far),
     )
     y_acc = call(
         near_y_kernel,
@@ -248,9 +256,10 @@
         functools.partial(far_kernel, 1),
         (own_shape, sent_shape),
         scalars,
-        (y_half, y_cross, mate_far, y_acc),
-        [pair],
+        (y_half, y_acc),
+        [pair, sems],
         2 * unit,
+        (y_cross, mate_far),
     )
     x_back = lax.ppermute(x_sent, AXES, first)
     y_back = lax.ppermute(y_sent, AXES, second)

time: 193 us -> 193 us (level)
  no operation moved by 1% of the time
where the time goes in v17:
time: 193 us
  waiting for transfers between devices  125 us (65%)
  starting transfers between devices  55.5 us (29%)
  Pallas kernels  8.65 us (4%)
  between operations  2.07 us (1%)
    ppermute x1, waiting for transfers between devices, local(): x_there = lax.ppermute(x, AXES, first)  44 us
    ppermute x1, waiting for transfers between devices, local(): y_cross = lax.ppermute(y_far, AXES, to_cross)  37.9 us
    ppermute x1, waiting for transfers between devices, local(): x_back = lax.ppermute(x_sent, AXES, first)  16.6 us
    ppermute x1, starting transfers between devices, local(): x_there = lax.ppermute(x, AXES, first)  15.7 us
    ppermute x1, starting transfers between devices, local(): y_there = lax.ppermute(y, AXES, second)  15.7 us
    ppermute x1, waiting for transfers between devices, local(): y_there = lax.ppermute(y, AXES, second)  15.1 us
    ppermute x1, waiting for transfers between devices, local(): y_back = lax.ppermute(y_sent, AXES, second)  9.51 us
    pallas_call x7, Pallas kernels, call(): pl.pallas_call(kernel, out_shape=outs, in_specs=[pl.BlockSpec(memory_spac...  7.61 us
  transfers between devices with their start and end apart: 9, of which 6 were waited for; matrix products, arithmetic and copies ran while one was open for 0% of the time, Pallas kernels for 4%

profile of v17, /device:TPU:24, one launch (start us, length us, event | category | flops | bytes accessed | tf_op | source)
XLA Modules:
  0.0 192.8 jit_solution(5300628028252986219)
XLA Ops:
  0.6 1.2 broadcast_select_fusion
  1.8 15.7 %collective-permute-start = (bf16[128,1536]{1,0:T(8,128)(2,1)S(1)}, bf16[128,1536]{1,0:T(8,128)(2,1)S(1)}, u32[]{:S(2)}, u32[]{:S(2)}) collective-permute-start(bf16[128,1536]{1,0:T(8,128)(2,1)S(1)} %get-tuple-element.21.x_ref), channel_id=1, source_target_pairs={{0,1},{1,0},{2,3},{3,2},{4,7},{5,6},{6,5},{7,4},{8,9},{9,8},{10,11... | collective-permute-start | bytes 1179656 | tf_op jit(solution)/shard_map/ppermute | solution.py:219
  17.5 15.7 %collective-permute-start.1 = (bf16[128,1536]{1,0:T(8,128)(2,1)S(1)}, bf16[128,1536]{1,0:T(8,128)(2,1)S(1)}, u32[]{:S(2)}, u32[]{:S(2)}) collective-permute-start(bf16[128,1536]{1,0:T(8,128)(2,1)S(1)} %get-tuple-element.20.y_ref), channel_id=1, source_target_pairs={{0,3},{1,2},{2,1},{3,0},{4,5},{5,4},{6,7},{7,6},{8,11},{9,10},{10,... | collective-permute-start | bytes 1179656 | tf_op jit(solution)/shard_map/ppermute | solution.py:220
  33.3 0.2 shard_map.59.own
  33.5 1.9 collective-permute-start.2
  35.5 4.5 %collective-permute-start.3 = (bf16[256,1536]{1,0:T(8,128)(2,1)S(1)}, bf16[256,1536]{1,0:T(8,128)(2,1)S(1)}, u32[]{:S(2)}, u32[]{:S(2)}) collective-permute-start(bf16[256,1536]{1,0:T(8,128)(2,1)S(1)} %shard_map.59.own), channel_id=1, source_target_pairs={{0,1023},{1,1020},{2,1021},{3,1022},{4,8},{5,9},{6,10},{7,11},{8,4... | collective-permute-start | bytes 2359304 | tf_op jit(solution)/shard_map/ppermute | solution.py:222
  40.0 44.0 %collective-permute-done.x_ref = bf16[128,1536]{1,0:T(8,128)(2,1)S(1)} collective-permute-done((bf16[128,1536]{1,0:T(8,128)(2,1)S(1)}, bf16[128,1536]{1,0:T(8,128)(2,1)S(1)}, u32[]{:S(2)}, u32[]{:S(2)}) %collective-permute-start) | collective-permute-done | bytes 393248 | tf_op jit(solution)/shard_map/ppermute | solution.py:219
  84.0 15.1 %collective-permute-done.1.y_ref = bf16[128,1536]{1,0:T(8,128)(2,1)S(1)} collective-permute-done((bf16[128,1536]{1,0:T(8,128)(2,1)S(1)}, bf16[128,1536]{1,0:T(8,128)(2,1)S(1)}, u32[]{:S(2)}, u32[]{:S(2)}) %collective-permute-start.1) | collective-permute-done | bytes 393248 | tf_op jit(solution)/shard_map/ppermute | solution.py:220
  99.1 0.2 shard_map.60.far
  99.4 1.9 collective-permute-start.5
  101.3 0.9 fusion
  102.2 2.6 %collective-permute-start.4 = (bf16[128,1536]{1,0:T(8,128)(2,1)}, bf16[128,1536]{1,0:T(8,128)(2,1)}, u32[]{:S(2)}, u32[]{:S(2)}) collective-permute-start(bf16[128,1536]{1,0:T(8,128)(2,1)} %get-tuple-element.19), channel_id=1, source_target_pairs={{0,1023},{1,1020},{2,1021},{3,1022},{4,8},{5,9},{6,10},{7,11},{8,4... | collective-permute-start | bytes 1179656 | tf_op jit(solution)/shard_map/ppermute | solution.py:226
  104.8 7.2 %collective-permute-start.6 = (bf16[128,1536]{1,0:T(8,128)(2,1)}, bf16[128,1536]{1,0:T(8,128)(2,1)S(1)}, u32[]{:S(2)}, u32[]{:S(2)}) collective-permute-start(bf16[128,1536]{1,0:T(8,128)(2,1)} %get-tuple-element.18), channel_id=1, source_target_pairs={{0,1023},{1,1020},{2,1021},{3,1022},{4,8},{5,9},{6,10},{7,11},{8,4... | collective-permute-start | bytes 1179656 | tf_op jit(solution)/shard_map/ppermute | solution.py:228
  113.3 0.0 collective-permute-done.2.mate
  113.3 0.0 collective-permute-done.3.cross
  113.3 1.1 shard_map.61
  114.5 1.4 collective-permute-done.4.cross
  115.8 0.0 collective-permute-done.5.mate
  115.8 2.2 %shard_map.62 = (f32[128,1536]{1,0:T(8,128)S(1)}, bf16[128,1536]{1,0:T(8,128)(2,1)S(1)}) custom-call(f32[1]{0:T(128)} %bitcast.5.scale_ref, f32[1]{0:T(128)} %bitcast.9.bias_ref, bf16[256,1536]{1,0:T(8,128)(2,1)S(1)} %get-tuple-element.11.side.x, f32[256,1536]{1,0:T(8,128)S(1)} %get-tuple-element.13.acc, bf16[128,1536]{1,0:T(8,128)(2,1)} %collective-permute-done.4.cross, ...), custom_call_target="tpu_custom_call" | custom-call | flops 402653184 | bytes 2359296 | tf_op jit(solution)/shard_map/pallas_call | solution.py:191
  118.0 4.0 %collective-permute-start.8 = (bf16[128,1536]{1,0:T(8,128)(2,1)S(1)}, bf16[128,1536]{1,0:T(8,128)(2,1)S(1)}, u32[]{:S(2)}, u32[]{:S(2)}) collective-permute-start(bf16[128,1536]{1,0:T(8,128)(2,1)S(1)} %get-tuple-element.14.after), channel_id=1, source_target_pairs={{0,1},{1,0},{2,3},{3,2},{4,7},{5,6},{6,5},{7,4},{8,9},{9,8},{10,11... | collective-permute-start | bytes 1179656 | tf_op jit(solution)/shard_map/ppermute | solution.py:264
  122.0 1.3 shard_map.63.acc
  123.4 37.9 %collective-permute-done.6.cross = bf16[128,1536]{1,0:T(8,128)(2,1)S(1)} collective-permute-done((bf16[128,1536]{1,0:T(8,128)(2,1)}, bf16[128,1536]{1,0:T(8,128)(2,1)S(1)}, u32[]{:S(2)}, u32[]{:S(2)}) %collective-permute-start.6) | collective-permute-done | bytes 393248 | tf_op jit(solution)/shard_map/ppermute | solution.py:228
  161.2 0.0 copy-start
  161.2 0.0 copy-start.1
  161.2 2.1 %shard_map.64 = (f32[128,1536]{1,0:T(8,128)S(1)}, bf16[128,1536]{1,0:T(8,128)(2,1)S(1)}) custom-call(f32[1]{0:T(128)} %bitcast.7.scale_ref, f32[1]{0:T(128)} %bitcast.11.bias_ref, bf16[256,1536]{1,0:T(8,128)(2,1)S(1)} %get-tuple-element.10.y.side, f32[256,1536]{1,0:T(8,128)S(1)} %shard_map.63.acc, bf16[128,1536]{1,0:T(8,128)(2,1)S(1)} %collective-permute-done.6.cross, ...), custom_call_target="tpu_custom_call" | custom-call | flops 402653184 | bytes 2359296 | tf_op jit(solution)/shard_map/pallas_call | solution.py:191
  163.4 1.9 collective-permute-start.7
  165.3 16.6 %collective-permute-done.8.there = bf16[128,1536]{1,0:T(8,128)(2,1)S(1)} collective-permute-done((bf16[128,1536]{1,0:T(8,128)(2,1)S(1)}, bf16[128,1536]{1,0:T(8,128)(2,1)S(1)}, u32[]{:S(2)}, u32[]{:S(2)}) %collective-permute-start.8) | collective-permute-done | bytes 393248 | tf_op jit(solution)/shard_map/ppermute | solution.py:264
  181.9 0.0 copy-done
  181.9 0.0 copy-done.1
  181.9 0.3 shard_map.65.x_grad
  182.3 9.5 %collective-permute-done.7.there = bf16[128,1536]{1,0:T(8,128)(2,1)S(1)} collective-permute-done((bf16[128,1536]{1,0:T(8,128)(2,1)S(1)}, bf16[128,1536]{1,0:T(8,128)(2,1)S(1)}, u32[]{:S(2)}, u32[]{:S(2)}) %collective-permute-start.7) | collective-permute-done | bytes 393248 | tf_op jit(solution)/shard_map/ppermute | solution.py:265
  191.8 1.0 shard_map.66
Async XLA Ops:
  1.8 82.2 %collective-permute-start = (bf16[128,1536]{1,0:T(8,128)(2,1)S(1)}, bf16[128,1536]{1,0:T(8,128)(2,1)S(1)}, u32[]{:S(2)}, u32[]{:S(2)}) collective-permute-start(bf16[128,1536]{1,0:T(8,128)(2,1)S(1)} %get-tuple-element.21.x_ref), channel_id=1, source_target_pairs={{0,1},{1,0},{2,3},{3,2},{4,7},{5,6},{6,5},{7,4},{8,9},{9,8},{10,11... | collective-permute-start | bytes 1179656 | tf_op jit(solution)/shard_map/ppermute | solution.py:219
  17.5 81.6 %collective-permute-start.1 = (bf16[128,1536]{1,0:T(8,128)(2,1)S(1)}, bf16[128,1536]{1,0:T(8,128)(2,1)S(1)}, u32[]{:S(2)}, u32[]{:S(2)}) collective-permute-start(bf16[128,1536]{1,0:T(8,128)(2,1)S(1)} %get-tuple-element.20.y_ref), channel_id=1, source_target_pairs={{0,3},{1,2},{2,1},{3,0},{4,5},{5,4},{6,7},{7,6},{8,11},{9,10},{10,... | collective-permute-start | bytes 1179656 | tf_op jit(solution)/shard_map/ppermute | solution.py:220
  33.5 79.8 %collective-permute-start.2 = (bf16[256,1536]{1,0:T(8,128)(2,1)S(1)}, bf16[256,1536]{1,0:T(8,128)(2,1)S(1)}, u32[]{:S(2)}, u32[]{:S(2)}) collective-permute-start(bf16[256,1536]{1,0:T(8,128)(2,1)S(1)} %shard_map.59.own), channel_id=1, source_target_pairs={{0,4},{1,5},{2,6},{3,7},{4,0},{5,1},{6,2},{7,3},{8,12},{9,13},{10,... | collective-permute-start | bytes 2359304 | tf_op jit(solution)/shard_map/ppermute | solution.py:223
  35.5 77.9 %collective-permute-start.3 = (bf16[256,1536]{1,0:T(8,128)(2,1)S(1)}, bf16[256,1536]{1,0:T(8,128)(2,1)S(1)}, u32[]{:S(2)}, u32[]{:S(2)}) collective-permute-start(bf16[256,1536]{1,0:T(8,128)(2,1)S(1)} %shard_map.59.own), channel_id=1, source_target_pairs={{0,1023},{1,1020},{2,1021},{3,1022},{4,8},{5,9},{6,10},{7,11},{8,4... | collective-permute-start | bytes 2359304 | tf_op jit(solution)/shard_map/ppermute | solution.py:222
  99.4 16.5 %collective-permute-start.5 = (bf16[256,1536]{1,0:T(8,128)(2,1)S(1)}, bf16[256,1536]{1,0:T(8,128)(2,1)}, u32[]{:S(2)}, u32[]{:S(2)}) collective-permute-start(bf16[256,1536]{1,0:T(8,128)(2,1)S(1)} %shard_map.60.far), channel_id=1, source_target_pairs={{0,4},{1,5},{2,6},{3,7},{4,0},{5,1},{6,2},{7,3},{8,12},{9,13},{10,... | collective-permute-start | bytes 2359304 | tf_op jit(solution)/shard_map/ppermute | solution.py:227
  102.2 13.6 %collective-permute-start.4 = (bf16[128,1536]{1,0:T(8,128)(2,1)}, bf16[128,1536]{1,0:T(8,128)(2,1)}, u32[]{:S(2)}, u32[]{:S(2)}) collective-permute-start(bf16[128,1536]{1,0:T(8,128)(2,1)} %get-tuple-element.19), channel_id=1, source_target_pairs={{0,1023},{1,1020},{2,1021},{3,1022},{4,8},{5,9},{6,10},{7,11},{8,4... | collective-permute-start | bytes 1179656 | tf_op jit(solution)/shard_map/ppermute | solution.py:226
  104.8 56.4 %collective-permute-start.6 = (bf16[128,1536]{1,0:T(8,128)(2,1)}, bf16[128,1536]{1,0:T(8,128)(2,1)S(1)}, u32[]{:S(2)}, u32[]{:S(2)}) collective-permute-start(bf16[128,1536]{1,0:T(8,128)(2,1)} %get-tuple-element.18), channel_id=1, source_target_pairs={{0,1023},{1,1020},{2,1021},{3,1022},{4,8},{5,9},{6,10},{7,11},{8,4... | collective-permute-start | bytes 1179656 | tf_op jit(solution)/shard_map/ppermute | solution.py:228
  118.0 63.9 %collective-permute-start.8 = (bf16[128,1536]{1,0:T(8,128)(2,1)S(1)}, bf16[128,1536]{1,0:T(8,128)(2,1)S(1)}, u32[]{:S(2)}, u32[]{:S(2)}) collective-permute-start(bf16[128,1536]{1,0:T(8,128)(2,1)S(1)} %get-tuple-element.14.after), channel_id=1, source_target_pairs={{0,1},{1,0},{2,3},{3,2},{4,7},{5,6},{6,5},{7,4},{8,9},{9,8},{10,11... | collective-permute-start | bytes 1179656 | tf_op jit(solution)/shard_map/ppermute | solution.py:264
  161.2 20.7 %copy-start = (bf16[128,1536]{1,0:T(8,128)(2,1)S(1)}, bf16[128,1536]{1,0:T(8,128)(2,1)}, u32[]{:S(2)}) copy-start(bf16[128,1536]{1,0:T(8,128)(2,1)} %img_raw.3) | copy-start | bytes 1179652
  161.2 20.7 %copy-start.1 = (bf16[128,1536]{1,0:T(8,128)(2,1)S(1)}, bf16[128,1536]{1,0:T(8,128)(2,1)}, u32[]{:S(2)}) copy-start(bf16[128,1536]{1,0:T(8,128)(2,1)} %txt_raw.3) | copy-start | bytes 1179652
  163.4 28.4 %collective-permute-start.7 = (bf16[128,1536]{1,0:T(8,128)(2,1)S(1)}, bf16[128,1536]{1,0:T(8,128)(2,1)S(1)}, u32[]{:S(2)}, u32[]{:S(2)}) collective-permute-start(bf16[128,1536]{1,0:T(8,128)(2,1)S(1)} %get-tuple-element.16), channel_id=1, source_target_pairs={{0,3},{1,2},{2,1},{3,0},{4,5},{5,4},{6,7},{7,6},{8,11},{9,10},{10,... | collective-permute-start | bytes 1179656 | tf_op jit(solution)/shard_map/ppermute | solution.py:265
